TPU v7x, 32 devices: a whole 2x2x4 slice. The times are simulated.
32 devices in a mesh: gx: 4 (over z), gy: 2 (over y), gz: 4 (over x, core).
Axes of the slice: x: 2, y: 2, z: 4, core: 2. Of those that a mesh axis runs over, the one named last changes fastest.
Arguments:
- saved_heat_state: float32 [32, 32, 512], P('gx', 'gy', 'gz'), may hold values from 0 to 1
- forward_motion: float32 [3, 32, 32, 512], P(None, 'gx', 'gy', 'gz'), may hold values from -1 to 1
- dual_heat_after: float32 [32, 32, 512], P('gx', 'gy', 'gz'), may hold values from -1 to 6
- rheology_class: int32 [32, 32, 512], P('gx', 'gy', 'gz'), may hold values from 0 to 7, as said below
- class_base_stiffness: float32 [8], replicated, may hold values from 0.01 to 100
Outputs:
- adj_temp_prev: float32 [32, 32, 512], P('gx', 'gy', 'gz')
- adj_velocity: float32 [3, 32, 32, 512], P(None, 'gx', 'gy', 'gz')
- adj_pressure: float32 [32, 32, 512], P('gx', 'gy', 'gz')
Inputs may be any that keep to these rules, and one draw needn't show every extreme that they name: `rheology_class`: each cell's viscosity class.
All inputs are finite; a program needn't handle non-finite values.
Results may differ from a plain program's by a relative error of at most 0.0003.
Values sent between devices are 32-bit elements; how exact they have to be, the bound alone decides.
No kernel may reach another device: no remote copies, remote signals or barrier semaphores. Data moves between devices by JAX's collectives and lax.ppermute only.
A program may use at most 128 MiB of HBM per device.

v0:
```python
import jax
import jax.numpy as jnp
from jax import lax
from jax.sharding import PartitionSpec as P

RECOMPUTE = 2
SCHUR_ITERS = 4
COARSE_SWEEPS = 3
LAYERS = 8


INCREMENT_DT = 0.2
DIFFUSIVITY = 0.3
ACTIVATION_ENERGY = 2.3
JACOBI_WEIGHT = 0.7
SCHUR_WEIGHT = 0.5
RAYLEIGH = 1.0


def extended(block, sides, width):
    for axis, dim in sides:
        count = lax.axis_size(axis)
        forward = [(i, i + 1) for i in range(count - 1)]
        backward = [(target, source) for source, target in forward]
        low = lax.ppermute(
            lax.slice_in_dim(block, block.shape[dim] - width, None, axis=dim), axis, forward
        )
        high = lax.ppermute(lax.slice_in_dim(block, 0, width, axis=dim), axis, backward)
        block = jnp.concatenate([low, block, high], axis=dim)
    return block


def neighbours(bordered_array):
    centre = bordered_array[..., 1:-1, 1:-1, 1:-1]
    beside_all = [
        bordered_array[..., 2:, 1:-1, 1:-1],
        bordered_array[..., :-2, 1:-1, 1:-1],
        bordered_array[..., 1:-1, 2:, 1:-1],
        bordered_array[..., 1:-1, :-2, 1:-1],
        bordered_array[..., 1:-1, 1:-1, 2:],
        bordered_array[..., 1:-1, 1:-1, :-2],
    ]
    return (centre, beside_all)


def finest_halo_cells(field):
    return extended(field, (("gx", 1), ("gy", 2), ("gz", 3)), 1)


def deep_halo(field):
    return extended(field, (("gx", 1), ("gy", 2), ("gz", 3)), 2)


def coarse_halo(field):
    return extended(field, (("gx", 1), ("gy", 2), ("gz", 3)), 1)


def march_backward(bordered_array, shallower_adjacent, deeper_adjacent):
    centre, beside_all = neighbours(bordered_array)
    drift = 0.0
    for dim_index in range(3):
        drift = (
            drift
            + shallower_adjacent[dim_index] * (centre - beside_all[2 * dim_index + 1])
            + deeper_adjacent[dim_index] * (beside_all[2 * dim_index] - centre)
        )
    spread = sum(beside_all) - 6.0 * centre
    return centre - INCREMENT_DT * drift + INCREMENT_DT * DIFFUSIVITY * spread


def motion_source(bordered_heat, forward_motion, dual_heat_after):
    centre, beside_all = neighbours(bordered_heat)
    device_pieces = [
        jnp.where(
            forward_motion[dim_index] > 0,
            centre - beside_all[2 * dim_index + 1],
            beside_all[2 * dim_index] - centre,
        )
        for dim_index in range(3)
    ]
    return -INCREMENT_DT * dual_heat_after[None] * jnp.stack(device_pieces)


def advect_dual_heat(pos_padded, neg_padded, lam_padded):
    centre, beside_all = neighbours(lam_padded)
    result = centre + INCREMENT_DT * DIFFUSIVITY * (sum(beside_all) - 6.0 * centre)
    for dim_index in range(3):
        pos_centre, pos_around = neighbours(pos_padded[dim_index])
        neg_centre, neg_around = neighbours(neg_padded[dim_index])
        result = result - INCREMENT_DT * (
            pos_centre - pos_around[2 * dim_index] + neg_around[2 * dim_index + 1] - neg_centre
        )
    return result


def coefficients(bordered_array, factor):
    centre, beside_all = neighbours(bordered_array)
    return [factor * (0.5 * (centre + other)) for other in beside_all]


def apply_operator(face_coef, bordered_array):
    centre, beside_all = neighbours(bordered_array)
    return sum((coef * (centre - other) for coef, other in zip(face_coef, beside_all)))


def gradient(bordered_array):
    centre, beside_all = neighbours(bordered_array)
    return jnp.stack(
        [
            0.5 * (beside_all[2 * dim_index] - beside_all[2 * dim_index + 1])
            for dim_index in range(3)
        ]
    )


def divergence(bordered_array):
    centre, beside_all = neighbours(bordered_array)
    return sum(
        (
            0.5 * (beside_all[2 * dim_index][dim_index] - beside_all[2 * dim_index + 1][dim_index])
            for dim_index in range(3)
        )
    )


def restrict(field):
    leading = field.shape[:-3]
    cells_x, cells_y, cells_z = field.shape[-3:]
    blocks = field.reshape(leading + (cells_x // 2, 2, cells_y // 2, 2, cells_z // 2, 2))
    return blocks.mean(axis=(-5, -3, -1))


def prolong(field):
    return jnp.repeat(jnp.repeat(jnp.repeat(field, 2, axis=-3), 2, axis=-2), 2, axis=-1)


def evaluate_viscosity(rheology_class, class_base_stiffness):
    base = jnp.zeros(rheology_class.shape, jnp.float32)
    for layer_index in range(LAYERS):
        base = base + jnp.where(
            rheology_class == layer_index, class_base_stiffness[layer_index], 0.0
        )
    return base


def inside_mask(extent_first, extent_second, extent_vertical):
    index_x = (
        lax.axis_index("gx") * extent_first + jnp.arange(extent_first + 2, dtype=jnp.int32) - 1
    )
    index_y = (
        lax.axis_index("gy") * extent_second + jnp.arange(extent_second + 2, dtype=jnp.int32) - 1
    )
    index_z = (
        lax.axis_index("gz") * extent_vertical
        + jnp.arange(extent_vertical + 2, dtype=jnp.int32)
        - 1
    )
    inside_x = (index_x >= 0) & (index_x < extent_first * lax.axis_size("gx"))
    inside_y = (index_y >= 0) & (index_y < extent_second * lax.axis_size("gy"))
    inside_z = (index_z >= 0) & (index_z < extent_vertical * lax.axis_size("gz"))
    return inside_x[:, None, None] & inside_y[None, :, None] & inside_z[None, None, :]


def coarse_solve(coarse_res, coarse_coef, coarse_diag, pad_field):
    coarse_corr = JACOBI_WEIGHT * coarse_res / coarse_diag
    for sweep in range(COARSE_SWEEPS - 1):
        coarse_corr = (
            coarse_corr
            + JACOBI_WEIGHT
            * (coarse_res - apply_operator(coarse_coef, pad_field(coarse_corr)))
            / coarse_diag
        )
    return coarse_corr


def shards(saved_heat_state, forward_motion, dual_heat_after, rheology_class, class_base_stiffness):
    extent_first, extent_second, extent_vertical = saved_heat_state.shape
    shallower_adjacent = jnp.maximum(forward_motion, 0.0)
    deeper_adjacent = jnp.minimum(forward_motion, 0.0)
    heat_state = saved_heat_state
    for repeat_index in range(RECOMPUTE):
        heat_state = march_backward(
            finest_halo_cells(heat_state[None])[0], shallower_adjacent, deeper_adjacent
        )
    local_viscosity = evaluate_viscosity(rheology_class, class_base_stiffness) * jnp.exp(
        -ACTIVATION_ENERGY * heat_state
    )
    stacked = jnp.concatenate(
        [
            heat_state[None],
            dual_heat_after[None],
            shallower_adjacent * dual_heat_after[None],
            deeper_adjacent * dual_heat_after[None],
            local_viscosity[None],
        ],
        0,
    )
    bordered_array = finest_halo_cells(stacked)
    driving_source = motion_source(bordered_array[0], forward_motion, dual_heat_after)
    advected_result = advect_dual_heat(bordered_array[2:5], bordered_array[5:8], bordered_array[1])
    face_coef = coefficients(bordered_array[8], 1.0)
    diagonal = sum(face_coef)
    coarse_visc = restrict(local_viscosity)
    coarse_coef = coefficients(coarse_halo(coarse_visc[None])[0], 0.25)
    coarse_diag = sum(coarse_coef)
    deep_static = deep_halo(jnp.concatenate([local_viscosity[None], driving_source], 0))
    cycle_coef = coefficients(deep_static[0], 1.0)
    cycle_source = deep_static[1:4, 1:-1, 1:-1, 1:-1]
    inside = inside_mask(extent_first, extent_second, extent_vertical)
    safe_diag = jnp.where(inside, sum(cycle_coef), 1.0)
    total_cells = (
        extent_first
        * extent_second
        * extent_vertical
        * lax.axis_size("gx")
        * lax.axis_size("gy")
        * lax.axis_size("gz")
    )
    velocity = jnp.zeros(forward_motion.shape, jnp.float32)
    mean_stress = jnp.zeros(saved_heat_state.shape, jnp.float32)
    for iteration in range(SCHUR_ITERS):
        if iteration == 0:
            cycle_resid = cycle_source
        else:
            flow_press = deep_halo(jnp.concatenate([velocity, mean_stress[None]], 0))
            cycle_resid = (
                cycle_source - apply_operator(cycle_coef, flow_press[0:3]) - gradient(flow_press[3])
            )
        cycle_corr = jnp.where(inside, JACOBI_WEIGHT * cycle_resid / safe_diag, 0.0)
        residual = cycle_resid[:, 1:-1, 1:-1, 1:-1]
        correction = cycle_corr[:, 1:-1, 1:-1, 1:-1]
        residual_two = residual - apply_operator(face_coef, cycle_corr)
        coarse_res = restrict(residual_two)
        coarse_corr = coarse_solve(coarse_res, coarse_coef, coarse_diag, coarse_halo)
        correction = correction + prolong(coarse_corr)
        correction = (
            correction
            + JACOBI_WEIGHT
            * (residual - apply_operator(face_coef, finest_halo_cells(correction)))
            / diagonal
        )
        velocity = velocity + correction
        spread_flow = divergence(finest_halo_cells(velocity))
        mean_stress = mean_stress - SCHUR_WEIGHT * local_viscosity * spread_flow
        mean_stress = mean_stress - lax.psum(jnp.sum(mean_stress), ("gx", "gy", "gz")) / total_cells
    adj_temp_prev = advected_result + RAYLEIGH * velocity[2]
    return (adj_temp_prev, velocity, mean_stress)


def solution(mesh):
    in_specs = (
        P("gx", "gy", "gz"),
        P(None, "gx", "gy", "gz"),
        P("gx", "gy", "gz"),
        P("gx", "gy", "gz"),
        P(),
    )
    out_specs = (P("gx", "gy", "gz"), P(None, "gx", "gy", "gz"), P("gx", "gy", "gz"))
    return jax.shard_map(shards, mesh=mesh, in_specs=in_specs, out_specs=out_specs, check_vma=False)
```

profile of v0, /device:TPU:0, one launch (start us, length us, event | category | flops | bytes accessed | tf_op | source)
XLA Modules:
  0.0 922.8 jit_solution(5318571380137040410)
XLA Ops:
  1.3 4.9 collective-permute-start
  54.6 5.0 constant_dynamic-update-slice_fusion
  59.6 5.6 reshape.181
  72.6 4.5 collective-permute-start.12
  87.8 4.2 collective-permute-done.15
  99.5 4.5 collective-permute-start.28
  110.3 4.5 collective-permute-start.18
  133.2 4.7 collective-permute-done.23
  142.9 13.9 %reshape.180 = f32[3,4,2,8,2,64,2]{6,5,4,3,2,1,0:T(8,128)} reshape(f32[3,8,16,128]{3,2,1,0:T(8,128)S(1)} %fusion.185) | data formatting | bytes 393216 | tf_op jit(solution)/shard_map/reshape | solution.py:129
  156.8 5.5 reduce_sum.81
  166.0 4.2 collective-permute-done.30
  178.8 6.8 collective-permute-start.35
  190.1 4.2 collective-permute-done.36
  215.9 4.2 collective-permute-done.42
  223.5 4.2 collective-permute-done.44
  229.3 5.5 collective-permute-start.47
  240.2 4.2 collective-permute-done.48
  247.8 4.2 collective-permute-done.50
  253.5 7.6 collective-permute-start.53
  263.2 46.9 %psum.28 = f32[]{:T(128)} all-reduce(f32[]{:T(128)} %get-tuple-element.33), channel_id=1, replica_groups=mesh['gx'=4,'gy'=2,'gz'=4] {'gx','gy','gz'}, use_global_device_ids=true, to_apply=%region_3.4 | all-reduce | flops 1 | bytes 8 | tf_op jit(solution)/shard_map/psum | solution.py:245
  316.5 4.3 collective-permute-done.55
  320.8 4.4 collective-permute-start.56
  334.6 4.2 collective-permute-done.59
  345.3 13.9 %reshape.185 = f32[3,4,2,8,2,64,2]{6,5,4,3,2,1,0:T(8,128)} reshape(f32[3,8,16,128]{3,2,1,0:T(8,128)S(1)} %fusion.152) | data formatting | bytes 393216 | tf_op jit(solution)/shard_map/reshape | solution.py:129
  359.3 5.6 reduce_sum.84
  368.8 4.2 collective-permute-done.60
  381.7 6.8 collective-permute-start.65
  393.0 4.2 collective-permute-done.66
  418.8 4.2 collective-permute-done.72
  426.4 4.2 collective-permute-done.74
  432.1 5.5 collective-permute-start.77
  444.3 4.2 collective-permute-done.78
  451.9 4.2 collective-permute-done.80
  457.6 7.6 collective-permute-start.83
  467.3 47.0 %psum.29 = f32[]{:T(128)} all-reduce(f32[]{:T(128)} %get-tuple-element.29), channel_id=1, replica_groups=mesh['gx'=4,'gy'=2,'gz'=4] {'gx','gy','gz'}, use_global_device_ids=true, to_apply=%region_6.7 | all-reduce | flops 1 | bytes 8 | tf_op jit(solution)/shard_map/psum | solution.py:245
  520.7 4.3 collective-permute-done.85
  525.1 4.4 collective-permute-start.86
  538.6 4.5 collective-permute-done.89
  550.4 13.9 %reshape.189 = f32[3,4,2,8,2,64,2]{6,5,4,3,2,1,0:T(8,128)} reshape(f32[3,8,16,128]{3,2,1,0:T(8,128)S(1)} %fusion.118) | data formatting | bytes 393216 | tf_op jit(solution)/shard_map/reshape | solution.py:129
  564.3 5.6 reduce_sum.86
  573.9 4.2 collective-permute-done.90
  586.7 6.8 collective-permute-start.95
  598.0 4.2 collective-permute-done.96
  622.3 4.2 collective-permute-done.102
  629.9 4.2 collective-permute-done.104
  635.8 5.5 collective-permute-start.107
  648.0 4.2 collective-permute-done.108
  655.6 4.2 collective-permute-done.110
  661.3 7.6 collective-permute-start.113
  671.0 46.9 %psum.30 = f32[]{:T(128)} all-reduce(f32[]{:T(128)} %get-tuple-element.25), channel_id=1, replica_groups=mesh['gx'=4,'gy'=2,'gz'=4] {'gx','gy','gz'}, use_global_device_ids=true, to_apply=%region_9.10 | all-reduce | flops 1 | bytes 8 | tf_op jit(solution)/shard_map/psum | solution.py:245
  724.3 4.3 collective-permute-done.115
  728.6 4.4 collective-permute-start.116
  742.1 4.5 collective-permute-done.119
  754.0 13.9 %reshape.193 = f32[3,4,2,8,2,64,2]{6,5,4,3,2,1,0:T(8,128)} reshape(f32[3,8,16,128]{3,2,1,0:T(8,128)S(1)} %fusion.84) | data formatting | bytes 393216 | tf_op jit(solution)/shard_map/reshape | solution.py:129
  767.9 5.5 reduce_sum.88
  777.4 4.2 collective-permute-done.120
  790.2 6.8 collective-permute-start.125
  825.6 4.2 collective-permute-done.132
  833.3 4.2 collective-permute-done.134
  839.0 5.5 collective-permute-start.137
  851.2 4.2 collective-permute-done.138
  858.8 4.2 collective-permute-done.140
  864.6 7.6 collective-permute-start.143
  874.2 46.9 %psum.31 = f32[]{:T(128)} all-reduce(f32[]{:T(128)} %get-tuple-element.21), channel_id=1, replica_groups=mesh['gx'=4,'gy'=2,'gz'=4] {'gx','gy','gz'}, use_global_device_ids=true, to_apply=%region_12.13 | all-reduce | flops 1 | bytes 8 | tf_op jit(solution)/shard_map/psum | solution.py:245
  (707 shorter events, 396.3 us)
Async XLA Ops:
  1.3 8.1 collective-permute-start
  67.8 10.7 %collective-permute-start.24 = (f32[1,1,8,64]{3,2,1,0:T(8,128)S(1)}, f32[1,1,8,64]{3,2,1,0:T(8,128)S(1)}, u32[]{:S(2)}, u32[]{:S(2)}) collective-permute-start(f32[1,1,8,64]{3,2,1,0:T(8,128)S(1)} %get-tuple-element.246), channel_id=1, source_target_pairs={{0,8},{8,16},{16,24},{1,9},{9,17},{17,25},{2,10},{10,18},{18,26},{... | collective-permute-start | bytes 6152 | tf_op jit(solution)/shard_map/ppermute | solution.py:25
  71.3 7.2 collective-permute-start.25
  72.6 8.9 collective-permute-start.12
  77.1 6.2 collective-permute-start.13
  78.5 8.9 collective-permute-start.26
  80.2 7.3 collective-permute-start.27
  86.1 6.0 collective-permute-start.15
  94.5 11.5 %collective-permute-start.17 = (f32[9,10,18,1]{2,3,1,0:T(1,128)S(1)}, f32[9,10,18,1]{2,3,1,0:T(1,128)}, u32[]{:S(2)}, u32[]{:S(2)}) collective-permute-start(f32[9,10,18,1]{2,3,1,0:T(1,128)S(1)} %copy.1185), channel_id=1, source_target_pairs={{1,0},{2,1},{3,2},{5,4},{6,5},{7,6},{9,8},{10,9},{11,10},{13,12},{... | collective-permute-start | bytes 19448 | tf_op jit(solution)/shard_map/ppermute | solution.py:28
  95.8 9.6 %collective-permute-start.16 = (f32[9,10,18,1]{2,3,1,0:T(1,128)}, f32[9,10,18,1]{2,3,1,0:T(1,128)S(1)}, u32[]{:S(2)}, u32[]{:S(2)}) collective-permute-start(f32[9,10,18,1]{2,3,1,0:T(1,128)} %copy.1184), channel_id=1, source_target_pairs={{0,1},{1,2},{2,3},{4,5},{5,6},{6,7},{8,9},{9,10},{10,11},{12,13},{... | collective-permute-start | bytes 19448 | tf_op jit(solution)/shard_map/ppermute | solution.py:25
  99.5 16.6 %collective-permute-start.28 = (f32[1,6,10,1]{3,2,1,0:T(8,128)}, f32[1,6,10,1]{3,2,1,0:T(8,128)S(1)}, u32[]{:S(2)}, u32[]{:S(2)}) collective-permute-start(f32[1,6,10,1]{3,2,1,0:T(8,128)} %get-tuple-element.242), channel_id=1, source_target_pairs={{0,1},{1,2},{2,3},{4,5},{5,6},{6,7},{8,9},{9,10},{10,11},{12,13},{... | collective-permute-start | bytes 728 | tf_op jit(solution)/shard_map/ppermute | solution.py:25
  104.0 12.1 %collective-permute-start.29 = (f32[1,6,10,1]{3,2,1,0:T(8,128)}, f32[1,6,10,1]{3,2,1,0:T(8,128)}, u32[]{:S(2)}, u32[]{:S(2)}) collective-permute-start(f32[1,6,10,1]{3,2,1,0:T(8,128)} %get-tuple-element.243), channel_id=1, source_target_pairs={{1,0},{2,1},{3,2},{5,4},{6,5},{7,6},{9,8},{10,9},{11,10},{13,12},{... | collective-permute-start | bytes 728 | tf_op jit(solution)/shard_map/ppermute | solution.py:28
  110.3 6.8 collective-permute-start.18
  114.9 6.5 collective-permute-start.19
  123.2 6.0 collective-permute-start.21
  130.9 7.0 collective-permute-start.23
  177.5 8.1 collective-permute-start.34
  178.8 7.8 collective-permute-start.35
  214.4 5.7 collective-permute-start.42
  222.1 5.6 collective-permute-start.44
  228.0 6.8 collective-permute-start.46
  229.3 6.8 collective-permute-start.47
  238.7 5.7 collective-permute-start.48
  252.2 8.9 collective-permute-start.52
  253.5 8.9 collective-permute-start.53
  310.7 5.7 collective-permute-start.54
  314.6 6.2 collective-permute-start.55
  320.8 6.1 collective-permute-start.56
  325.2 6.0 collective-permute-start.57
  332.9 6.0 collective-permute-start.59
  380.4 8.1 collective-permute-start.64
  381.7 7.8 collective-permute-start.65
  417.3 5.7 collective-permute-start.72
  430.8 6.9 collective-permute-start.76
  432.1 6.8 collective-permute-start.77
  442.8 5.7 collective-permute-start.78
  456.3 8.9 collective-permute-start.82
  457.6 8.9 collective-permute-start.83
  515.0 5.7 collective-permute-start.84
  518.8 6.2 collective-permute-start.85
  525.1 6.1 collective-permute-start.86
  529.5 6.0 collective-permute-start.87
  537.1 6.0 collective-permute-start.89
  585.4 8.1 collective-permute-start.94
  586.7 7.8 collective-permute-start.95
  620.8 5.7 collective-permute-start.102
  634.3 7.1 collective-permute-start.106
  635.8 6.8 collective-permute-start.107
  646.5 5.7 collective-permute-start.108
  660.0 8.9 collective-permute-start.112
  661.3 8.9 collective-permute-start.113
  718.5 5.7 collective-permute-start.114
  722.4 6.2 collective-permute-start.115
  728.6 6.1 collective-permute-start.116
  733.0 6.0 collective-permute-start.117
  740.7 6.0 collective-permute-start.119
  788.9 8.1 collective-permute-start.124
  790.2 7.8 collective-permute-start.125
  824.1 5.7 collective-permute-start.132
  837.7 6.9 collective-permute-start.136
  839.0 6.8 collective-permute-start.137
  849.7 5.7 collective-permute-start.138
  863.3 10.0 %collective-permute-start.142 = (f32[3,10,18,1]{3,2,1,0:T(8,128)S(1)}, f32[3,10,18,1]{3,2,1,0:T(8,128)S(1)}, u32[]{:S(2)}, u32[]{:S(2)}) collective-permute-start(f32[3,10,18,1]{3,2,1,0:T(8,128)S(1)} %get-tuple-element.115), channel_id=1, source_target_pairs={{1,0},{2,1},{3,2},{5,4},{6,5},{7,6},{9,8},{10,9},{11,10},{13,12},{... | collective-permute-start | bytes 6488 | tf_op jit(solution)/shard_map/ppermute | solution.py:28
  864.6 8.9 collective-permute-start.143
  (199 other events, 4038.2 us)
where the time goes:
time: 936 us; the launch traced here: 923 us
  starting transfers between devices  324 us (35%)
  waiting for transfers between devices  237 us (25%)
  blocking collectives  188 us (20%)
  local copies, waits for them, and re-layouts  98.3 us (11%)
  other arithmetic  68.1 us (7%)
    ppermute x72, starting transfers between devices, extended(): lax.ppermute(lax.slice_in_dim(block, block.shape[dim] - width, None, axis...  230 us
    ppermute x72, waiting for transfers between devices, extended(): lax.ppermute(lax.slice_in_dim(block, 0, width, axis=dim), axis, backward)  213 us
    psum x4, blocking collectives, shards(): lax.psum(jnp.sum(mean_stress), ('gx', 'gy', 'gz')) / total_cells  188 us
    ppermute x72, starting transfers between devices, extended(): lax.ppermute(lax.slice_in_dim(block, 0, width, axis=dim), axis, backward)  93.8 us
    reshape x5, local copies, waits for them, and re-layouts, restrict(): field.reshape(leading + (cells_x // 2, 2, cells_y // 2, 2, cells_z // 2, 2))  61.2 us
    reduce_sum x5, other arithmetic, restrict(): return blocks.mean(axis=(-5, -3, -1))  24.7 us
    ppermute x72, waiting for transfers between devices, extended(): lax.ppermute(lax.slice_in_dim(block, block.shape[dim] - width, None, axis...  24.2 us
  transfers between devices with their start and end apart: 144, of which 110 were waited for; matrix products, arithmetic and copies ran while one was open for 1% of the time, Pallas kernels for 0%

commit v1 on v0

--- a/solution.py
+++ b/solution.py
@@ -1,6 +1,10 @@
+import functools
+
 import jax
 import jax.numpy as jnp
 from jax import lax
+from jax.experimental import pallas as pl
+from jax.experimental.pallas import tpu as pltpu
 from jax.sharding import PartitionSpec as P
 
 RECOMPUTE = 2
@@ -247,6 +251,604 @@
     return (adj_temp_prev, velocity, mean_stress)
 
 
+SUB = 8
+LANES = 128
+FIELDS = 6
+EDGE = 2
+PHASE = 8
+VMEM_LIMIT = 48 * 1024 * 1024
+
+
+def slab_plan_fits(mesh, shape):
+    sizes = mesh.shape
+    group = sizes["gx"] * sizes["gy"]
+    block = (shape[0] // sizes["gx"], shape[1] // sizes["gy"], shape[2] // sizes["gz"])
+    return (
+        group == SUB
+        and block[0] == SUB
+        and block[0] * block[1] == LANES
+        and block[1] * group == LANES
+        and block[2] == LANES
+        and block[2] == group * 2 * PHASE
+    )
+
+
+class Slabs:
+    def __init__(self, mesh, shape):
+        self.nx, self.ny, self.nz = mesh.shape["gx"], mesh.shape["gy"], mesh.shape["gz"]
+        self.group = self.nx * self.ny
+        self.width, self.breadth, self.height = shape
+        self.block_x, self.block_y, self.block_z = (
+            shape[0] // self.nx,
+            shape[1] // self.ny,
+            shape[2] // self.nz,
+        )
+        self.slab = self.block_z // self.group
+        self.halo = self.slab + EDGE
+        self.layers = self.slab + 2 * self.halo
+        self.cells = self.width * self.breadth * self.height
+        self.place = []
+        for ix in range(self.nx):
+            for iy in range(self.ny):
+                step = ix if iy % 2 == 0 else self.nx - 1 - ix
+                self.place.append(iy * self.nx + step)
+        self.holder = [self.place.index(j) for j in range(self.group)]
+
+    def device(self, slab):
+        return self.holder[slab % self.group] * self.nz + slab // self.group
+
+    def shifts(self, distance):
+        count = self.group * self.nz
+        return [
+            (self.device(p), self.device(p + distance))
+            for p in range(count)
+            if 0 <= p + distance < count
+        ]
+
+    def index(self):
+        ix, iy = lax.axis_index("gx"), lax.axis_index("gy")
+        step = jnp.where(iy % 2 == 0, ix, self.nx - 1 - ix)
+        return lax.axis_index("gz") * self.group + iy * self.nx + step
+
+
+def tile_iota():
+    s = lax.broadcasted_iota(jnp.int32, (1, SUB, LANES), 1)
+    l = lax.broadcasted_iota(jnp.int32, (1, SUB, LANES), 2)
+    return s, l
+
+
+def swap_granules(tiles, granule):
+    lane = lax.broadcasted_iota(jnp.int32, (SUB, LANES), 1) // granule
+    for bit in (1, 2, 4):
+        low = (lane & bit) == 0
+        new = list(tiles)
+        for a in range(SUB):
+            if a & bit:
+                continue
+            b = a | bit
+            new[a] = jnp.where(low, tiles[a], pltpu.roll(tiles[b], granule * bit, 1))
+            new[b] = jnp.where(low, pltpu.roll(tiles[a], LANES - granule * bit, 1), tiles[b])
+        tiles = new
+    return tiles
+
+
+class Tiles:
+    def __init__(self, breadth):
+        self.breadth = breadth
+        self.s, self.l = tile_iota()
+        self.x = (self.l // breadth) * SUB + self.s
+        self.y = self.l % breadth
+        self.width = SUB * (LANES // breadth)
+
+    def xs(self, f, d):
+        t = pltpu.roll(f, (-d) % SUB, 1)
+        u = pltpu.roll(t, (-self.breadth if d > 0 else self.breadth) % LANES, 2)
+        crosses = (self.s >= SUB - d) if d > 0 else (self.s < -d)
+        return jnp.where(crosses, u, t)
+
+    def ys(self, f, d):
+        return pltpu.roll(f, (-d) % LANES, 2)
+
+    def masks(self, d, value):
+        keep = (
+            self.x < self.width - d,
+            self.x >= d,
+            self.y < self.breadth - d,
+            self.y >= d,
+        )
+        return [jnp.where(k, jnp.float32(value), jnp.float32(0.0)) for k in keep]
+
+    def four(self, f, d):
+        return [self.xs(f, d), self.xs(f, -d), self.ys(f, d), self.ys(f, -d)]
+
+    def block_sum(self, f):
+        f = f + jnp.where(self.l % 2 == 0, pltpu.roll(f, LANES - 1, 2), pltpu.roll(f, 1, 2))
+        return f + jnp.where(self.s % 2 == 0, pltpu.roll(f, SUB - 1, 1), pltpu.roll(f, 1, 1))
+
+
+def get(ref, i, n, *lead):
+    return ref[(*lead, pl.ds(pl.multiple_of(i * SUB, SUB), n * SUB), slice(None))].reshape(
+        n, SUB, LANES
+    )
+
+
+def put(ref, i, value, *lead):
+    n = value.shape[0]
+    ref[(*lead, pl.ds(pl.multiple_of(i * SUB, SUB), n * SUB), slice(None))] = value.reshape(
+        n * SUB, LANES
+    )
+
+
+def sweep(lo, hi, n, body):
+    assert (hi - lo) % n == 0
+    lax.fori_loop(0, (hi - lo) // n, lambda t, _: (body(lo + t * n), 0)[1], 0)
+
+
+def pack_kernel(geo, heat, flow, dual, kind, out):
+    b, e = geo.slab, EDGE
+    flat = [heat[...], flow[0], flow[1], flow[2], dual[...], kind[...].astype(jnp.float32)]
+    turned = [f.reshape(LANES, LANES).T for f in flat]
+    for j in range(geo.group):
+        q = geo.holder[j]
+        for f in range(FIELDS):
+            out[q, f * b : (f + 1) * b, :] = turned[f][j * b : (j + 1) * b]
+        tail = FIELDS * b
+        first = jnp.concatenate([turned[f][j * b : j * b + e] for f in range(4)], 0)
+        last = jnp.concatenate([turned[f][(j + 1) * b - e : (j + 1) * b] for f in range(4)], 0)
+        out[q, tail : tail + SUB, :] = first
+        out[q, tail + SUB : tail + 2 * SUB, :] = last
+
+
+STATIC_FINE = ("s0", "s1", "s2", "visc", "w", "diag", "cxp", "cxm", "cyp", "cym", "cz")
+STATIC_COARSE = ("kxp", "kxm", "kyp", "kym", "kzp", "kzm")
+
+
+def iterate(geo, st, v, p, res, cor, cor2, cc0, cc1, seqs, lo, hi, first):
+    tl = Tiles(geo.breadth)
+    half = tl.masks(1, 0.5)
+    comps = [3 * q + k for q in seqs for k in range(3)]
+    keep = 1.0 - JACOBI_WEIGHT
+
+    def faces(i, n):
+        c = [get(st[name], i, n) for name in ("cxp", "cxm", "cyp", "cym")]
+        return c, get(st["cz"], i, n), get(st["cz"], i - 1, n)
+
+    def around(coef, ref, i, n, *lead):
+        (c, up, down) = coef
+        f = get(ref, i, n, *lead)
+        total = up * get(ref, i + 1, n, *lead) + down * get(ref, i - 1, n, *lead)
+        for a, b in zip(c, tl.four(f, 1)):
+            total = total + a * b
+        return f, total
+
+    def residual(i):
+        n = 4
+        coef = None if first else faces(i, n)
+        w = get(st["w"], i, n)
+        for q in seqs:
+            if not (first and q == 0):
+                pq = get(p, i, n, q)
+                xp, xm, yp, ym = tl.four(pq, 1)
+                slope = [
+                    half[0] * xp - half[1] * xm,
+                    half[2] * yp - half[3] * ym,
+                    0.5 * (get(p, i + 1, n, q) - get(p, i - 1, n, q)),
+                ]
+            for k in range(3):
+                value = get(st["s%d" % k], i, n) if q == 0 else None
+                if not (first and q == 0):
+                    value = -slope[k] if value is None else value - slope[k]
+                if not first:
+                    f, total = around(coef, v, i, n, 3 * q + k)
+                    value = value - (get(st["diag"], i, n) * f - total)
+                put(res, i, value, 3 * q + k)
+                put(cor, i, w * value, 3 * q + k)
+
+    sweep(lo - 8, hi + 8, 4, residual)
+
+    def restricted(i):
+        m = 1
+        pair = i // 2
+        coef = faces(i, 2 * m)
+        for c in comps:
+            _, total = around(coef, cor, i, 2 * m, c)
+            left = keep * get(res, i, 2 * m, c) + total
+            left = tl.block_sum(left.reshape(m, 2, SUB, LANES).sum(1))
+            put(cc0, pair, get(st["wc"], pair, m) * 0.125 * left, c)
+
+    sweep(lo - 6, hi + 6, 2, restricted)
+
+    def coarse_step(src, c, pair, m):
+        f = get(src, pair, m, c)
+        value = get(cc0, pair, m, c) + keep * f
+        value = value + get(st["kzp"], pair, m) * get(src, pair + 1, m, c)
+        value = value + get(st["kzm"], pair, m) * get(src, pair - 1, m, c)
+        for name, b in zip(("kxp", "kxm", "kyp", "kym"), tl.four(f, 2)):
+            value = value + get(st[name], pair, m) * b
+        return value
+
+    def sweep_one(pair):
+        for c in comps:
+            put(cc1, pair, coarse_step(cc0, c, pair, 2), c)
+
+    sweep((lo - 4) // 2, (hi + 4) // 2, 2, sweep_one)
+
+    def sweep_two(pair):
+        for c in comps:
+            value = coarse_step(cc1, c, pair, 2)
+            fine = jnp.broadcast_to(value[:, None], (2, 2, SUB, LANES)).reshape(4, SUB, LANES)
+            put(cor2, 2 * pair, get(cor, 2 * pair, 4, c) + fine, c)
+
+    sweep((lo - 2) // 2, (hi + 2) // 2, 2, sweep_two)
+
+    def velocity(i):
+        n = 4
+        coef = faces(i, n)
+        w = get(st["w"], i, n)
+        for c in comps:
+            f, total = around(coef, cor2, i, n, c)
+            value = get(cor, i, n, c) + keep * f + w * total
+            if not first:
+                value = get(v, i, n, c) + value
+            put(v, i, value, c)
+
+    sweep(lo - 2, hi + 2, 4, velocity)
+
+    def pressure(i):
+        n = 4
+        visc = SCHUR_WEIGHT * get(st["visc"], i, n)
+        for q in seqs:
+            a, b = get(v, i, n, 3 * q), get(v, i, n, 3 * q + 1)
+            div = half[0] * tl.xs(a, 1) - half[1] * tl.xs(a, -1)
+            div = div + half[2] * tl.ys(b, 1) - half[3] * tl.ys(b, -1)
+            div = div + 0.5 * (get(v, i + 1, n, 3 * q + 2) - get(v, i - 1, n, 3 * q + 2))
+            if first and q == 0:
+                put(p, i, -(visc * div), q)
+            else:
+                put(p, i, get(p, i, n, q) - visc * div, q)
+
+    sweep(lo, hi, 4, pressure)
+
+
+def slab_total(geo, p, q):
+    own = get(p, geo.halo, geo.slab, q)
+    return jnp.sum(jnp.sum(own, axis=0), axis=(0, 1), keepdims=True)
+
+
+def in_lanes(values, rows):
+    lane = lax.broadcasted_iota(jnp.int32, (rows, LANES), 1)
+    out = jnp.zeros((rows, LANES), jnp.float32)
+    for k, value in values:
+        out = jnp.where(lane == k, value, out)
+    return out
+
+
+def first_kernel(geo, stiffness, own, low, high, low_edge, high_edge, *refs):
+    names = STATIC_FINE + STATIC_COARSE + ("wc",)
+    st = dict(zip(names, refs[: len(names)]))
+    moved, state, message_down, message_up, response, sums, raw, spare, heat, vc, *work = refs[
+        len(names) :
+    ]
+    v, p, res, cor, cor2, cc0, cc1 = work
+    tl = Tiles(geo.breadth)
+    b, h, n_layers = geo.slab, geo.halo, geo.layers
+    granule = geo.block_y
+
+    for source, base in ((low, EDGE), (own, h), (high, h + b)):
+
+        def place(t, _, source=source, base=base):
+            f, d = t // (b // SUB), (t % (b // SUB)) * SUB
+            row = pl.multiple_of(f * b + d, SUB)
+            tiles = [source[q, pl.ds(row, SUB), :] for q in range(geo.group)]
+            start = (f * n_layers + base + d) * SUB
+            for s, tile in enumerate(swap_granules(tiles, granule)):
+                raw[pl.ds(start + s, SUB, stride=SUB), :] = tile
+            return 0
+
+        lax.fori_loop(0, FIELDS * (b // SUB), place, 0)
+    for source, base in ((low_edge, 0), (high_edge, n_layers - EDGE)):
+        tiles = [source[q] for q in range(geo.group)]
+        for s, tile in enumerate(swap_granules(tiles, granule)):
+            spare[pl.ds(s, SUB, stride=SUB), :] = tile
+        for f in range(4):
+            start = (f * n_layers + base) * SUB
+            raw[start : start + EDGE * SUB, :] = spare[f * EDGE * SUB : (f + 1) * EDGE * SUB, :]
+
+    def field(f, i, n):
+        return get(raw, f * n_layers + i, n)
+
+    first_layer = geo.index() * b - h
+
+    def inside(i, n):
+        layer = first_layer + i + lax.broadcasted_iota(jnp.int32, (n, 1, 1), 0)
+        return (layer >= 0) & (layer < geo.height)
+
+    one = tl.masks(1, 1.0)
+
+    def masked_four(f):
+        return [m * g for m, g in zip(one, tl.four(f, 1))]
+
+    def advance(old, new):
+        def body(i):
+            n = 2
+            f = old(i, n)
+            beside = masked_four(f) + [old(i + 1, n), old(i - 1, n)]
+            drift = 0.0
+            for k in range(3):
+                flow = field(1 + k, i, n)
+                drift = drift + jnp.maximum(flow, 0.0) * (f - beside[2 * k + 1])
+                drift = drift + jnp.minimum(flow, 0.0) * (beside[2 * k] - f)
+            spread = sum(beside) - 6.0 * f
+            value = f - INCREMENT_DT * drift + INCREMENT_DT * DIFFUSIVITY * spread
+            put(heat, i, jnp.where(inside(i, n), value, 0.0), new)
+
+        return body
+
+    sweep(1, n_layers - 1, 2, advance(lambda i, n: field(0, i, n), 0))
+    sweep(2, n_layers - 2, 2, advance(lambda i, n: get(heat, i, n, 0), 1))
+
+    def viscosity(i):
+        n = 2
+        kind = field(5, i, n)
+        base = jnp.zeros(kind.shape, jnp.float32)
+        for layer in range(LAYERS):
+            base = base + jnp.where(kind == float(layer), stiffness[layer], 0.0)
+        value = base * jnp.exp(-ACTIVATION_ENERGY * get(heat, i, n, 1))
+        value = jnp.where(inside(i, n), value, 0.0)
+        put(st["visc"], i, value)
+        put(vc, i // 2, 0.125 * tl.block_sum(value[0:1] + value[1:2]))
+
+    sweep(2, n_layers - 2, 2, viscosity)
+
+    def statics(i):
+        n = 2
+        c = get(st["visc"], i, n)
+        beside = masked_four(c) + [get(st["visc"], i + 1, n), get(st["visc"], i - 1, n)]
+        face = [0.5 * (c + o) for o in beside]
+        diag = sum(face)
+        for name, m, f in zip(("cxp", "cxm", "cyp", "cym"), one, face):
+            put(st[name], i, m * f)
+        put(st["cz"], i, face[4])
+        put(st["diag"], i, diag)
+        put(st["w"], i, jnp.where(inside(i, n), JACOBI_WEIGHT / diag, 0.0))
+        f = get(heat, i, n, 1)
+        beside = masked_four(f) + [get(heat, i + 1, n, 1), get(heat, i - 1, n, 1)]
+        dual = -INCREMENT_DT * field(4, i, n)
+        for k in range(3):
+            flow = field(1 + k, i, n)
+            step = jnp.where(flow > 0, f - beside[2 * k + 1], beside[2 * k] - f)
+            put(st["s%d" % k], i, dual * step)
+
+    sweep(2, n_layers - 2, 2, statics)
+
+    two = tl.masks(2, 1.0)
+
+    def coarse_statics(pair):
+        n = 1
+        c = get(vc, pair, n)
+        beside = [m * g for m, g in zip(two, tl.four(c, 2))]
+        beside = beside + [get(vc, pair + 1, n), get(vc, pair - 1, n)]
+        face = [0.25 * (0.5 * (c + o)) for o in beside]
+        wc = JACOBI_WEIGHT / sum(face)
+        wc = jnp.where(inside(2 * pair, 1), wc, 0.0)
+        put(st["wc"], pair, wc)
+        for name, m, f in zip(STATIC_COARSE, two + [1.0, 1.0], face):
+            put(st[name], pair, wc * (m * f))
+
+    sweep(1, n_layers // 2 - 1, 1, coarse_statics)
+
+    def transport(i):
+        n = 2
+        dual = field(4, i, n)
+        up, down = field(4, i + 1, n), field(4, i - 1, n)
+        value = dual + INCREMENT_DT * DIFFUSIVITY * (
+            sum(masked_four(dual)) + up + down - 6.0 * dual
+        )
+        for k in range(3):
+            a = jnp.maximum(field(1 + k, i, n), 0.0) * dual
+            c = jnp.minimum(field(1 + k, i, n), 0.0) * dual
+            if k == 0:
+                ahead, behind = one[0] * tl.xs(a, 1), one[1] * tl.xs(c, -1)
+            elif k == 1:
+                ahead, behind = one[2] * tl.ys(a, 1), one[3] * tl.ys(c, -1)
+            else:
+                ahead = jnp.maximum(field(3, i + 1, n), 0.0) * up
+                behind = jnp.minimum(field(3, i - 1, n), 0.0) * down
+            value = value - INCREMENT_DT * (a - ahead + behind - c)
+        put(moved, i - h, value)
+
+    sweep(h, h + b, 2, transport)
+
+    def unit(i):
+        put(p, i, jnp.broadcast_to(jnp.where(inside(i, 4), 1.0, 0.0), (4, SUB, LANES)), 1)
+
+    sweep(0, n_layers, 4, unit)
+
+    work = (v, p, res, cor, cor2, cc0, cc1)
+    iterate(geo, st, *work, (0, 1), h - PHASE, h + b + PHASE, True)
+    totals = [slab_total(geo, p, 0), slab_total(geo, p, 1)]
+    for k in range(3):
+        put(response, 0, get(v, h, b, 3 + k), k)
+    put(response, 0, get(p, h, b, 1), 3)
+    iterate(geo, st, *work, (0, 1), h, h + b, False)
+    totals += [slab_total(geo, p, 0), slab_total(geo, p, 1)]
+    sums[...] = in_lanes(enumerate(totals), SUB)
+    for q in range(2):
+        for k in range(4):
+            value = get(v, h, b, 3 * q + k) if k < 3 else get(p, h, b, q)
+            put(state, 0, value, 4 * q + k)
+            if q == 0:
+                put(message_down, k * b, value)
+                put(message_up, k * b, value)
+            else:
+                put(message_down, 4 * b + k * PHASE, value[:PHASE])
+                put(message_up, 4 * b + k * PHASE, value[b - PHASE :])
+
+
+def second_kernel(geo, *refs):
+    names = STATIC_FINE + STATIC_COARSE + ("wc",)
+    st = dict(zip(names, refs[: len(names)]))
+    state, low, high, earlier, final, sums, v, p, res, cor, cor2, cc0, cc1 = refs[len(names) :]
+    b, h = geo.slab, geo.halo
+    for q in range(2):
+        for k in range(4):
+            ref, lead = (v, 3 * q + k) if k < 3 else (p, q)
+            put(ref, h, get(state, 0, b, 4 * q + k), lead)
+            thick = b if q == 0 else PHASE
+            at = k * b if q == 0 else 4 * b + k * PHASE
+            put(ref, h - thick, get(low, at, thick), lead)
+            put(ref, h + b, get(high, at, thick), lead)
+    work = (v, p, res, cor, cor2, cc0, cc1)
+    iterate(geo, st, *work, (0,), h - PHASE, h + b + PHASE, False)
+    totals = [(4, slab_total(geo, p, 0))]
+    iterate(geo, st, *work, (0, 1), h, h + b, False)
+    totals += [(5, slab_total(geo, p, 0)), (6, slab_total(geo, p, 1))]
+    row = in_lanes(totals, SUB) + earlier[...]
+    for r in range(0, sums.shape[0], SUB):
+        sums[r : r + SUB, :] = row
+    for q in range(2):
+        for k in range(3):
+            put(final, 0, get(v, h, b, 3 * q + k), 4 * q + k)
+        put(final, 0, get(p, h, b, q), 4 * q + 3)
+
+
+def means(geo, sums):
+    row = jnp.sum(sums, axis=0, keepdims=True) / geo.cells
+    lane = lax.broadcasted_iota(jnp.int32, row.shape, 1)
+
+    def at(k):
+        return jnp.sum(jnp.where(lane == k, row, 0.0), axis=1, keepdims=True)
+
+    s1, r1, s2, r2, s3, s4, r3 = [at(k) for k in range(7)]
+    m1 = s1
+    m2 = s2 - m1 * r1
+    m3 = s3 - m1 * r2 - m2 * r1
+    m4 = s4 - m1 * r3 - m2 * r2 - m3 * r1
+    return m1, m2, m3, m4
+
+
+def combine_kernel(geo, sums, final, state, response, moved, out, mixed):
+    b = geo.slab
+    m1, m2, m3, m4 = means(geo, sums[...])
+    for k in range(4):
+        value = final[k] - m1 * final[4 + k] - m2 * state[4 + k] - m3 * response[k]
+        mixed[k] = value - m4 if k == 3 else value
+    mixed[4] = moved[...] + mixed[2]
+
+    def place(t, _):
+        f, d = t // (b // SUB), (t % (b // SUB)) * SUB
+        tiles = [mixed[f, pl.ds(d * SUB + s, SUB, stride=SUB), :] for s in range(SUB)]
+        for q, tile in enumerate(swap_granules(tiles, geo.block_y)):
+            out[q, pl.ds(pl.multiple_of(f * b + d, SUB), SUB), :] = tile
+        return 0
+
+    lax.fori_loop(0, 5 * (b // SUB), place, 0)
+
+
+def unpack_kernel(geo, chunks, heat, flow, pressure):
+    b = geo.slab
+    shape = (geo.block_x, geo.block_y, geo.block_z)
+    for f in range(5):
+        rows = [chunks[geo.holder[j], f * b : (f + 1) * b, :] for j in range(geo.group)]
+        block = jnp.concatenate(rows, 0).T.reshape(shape)
+        if f < 3:
+            flow[f] = block
+        elif f == 3:
+            pressure[...] = block
+        else:
+            heat[...] = block
+
+
+def call(kernel, out, scratch, *args, smem=()):
+    f32 = jnp.float32
+    specs = [
+        pl.BlockSpec(memory_space=pltpu.SMEM if i in smem else pltpu.VMEM)
+        for i in range(len(args))
+    ]
+    return pl.pallas_call(
+        kernel,
+        out_shape=[jax.ShapeDtypeStruct(s, f32) for s in out],
+        in_specs=specs,
+        out_specs=[pl.BlockSpec(memory_space=pltpu.VMEM) for _ in out],
+        scratch_shapes=[pltpu.VMEM(s, f32) for s in scratch],
+        compiler_params=pltpu.CompilerParams(vmem_limit_bytes=VMEM_LIMIT),
+    )(*args)
+
+
+def slab_shards(geo, heat, flow, dual, kind, stiffness):
+    b, n_layers, group = geo.slab, geo.layers, geo.group
+    rows = FIELDS * b
+    (chunks,) = call(
+        functools.partial(pack_kernel, geo),
+        [(group, rows + 2 * SUB, LANES)],
+        [],
+        heat,
+        flow,
+        dual,
+        kind,
+    )
+    own = lax.all_to_all(chunks, ("gx", "gy"), 0, 0, tiled=True)
+    axes = ("gx", "gy", "gz")
+    low = lax.ppermute(own, axes, geo.shifts(1))
+    high = lax.ppermute(own, axes, geo.shifts(-1))
+    high_edge = lax.ppermute(own[:, rows : rows + SUB], axes, geo.shifts(-2))
+    low_edge = lax.ppermute(own[:, rows + SUB :], axes, geo.shifts(2))
+
+    fine, coarse = (n_layers * SUB, LANES), (n_layers // 2 * SUB, LANES)
+    n_fine, n_coarse = len(STATIC_FINE), len(STATIC_COARSE) + 1
+    slab = (b * SUB, LANES)
+    message = ((4 * b + 4 * PHASE) * SUB, LANES)
+    work = [(6, *fine), (2, *fine)] + [(6, *fine)] * 3 + [(6, *coarse)] * 2
+    *static, moved, state, down, up, response, sums = call(
+        functools.partial(first_kernel, geo),
+        [fine] * n_fine
+        + [coarse] * n_coarse
+        + [slab, (8, *slab), message, message, (4, *slab), (SUB, LANES)],
+        [(FIELDS * n_layers * SUB, LANES), (SUB * SUB, LANES), (2, *fine), coarse] + work,
+        stiffness,
+        own,
+        low,
+        high,
+        low_edge,
+        high_edge,
+        smem=(0,),
+    )
+    from_low = lax.ppermute(up, axes, geo.shifts(1))
+    from_high = lax.ppermute(down, axes, geo.shifts(-1))
+    devices = group * geo.nz
+    final, sums = call(
+        functools.partial(second_kernel, geo),
+        [(8, *slab), (devices, LANES)],
+        work,
+        *static,
+        state,
+        from_low,
+        from_high,
+        sums,
+    )
+    sums = lax.all_to_all(sums, axes, 0, 0, tiled=True)
+    (chunks,) = call(
+        functools.partial(combine_kernel, geo),
+        [(group, 5 * b, LANES)],
+        [(5, *slab)],
+        sums,
+        final,
+        state,
+        response,
+        moved,
+    )
+    chunks = lax.all_to_all(chunks, ("gx", "gy"), 0, 0, tiled=True)
+    block = (geo.block_x, geo.block_y, geo.block_z)
+    return tuple(
+        call(
+            functools.partial(unpack_kernel, geo),
+            [block, (3, *block), block],
+            [],
+            chunks,
+        )
+    )
+
+
 def solution(mesh):
     in_specs = (
         P("gx", "gy", "gz"),
@@ -256,4 +858,14 @@
         P(),
     )
     out_specs = (P("gx", "gy", "gz"), P(None, "gx", "gy", "gz"), P("gx", "gy", "gz"))
-    return jax.shard_map(shards, mesh=mesh, in_specs=in_specs, out_specs=out_specs, check_vma=False)
+
+    def program(saved_heat_state, *others):
+        shape = saved_heat_state.shape
+        plan = shards
+        if slab_plan_fits(mesh, shape):
+            plan = functools.partial(slab_shards, Slabs(mesh, shape))
+        return jax.shard_map(
+            plan, mesh=mesh, in_specs=in_specs, out_specs=out_specs, check_vma=False
+        )(saved_heat_state, *others)
+
+    return program

time: 936 us -> 141 us (0.15); the launches traced: 923 us -> 140 us
  starting transfers between devices: 324 us -> 17.9 us
  waiting for transfers between devices: 237 us -> 14.5 us
  blocking collectives: 188 us -> 45.4 us
  local copies, waits for them, and re-layouts: 98.3 us -> 3.45 us
  other arithmetic: 68.1 us -> 0 us
  Pallas kernels: 0 us -> 58.2 us
    ppermute x144 -> x6, starting transfers between devices: 324 us -> 17.9 us  [the longest x1 5.45 us: slab_shards(): low_edge = lax.ppermute(own[:, rows + SUB:], axes, geo.shifts(2))]
    ppermute x144 -> x6, waiting for transfers between devices: 237 us -> 14.5 us  [the longest x1 5.75 us: slab_shards(): from_low = lax.ppermute(up, axes, geo.shifts(1))]
    psum x4 -> x0, blocking collectives: 188 us -> none  [shards(): lax.psum(jnp.sum(mean_stress), ('gx', 'gy', 'gz')) / total_cells]
    reshape x13 -> x0, local copies, waits for them, and re-layouts: 69.2 us -> none  [the longest x5 61.2 us: restrict(): field.reshape(leading + (cells_x // 2, 2, cells_y // 2, 2, cells_z // 2, 2))]
    pallas_call x0 -> x5, Pallas kernels: none -> 58.2 us  [call(): pl.pallas_call(kernel, out_shape=[jax.ShapeDtypeStruct(s, f32) for s in o...]
    all_to_all x0 -> x3, blocking collectives: none -> 45.4 us  [the longest x1 20.3 us: slab_shards(): own = lax.all_to_all(chunks, ('gx', 'gy'), 0, 0, tiled=True)]
    reduce_sum x9 -> x0, other arithmetic: 27.7 us -> none  [the longest x5 24.7 us: restrict(): return blocks.mean(axis=(-5, -3, -1))]
    concatenate x53 -> x0, other arithmetic: 16.9 us -> none  [the longest x52 11.8 us: extended(): block = jnp.concatenate([low, block, high], axis=dim)]
  transfers between devices with their start and end apart: 144 -> 6, of which waited for: 110 -> 4; matrix products, arithmetic and copies ran while one was open for 1% -> 0% of each run, Pallas kernels for 0% -> 0%
where the time goes in v1:
time: 141 us; the launch traced here: 140 us
  Pallas kernels  58.2 us (41%)
  blocking collectives  45.4 us (32%)
  starting transfers between devices  17.9 us (13%)
  waiting for transfers between devices  14.5 us (10%)
  local copies, waits for them, and re-layouts  3.45 us (2%)
    pallas_call x5, Pallas kernels, call(): pl.pallas_call(kernel, out_shape=[jax.ShapeDtypeStruct(s, f32) for s in o...  58.2 us
    all_to_all x1, blocking collectives, slab_shards(): own = lax.all_to_all(chunks, ('gx', 'gy'), 0, 0, tiled=True)  20.3 us
    all_to_all x1, blocking collectives, slab_shards(): chunks = lax.all_to_all(chunks, ('gx', 'gy'), 0, 0, tiled=True)  13.6 us
    all_to_all x1, blocking collectives, slab_shards(): sums = lax.all_to_all(sums, axes, 0, 0, tiled=True)  11.5 us
    ppermute x1, waiting for transfers between devices, slab_shards(): from_low = lax.ppermute(up, axes, geo.shifts(1))  5.75 us
    ppermute x1, starting transfers between devices, slab_shards(): low_edge = lax.ppermute(own[:, rows + SUB:], axes, geo.shifts(2))  5.45 us
    ppermute x1, waiting for transfers between devices, slab_shards(): from_high = lax.ppermute(down, axes, geo.shifts(-1))  4.89 us
    ppermute x1, starting transfers between devices, slab_shards(): low = lax.ppermute(own, axes, geo.shifts(1))  4.57 us
  transfers between devices with their start and end apart: 6, of which 4 were waited for; matrix products, arithmetic and copies ran while one was open for 0% of the time, Pallas kernels for 0%

profile of v1, /device:TPU:0, one launch (start us, length us, event | category | flops | bytes accessed | tf_op | source)
XLA Modules:
  0.0 140.2 jit_solution(15458329239848113023)
XLA Ops:
  0.6 0.0 copy-start
  0.6 0.9 copy-done
  1.6 0.0 copy-start.1
  1.6 0.8 copy-done.1
  2.4 0.0 copy-start.2
  2.4 0.8 copy-done.2
  3.2 0.0 copy-start.3
  3.2 0.8 copy-done.3
  4.1 0.2 shard_map.76
  4.2 20.3 %all_to_all.21.own = f32[8,112,128]{2,1,0:T(8,128)S(1)} all-to-all(f32[8,112,128]{2,1,0:T(8,128)S(1)} %shard_map.76), channel_id=1, replica_groups=mesh['gx'=4,'gy'=2,'gz'=4] {'gx','gy'}, dimensions={0} | all-to-all | bytes 917504 | tf_op jit(solution)/shard_map/all_to_all | solution.py:790
  24.6 1.3 collective-permute-start.1
  25.9 4.6 %collective-permute-start = (f32[8,112,128]{2,1,0:T(8,128)S(1)}, f32[8,112,128]{2,1,0:T(8,128)S(1)}, u32[]{:S(2)}, u32[]{:S(2)}) collective-permute-start(f32[8,112,128]{2,1,0:T(8,128)S(1)} %all_to_all.21.own), channel_id=1, source_target_pairs={{0,8},{8,16},{16,24},{24,28},{28,20},{20,12},{12,4},{4,1},{1,9},{9... | collective-permute-start | bytes 1376264 | tf_op jit(solution)/shard_map/ppermute | solution.py:792
  30.4 0.0 copy-start.4
  30.5 1.3 collective-permute-start.3
  31.8 5.4 %collective-permute-start.2 = (f32[8,8,128]{2,1,0:T(8,128)S(1)}, f32[8,8,128]{2,1,0:T(8,128)S(1)}, u32[]{:S(2)}, u32[]{:S(2)}) collective-permute-start(f32[8,8,128]{2,1,0:T(8,128)S(1)} %get-tuple-element.56), channel_id=1, source_target_pairs={{0,16},{8,24},{16,28},{24,20},{28,12},{20,4},{12,1},{4,9},{1,17},{... | collective-permute-start | bytes 98312 | tf_op jit(solution)/shard_map/ppermute | solution.py:795
  37.2 1.4 collective-permute-done.3.high_edge
  38.6 2.5 %collective-permute-done.2.low_edge = f32[8,8,128]{2,1,0:T(8,128)S(1)} collective-permute-done((f32[8,8,128]{2,1,0:T(8,128)S(1)}, f32[8,8,128]{2,1,0:T(8,128)S(1)}, u32[]{:S(2)}, u32[]{:S(2)}) %collective-permute-start.2) | collective-permute-done | bytes 32800 | tf_op jit(solution)/shard_map/ppermute | solution.py:795
  41.1 0.0 collective-permute-done.1.high
  41.1 0.0 collective-permute-done.low
  41.1 0.0 copy-done.4
  41.1 38.0 %shard_map.77 = (f32[416,128]{1,0:T(8,128)S(1)}, f32[416,128]{1,0:T(8,128)S(1)}, f32[416,128]{1,0:T(8,128)S(1)}, f32[416,128]{1,0:T(8,128)S(1)}, f32[416,128]{1,...) custom-call(f32[8]{0:T(128)S(1)} %copy-done.4, ...), custom_call_target="tpu_custom_call" | custom-call | tf_op jit(solution)/shard_map/pallas_call | solution.py:768
  79.1 4.0 %collective-permute-start.4 = (f32[768,128]{1,0:T(8,128)S(1)}, f32[768,128]{1,0:T(8,128)S(1)}, u32[]{:S(2)}, u32[]{:S(2)}) collective-permute-start(f32[768,128]{1,0:T(8,128)S(1)} %get-tuple-element.48), channel_id=1, source_target_pairs={{0,8},{8,16},{16,24},{24,28},{28,20},{20,12},{12,4},{4,1},{1,9},{9... | collective-permute-start | bytes 1179656 | tf_op jit(solution)/shard_map/ppermute | solution.py:816
  83.1 1.3 collective-permute-start.5
  84.4 5.7 %collective-permute-done.4.refs_19_ = f32[768,128]{1,0:T(8,128)S(1)} collective-permute-done((f32[768,128]{1,0:T(8,128)S(1)}, f32[768,128]{1,0:T(8,128)S(1)}, u32[]{:S(2)}, u32[]{:S(2)}) %collective-permute-start.4) | collective-permute-done | bytes 393248 | tf_op jit(solution)/shard_map/ppermute | solution.py:816
  90.2 4.9 %collective-permute-done.5.refs_20_ = f32[768,128]{1,0:T(8,128)S(1)} collective-permute-done((f32[768,128]{1,0:T(8,128)S(1)}, f32[768,128]{1,0:T(8,128)S(1)}, u32[]{:S(2)}, u32[]{:S(2)}) %collective-permute-start.5) | collective-permute-done | bytes 393248 | tf_op jit(solution)/shard_map/ppermute | solution.py:817
  95.1 16.7 %shard_map.78 = (f32[8,128,128]{2,1,0:T(8,128)S(1)}, f32[32,128]{1,0:T(8,128)S(1)}) custom-call(f32[416,128]{1,0:T(8,128)S(1)} %get-tuple-element.29.refs_0_, f32[416,128]{1,0:T(8,128)S(1)} %get-tuple-element.30.refs_1_, f32[416,128]{1,0:T(8,128)S(1)} %get-tuple-element.31.refs_2_, f32[416,128]{1,0:T(8,128)S(1)} %get-tuple-element.32.refs_3_, ...), custom_call_target="tpu_custom_call" | custom-call | tf_op jit(solution)/shard_map/pallas_call | solution.py:768
  111.8 11.5 %all_to_all.22 = f32[32,1,128]{2,1,0:T(1,128)S(1)} all-to-all(f32[32,1,128]{2,1,0:T(1,128)S(1)} %bitcast.5), channel_id=1, replica_groups=mesh['gx'=4,'gy'=2,'gz'=4] {'gx','gy','gz'}, dimensions={0} | all-to-all | bytes 32768 | tf_op jit(solution)/shard_map/all_to_all | solution.py:829
  123.3 2.4 %shard_map.79 = f32[8,80,128]{2,1,0:T(8,128)S(1)} custom-call(f32[32,128]{1,0:T(8,128)S(1)} %bitcast.4, f32[8,128,128]{2,1,0:T(8,128)S(1)} %get-tuple-element.52.final, f32[8,128,128]{2,1,0:T(8,128)S(1)} %get-tuple-element.47.refs_18_.state, f32[4,128,128]{2,1,0:T(8,128)S(1)} %get-tuple-element.53.response, f32[128,128]{1,0:T(8,128)S(1)} %get-tuple-element.54.moved), custom_call_target="tpu_custom_call" | custom-call | tf_op jit(solution)/shard_map/pallas_call | solution.py:768
  125.8 13.6 %all_to_all.23.chunks = f32[8,80,128]{2,1,0:T(8,128)S(1)} all-to-all(f32[8,80,128]{2,1,0:T(8,128)S(1)} %shard_map.79), channel_id=1, replica_groups=mesh['gx'=4,'gy'=2,'gz'=4] {'gx','gy'}, dimensions={0} | all-to-all | bytes 655360 | tf_op jit(solution)/shard_map/all_to_all | solution.py:840
  139.4 0.9 shard_map.80
  (1 shorter events, 0.0 us)
Async XLA Ops:
  0.6 0.9 copy-start
  1.6 0.8 copy-start.1
  2.4 0.8 copy-start.2
  3.2 0.8 copy-start.3
  24.6 16.6 %collective-permute-start.1 = (f32[8,112,128]{2,1,0:T(8,128)S(1)}, f32[8,112,128]{2,1,0:T(8,128)S(1)}, u32[]{:S(2)}, u32[]{:S(2)}) collective-permute-start(f32[8,112,128]{2,1,0:T(8,128)S(1)} %all_to_all.21.own), channel_id=1, source_target_pairs={{8,0},{16,8},{24,16},{28,24},{20,28},{12,20},{4,12},{1,4},{9,1},{1... | collective-permute-start | bytes 1376264 | tf_op jit(solution)/shard_map/ppermute | solution.py:793
  25.9 15.3 %collective-permute-start = (f32[8,112,128]{2,1,0:T(8,128)S(1)}, f32[8,112,128]{2,1,0:T(8,128)S(1)}, u32[]{:S(2)}, u32[]{:S(2)}) collective-permute-start(f32[8,112,128]{2,1,0:T(8,128)S(1)} %all_to_all.21.own), channel_id=1, source_target_pairs={{0,8},{8,16},{16,24},{24,28},{28,20},{20,12},{12,4},{4,1},{1,9},{9... | collective-permute-start | bytes 1376264 | tf_op jit(solution)/shard_map/ppermute | solution.py:792
  30.4 10.7 %copy-start.4 = (f32[8]{0:T(128)S(1)}, f32[8]{0:T(128)}, u32[]{:S(2)}) copy-start(f32[8]{0:T(128)} %stiffness.1) | copy-start | bytes 100
  30.5 8.1 %collective-permute-start.3 = (f32[8,8,128]{2,1,0:T(8,128)S(1)}, f32[8,8,128]{2,1,0:T(8,128)S(1)}, u32[]{:S(2)}, u32[]{:S(2)}) collective-permute-start(f32[8,8,128]{2,1,0:T(8,128)S(1)} %get-tuple-element.55), channel_id=1, source_target_pairs={{16,0},{24,8},{28,16},{20,24},{12,28},{4,20},{1,12},{9,4},{17,1},{... | collective-permute-start | bytes 98312 | tf_op jit(solution)/shard_map/ppermute | solution.py:794
  31.8 9.4 %collective-permute-start.2 = (f32[8,8,128]{2,1,0:T(8,128)S(1)}, f32[8,8,128]{2,1,0:T(8,128)S(1)}, u32[]{:S(2)}, u32[]{:S(2)}) collective-permute-start(f32[8,8,128]{2,1,0:T(8,128)S(1)} %get-tuple-element.56), channel_id=1, source_target_pairs={{0,16},{8,24},{16,28},{24,20},{28,12},{20,4},{12,1},{4,9},{1,17},{... | collective-permute-start | bytes 98312 | tf_op jit(solution)/shard_map/ppermute | solution.py:795
  79.1 11.1 %collective-permute-start.4 = (f32[768,128]{1,0:T(8,128)S(1)}, f32[768,128]{1,0:T(8,128)S(1)}, u32[]{:S(2)}, u32[]{:S(2)}) collective-permute-start(f32[768,128]{1,0:T(8,128)S(1)} %get-tuple-element.48), channel_id=1, source_target_pairs={{0,8},{8,16},{16,24},{24,28},{28,20},{20,12},{12,4},{4,1},{1,9},{9... | collective-permute-start | bytes 1179656 | tf_op jit(solution)/shard_map/ppermute | solution.py:816
  83.1 11.9 %collective-permute-start.5 = (f32[768,128]{1,0:T(8,128)S(1)}, f32[768,128]{1,0:T(8,128)S(1)}, u32[]{:S(2)}, u32[]{:S(2)}) collective-permute-start(f32[768,128]{1,0:T(8,128)S(1)} %get-tuple-element.49), channel_id=1, source_target_pairs={{8,0},{16,8},{24,16},{28,24},{20,28},{12,20},{4,12},{1,4},{9,1},{1... | collective-permute-start | bytes 1179656 | tf_op jit(solution)/shard_map/ppermute | solution.py:817

commit v2 on v1

--- a/solution.py
+++ b/solution.py
@@ -254,6 +254,7 @@
 SUB = 8
 LANES = 128
 FIELDS = 6
+BACK = 9
 EDGE = 2
 PHASE = 8
 VMEM_LIMIT = 48 * 1024 * 1024
@@ -379,13 +380,46 @@
     )
 
 
-def sweep(lo, hi, n, body):
-    assert (hi - lo) % n == 0
-    lax.fori_loop(0, (hi - lo) // n, lambda t, _: (body(lo + t * n), 0)[1], 0)
-
-
-def pack_kernel(geo, heat, flow, dual, kind, out):
+def sweep(lo, hi, n, body, most=4):
+    count = (hi - lo) // n
+    assert count * n == hi - lo
+    unroll = max(u for u in range(1, most + 1) if count % u == 0)
+
+    def step(t, _):
+        todo = []
+        for u in range(unroll):
+            todo += body(lo + (t * unroll + u) * n)
+        for ref, i, value, *lead in todo:
+            put(ref, i, value, *lead)
+        return 0
+
+    lax.fori_loop(0, count // unroll, step, 0)
+
+
+def regroup(source, target, granule, count, most=3):
+    unroll = max(u for u in range(1, most + 1) if count % u == 0)
+
+    def step(t, _):
+        groups = [source(t * unroll + u) for u in range(unroll)]
+        groups = [swap_granules(tiles, granule) for tiles in groups]
+        for u in range(unroll):
+            target(t * unroll + u, groups[u])
+        return 0
+
+    lax.fori_loop(0, count // unroll, step, 0)
+
+
+def pack_kernel(geo, heat_in, flow_in, dual_in, kind_in, out, heat, flow, dual, kind, sems):
     b, e = geo.slab, EDGE
+    pairs = ((heat_in, heat), (flow_in, flow), (dual_in, dual), (kind_in, kind))
+    copies = [
+        pltpu.make_async_copy(source, target, sems.at[k])
+        for k, (source, target) in enumerate(pairs)
+    ]
+    for copy in copies:
+        copy.start()
+    for copy in copies:
+        copy.wait()
     flat = [heat[...], flow[0], flow[1], flow[2], dual[...], kind[...].astype(jnp.float32)]
     turned = [f.reshape(LANES, LANES).T for f in flat]
     for j in range(geo.group):
@@ -422,9 +456,10 @@
         return f, total
 
     def residual(i):
-        n = 4
+        n, todo = 2, []
         coef = None if first else faces(i, n)
         w = get(st["w"], i, n)
+        diag = None if first else get(st["diag"], i, n)
         for q in seqs:
             if not (first and q == 0):
                 pq = get(p, i, n, q)
@@ -440,49 +475,50 @@
                     value = -slope[k] if value is None else value - slope[k]
                 if not first:
                     f, total = around(coef, v, i, n, 3 * q + k)
-                    value = value - (get(st["diag"], i, n) * f - total)
-                put(res, i, value, 3 * q + k)
-                put(cor, i, w * value, 3 * q + k)
-
-    sweep(lo - 8, hi + 8, 4, residual)
+                    value = value - (diag * f - total)
+                todo += [(res, i, value, 3 * q + k), (cor, i, w * value, 3 * q + k)]
+        return todo
+
+    sweep(lo - 8, hi + 8, 2, residual)
 
     def restricted(i):
-        m = 1
-        pair = i // 2
-        coef = faces(i, 2 * m)
+        pair, todo = i // 2, []
+        coef = faces(i, 2)
+        wc = 0.125 * get(st["wc"], pair, 1)
         for c in comps:
-            _, total = around(coef, cor, i, 2 * m, c)
-            left = keep * get(res, i, 2 * m, c) + total
-            left = tl.block_sum(left.reshape(m, 2, SUB, LANES).sum(1))
-            put(cc0, pair, get(st["wc"], pair, m) * 0.125 * left, c)
+            _, total = around(coef, cor, i, 2, c)
+            left = keep * get(res, i, 2, c) + total
+            todo.append((cc0, pair, wc * tl.block_sum(left[0:1] + left[1:2]), c))
+        return todo
 
     sweep(lo - 6, hi + 6, 2, restricted)
 
-    def coarse_step(src, c, pair, m):
-        f = get(src, pair, m, c)
-        value = get(cc0, pair, m, c) + keep * f
-        value = value + get(st["kzp"], pair, m) * get(src, pair + 1, m, c)
-        value = value + get(st["kzm"], pair, m) * get(src, pair - 1, m, c)
+    def coarse_step(src, c, pair, n):
+        f = get(src, pair, n, c)
+        value = get(cc0, pair, n, c) + keep * f
+        value = value + get(st["kzp"], pair, n) * get(src, pair + 1, n, c)
+        value = value + get(st["kzm"], pair, n) * get(src, pair - 1, n, c)
         for name, b in zip(("kxp", "kxm", "kyp", "kym"), tl.four(f, 2)):
-            value = value + get(st[name], pair, m) * b
+            value = value + get(st[name], pair, n) * b
         return value
 
     def sweep_one(pair):
-        for c in comps:
-            put(cc1, pair, coarse_step(cc0, c, pair, 2), c)
+        return [(cc1, pair, coarse_step(cc0, c, pair, 2), c) for c in comps]
 
     sweep((lo - 4) // 2, (hi + 4) // 2, 2, sweep_one)
 
     def sweep_two(pair):
+        todo = []
         for c in comps:
             value = coarse_step(cc1, c, pair, 2)
             fine = jnp.broadcast_to(value[:, None], (2, 2, SUB, LANES)).reshape(4, SUB, LANES)
-            put(cor2, 2 * pair, get(cor, 2 * pair, 4, c) + fine, c)
+            todo.append((cor2, 2 * pair, get(cor, 2 * pair, 4, c) + fine, c))
+        return todo
 
     sweep((lo - 2) // 2, (hi + 2) // 2, 2, sweep_two)
 
     def velocity(i):
-        n = 4
+        n, todo = 2, []
         coef = faces(i, n)
         w = get(st["w"], i, n)
         for c in comps:
@@ -490,24 +526,24 @@
             value = get(cor, i, n, c) + keep * f + w * total
             if not first:
                 value = get(v, i, n, c) + value
-            put(v, i, value, c)
-
-    sweep(lo - 2, hi + 2, 4, velocity)
+            todo.append((v, i, value, c))
+        return todo
+
+    sweep(lo - 2, hi + 2, 2, velocity)
 
     def pressure(i):
-        n = 4
+        n, todo = 2, []
         visc = SCHUR_WEIGHT * get(st["visc"], i, n)
         for q in seqs:
             a, b = get(v, i, n, 3 * q), get(v, i, n, 3 * q + 1)
             div = half[0] * tl.xs(a, 1) - half[1] * tl.xs(a, -1)
             div = div + half[2] * tl.ys(b, 1) - half[3] * tl.ys(b, -1)
             div = div + 0.5 * (get(v, i + 1, n, 3 * q + 2) - get(v, i - 1, n, 3 * q + 2))
-            if first and q == 0:
-                put(p, i, -(visc * div), q)
-            else:
-                put(p, i, get(p, i, n, q) - visc * div, q)
-
-    sweep(lo, hi, 4, pressure)
+            value = -(visc * div)
+            todo.append((p, i, value if first and q == 0 else get(p, i, n, q) + value, q))
+        return todo
+
+    sweep(lo, hi, 2, pressure)
 
 
 def slab_total(geo, p, q):
@@ -536,16 +572,17 @@
 
     for source, base in ((low, EDGE), (own, h), (high, h + b)):
 
-        def place(t, _, source=source, base=base):
+        def load(t, source=source):
+            row = pl.multiple_of(t * SUB, SUB)
+            return [source[q, pl.ds(row, SUB), :] for q in range(geo.group)]
+
+        def store(t, tiles, base=base):
             f, d = t // (b // SUB), (t % (b // SUB)) * SUB
-            row = pl.multiple_of(f * b + d, SUB)
-            tiles = [source[q, pl.ds(row, SUB), :] for q in range(geo.group)]
             start = (f * n_layers + base + d) * SUB
-            for s, tile in enumerate(swap_granules(tiles, granule)):
+            for s, tile in enumerate(tiles):
                 raw[pl.ds(start + s, SUB, stride=SUB), :] = tile
-            return 0
-
-        lax.fori_loop(0, FIELDS * (b // SUB), place, 0)
+
+        regroup(load, store, granule, FIELDS * (b // SUB))
     for source, base in ((low_edge, 0), (high_edge, n_layers - EDGE)):
         tiles = [source[q] for q in range(geo.group)]
         for s, tile in enumerate(swap_granules(tiles, granule)):
@@ -580,11 +617,11 @@
                 drift = drift + jnp.minimum(flow, 0.0) * (beside[2 * k] - f)
             spread = sum(beside) - 6.0 * f
             value = f - INCREMENT_DT * drift + INCREMENT_DT * DIFFUSIVITY * spread
-            put(heat, i, jnp.where(inside(i, n), value, 0.0), new)
+            return [(heat, i, jnp.where(inside(i, n), value, 0.0), new)]
 
         return body
 
-    sweep(1, n_layers - 1, 2, advance(lambda i, n: field(0, i, n), 0))
+    sweep(1, n_layers - 1, 2, advance(lambda i, n: field(0, i, n), 0), 5)
     sweep(2, n_layers - 2, 2, advance(lambda i, n: get(heat, i, n, 0), 1))
 
     def viscosity(i):
@@ -595,8 +632,8 @@
             base = base + jnp.where(kind == float(layer), stiffness[layer], 0.0)
         value = base * jnp.exp(-ACTIVATION_ENERGY * get(heat, i, n, 1))
         value = jnp.where(inside(i, n), value, 0.0)
-        put(st["visc"], i, value)
-        put(vc, i // 2, 0.125 * tl.block_sum(value[0:1] + value[1:2]))
+        coarse = 0.125 * tl.block_sum(value[0:1] + value[1:2])
+        return [(st["visc"], i, value), (vc, i // 2, coarse)]
 
     sweep(2, n_layers - 2, 2, viscosity)
 
@@ -606,18 +643,20 @@
         beside = masked_four(c) + [get(st["visc"], i + 1, n), get(st["visc"], i - 1, n)]
         face = [0.5 * (c + o) for o in beside]
         diag = sum(face)
-        for name, m, f in zip(("cxp", "cxm", "cyp", "cym"), one, face):
-            put(st[name], i, m * f)
-        put(st["cz"], i, face[4])
-        put(st["diag"], i, diag)
-        put(st["w"], i, jnp.where(inside(i, n), JACOBI_WEIGHT / diag, 0.0))
+        todo = [
+            (st[name], i, m * f)
+            for name, m, f in zip(("cxp", "cxm", "cyp", "cym"), one, face)
+        ]
+        todo += [(st["cz"], i, face[4]), (st["diag"], i, diag)]
+        todo.append((st["w"], i, jnp.where(inside(i, n), JACOBI_WEIGHT / diag, 0.0)))
         f = get(heat, i, n, 1)
         beside = masked_four(f) + [get(heat, i + 1, n, 1), get(heat, i - 1, n, 1)]
         dual = -INCREMENT_DT * field(4, i, n)
         for k in range(3):
             flow = field(1 + k, i, n)
             step = jnp.where(flow > 0, f - beside[2 * k + 1], beside[2 * k] - f)
-            put(st["s%d" % k], i, dual * step)
+            todo.append((st["s%d" % k], i, dual * step))
+        return todo
 
     sweep(2, n_layers - 2, 2, statics)
 
@@ -631,9 +670,10 @@
         face = [0.25 * (0.5 * (c + o)) for o in beside]
         wc = JACOBI_WEIGHT / sum(face)
         wc = jnp.where(inside(2 * pair, 1), wc, 0.0)
-        put(st["wc"], pair, wc)
-        for name, m, f in zip(STATIC_COARSE, two + [1.0, 1.0], face):
-            put(st[name], pair, wc * (m * f))
+        return [(st["wc"], pair, wc)] + [
+            (st[name], pair, wc * (m * f))
+            for name, m, f in zip(STATIC_COARSE, two + [1.0, 1.0], face)
+        ]
 
     sweep(1, n_layers // 2 - 1, 1, coarse_statics)
 
@@ -655,12 +695,12 @@
                 ahead = jnp.maximum(field(3, i + 1, n), 0.0) * up
                 behind = jnp.minimum(field(3, i - 1, n), 0.0) * down
             value = value - INCREMENT_DT * (a - ahead + behind - c)
-        put(moved, i - h, value)
+        return [(moved, i - h, value)]
 
     sweep(h, h + b, 2, transport)
 
     def unit(i):
-        put(p, i, jnp.broadcast_to(jnp.where(inside(i, 4), 1.0, 0.0), (4, SUB, LANES)), 1)
+        return [(p, i, jnp.broadcast_to(jnp.where(inside(i, 4), 1.0, 0.0), (4, SUB, LANES)), 1)]
 
     sweep(0, n_layers, 4, unit)
 
@@ -672,7 +712,7 @@
     put(response, 0, get(p, h, b, 1), 3)
     iterate(geo, st, *work, (0, 1), h, h + b, False)
     totals += [slab_total(geo, p, 0), slab_total(geo, p, 1)]
-    sums[...] = in_lanes(enumerate(totals), SUB)
+    sums[...] = in_lanes(enumerate(totals), 1)
     for q in range(2):
         for k in range(4):
             value = get(v, h, b, 3 * q + k) if k < 3 else get(p, h, b, q)
@@ -688,7 +728,8 @@
 def second_kernel(geo, *refs):
     names = STATIC_FINE + STATIC_COARSE + ("wc",)
     st = dict(zip(names, refs[: len(names)]))
-    state, low, high, earlier, final, sums, v, p, res, cor, cor2, cc0, cc1 = refs[len(names) :]
+    state, low, high, earlier, response, moved, out, sums, mixed, *work = refs[len(names) :]
+    v, p, res, cor, cor2, cc0, cc1 = work
     b, h = geo.slab, geo.halo
     for q in range(2):
         for k in range(4):
@@ -698,18 +739,28 @@
             at = k * b if q == 0 else 4 * b + k * PHASE
             put(ref, h - thick, get(low, at, thick), lead)
             put(ref, h + b, get(high, at, thick), lead)
-    work = (v, p, res, cor, cor2, cc0, cc1)
     iterate(geo, st, *work, (0,), h - PHASE, h + b + PHASE, False)
     totals = [(4, slab_total(geo, p, 0))]
     iterate(geo, st, *work, (0, 1), h, h + b, False)
     totals += [(5, slab_total(geo, p, 0)), (6, slab_total(geo, p, 1))]
-    row = in_lanes(totals, SUB) + earlier[...]
-    for r in range(0, sums.shape[0], SUB):
-        sums[r : r + SUB, :] = row
-    for q in range(2):
-        for k in range(3):
-            put(final, 0, get(v, h, b, 3 * q + k), 4 * q + k)
-        put(final, 0, get(p, h, b, q), 4 * q + 3)
+    sums[...] = in_lanes(totals, 1)
+
+    m1, m2 = means(geo, earlier[...])[:2]
+    for k in range(4):
+        last = [get(p, h, b, q) if k == 3 else get(v, h, b, 3 * q + k) for q in range(2)]
+        value = last[0] - m1 * last[1] - m2 * get(state, 0, b, 4 + k)
+        put(mixed, k * b, value)
+        put(mixed, (4 + k) * b, get(response, 0, b, k))
+    put(mixed, 8 * b, get(moved, 0, b))
+
+    def load(t):
+        return [mixed[pl.ds(t * SUB * SUB + s, SUB, stride=SUB), :] for s in range(SUB)]
+
+    def store(t, tiles):
+        for q, tile in enumerate(tiles):
+            out[q, pl.ds(pl.multiple_of(t * SUB, SUB), SUB), :] = tile
+
+    regroup(load, store, geo.block_y, BACK * (b // SUB))
 
 
 def means(geo, sums):
@@ -727,42 +778,31 @@
     return m1, m2, m3, m4
 
 
-def combine_kernel(geo, sums, final, state, response, moved, out, mixed):
-    b = geo.slab
-    m1, m2, m3, m4 = means(geo, sums[...])
-    for k in range(4):
-        value = final[k] - m1 * final[4 + k] - m2 * state[4 + k] - m3 * response[k]
-        mixed[k] = value - m4 if k == 3 else value
-    mixed[4] = moved[...] + mixed[2]
-
-    def place(t, _):
-        f, d = t // (b // SUB), (t % (b // SUB)) * SUB
-        tiles = [mixed[f, pl.ds(d * SUB + s, SUB, stride=SUB), :] for s in range(SUB)]
-        for q, tile in enumerate(swap_granules(tiles, geo.block_y)):
-            out[q, pl.ds(pl.multiple_of(f * b + d, SUB), SUB), :] = tile
-        return 0
-
-    lax.fori_loop(0, 5 * (b // SUB), place, 0)
-
-
-def unpack_kernel(geo, chunks, heat, flow, pressure):
+def unpack_kernel(geo, chunks, earlier, later, heat, flow, pressure):
     b = geo.slab
     shape = (geo.block_x, geo.block_y, geo.block_z)
-    for f in range(5):
+    m3, m4 = means(geo, earlier[...] + later[...])[2:]
+
+    def block(f):
         rows = [chunks[geo.holder[j], f * b : (f + 1) * b, :] for j in range(geo.group)]
-        block = jnp.concatenate(rows, 0).T.reshape(shape)
-        if f < 3:
-            flow[f] = block
-        elif f == 3:
-            pressure[...] = block
+        return jnp.concatenate(rows, 0)
+
+    for k in range(4):
+        value = block(k) - m3 * block(4 + k)
+        if k == 3:
+            pressure[...] = (value - m4).T.reshape(shape)
         else:
-            heat[...] = block
-
-
-def call(kernel, out, scratch, *args, smem=()):
+            flow[k] = value.T.reshape(shape)
+        if k == 2:
+            heat[...] = (block(8) + value).T.reshape(shape)
+
+
+def call(kernel, out, scratch, *args, smem=(), hbm=()):
     f32 = jnp.float32
     specs = [
-        pl.BlockSpec(memory_space=pltpu.SMEM if i in smem else pltpu.VMEM)
+        pl.BlockSpec(
+            memory_space=pltpu.SMEM if i in smem else pltpu.HBM if i in hbm else pltpu.VMEM
+        )
         for i in range(len(args))
     ]
     return pl.pallas_call(
@@ -770,7 +810,7 @@
         out_shape=[jax.ShapeDtypeStruct(s, f32) for s in out],
         in_specs=specs,
         out_specs=[pl.BlockSpec(memory_space=pltpu.VMEM) for _ in out],
-        scratch_shapes=[pltpu.VMEM(s, f32) for s in scratch],
+        scratch_shapes=[pltpu.VMEM(s, f32) if isinstance(s, tuple) else s for s in scratch],
         compiler_params=pltpu.CompilerParams(vmem_limit_bytes=VMEM_LIMIT),
     )(*args)
 
@@ -778,14 +818,13 @@
 def slab_shards(geo, heat, flow, dual, kind, stiffness):
     b, n_layers, group = geo.slab, geo.layers, geo.group
     rows = FIELDS * b
+    inputs = (heat, flow, dual, kind)
     (chunks,) = call(
         functools.partial(pack_kernel, geo),
         [(group, rows + 2 * SUB, LANES)],
-        [],
-        heat,
-        flow,
-        dual,
-        kind,
+        [pltpu.VMEM(a.shape, a.dtype) for a in inputs] + [pltpu.SemaphoreType.DMA((4,))],
+        *inputs,
+        hbm=range(4),
     )
     own = lax.all_to_all(chunks, ("gx", "gy"), 0, 0, tiled=True)
     axes = ("gx", "gy", "gz")
@@ -803,7 +842,7 @@
         functools.partial(first_kernel, geo),
         [fine] * n_fine
         + [coarse] * n_coarse
-        + [slab, (8, *slab), message, message, (4, *slab), (SUB, LANES)],
+        + [slab, (8, *slab), message, message, (4, *slab), (1, LANES)],
         [(FIELDS * n_layers * SUB, LANES), (SUB * SUB, LANES), (2, *fine), coarse] + work,
         stiffness,
         own,
@@ -813,30 +852,22 @@
         high_edge,
         smem=(0,),
     )
+    earlier = lax.all_gather(sums, axes, axis=0, tiled=True)
     from_low = lax.ppermute(up, axes, geo.shifts(1))
     from_high = lax.ppermute(down, axes, geo.shifts(-1))
-    devices = group * geo.nz
-    final, sums = call(
+    chunks, sums = call(
         functools.partial(second_kernel, geo),
-        [(8, *slab), (devices, LANES)],
-        work,
+        [(group, BACK * b, LANES), (1, LANES)],
+        [(BACK * b * SUB, LANES)] + work,
         *static,
         state,
         from_low,
         from_high,
-        sums,
-    )
-    sums = lax.all_to_all(sums, axes, 0, 0, tiled=True)
-    (chunks,) = call(
-        functools.partial(combine_kernel, geo),
-        [(group, 5 * b, LANES)],
-        [(5, *slab)],
-        sums,
-        final,
-        state,
+        earlier,
         response,
         moved,
     )
+    later = lax.all_gather(sums, axes, axis=0, tiled=True)
     chunks = lax.all_to_all(chunks, ("gx", "gy"), 0, 0, tiled=True)
     block = (geo.block_x, geo.block_y, geo.block_z)
     return tuple(
@@ -845,6 +876,8 @@
             [block, (3, *block), block],
             [],
             chunks,
+            earlier,
+            later,
         )
     )
 

time: 141 us -> 173 us (1.23)
  blocking collectives: 45.4 us -> 106 us
  Pallas kernels: 58.2 us -> 36.3 us
  waiting for transfers between devices: 14.5 us -> 3.92 us
  starting transfers between devices: 17.9 us -> 21.4 us
    all_gather x0 -> x2, blocking collectives: none -> 86.1 us  [the longest x1 45.2 us: slab_shards(): later = lax.all_gather(sums, axes, axis=0, tiled=True)]
    all_to_all x2 -> x0, blocking collectives: 25.1 us -> none  [the longest x1 13.6 us: slab_shards(): chunks = lax.all_to_all(chunks, ('gx', 'gy'), 0, 0, tiled=True)]
    pallas_call x5 -> x4, Pallas kernels: 58.2 us -> 36.3 us  [call(): pl.pallas_call(kernel, out_shape=[jax.ShapeDtypeStruct(s, f32) for s in o...]
    ppermute x1, waiting for transfers between devices: 5.75 us -> 0.01 us  [slab_shards(): from_low = lax.ppermute(up, axes, geo.shifts(1))]
    ppermute x1, waiting for transfers between devices: 4.89 us -> 0.01 us  [slab_shards(): from_high = lax.ppermute(down, axes, geo.shifts(-1))]
    all_to_all x0 -> x1, starting transfers between devices: none -> 3.54 us  [slab_shards(): chunks = lax.all_to_all(chunks, ('gx', 'gy'), 0, 0, tiled=True)]
  transfers between devices with their start and end apart: 6 -> 7, of which waited for: 4 -> 2; matrix products, arithmetic and copies ran while one was open for 0% -> 0% of each run, Pallas kernels for 0% -> 0%
where the time goes in v2:
time: 173 us; the launch traced here: 172 us
  blocking collectives  106 us (61%)
  Pallas kernels  36.3 us (21%)
  starting transfers between devices  21.4 us (12%)
  waiting for transfers between devices  3.92 us (2%)
  local copies, waits for them, and re-layouts  3.45 us (2%)
    all_gather x1, blocking collectives, slab_shards(): later = lax.all_gather(sums, axes, axis=0, tiled=True)  45.2 us
    all_gather x1, blocking collectives, slab_shards(): earlier = lax.all_gather(sums, axes, axis=0, tiled=True)  40.9 us
    pallas_call x4, Pallas kernels, call(): pl.pallas_call(kernel, out_shape=[jax.ShapeDtypeStruct(s, f32) for s in o...  36.3 us
    all_to_all x1, blocking collectives, slab_shards(): own = lax.all_to_all(chunks, ('gx', 'gy'), 0, 0, tiled=True)  20.3 us
    ppermute x1, starting transfers between devices, slab_shards(): low_edge = lax.ppermute(own[:, rows + SUB:], axes, geo.shifts(2))  5.45 us
    ppermute x1, starting transfers between devices, slab_shards(): low = lax.ppermute(own, axes, geo.shifts(1))  4.57 us
    ppermute x1, starting transfers between devices, slab_shards(): from_low = lax.ppermute(up, axes, geo.shifts(1))  4 us
    all_to_all x1, starting transfers between devices, slab_shards(): chunks = lax.all_to_all(chunks, ('gx', 'gy'), 0, 0, tiled=True)  3.54 us
  transfers between devices with their start and end apart: 7, of which 2 were waited for; matrix products, arithmetic and copies ran while one was open for 0% of the time, Pallas kernels for 0%

profile of v2, /device:TPU:0, one launch (start us, length us, event | category | flops | bytes accessed | tf_op | source)
XLA Modules:
  0.0 172.3 jit_solution(13027498986722497450)
XLA Ops:
  0.6 0.0 copy-start
  0.6 0.9 copy-done
  1.6 0.0 copy-start.1
  1.6 0.8 copy-done.1
  2.4 0.0 copy-start.2
  2.4 0.8 copy-done.2
  3.2 0.0 copy-start.3
  3.2 0.8 copy-done.3
  4.1 0.7 shard_map.76
  4.8 20.3 %all_to_all.10.own = f32[8,112,128]{2,1,0:T(8,128)S(1)} all-to-all(f32[8,112,128]{2,1,0:T(8,128)S(1)} %shard_map.76), channel_id=1, replica_groups=mesh['gx'=4,'gy'=2,'gz'=4] {'gx','gy'}, dimensions={0} | all-to-all | bytes 917504 | tf_op jit(solution)/shard_map/all_to_all | solution.py:829
  25.1 1.3 collective-permute-start.1
  26.4 4.6 %collective-permute-start = (f32[8,112,128]{2,1,0:T(8,128)S(1)}, f32[8,112,128]{2,1,0:T(8,128)S(1)}, u32[]{:S(2)}, u32[]{:S(2)}) collective-permute-start(f32[8,112,128]{2,1,0:T(8,128)S(1)} %all_to_all.10.own), channel_id=1, source_target_pairs={{0,8},{8,16},{16,24},{24,28},{28,20},{20,12},{12,4},{4,1},{1,9},{9... | collective-permute-start | bytes 1376264 | tf_op jit(solution)/shard_map/ppermute | solution.py:831
  31.0 0.0 copy-start.4
  31.0 1.3 collective-permute-start.3
  32.3 5.4 %collective-permute-start.2 = (f32[8,8,128]{2,1,0:T(8,128)S(1)}, f32[8,8,128]{2,1,0:T(8,128)S(1)}, u32[]{:S(2)}, u32[]{:S(2)}) collective-permute-start(f32[8,8,128]{2,1,0:T(8,128)S(1)} %get-tuple-element.56), channel_id=1, source_target_pairs={{0,16},{8,24},{16,28},{24,20},{28,12},{20,4},{12,1},{4,9},{1,17},{... | collective-permute-start | bytes 98312 | tf_op jit(solution)/shard_map/ppermute | solution.py:834
  37.7 1.4 collective-permute-done.3.high_edge
  39.1 2.5 %collective-permute-done.2.low_edge = f32[8,8,128]{2,1,0:T(8,128)S(1)} collective-permute-done((f32[8,8,128]{2,1,0:T(8,128)S(1)}, f32[8,8,128]{2,1,0:T(8,128)S(1)}, u32[]{:S(2)}, u32[]{:S(2)}) %collective-permute-start.2) | collective-permute-done | bytes 32800 | tf_op jit(solution)/shard_map/ppermute | solution.py:834
  41.6 0.0 collective-permute-done.1.high
  41.6 0.0 collective-permute-done.low
  41.6 0.0 copy-done.4
  41.6 20.7 %shard_map.77 = (f32[416,128]{1,0:T(8,128)S(1)}, f32[416,128]{1,0:T(8,128)S(1)}, f32[416,128]{1,0:T(8,128)S(1)}, f32[416,128]{1,0:T(8,128)S(1)}, f32[416,128]{1,...) custom-call(f32[8]{0:T(128)S(1)} %copy-done.4, ...), custom_call_target="tpu_custom_call" | custom-call | tf_op jit(solution)/shard_map/pallas_call | solution.py:808
  62.3 4.0 %collective-permute-start.4 = (f32[768,128]{1,0:T(8,128)S(1)}, f32[768,128]{1,0:T(8,128)S(1)}, u32[]{:S(2)}, u32[]{:S(2)}) collective-permute-start(f32[768,128]{1,0:T(8,128)S(1)} %get-tuple-element.48), channel_id=1, source_target_pairs={{0,8},{8,16},{16,24},{24,28},{28,20},{20,12},{12,4},{4,1},{1,9},{9... | collective-permute-start | bytes 1179656 | tf_op jit(solution)/shard_map/ppermute | solution.py:856
  66.3 1.3 collective-permute-start.5
  67.6 40.9 %all-gather = f32[32,1,128]{2,1,0:T(1,128)S(1)} all-gather(f32[1,1,128]{2,1,0:T(1,128)S(1)} %bitcast.7), channel_id=1, replica_groups=mesh['gx'=4,'gy'=2,'gz'=4] {'gx','gy','gz'}, dimensions={0}, use_global_device_ids=true | all-gather | bytes 16896 | tf_op jit(solution)/shard_map/all_gather | solution.py:855
  108.5 0.0 collective-permute-done.4.refs_19_
  108.5 0.0 collective-permute-done.5.refs_20_
  108.5 14.0 %shard_map.78 = (f32[8,144,128]{2,1,0:T(8,128)}, f32[1,128]{1,0:T(1,128)S(1)}) custom-call(f32[416,128]{1,0:T(8,128)S(1)} %get-tuple-element.29.refs_0_, f32[416,128]{1,0:T(8,128)S(1)} %get-tuple-element.30.refs_1_, f32[416,128]{1,0:T(8,128)S(1)} %get-tuple-element.31.refs_2_, f32[416,128]{1,0:T(8,128)S(1)} %get-tuple-element.32.refs_3_, ...), custom_call_target="tpu_custom_call" | custom-call | tf_op jit(solution)/shard_map/pallas_call | solution.py:808
  122.6 3.5 %all-to-all-start.1 = ((f32[8,144,128]{2,1,0:T(8,128)}), f32[8,144,128]{2,1,0:T(8,128)S(1)}, u32[]{:S(2)}, u32[]{:S(2)}) async-start(f32[8,144,128]{2,1,0:T(8,128)} %get-tuple-element.53), calls=%async_computation.1 | async-start | bytes 1179648 | tf_op jit(solution)/shard_map/all_to_all | solution.py:871
  126.1 45.2 %all-gather.1 = f32[32,1,128]{2,1,0:T(1,128)S(1)} all-gather(f32[1,1,128]{2,1,0:T(1,128)S(1)} %bitcast.8), channel_id=1, replica_groups=mesh['gx'=4,'gy'=2,'gz'=4] {'gx','gy','gz'}, dimensions={0}, use_global_device_ids=true | all-gather | bytes 16896 | tf_op jit(solution)/shard_map/all_gather | solution.py:870
  171.3 0.0 all-to-all-done.1.chunks
  171.3 0.9 shard_map.79
  (1 shorter events, 0.0 us)
Async XLA Ops:
  0.6 0.9 copy-start
  1.6 0.8 copy-start.1
  2.4 0.8 copy-start.2
  3.2 0.8 copy-start.3
  25.1 16.6 %collective-permute-start.1 = (f32[8,112,128]{2,1,0:T(8,128)S(1)}, f32[8,112,128]{2,1,0:T(8,128)S(1)}, u32[]{:S(2)}, u32[]{:S(2)}) collective-permute-start(f32[8,112,128]{2,1,0:T(8,128)S(1)} %all_to_all.10.own), channel_id=1, source_target_pairs={{8,0},{16,8},{24,16},{28,24},{20,28},{12,20},{4,12},{1,4},{9,1},{1... | collective-permute-start | bytes 1376264 | tf_op jit(solution)/shard_map/ppermute | solution.py:832
  26.4 15.3 %collective-permute-start = (f32[8,112,128]{2,1,0:T(8,128)S(1)}, f32[8,112,128]{2,1,0:T(8,128)S(1)}, u32[]{:S(2)}, u32[]{:S(2)}) collective-permute-start(f32[8,112,128]{2,1,0:T(8,128)S(1)} %all_to_all.10.own), channel_id=1, source_target_pairs={{0,8},{8,16},{16,24},{24,28},{28,20},{20,12},{12,4},{4,1},{1,9},{9... | collective-permute-start | bytes 1376264 | tf_op jit(solution)/shard_map/ppermute | solution.py:831
  31.0 10.7 %copy-start.4 = (f32[8]{0:T(128)S(1)}, f32[8]{0:T(128)}, u32[]{:S(2)}) copy-start(f32[8]{0:T(128)} %stiffness.1) | copy-start | bytes 100
  31.0 8.1 %collective-permute-start.3 = (f32[8,8,128]{2,1,0:T(8,128)S(1)}, f32[8,8,128]{2,1,0:T(8,128)S(1)}, u32[]{:S(2)}, u32[]{:S(2)}) collective-permute-start(f32[8,8,128]{2,1,0:T(8,128)S(1)} %get-tuple-element.55), channel_id=1, source_target_pairs={{16,0},{24,8},{28,16},{20,24},{12,28},{4,20},{1,12},{9,4},{17,1},{... | collective-permute-start | bytes 98312 | tf_op jit(solution)/shard_map/ppermute | solution.py:833
  32.3 9.4 %collective-permute-start.2 = (f32[8,8,128]{2,1,0:T(8,128)S(1)}, f32[8,8,128]{2,1,0:T(8,128)S(1)}, u32[]{:S(2)}, u32[]{:S(2)}) collective-permute-start(f32[8,8,128]{2,1,0:T(8,128)S(1)} %get-tuple-element.56), channel_id=1, source_target_pairs={{0,16},{8,24},{16,28},{24,20},{28,12},{20,4},{12,1},{4,9},{1,17},{... | collective-permute-start | bytes 98312 | tf_op jit(solution)/shard_map/ppermute | solution.py:834
  62.3 46.2 %collective-permute-start.4 = (f32[768,128]{1,0:T(8,128)S(1)}, f32[768,128]{1,0:T(8,128)S(1)}, u32[]{:S(2)}, u32[]{:S(2)}) collective-permute-start(f32[768,128]{1,0:T(8,128)S(1)} %get-tuple-element.48), channel_id=1, source_target_pairs={{0,8},{8,16},{16,24},{24,28},{28,20},{20,12},{12,4},{4,1},{1,9},{9... | collective-permute-start | bytes 1179656 | tf_op jit(solution)/shard_map/ppermute | solution.py:856
  66.3 42.2 %collective-permute-start.5 = (f32[768,128]{1,0:T(8,128)S(1)}, f32[768,128]{1,0:T(8,128)S(1)}, u32[]{:S(2)}, u32[]{:S(2)}) collective-permute-start(f32[768,128]{1,0:T(8,128)S(1)} %get-tuple-element.49), channel_id=1, source_target_pairs={{8,0},{16,8},{24,16},{28,24},{20,28},{12,20},{4,12},{1,4},{9,1},{1... | collective-permute-start | bytes 1179656 | tf_op jit(solution)/shard_map/ppermute | solution.py:857
  122.6 48.8 %all-to-all-start.1 = ((f32[8,144,128]{2,1,0:T(8,128)}), f32[8,144,128]{2,1,0:T(8,128)S(1)}, u32[]{:S(2)}, u32[]{:S(2)}) async-start(f32[8,144,128]{2,1,0:T(8,128)} %get-tuple-element.53), calls=%async_computation.1 | async-start | bytes 1179648 | tf_op jit(solution)/shard_map/all_to_all | solution.py:871

commit v3 on v2

--- a/solution.py
+++ b/solution.py
@@ -712,7 +712,7 @@
     put(response, 0, get(p, h, b, 1), 3)
     iterate(geo, st, *work, (0, 1), h, h + b, False)
     totals += [slab_total(geo, p, 0), slab_total(geo, p, 1)]
-    sums[...] = in_lanes(enumerate(totals), 1)
+    sums[...] = in_lanes(enumerate(totals), sums.shape[0])
     for q in range(2):
         for k in range(4):
             value = get(v, h, b, 3 * q + k) if k < 3 else get(p, h, b, q)
@@ -743,7 +743,7 @@
     totals = [(4, slab_total(geo, p, 0))]
     iterate(geo, st, *work, (0, 1), h, h + b, False)
     totals += [(5, slab_total(geo, p, 0)), (6, slab_total(geo, p, 1))]
-    sums[...] = in_lanes(totals, 1)
+    sums[...] = in_lanes(totals, sums.shape[0])
 
     m1, m2 = means(geo, earlier[...])[:2]
     for k in range(4):
@@ -834,6 +834,7 @@
     low_edge = lax.ppermute(own[:, rows + SUB :], axes, geo.shifts(2))
 
     fine, coarse = (n_layers * SUB, LANES), (n_layers // 2 * SUB, LANES)
+    devices = group * geo.nz
     n_fine, n_coarse = len(STATIC_FINE), len(STATIC_COARSE) + 1
     slab = (b * SUB, LANES)
     message = ((4 * b + 4 * PHASE) * SUB, LANES)
@@ -842,7 +843,7 @@
         functools.partial(first_kernel, geo),
         [fine] * n_fine
         + [coarse] * n_coarse
-        + [slab, (8, *slab), message, message, (4, *slab), (1, LANES)],
+        + [slab, (8, *slab), message, message, (4, *slab), (devices, LANES)],
         [(FIELDS * n_layers * SUB, LANES), (SUB * SUB, LANES), (2, *fine), coarse] + work,
         stiffness,
         own,
@@ -852,12 +853,12 @@
         high_edge,
         smem=(0,),
     )
-    earlier = lax.all_gather(sums, axes, axis=0, tiled=True)
+    earlier = lax.all_to_all(sums, axes, 0, 0, tiled=True)
     from_low = lax.ppermute(up, axes, geo.shifts(1))
     from_high = lax.ppermute(down, axes, geo.shifts(-1))
     chunks, sums = call(
         functools.partial(second_kernel, geo),
-        [(group, BACK * b, LANES), (1, LANES)],
+        [(group, BACK * b, LANES), (devices, LANES)],
         [(BACK * b * SUB, LANES)] + work,
         *static,
         state,
@@ -867,7 +868,7 @@
         response,
         moved,
     )
-    later = lax.all_gather(sums, axes, axis=0, tiled=True)
+    later = lax.all_to_all(sums, axes, 0, 0, tiled=True)
     chunks = lax.all_to_all(chunks, ("gx", "gy"), 0, 0, tiled=True)
     block = (geo.block_x, geo.block_y, geo.block_z)
     return tuple(

time: 173 us -> 126 us (0.73)
  blocking collectives: 106 us -> 63.8 us
  starting transfers between devices: 21.4 us -> 17.9 us
    all_gather x2 -> x0, blocking collectives: 86.1 us -> none  [the longest x1 45.2 us: slab_shards(): later = lax.all_gather(sums, axes, axis=0, tiled=True)]
    all_to_all x0 -> x3, blocking collectives: none -> 43.5 us  [the longest x1 19.2 us: slab_shards(): chunks = lax.all_to_all(chunks, ('gx', 'gy'), 0, 0, tiled=True)]
    all_to_all x1 -> x0, starting transfers between devices: 3.54 us -> none  [slab_shards(): chunks = lax.all_to_all(chunks, ('gx', 'gy'), 0, 0, tiled=True)]
  transfers between devices with their start and end apart: 7 -> 6, of which waited for: 2 -> 2; matrix products, arithmetic and copies ran while one was open for 0% -> 0% of each run, Pallas kernels for 0% -> 0%
where the time goes in v3:
time: 126 us; the launch traced here: 125 us
  blocking collectives  63.8 us (51%)
  Pallas kernels  35.5 us (28%)
  starting transfers between devices  17.9 us (14%)
  waiting for transfers between devices  3.91 us (3%)
  local copies, waits for them, and re-layouts  3.45 us (3%)
    pallas_call x4, Pallas kernels, call(): pl.pallas_call(kernel, out_shape=[jax.ShapeDtypeStruct(s, f32) for s in o...  35.5 us
    all_to_all x1, blocking collectives, slab_shards(): own = lax.all_to_all(chunks, ('gx', 'gy'), 0, 0, tiled=True)  20.3 us
    all_to_all x1, blocking collectives, slab_shards(): chunks = lax.all_to_all(chunks, ('gx', 'gy'), 0, 0, tiled=True)  19.2 us
    all_to_all x1, blocking collectives, slab_shards(): earlier = lax.all_to_all(sums, axes, 0, 0, tiled=True)  13 us
    all_to_all x1, blocking collectives, slab_shards(): later = lax.all_to_all(sums, axes, 0, 0, tiled=True)  11.3 us
    ppermute x1, starting transfers between devices, slab_shards(): low_edge = lax.ppermute(own[:, rows + SUB:], axes, geo.shifts(2))  5.45 us
    ppermute x1, starting transfers between devices, slab_shards(): low = lax.ppermute(own, axes, geo.shifts(1))  4.57 us
    ppermute x1, starting transfers between devices, slab_shards(): from_low = lax.ppermute(up, axes, geo.shifts(1))  4 us
  transfers between devices with their start and end apart: 6, of which 2 were waited for; matrix products, arithmetic and copies ran while one was open for 0% of the time, Pallas kernels for 0%

profile of v3, /device:TPU:0, one launch (start us, length us, event | category | flops | bytes accessed | tf_op | source)
XLA Modules:
  0.0 125.3 jit_solution(11398924141189505712)
XLA Ops:
  0.6 0.0 copy-start
  0.6 0.9 copy-done
  1.6 0.0 copy-start.1
  1.6 0.8 copy-done.1
  2.4 0.0 copy-start.2
  2.4 0.8 copy-done.2
  3.2 0.0 copy-start.3
  3.2 0.8 copy-done.3
  4.1 0.7 shard_map.76
  4.8 20.3 %all_to_all.32.own = f32[8,112,128]{2,1,0:T(8,128)S(1)} all-to-all(f32[8,112,128]{2,1,0:T(8,128)S(1)} %shard_map.76), channel_id=1, replica_groups=mesh['gx'=4,'gy'=2,'gz'=4] {'gx','gy'}, dimensions={0} | all-to-all | bytes 917504 | tf_op jit(solution)/shard_map/all_to_all | solution.py:829
  25.1 1.3 %collective-permute-start.1 = (f32[8,112,128]{2,1,0:T(8,128)S(1)}, f32[8,112,128]{2,1,0:T(8,128)S(1)}, u32[]{:S(2)}, u32[]{:S(2)}) collective-permute-start(f32[8,112,128]{2,1,0:T(8,128)S(1)} %all_to_all.32.own), channel_id=1, source_target_pairs={{8,0},{16,8},{24,16},{28,24},{20,28},{12,20},{4,12},{1,4},{9,1},{1... | collective-permute-start | bytes 1376264 | tf_op jit(solution)/shard_map/ppermute | solution.py:832
  26.4 4.6 %collective-permute-start = (f32[8,112,128]{2,1,0:T(8,128)S(1)}, f32[8,112,128]{2,1,0:T(8,128)S(1)}, u32[]{:S(2)}, u32[]{:S(2)}) collective-permute-start(f32[8,112,128]{2,1,0:T(8,128)S(1)} %all_to_all.32.own), channel_id=1, source_target_pairs={{0,8},{8,16},{16,24},{24,28},{28,20},{20,12},{12,4},{4,1},{1,9},{9... | collective-permute-start | bytes 1376264 | tf_op jit(solution)/shard_map/ppermute | solution.py:831
  31.0 0.0 copy-start.4
  31.0 1.3 %collective-permute-start.3 = (f32[8,8,128]{2,1,0:T(8,128)S(1)}, f32[8,8,128]{2,1,0:T(8,128)S(1)}, u32[]{:S(2)}, u32[]{:S(2)}) collective-permute-start(f32[8,8,128]{2,1,0:T(8,128)S(1)} %get-tuple-element.55), channel_id=1, source_target_pairs={{16,0},{24,8},{28,16},{20,24},{12,28},{4,20},{1,12},{9,4},{17,1},{... | collective-permute-start | bytes 98312 | tf_op jit(solution)/shard_map/ppermute | solution.py:833
  32.3 5.4 %collective-permute-start.2 = (f32[8,8,128]{2,1,0:T(8,128)S(1)}, f32[8,8,128]{2,1,0:T(8,128)S(1)}, u32[]{:S(2)}, u32[]{:S(2)}) collective-permute-start(f32[8,8,128]{2,1,0:T(8,128)S(1)} %get-tuple-element.56), channel_id=1, source_target_pairs={{0,16},{8,24},{16,28},{24,20},{28,12},{20,4},{12,1},{4,9},{1,17},{... | collective-permute-start | bytes 98312 | tf_op jit(solution)/shard_map/ppermute | solution.py:834
  37.7 1.4 %collective-permute-done.3.high_edge = f32[8,8,128]{2,1,0:T(8,128)S(1)} collective-permute-done((f32[8,8,128]{2,1,0:T(8,128)S(1)}, f32[8,8,128]{2,1,0:T(8,128)S(1)}, u32[]{:S(2)}, u32[]{:S(2)}) %collective-permute-start.3) | collective-permute-done | bytes 32800 | tf_op jit(solution)/shard_map/ppermute | solution.py:833
  39.1 2.5 %collective-permute-done.2.low_edge = f32[8,8,128]{2,1,0:T(8,128)S(1)} collective-permute-done((f32[8,8,128]{2,1,0:T(8,128)S(1)}, f32[8,8,128]{2,1,0:T(8,128)S(1)}, u32[]{:S(2)}, u32[]{:S(2)}) %collective-permute-start.2) | collective-permute-done | bytes 32800 | tf_op jit(solution)/shard_map/ppermute | solution.py:834
  41.6 0.0 collective-permute-done.1.high
  41.6 0.0 collective-permute-done.low
  41.6 0.0 copy-done.4
  41.6 20.7 %shard_map.77 = (f32[416,128]{1,0:T(8,128)S(1)}, f32[416,128]{1,0:T(8,128)S(1)}, f32[416,128]{1,0:T(8,128)S(1)}, f32[416,128]{1,0:T(8,128)S(1)}, f32[416,128]{1,...) custom-call(f32[8]{0:T(128)S(1)} %copy-done.4, ...), custom_call_target="tpu_custom_call" | custom-call | tf_op jit(solution)/shard_map/pallas_call | solution.py:808
  62.3 4.0 %collective-permute-start.4 = (f32[768,128]{1,0:T(8,128)S(1)}, f32[768,128]{1,0:T(8,128)S(1)}, u32[]{:S(2)}, u32[]{:S(2)}) collective-permute-start(f32[768,128]{1,0:T(8,128)S(1)} %get-tuple-element.48), channel_id=1, source_target_pairs={{0,8},{8,16},{16,24},{24,28},{28,20},{20,12},{12,4},{4,1},{1,9},{9... | collective-permute-start | bytes 1179656 | tf_op jit(solution)/shard_map/ppermute | solution.py:857
  66.3 1.3 %collective-permute-start.5 = (f32[768,128]{1,0:T(8,128)S(1)}, f32[768,128]{1,0:T(8,128)S(1)}, u32[]{:S(2)}, u32[]{:S(2)}) collective-permute-start(f32[768,128]{1,0:T(8,128)S(1)} %get-tuple-element.49), channel_id=1, source_target_pairs={{8,0},{16,8},{24,16},{28,24},{20,28},{12,20},{4,12},{1,4},{9,1},{1... | collective-permute-start | bytes 1179656 | tf_op jit(solution)/shard_map/ppermute | solution.py:858
  67.6 13.0 %all_to_all.33 = f32[32,1,128]{2,1,0:T(1,128)S(1)} all-to-all(f32[32,1,128]{2,1,0:T(1,128)S(1)} %bitcast.11), channel_id=1, replica_groups=mesh['gx'=4,'gy'=2,'gz'=4] {'gx','gy','gz'}, dimensions={0} | all-to-all | bytes 32768 | tf_op jit(solution)/shard_map/all_to_all | solution.py:856
  80.6 0.0 collective-permute-done.4.refs_19_
  80.6 0.0 collective-permute-done.5.refs_20_
  80.6 13.2 %shard_map.78 = (f32[8,144,128]{2,1,0:T(8,128)S(1)}, f32[32,128]{1,0:T(8,128)S(1)}) custom-call(f32[416,128]{1,0:T(8,128)S(1)} %get-tuple-element.29.refs_0_, f32[416,128]{1,0:T(8,128)S(1)} %get-tuple-element.30.refs_1_, f32[416,128]{1,0:T(8,128)S(1)} %get-tuple-element.31.refs_2_, f32[416,128]{1,0:T(8,128)S(1)} %get-tuple-element.32.refs_3_, ...), custom_call_target="tpu_custom_call" | custom-call | tf_op jit(solution)/shard_map/pallas_call | solution.py:808
  93.9 11.3 %all_to_all.34 = f32[32,1,128]{2,1,0:T(1,128)S(1)} all-to-all(f32[32,1,128]{2,1,0:T(1,128)S(1)} %bitcast.12), channel_id=1, replica_groups=mesh['gx'=4,'gy'=2,'gz'=4] {'gx','gy','gz'}, dimensions={0} | all-to-all | bytes 32768 | tf_op jit(solution)/shard_map/all_to_all | solution.py:871
  105.1 19.2 %all_to_all.35.chunks = f32[8,144,128]{2,1,0:T(8,128)S(1)} all-to-all(f32[8,144,128]{2,1,0:T(8,128)S(1)} %get-tuple-element.53), channel_id=1, replica_groups=mesh['gx'=4,'gy'=2,'gz'=4] {'gx','gy'}, dimensions={0} | all-to-all | bytes 1179648 | tf_op jit(solution)/shard_map/all_to_all | solution.py:872
  124.4 0.9 shard_map.79
  (1 shorter events, 0.0 us)
Async XLA Ops:
  0.6 0.9 copy-start
  1.6 0.8 copy-start.1
  2.4 0.8 copy-start.2
  3.2 0.8 copy-start.3
  25.1 16.6 %collective-permute-start.1 = (f32[8,112,128]{2,1,0:T(8,128)S(1)}, f32[8,112,128]{2,1,0:T(8,128)S(1)}, u32[]{:S(2)}, u32[]{:S(2)}) collective-permute-start(f32[8,112,128]{2,1,0:T(8,128)S(1)} %all_to_all.32.own), channel_id=1, source_target_pairs={{8,0},{16,8},{24,16},{28,24},{20,28},{12,20},{4,12},{1,4},{9,1},{1... | collective-permute-start | bytes 1376264 | tf_op jit(solution)/shard_map/ppermute | solution.py:832
  26.4 15.3 %collective-permute-start = (f32[8,112,128]{2,1,0:T(8,128)S(1)}, f32[8,112,128]{2,1,0:T(8,128)S(1)}, u32[]{:S(2)}, u32[]{:S(2)}) collective-permute-start(f32[8,112,128]{2,1,0:T(8,128)S(1)} %all_to_all.32.own), channel_id=1, source_target_pairs={{0,8},{8,16},{16,24},{24,28},{28,20},{20,12},{12,4},{4,1},{1,9},{9... | collective-permute-start | bytes 1376264 | tf_op jit(solution)/shard_map/ppermute | solution.py:831
  31.0 10.7 %copy-start.4 = (f32[8]{0:T(128)S(1)}, f32[8]{0:T(128)}, u32[]{:S(2)}) copy-start(f32[8]{0:T(128)} %stiffness.1) | copy-start | bytes 100
  31.0 8.1 %collective-permute-start.3 = (f32[8,8,128]{2,1,0:T(8,128)S(1)}, f32[8,8,128]{2,1,0:T(8,128)S(1)}, u32[]{:S(2)}, u32[]{:S(2)}) collective-permute-start(f32[8,8,128]{2,1,0:T(8,128)S(1)} %get-tuple-element.55), channel_id=1, source_target_pairs={{16,0},{24,8},{28,16},{20,24},{12,28},{4,20},{1,12},{9,4},{17,1},{... | collective-permute-start | bytes 98312 | tf_op jit(solution)/shard_map/ppermute | solution.py:833
  32.3 9.4 %collective-permute-start.2 = (f32[8,8,128]{2,1,0:T(8,128)S(1)}, f32[8,8,128]{2,1,0:T(8,128)S(1)}, u32[]{:S(2)}, u32[]{:S(2)}) collective-permute-start(f32[8,8,128]{2,1,0:T(8,128)S(1)} %get-tuple-element.56), channel_id=1, source_target_pairs={{0,16},{8,24},{16,28},{24,20},{28,12},{20,4},{12,1},{4,9},{1,17},{... | collective-permute-start | bytes 98312 | tf_op jit(solution)/shard_map/ppermute | solution.py:834
  62.3 18.3 %collective-permute-start.4 = (f32[768,128]{1,0:T(8,128)S(1)}, f32[768,128]{1,0:T(8,128)S(1)}, u32[]{:S(2)}, u32[]{:S(2)}) collective-permute-start(f32[768,128]{1,0:T(8,128)S(1)} %get-tuple-element.48), channel_id=1, source_target_pairs={{0,8},{8,16},{16,24},{24,28},{28,20},{20,12},{12,4},{4,1},{1,9},{9... | collective-permute-start | bytes 1179656 | tf_op jit(solution)/shard_map/ppermute | solution.py:857
  66.3 14.3 %collective-permute-start.5 = (f32[768,128]{1,0:T(8,128)S(1)}, f32[768,128]{1,0:T(8,128)S(1)}, u32[]{:S(2)}, u32[]{:S(2)}) collective-permute-start(f32[768,128]{1,0:T(8,128)S(1)} %get-tuple-element.49), channel_id=1, source_target_pairs={{8,0},{16,8},{24,16},{28,24},{20,28},{12,20},{4,12},{1,4},{9,1},{1... | collective-permute-start | bytes 1179656 | tf_op jit(solution)/shard_map/ppermute | solution.py:858

commit v4 on v3

--- a/solution.py
+++ b/solution.py
@@ -254,7 +254,7 @@
 SUB = 8
 LANES = 128
 FIELDS = 6
-BACK = 9
+BACK = 5
 EDGE = 2
 PHASE = 8
 VMEM_LIMIT = 48 * 1024 * 1024
@@ -437,7 +437,16 @@
 STATIC_COARSE = ("kxp", "kxm", "kyp", "kym", "kzp", "kzm")
 
 
-def iterate(geo, st, v, p, res, cor, cor2, cc0, cc1, seqs, lo, hi, first):
+FORWARD, ADJOINT, RESPONSE = range(3)
+
+
+def inside(geo, i, n):
+    layer = geo.index() * geo.slab - geo.halo + i
+    layer = layer + lax.broadcasted_iota(jnp.int32, (n, 1, 1), 0)
+    return (layer >= 0) & (layer < geo.height)
+
+
+def iterate(geo, st, v, p, res, cor, cor2, cc0, cc1, seqs, lo, hi, first=(), mean=None):
     tl = Tiles(geo.breadth)
     half = tl.masks(1, 0.5)
     comps = [3 * q + k for q in seqs for k in range(3)]
@@ -455,28 +464,39 @@
             total = total + a * b
         return f, total
 
+    def spread(i, n, q):
+        if q != ADJOINT:
+            return get(p, i, n, q)
+        value = SCHUR_WEIGHT * get(st["visc"], i, n)
+        return value if q in first else value * get(p, i, n, q)
+
     def residual(i):
         n, todo = 2, []
-        coef = None if first else faces(i, n)
+        apply = FORWARD in seqs and FORWARD not in first
+        coef = faces(i, n) if apply else None
+        diag = get(st["diag"], i, n) if apply else None
         w = get(st["w"], i, n)
-        diag = None if first else get(st["diag"], i, n)
         for q in seqs:
-            if not (first and q == 0):
-                pq = get(p, i, n, q)
-                xp, xm, yp, ym = tl.four(pq, 1)
+            slope = None
+            if not (q == FORWARD and q in first):
+                xp, xm, yp, ym = tl.four(spread(i, n, q), 1)
                 slope = [
                     half[0] * xp - half[1] * xm,
                     half[2] * yp - half[3] * ym,
-                    0.5 * (get(p, i + 1, n, q) - get(p, i - 1, n, q)),
+                    0.5 * (spread(i + 1, n, q) - spread(i - 1, n, q)),
                 ]
             for k in range(3):
-                value = get(st["s%d" % k], i, n) if q == 0 else None
-                if not (first and q == 0):
-                    value = -slope[k] if value is None else value - slope[k]
-                if not first:
-                    f, total = around(coef, v, i, n, 3 * q + k)
-                    value = value - (diag * f - total)
-                todo += [(res, i, value, 3 * q + k), (cor, i, w * value, 3 * q + k)]
+                c = 3 * q + k
+                if q == FORWARD:
+                    value = get(st["s%d" % k], i, n)
+                    if slope is not None:
+                        f, total = around(coef, v, i, n, c)
+                        value = value - slope[k] - (diag * f - total)
+                elif q == RESPONSE:
+                    value = -slope[k]
+                else:
+                    value = slope[k] if q in first else get(cor, i, n, c) + slope[k]
+                todo += [(res, i, value, c), (cor, i, w * value, c)]
         return todo
 
     sweep(lo - 8, hi + 8, 2, residual)
@@ -524,7 +544,7 @@
         for c in comps:
             f, total = around(coef, cor2, i, n, c)
             value = get(cor, i, n, c) + keep * f + w * total
-            if not first:
+            if c // 3 == FORWARD and FORWARD not in first:
                 value = get(v, i, n, c) + value
             todo.append((v, i, value, c))
         return todo
@@ -534,21 +554,39 @@
     def pressure(i):
         n, todo = 2, []
         visc = SCHUR_WEIGHT * get(st["visc"], i, n)
+        coef = faces(i, n) if ADJOINT in seqs else None
         for q in seqs:
             a, b = get(v, i, n, 3 * q), get(v, i, n, 3 * q + 1)
             div = half[0] * tl.xs(a, 1) - half[1] * tl.xs(a, -1)
             div = div + half[2] * tl.ys(b, 1) - half[3] * tl.ys(b, -1)
             div = div + 0.5 * (get(v, i + 1, n, 3 * q + 2) - get(v, i - 1, n, 3 * q + 2))
+            if q == ADJOINT:
+                todo.append((p, i, get(p, i, n, q) + div, q))
+                for c in range(3 * q, 3 * q + 3):
+                    f, total = around(coef, v, i, n, c)
+                    value = get(res, i, n, c) - (get(st["diag"], i, n) * f - total)
+                    todo.append((cor, i, value, c))
+                continue
             value = -(visc * div)
-            todo.append((p, i, value if first and q == 0 else get(p, i, n, q) + value, q))
+            if not (q == FORWARD and q in first):
+                value = get(p, i, n, q) + value
+            if mean is not None:
+                value = value - jnp.where(inside(geo, i, n), mean, 0.0)
+            todo.append((p, i, value, q))
         return todo
 
     sweep(lo, hi, 2, pressure)
 
 
-def slab_total(geo, p, q):
-    own = get(p, geo.halo, geo.slab, q)
-    return jnp.sum(jnp.sum(own, axis=0), axis=(0, 1), keepdims=True)
+def total(value):
+    return jnp.sum(jnp.sum(value, axis=0), axis=(0, 1), keepdims=True)
+
+
+def product(geo, left, right):
+    value = 0.0
+    for a, b in zip(left, right):
+        value = value + get(a[0], a[1], geo.slab, *a[2:]) * get(b[0], b[1], geo.slab, *b[2:])
+    return total(value)
 
 
 def in_lanes(values, rows):
@@ -562,9 +600,7 @@
 def first_kernel(geo, stiffness, own, low, high, low_edge, high_edge, *refs):
     names = STATIC_FINE + STATIC_COARSE + ("wc",)
     st = dict(zip(names, refs[: len(names)]))
-    moved, state, message_down, message_up, response, sums, raw, spare, heat, vc, *work = refs[
-        len(names) :
-    ]
+    moved, state, sums, raw, spare, heat, vc, kept, *work = refs[len(names) :]
     v, p, res, cor, cor2, cc0, cc1 = work
     tl = Tiles(geo.breadth)
     b, h, n_layers = geo.slab, geo.halo, geo.layers
@@ -593,12 +629,6 @@
 
     def field(f, i, n):
         return get(raw, f * n_layers + i, n)
-
-    first_layer = geo.index() * b - h
-
-    def inside(i, n):
-        layer = first_layer + i + lax.broadcasted_iota(jnp.int32, (n, 1, 1), 0)
-        return (layer >= 0) & (layer < geo.height)
 
     one = tl.masks(1, 1.0)
 
@@ -617,7 +647,7 @@
                 drift = drift + jnp.minimum(flow, 0.0) * (beside[2 * k] - f)
             spread = sum(beside) - 6.0 * f
             value = f - INCREMENT_DT * drift + INCREMENT_DT * DIFFUSIVITY * spread
-            return [(heat, i, jnp.where(inside(i, n), value, 0.0), new)]
+            return [(heat, i, jnp.where(inside(geo, i, n), value, 0.0), new)]
 
         return body
 
@@ -631,7 +661,7 @@
         for layer in range(LAYERS):
             base = base + jnp.where(kind == float(layer), stiffness[layer], 0.0)
         value = base * jnp.exp(-ACTIVATION_ENERGY * get(heat, i, n, 1))
-        value = jnp.where(inside(i, n), value, 0.0)
+        value = jnp.where(inside(geo, i, n), value, 0.0)
         coarse = 0.125 * tl.block_sum(value[0:1] + value[1:2])
         return [(st["visc"], i, value), (vc, i // 2, coarse)]
 
@@ -648,7 +678,7 @@
             for name, m, f in zip(("cxp", "cxm", "cyp", "cym"), one, face)
         ]
         todo += [(st["cz"], i, face[4]), (st["diag"], i, diag)]
-        todo.append((st["w"], i, jnp.where(inside(i, n), JACOBI_WEIGHT / diag, 0.0)))
+        todo.append((st["w"], i, jnp.where(inside(geo, i, n), JACOBI_WEIGHT / diag, 0.0)))
         f = get(heat, i, n, 1)
         beside = masked_four(f) + [get(heat, i + 1, n, 1), get(heat, i - 1, n, 1)]
         dual = -INCREMENT_DT * field(4, i, n)
@@ -669,7 +699,7 @@
         beside = beside + [get(vc, pair + 1, n), get(vc, pair - 1, n)]
         face = [0.25 * (0.5 * (c + o)) for o in beside]
         wc = JACOBI_WEIGHT / sum(face)
-        wc = jnp.where(inside(2 * pair, 1), wc, 0.0)
+        wc = jnp.where(inside(geo, 2 * pair, 1), wc, 0.0)
         return [(st["wc"], pair, wc)] + [
             (st[name], pair, wc * (m * f))
             for name, m, f in zip(STATIC_COARSE, two + [1.0, 1.0], face)
@@ -700,58 +730,71 @@
     sweep(h, h + b, 2, transport)
 
     def unit(i):
-        return [(p, i, jnp.broadcast_to(jnp.where(inside(i, 4), 1.0, 0.0), (4, SUB, LANES)), 1)]
+        value = jnp.where(inside(geo, i, 4), 1.0, 0.0)
+        value = jnp.broadcast_to(value, (4, SUB, LANES))
+        return [(p, i, value, ADJOINT), (p, i, value, RESPONSE)]
 
     sweep(0, n_layers, 4, unit)
 
     work = (v, p, res, cor, cor2, cc0, cc1)
-    iterate(geo, st, *work, (0, 1), h - PHASE, h + b + PHASE, True)
-    totals = [slab_total(geo, p, 0), slab_total(geo, p, 1)]
-    for k in range(3):
-        put(response, 0, get(v, h, b, 3 + k), k)
-    put(response, 0, get(p, h, b, 1), 3)
-    iterate(geo, st, *work, (0, 1), h, h + b, False)
-    totals += [slab_total(geo, p, 0), slab_total(geo, p, 1)]
-    sums[...] = in_lanes(enumerate(totals), sums.shape[0])
-    for q in range(2):
-        for k in range(4):
-            value = get(v, h, b, 3 * q + k) if k < 3 else get(p, h, b, q)
-            put(state, 0, value, 4 * q + k)
-            if q == 0:
-                put(message_down, k * b, value)
-                put(message_up, k * b, value)
-            else:
-                put(message_down, 4 * b + k * PHASE, value[:PHASE])
-                put(message_up, 4 * b + k * PHASE, value[b - PHASE :])
+    both = (FORWARD, ADJOINT)
+    iterate(geo, st, *work, both, h - PHASE, h + b + PHASE, both)
+
+    def fields(q):
+        three = cor if q == ADJOINT else v
+        return [(three, h, 3 * q + k) for k in range(3)] + [(p, h, q)]
+
+    def count(q):
+        return total(get(p, h, b, q))
+
+    sums_of = [count(FORWARD), count(ADJOINT), product(geo, fields(ADJOINT), fields(FORWARD))]
+    for k, (ref, layer, lead) in enumerate(fields(ADJOINT)):
+        put(kept, 0, get(ref, layer, b, lead), k)
+    iterate(geo, st, *work, (FORWARD, ADJOINT, RESPONSE), h, h + b, (RESPONSE,))
+    earlier = [(kept, 0, k) for k in range(4)]
+    sums_of += [count(FORWARD), count(ADJOINT), product(geo, earlier, fields(FORWARD))]
+    sums_of += [product(geo, fields(ADJOINT), fields(q)) for q in (FORWARD, RESPONSE)]
+    sums[...] = in_lanes(enumerate(sums_of), sums.shape[0])
+    for at, q in enumerate((FORWARD, RESPONSE)):
+        for k, (ref, layer, lead) in enumerate(fields(q)):
+            put(state, 0, get(ref, layer, b, lead), 4 * at + k)
+
+
+def means(geo, sums):
+    row = jnp.sum(sums, axis=0, keepdims=True) / geo.cells
+    lane = lax.broadcasted_iota(jnp.int32, row.shape, 1)
+
+    def at(k):
+        return jnp.sum(jnp.where(lane == k, row, 0.0), axis=1, keepdims=True)
+
+    p1, q1, l1_x1, p2, q2, l1_x2, l2_x2, l2_r1 = [at(k) for k in range(8)]
+    m1 = p1
+    m2 = p2 - m1 * q1
+    m3 = l1_x2 - m1 * q2 - m2 * q1 + p1
+    m4 = l2_x2 - m1 * l2_r1 - m2 * q2 + l1_x1 - m3 * q1 + p1
+    return m1, m2, m3, m4
 
 
 def second_kernel(geo, *refs):
     names = STATIC_FINE + STATIC_COARSE + ("wc",)
     st = dict(zip(names, refs[: len(names)]))
-    state, low, high, earlier, response, moved, out, sums, mixed, *work = refs[len(names) :]
+    state, low, high, sums, moved, out, mixed, *work = refs[len(names) :]
     v, p, res, cor, cor2, cc0, cc1 = work
     b, h = geo.slab, geo.halo
-    for q in range(2):
+    m1, m2, m3, m4 = means(geo, sums[...])
+    for source, base in ((low, h - b), (state, h), (high, h + b)):
         for k in range(4):
-            ref, lead = (v, 3 * q + k) if k < 3 else (p, q)
-            put(ref, h, get(state, 0, b, 4 * q + k), lead)
-            thick = b if q == 0 else PHASE
-            at = k * b if q == 0 else 4 * b + k * PHASE
-            put(ref, h - thick, get(low, at, thick), lead)
-            put(ref, h + b, get(high, at, thick), lead)
-    iterate(geo, st, *work, (0,), h - PHASE, h + b + PHASE, False)
-    totals = [(4, slab_total(geo, p, 0))]
-    iterate(geo, st, *work, (0, 1), h, h + b, False)
-    totals += [(5, slab_total(geo, p, 0)), (6, slab_total(geo, p, 1))]
-    sums[...] = in_lanes(totals, sums.shape[0])
-
-    m1, m2 = means(geo, earlier[...])[:2]
-    for k in range(4):
-        last = [get(p, h, b, q) if k == 3 else get(v, h, b, 3 * q + k) for q in range(2)]
-        value = last[0] - m1 * last[1] - m2 * get(state, 0, b, 4 + k)
-        put(mixed, k * b, value)
-        put(mixed, (4 + k) * b, get(response, 0, b, k))
-    put(mixed, 8 * b, get(moved, 0, b))
+            value = get(source, 0, b, k) - m1 * get(source, 0, b, 4 + k)
+            if k < 3:
+                put(v, base, value, k)
+            else:
+                put(p, base, value - jnp.where(inside(geo, base, b), m2, 0.0), 0)
+    iterate(geo, st, *work, (FORWARD,), h - PHASE, h + b + PHASE, mean=m3)
+    iterate(geo, st, *work, (FORWARD,), h, h + b, mean=m4)
+    for k in range(3):
+        put(mixed, k * b, get(v, h, b, k))
+    put(mixed, 3 * b, get(p, h, b, 0))
+    put(mixed, 4 * b, get(moved, 0, b) + get(v, h, b, 2))
 
     def load(t):
         return [mixed[pl.ds(t * SUB * SUB + s, SUB, stride=SUB), :] for s in range(SUB)]
@@ -763,38 +806,18 @@
     regroup(load, store, geo.block_y, BACK * (b // SUB))
 
 
-def means(geo, sums):
-    row = jnp.sum(sums, axis=0, keepdims=True) / geo.cells
-    lane = lax.broadcasted_iota(jnp.int32, row.shape, 1)
-
-    def at(k):
-        return jnp.sum(jnp.where(lane == k, row, 0.0), axis=1, keepdims=True)
-
-    s1, r1, s2, r2, s3, s4, r3 = [at(k) for k in range(7)]
-    m1 = s1
-    m2 = s2 - m1 * r1
-    m3 = s3 - m1 * r2 - m2 * r1
-    m4 = s4 - m1 * r3 - m2 * r2 - m3 * r1
-    return m1, m2, m3, m4
-
-
-def unpack_kernel(geo, chunks, earlier, later, heat, flow, pressure):
+def unpack_kernel(geo, chunks, heat, flow, pressure):
     b = geo.slab
     shape = (geo.block_x, geo.block_y, geo.block_z)
-    m3, m4 = means(geo, earlier[...] + later[...])[2:]
-
-    def block(f):
+    for f in range(BACK):
         rows = [chunks[geo.holder[j], f * b : (f + 1) * b, :] for j in range(geo.group)]
-        return jnp.concatenate(rows, 0)
-
-    for k in range(4):
-        value = block(k) - m3 * block(4 + k)
-        if k == 3:
-            pressure[...] = (value - m4).T.reshape(shape)
+        block = jnp.concatenate(rows, 0).T.reshape(shape)
+        if f < 3:
+            flow[f] = block
+        elif f == 3:
+            pressure[...] = block
         else:
-            flow[k] = value.T.reshape(shape)
-        if k == 2:
-            heat[...] = (block(8) + value).T.reshape(shape)
+            heat[...] = block
 
 
 def call(kernel, out, scratch, *args, smem=(), hbm=()):
@@ -837,14 +860,16 @@
     devices = group * geo.nz
     n_fine, n_coarse = len(STATIC_FINE), len(STATIC_COARSE) + 1
     slab = (b * SUB, LANES)
-    message = ((4 * b + 4 * PHASE) * SUB, LANES)
-    work = [(6, *fine), (2, *fine)] + [(6, *fine)] * 3 + [(6, *coarse)] * 2
-    *static, moved, state, down, up, response, sums = call(
+
+    def work(n):
+        fields = [(3 * n, *fine), (n, *fine)] + [(3 * n, *fine)] * 3
+        return fields + [(3 * n, *coarse)] * 2
+
+    *static, moved, state, sums = call(
         functools.partial(first_kernel, geo),
-        [fine] * n_fine
-        + [coarse] * n_coarse
-        + [slab, (8, *slab), message, message, (4, *slab), (devices, LANES)],
-        [(FIELDS * n_layers * SUB, LANES), (SUB * SUB, LANES), (2, *fine), coarse] + work,
+        [fine] * n_fine + [coarse] * n_coarse + [slab, (8, *slab), (devices, LANES)],
+        [(FIELDS * n_layers * SUB, LANES), (SUB * SUB, LANES), (2, *fine), coarse, (4, *slab)]
+        + work(3),
         stiffness,
         own,
         low,
@@ -853,33 +878,24 @@
         high_edge,
         smem=(0,),
     )
-    earlier = lax.all_to_all(sums, axes, 0, 0, tiled=True)
-    from_low = lax.ppermute(up, axes, geo.shifts(1))
-    from_high = lax.ppermute(down, axes, geo.shifts(-1))
-    chunks, sums = call(
+    sums = lax.all_to_all(sums, axes, 0, 0, tiled=True)
+    from_low = lax.ppermute(state, axes, geo.shifts(1))
+    from_high = lax.ppermute(state, axes, geo.shifts(-1))
+    (chunks,) = call(
         functools.partial(second_kernel, geo),
-        [(group, BACK * b, LANES), (devices, LANES)],
-        [(BACK * b * SUB, LANES)] + work,
+        [(group, BACK * b, LANES)],
+        [(BACK * b * SUB, LANES)] + work(1),
         *static,
         state,
         from_low,
         from_high,
-        earlier,
-        response,
+        sums,
         moved,
     )
-    later = lax.all_to_all(sums, axes, 0, 0, tiled=True)
     chunks = lax.all_to_all(chunks, ("gx", "gy"), 0, 0, tiled=True)
     block = (geo.block_x, geo.block_y, geo.block_z)
     return tuple(
-        call(
-            functools.partial(unpack_kernel, geo),
-            [block, (3, *block), block],
-            [],
-            chunks,
-            earlier,
-            later,
-        )
+        call(functools.partial(unpack_kernel, geo), [block, (3, *block), block], [], chunks)
     )
 
 

time: 126 us -> 115 us (0.913)
  blocking collectives: 63.8 us -> 51 us
    all_to_all x2 -> x1, blocking collectives: 24.3 us -> 15.7 us  [slab_shards(): sums = lax.all_to_all(sums, axes, 0, 0, tiled=True)]
    all_to_all x1, blocking collectives: 19.2 us -> 14.9 us  [slab_shards(): chunks = lax.all_to_all(chunks, ('gx', 'gy'), 0, 0, tiled=True)]
where the time goes in v4:
time: 115 us; the launch traced here: 114 us
  blocking collectives  51 us (44%)
  Pallas kernels  36.5 us (32%)
  starting transfers between devices  18.6 us (16%)
  waiting for transfers between devices  3.91 us (3%)
  local copies, waits for them, and re-layouts  3.45 us (3%)
    pallas_call x4, Pallas kernels, call(): pl.pallas_call(kernel, out_shape=[jax.ShapeDtypeStruct(s, f32) for s in o...  36.5 us
    all_to_all x1, blocking collectives, slab_shards(): own = lax.all_to_all(chunks, ('gx', 'gy'), 0, 0, tiled=True)  20.3 us
    all_to_all x1, blocking collectives, slab_shards(): sums = lax.all_to_all(sums, axes, 0, 0, tiled=True)  15.7 us
    all_to_all x1, blocking collectives, slab_shards(): chunks = lax.all_to_all(chunks, ('gx', 'gy'), 0, 0, tiled=True)  14.9 us
    ppermute x1, starting transfers between devices, slab_shards(): low_edge = lax.ppermute(own[:, rows + SUB:], axes, geo.shifts(2))  5.45 us
    ppermute x1, starting transfers between devices, slab_shards(): from_low = lax.ppermute(state, axes, geo.shifts(1))  4.67 us
    ppermute x1, starting transfers between devices, slab_shards(): low = lax.ppermute(own, axes, geo.shifts(1))  4.57 us
    unnamed x10, local copies, waits for them, and re-layouts  3.44 us
  transfers between devices with their start and end apart: 6, of which 2 were waited for; matrix products, arithmetic and copies ran while one was open for 0% of the time, Pallas kernels for 0%

profile of v4, /device:TPU:0, one launch (start us, length us, event | category | flops | bytes accessed | tf_op | source)
XLA Modules:
  0.0 114.1 jit_solution(609522837340258694)
XLA Ops:
  0.6 0.0 copy-start
  0.6 0.9 copy-done
  1.6 0.0 copy-start.1
  1.6 0.8 copy-done.1
  2.4 0.0 copy-start.2
  2.4 0.8 copy-done.2
  3.2 0.0 copy-start.3
  3.2 0.8 copy-done.3
  4.1 0.7 shard_map.76
  4.8 20.3 %all_to_all.21.own = f32[8,112,128]{2,1,0:T(8,128)S(1)} all-to-all(f32[8,112,128]{2,1,0:T(8,128)S(1)} %shard_map.76), channel_id=1, replica_groups=mesh['gx'=4,'gy'=2,'gz'=4] {'gx','gy'}, dimensions={0} | all-to-all | bytes 917504 | tf_op jit(solution)/shard_map/all_to_all | solution.py:852
  25.1 1.3 %collective-permute-start.1 = (f32[8,112,128]{2,1,0:T(8,128)S(1)}, f32[8,112,128]{2,1,0:T(8,128)S(1)}, u32[]{:S(2)}, u32[]{:S(2)}) collective-permute-start(f32[8,112,128]{2,1,0:T(8,128)S(1)} %all_to_all.21.own), channel_id=1, source_target_pairs={{8,0},{16,8},{24,16},{28,24},{20,28},{12,20},{4,12},{1,4},{9,1},{1... | collective-permute-start | bytes 1376264 | tf_op jit(solution)/shard_map/ppermute | solution.py:855
  26.4 4.6 %collective-permute-start = (f32[8,112,128]{2,1,0:T(8,128)S(1)}, f32[8,112,128]{2,1,0:T(8,128)S(1)}, u32[]{:S(2)}, u32[]{:S(2)}) collective-permute-start(f32[8,112,128]{2,1,0:T(8,128)S(1)} %all_to_all.21.own), channel_id=1, source_target_pairs={{0,8},{8,16},{16,24},{24,28},{28,20},{20,12},{12,4},{4,1},{1,9},{9... | collective-permute-start | bytes 1376264 | tf_op jit(solution)/shard_map/ppermute | solution.py:854
  31.0 0.0 copy-start.4
  31.0 1.3 %collective-permute-start.3 = (f32[8,8,128]{2,1,0:T(8,128)S(1)}, f32[8,8,128]{2,1,0:T(8,128)S(1)}, u32[]{:S(2)}, u32[]{:S(2)}) collective-permute-start(f32[8,8,128]{2,1,0:T(8,128)S(1)} %get-tuple-element.45), channel_id=1, source_target_pairs={{16,0},{24,8},{28,16},{20,24},{12,28},{4,20},{1,12},{9,4},{17,1},{... | collective-permute-start | bytes 98312 | tf_op jit(solution)/shard_map/ppermute | solution.py:856
  32.3 5.4 %collective-permute-start.2 = (f32[8,8,128]{2,1,0:T(8,128)S(1)}, f32[8,8,128]{2,1,0:T(8,128)S(1)}, u32[]{:S(2)}, u32[]{:S(2)}) collective-permute-start(f32[8,8,128]{2,1,0:T(8,128)S(1)} %get-tuple-element.46), channel_id=1, source_target_pairs={{0,16},{8,24},{16,28},{24,20},{28,12},{20,4},{12,1},{4,9},{1,17},{... | collective-permute-start | bytes 98312 | tf_op jit(solution)/shard_map/ppermute | solution.py:857
  37.7 1.4 %collective-permute-done.3.high_edge = f32[8,8,128]{2,1,0:T(8,128)S(1)} collective-permute-done((f32[8,8,128]{2,1,0:T(8,128)S(1)}, f32[8,8,128]{2,1,0:T(8,128)S(1)}, u32[]{:S(2)}, u32[]{:S(2)}) %collective-permute-start.3) | collective-permute-done | bytes 32800 | tf_op jit(solution)/shard_map/ppermute | solution.py:856
  39.1 2.5 %collective-permute-done.2.low_edge = f32[8,8,128]{2,1,0:T(8,128)S(1)} collective-permute-done((f32[8,8,128]{2,1,0:T(8,128)S(1)}, f32[8,8,128]{2,1,0:T(8,128)S(1)}, u32[]{:S(2)}, u32[]{:S(2)}) %collective-permute-start.2) | collective-permute-done | bytes 32800 | tf_op jit(solution)/shard_map/ppermute | solution.py:857
  41.6 0.0 collective-permute-done.1.high
  41.6 0.0 collective-permute-done.low
  41.6 0.0 copy-done.4
  41.6 23.8 %shard_map.77 = (f32[416,128]{1,0:T(8,128)S(1)}, f32[416,128]{1,0:T(8,128)S(1)}, f32[416,128]{1,0:T(8,128)S(1)}, f32[416,128]{1,0:T(8,128)S(1)}, f32[416,128]{1,...) custom-call(f32[8]{0:T(128)S(1)} %copy-done.4, ...), custom_call_target="tpu_custom_call" | custom-call | tf_op jit(solution)/shard_map/pallas_call | solution.py:831
  65.5 1.3 %collective-permute-start.5 = (f32[8,128,128]{2,1,0:T(8,128)S(1)}, f32[8,128,128]{2,1,0:T(8,128)S(1)}, u32[]{:S(2)}, u32[]{:S(2)}) collective-permute-start(f32[8,128,128]{2,1,0:T(8,128)S(1)} %get-tuple-element.42.refs_18_), channel_id=1, source_target_pairs={{8,0},{16,8},{24,16},{28,24},{20,28},{12,20},{4,12},{1,4},{9,1},{1... | collective-permute-start | bytes 1572872 | tf_op jit(solution)/shard_map/ppermute | solution.py:883
  66.8 4.7 %collective-permute-start.4 = (f32[8,128,128]{2,1,0:T(8,128)S(1)}, f32[8,128,128]{2,1,0:T(8,128)S(1)}, u32[]{:S(2)}, u32[]{:S(2)}) collective-permute-start(f32[8,128,128]{2,1,0:T(8,128)S(1)} %get-tuple-element.42.refs_18_), channel_id=1, source_target_pairs={{0,8},{8,16},{16,24},{24,28},{28,20},{20,12},{12,4},{4,1},{1,9},{9... | collective-permute-start | bytes 1572872 | tf_op jit(solution)/shard_map/ppermute | solution.py:882
  71.4 15.7 %all_to_all.22 = f32[32,1,128]{2,1,0:T(1,128)S(1)} all-to-all(f32[32,1,128]{2,1,0:T(1,128)S(1)} %bitcast.5), channel_id=1, replica_groups=mesh['gx'=4,'gy'=2,'gz'=4] {'gx','gy','gz'}, dimensions={0} | all-to-all | bytes 32768 | tf_op jit(solution)/shard_map/all_to_all | solution.py:881
  87.2 0.0 collective-permute-done.5.refs_20_
  87.2 0.0 collective-permute-done.4.refs_19_
  87.2 11.1 %shard_map.78 = f32[8,80,128]{2,1,0:T(8,128)S(1)} custom-call(f32[416,128]{1,0:T(8,128)S(1)} %get-tuple-element.24.refs_0_, f32[416,128]{1,0:T(8,128)S(1)} %get-tuple-element.25.refs_1_, f32[416,128]{1,0:T(8,128)S(1)} %get-tuple-element.26.refs_2_, f32[416,128]{1,0:T(8,128)S(1)} %get-tuple-element.27.refs_3_, f32[416,128]{1,0:T(8,128)S(1)} %get-tuple-element.28.refs_4_, ...), custom_call_target="tpu_custom_call" | custom-call | tf_op jit(solution)/shard_map/pallas_call | solution.py:831
  98.3 14.9 %all_to_all.23.chunks = f32[8,80,128]{2,1,0:T(8,128)S(1)} all-to-all(f32[8,80,128]{2,1,0:T(8,128)S(1)} %shard_map.78), channel_id=1, replica_groups=mesh['gx'=4,'gy'=2,'gz'=4] {'gx','gy'}, dimensions={0} | all-to-all | bytes 655360 | tf_op jit(solution)/shard_map/all_to_all | solution.py:895
  113.2 0.9 shard_map.79
  (1 shorter events, 0.0 us)
Async XLA Ops:
  0.6 0.9 copy-start
  1.6 0.8 copy-start.1
  2.4 0.8 copy-start.2
  3.2 0.8 copy-start.3
  25.1 16.6 %collective-permute-start.1 = (f32[8,112,128]{2,1,0:T(8,128)S(1)}, f32[8,112,128]{2,1,0:T(8,128)S(1)}, u32[]{:S(2)}, u32[]{:S(2)}) collective-permute-start(f32[8,112,128]{2,1,0:T(8,128)S(1)} %all_to_all.21.own), channel_id=1, source_target_pairs={{8,0},{16,8},{24,16},{28,24},{20,28},{12,20},{4,12},{1,4},{9,1},{1... | collective-permute-start | bytes 1376264 | tf_op jit(solution)/shard_map/ppermute | solution.py:855
  26.4 15.3 %collective-permute-start = (f32[8,112,128]{2,1,0:T(8,128)S(1)}, f32[8,112,128]{2,1,0:T(8,128)S(1)}, u32[]{:S(2)}, u32[]{:S(2)}) collective-permute-start(f32[8,112,128]{2,1,0:T(8,128)S(1)} %all_to_all.21.own), channel_id=1, source_target_pairs={{0,8},{8,16},{16,24},{24,28},{28,20},{20,12},{12,4},{4,1},{1,9},{9... | collective-permute-start | bytes 1376264 | tf_op jit(solution)/shard_map/ppermute | solution.py:854
  31.0 10.7 %copy-start.4 = (f32[8]{0:T(128)S(1)}, f32[8]{0:T(128)}, u32[]{:S(2)}) copy-start(f32[8]{0:T(128)} %stiffness.1) | copy-start | bytes 100
  31.0 8.1 %collective-permute-start.3 = (f32[8,8,128]{2,1,0:T(8,128)S(1)}, f32[8,8,128]{2,1,0:T(8,128)S(1)}, u32[]{:S(2)}, u32[]{:S(2)}) collective-permute-start(f32[8,8,128]{2,1,0:T(8,128)S(1)} %get-tuple-element.45), channel_id=1, source_target_pairs={{16,0},{24,8},{28,16},{20,24},{12,28},{4,20},{1,12},{9,4},{17,1},{... | collective-permute-start | bytes 98312 | tf_op jit(solution)/shard_map/ppermute | solution.py:856
  32.3 9.4 %collective-permute-start.2 = (f32[8,8,128]{2,1,0:T(8,128)S(1)}, f32[8,8,128]{2,1,0:T(8,128)S(1)}, u32[]{:S(2)}, u32[]{:S(2)}) collective-permute-start(f32[8,8,128]{2,1,0:T(8,128)S(1)} %get-tuple-element.46), channel_id=1, source_target_pairs={{0,16},{8,24},{16,28},{24,20},{28,12},{20,4},{12,1},{4,9},{1,17},{... | collective-permute-start | bytes 98312 | tf_op jit(solution)/shard_map/ppermute | solution.py:857
  65.5 21.7 %collective-permute-start.5 = (f32[8,128,128]{2,1,0:T(8,128)S(1)}, f32[8,128,128]{2,1,0:T(8,128)S(1)}, u32[]{:S(2)}, u32[]{:S(2)}) collective-permute-start(f32[8,128,128]{2,1,0:T(8,128)S(1)} %get-tuple-element.42.refs_18_), channel_id=1, source_target_pairs={{8,0},{16,8},{24,16},{28,24},{20,28},{12,20},{4,12},{1,4},{9,1},{1... | collective-permute-start | bytes 1572872 | tf_op jit(solution)/shard_map/ppermute | solution.py:883
  66.8 20.4 %collective-permute-start.4 = (f32[8,128,128]{2,1,0:T(8,128)S(1)}, f32[8,128,128]{2,1,0:T(8,128)S(1)}, u32[]{:S(2)}, u32[]{:S(2)}) collective-permute-start(f32[8,128,128]{2,1,0:T(8,128)S(1)} %get-tuple-element.42.refs_18_), channel_id=1, source_target_pairs={{0,8},{8,16},{16,24},{24,28},{28,20},{20,12},{12,4},{4,1},{1,9},{9... | collective-permute-start | bytes 1572872 | tf_op jit(solution)/shard_map/ppermute | solution.py:882

commit v5 on v0

--- a/solution.py
+++ b/solution.py
@@ -1,6 +1,10 @@
+import functools
+
 import jax
 import jax.numpy as jnp
 from jax import lax
+from jax.experimental import pallas as pl
+from jax.experimental.pallas import tpu as pltpu
 from jax.sharding import PartitionSpec as P
 
 RECOMPUTE = 2
@@ -247,6 +251,648 @@
     return (adj_temp_prev, velocity, mean_stress)
 
 
+SUB = 8
+LANES = 128
+FIELDS = 6
+BACK = 5
+EDGE = 2
+PHASE = 8
+HELD = 16
+VMEM_LIMIT = 48 * 1024 * 1024
+FORWARD, ADJOINT, RESPONSE = range(3)
+
+
+def slab_plan_fits(mesh, shape):
+    sizes = mesh.shape
+    group = sizes["gx"] * sizes["gy"]
+    block = (shape[0] // sizes["gx"], shape[1] // sizes["gy"], shape[2] // sizes["gz"])
+    return (
+        group == SUB
+        and block[0] == SUB
+        and block[0] * block[1] == LANES
+        and block[1] * group == LANES
+        and block[2] == LANES
+        and block[2] == group * 2 * PHASE
+    )
+
+
+class Slabs:
+    def __init__(self, mesh, shape):
+        self.nx, self.ny, self.nz = mesh.shape["gx"], mesh.shape["gy"], mesh.shape["gz"]
+        self.group = self.nx * self.ny
+        self.width, self.breadth, self.height = shape
+        self.block = (shape[0] // self.nx, shape[1] // self.ny, shape[2] // self.nz)
+        self.slab = self.block[2] // self.group
+        self.margin = self.slab + SUB
+        self.rows = self.slab + 2 * self.margin
+        self.cells = self.width * self.breadth * self.height
+        self.place = []
+        for ix in range(self.nx):
+            for iy in range(self.ny):
+                step = ix if iy % 2 == 0 else self.nx - 1 - ix
+                self.place.append(iy * self.nx + step)
+        self.holder = [self.place.index(j) for j in range(self.group)]
+
+    def device(self, slab):
+        return self.holder[slab % self.group] * self.nz + slab // self.group
+
+    def shifts(self, distance):
+        count = self.group * self.nz
+        return [
+            (self.device(p), self.device(p + distance))
+            for p in range(count)
+            if 0 <= p + distance < count
+        ]
+
+    def index(self):
+        ix, iy = lax.axis_index("gx"), lax.axis_index("gy")
+        step = jnp.where(iy % 2 == 0, ix, self.nx - 1 - ix)
+        return lax.axis_index("gz") * self.group + iy * self.nx + step
+
+    def inside(self, z, n=SUB):
+        layer = self.index() * self.slab - self.margin + z
+        layer = layer + lax.broadcasted_iota(jnp.int32, (n, LANES), 0)
+        return (layer >= 0) & (layer < self.height)
+
+
+def swap_granules(tiles, granule):
+    lane = lax.broadcasted_iota(jnp.int32, (SUB, LANES), 1) // granule
+    for bit in (1, 2, 4):
+        low = (lane & bit) == 0
+        new = list(tiles)
+        for a in range(SUB):
+            if a & bit:
+                continue
+            b = a | bit
+            new[a] = jnp.where(low, tiles[a], pltpu.roll(tiles[b], granule * bit, 1))
+            new[b] = jnp.where(low, pltpu.roll(tiles[a], LANES - granule * bit, 1), tiles[b])
+        tiles = new
+    return tiles
+
+
+class Tiles:
+    def __init__(self, geo):
+        self.breadth = geo.breadth
+        self.row = lax.broadcasted_iota(jnp.int32, (SUB, LANES), 0)
+        self.lane = lax.broadcasted_iota(jnp.int32, (SUB, LANES), 1)
+        self.y = self.lane % self.breadth
+
+    def x(self, load, x, count, step):
+        j = x + step
+        if 0 <= j < count:
+            return load(j)
+        if step > 0:
+            turned = pltpu.roll(load(0), LANES - self.breadth, 1)
+            return jnp.where(self.lane < LANES - self.breadth, turned, 0.0)
+        turned = pltpu.roll(load(count - 1), self.breadth, 1)
+        return jnp.where(self.lane >= self.breadth, turned, 0.0)
+
+    def ys(self, f, d):
+        return pltpu.roll(f, LANES - d, 1), pltpu.roll(f, d, 1)
+
+    def y_masks(self, d, value):
+        up, down = self.y < self.breadth - d, self.y >= d
+        value = jnp.float32(value)
+        return jnp.where(up, value, 0.0), jnp.where(down, value, 0.0)
+
+    def pair_sum(self, f):
+        f = f + jnp.where(self.lane % 2 == 0, pltpu.roll(f, LANES - 1, 1), pltpu.roll(f, 1, 1))
+        return f + jnp.where(self.row % 2 == 0, pltpu.roll(f, SUB - 1, 0), pltpu.roll(f, 1, 0))
+
+
+def get(ref, z, *index):
+    return ref[(*index, pl.ds(z, SUB), slice(None))]
+
+
+def sweep(lo, hi, body):
+    assert (hi - lo) % SUB == 0
+
+    def step(t, _):
+        late = []
+
+        def store(ref, value, z, *index):
+            ref[(*index, pl.ds(z, SUB), slice(None))] = value
+
+        def put(*item):
+            late.append(item)
+            if len(late) > HELD:
+                store(*late.pop(0))
+
+        body(pl.multiple_of(t * SUB, SUB) + lo, put)
+        for item in late:
+            store(*item)
+        return 0
+
+    lax.fori_loop(0, (hi - lo) // SUB, step, 0)
+
+
+def pack_kernel(geo, heat_in, flow_in, dual_in, kind_in, out, heat, flow, dual, kind, sems):
+    b, e = geo.slab, EDGE
+    pairs = ((heat_in, heat), (flow_in, flow), (dual_in, dual), (kind_in, kind))
+    copies = [
+        pltpu.make_async_copy(source, target, sems.at[k])
+        for k, (source, target) in enumerate(pairs)
+    ]
+    for copy in copies:
+        copy.start()
+    for copy in copies:
+        copy.wait()
+    flat = [heat[...], flow[0], flow[1], flow[2], dual[...], kind[...].astype(jnp.float32)]
+    turned = [f.reshape(LANES, LANES).T for f in flat]
+    for j in range(geo.group):
+        q = geo.holder[j]
+        for f in range(FIELDS):
+            out[q, f * b : (f + 1) * b, :] = turned[f][j * b : (j + 1) * b]
+        tail = FIELDS * b
+        first = jnp.concatenate([turned[f][j * b : j * b + e] for f in range(4)], 0)
+        last = jnp.concatenate([turned[f][(j + 1) * b - e : (j + 1) * b] for f in range(4)], 0)
+        out[q, tail : tail + SUB, :] = first
+        out[q, tail + SUB : tail + 2 * SUB, :] = last
+
+
+STATIC_FINE = ("s0", "s1", "s2", "visc", "w", "diag", "cxp", "cxm", "cyp", "cym", "cz")
+STATIC_COARSE = ("kxp", "kxm", "kyp", "kym", "kzp", "kzm", "wc")
+STATIC = STATIC_FINE + STATIC_COARSE
+
+
+def iterate(geo, st, work, seqs, lo, hi, first=(), mean=None):
+    v, p, res, cor, cor2, cc0, cc1 = work
+    tl = Tiles(geo)
+    half_up, half_down = tl.y_masks(1, 0.5)
+    keep = 1.0 - JACOBI_WEIGHT
+    slots = [(q, 3 * s + k) for s, q in enumerate(seqs) for k in range(3)]
+    transposed = 2
+
+    def faces(x, z):
+        c = [get(st[name], z, x) for name in ("cxp", "cxm", "cyp", "cym", "cz")]
+        return c + [get(st["cz"], z - 1, x)]
+
+    def beside(ref, c, x, z):
+        f = get(ref, z, c, x)
+        load = lambda j: get(ref, z, c, j)
+        near = [tl.x(load, x, SUB, 1), tl.x(load, x, SUB, -1), *tl.ys(f, 1)]
+        return f, near + [get(ref, z + 1, c, x), get(ref, z - 1, c, x)]
+
+    def around(coef, ref, c, x, z):
+        f, near = beside(ref, c, x, z)
+        return f, sum(a * b for a, b in zip(coef, near))
+
+    def residual(z, put):
+        for x in range(SUB):
+            w = get(st["w"], z, x)
+            if FORWARD in seqs and FORWARD not in first:
+                coef, diag = faces(x, z), get(st["diag"], z, x)
+            for s, q in enumerate(seqs):
+                start = q == FORWARD and q in first
+                if not start:
+                    _, near = beside(p, transposed if q == ADJOINT else s, x, z)
+                    slope = [
+                        0.5 * (near[0] - near[1]),
+                        half_up * near[2] - half_down * near[3],
+                        0.5 * (near[4] - near[5]),
+                    ]
+                for k in range(3):
+                    c = 3 * s + k
+                    if q == FORWARD:
+                        value = get(st["s%d" % k], z, x)
+                        if not start:
+                            f, total = around(coef, v, c, x, z)
+                            value = value - slope[k] - (diag * f - total)
+                    elif q == RESPONSE:
+                        value = -slope[k]
+                    else:
+                        value = slope[k] if q in first else get(cor, z, c, x) + slope[k]
+                    put(res, value, z, c, x)
+                    put(cor, w * value, z, c, x)
+
+    sweep(lo - 8, hi + 8, residual)
+
+    def restricted(z, put):
+        for pair in range(SUB // 2):
+            coefs = [faces(2 * pair + side, z) for side in range(2)]
+            wc = 0.125 * get(st["wc"], z, pair)
+            for _, c in slots:
+                left = 0.0
+                for side in range(2):
+                    _, total = around(coefs[side], cor, c, 2 * pair + side, z)
+                    left = left + (keep * get(res, z, c, 2 * pair + side) + total)
+                put(cc0, wc * tl.pair_sum(left), z, c, pair)
+
+    sweep(lo - 8, hi + 8, restricted)
+
+    def coarse_step(ref, c, pair, z):
+        f = get(ref, z, c, pair)
+        load = lambda j: get(ref, z, c, j)
+        near = [tl.x(load, pair, SUB // 2, 1), tl.x(load, pair, SUB // 2, -1), *tl.ys(f, 2)]
+        near += [get(ref, z + 2, c, pair), get(ref, z - 2, c, pair)]
+        value = get(cc0, z, c, pair) + keep * f
+        for name, b in zip(STATIC_COARSE, near):
+            value = value + get(st[name], z, pair) * b
+        return value
+
+    def sweep_one(z, put):
+        for pair in range(SUB // 2):
+            for _, c in slots:
+                put(cc1, coarse_step(cc0, c, pair, z), z, c, pair)
+
+    sweep(lo - 4, hi + 4, sweep_one)
+
+    def sweep_two(z, put):
+        for pair in range(SUB // 2):
+            for _, c in slots:
+                value = coarse_step(cc1, c, pair, z)
+                for x in (2 * pair, 2 * pair + 1):
+                    put(cor2, get(cor, z, c, x) + value, z, c, x)
+
+    sweep(lo - 4, hi + 4, sweep_two)
+
+    def velocity(z, put):
+        for x in range(SUB):
+            coef, w = faces(x, z), get(st["w"], z, x)
+            for q, c in slots:
+                f, total = around(coef, cor2, c, x, z)
+                value = get(cor, z, c, x) + keep * f + w * total
+                if q == FORWARD and q not in first:
+                    value = get(v, z, c, x) + value
+                put(v, value, z, c, x)
+
+    sweep(lo - 4, hi + 4, velocity)
+
+    def pressure(z, put):
+        for x in range(SUB):
+            visc = SCHUR_WEIGHT * get(st["visc"], z, x)
+            for s, q in enumerate(seqs):
+                load = lambda j: get(v, z, 3 * s, j)
+                div = 0.5 * (tl.x(load, x, SUB, 1) - tl.x(load, x, SUB, -1))
+                up, down = tl.ys(get(v, z, 3 * s + 1, x), 1)
+                div = div + (half_up * up - half_down * down)
+                div = div + 0.5 * (get(v, z + 1, 3 * s + 2, x) - get(v, z - 1, 3 * s + 2, x))
+                if q == ADJOINT:
+                    value = get(p, z, s, x) + div
+                    put(p, value, z, s, x)
+                    put(p, visc * value, z, transposed, x)
+                    coef, diag = faces(x, z), get(st["diag"], z, x)
+                    for c in range(3 * s, 3 * s + 3):
+                        f, total = around(coef, v, c, x, z)
+                        put(cor, get(res, z, c, x) - (diag * f - total), z, c, x)
+                    continue
+                value = -(visc * div)
+                if not (q == FORWARD and q in first):
+                    value = get(p, z, s, x) + value
+                if mean is not None:
+                    value = value - jnp.where(geo.inside(z), mean, 0.0)
+                put(p, value, z, s, x)
+
+    sweep(lo, hi, pressure)
+
+
+def whole_sum(value):
+    return jnp.sum(jnp.sum(value, axis=0), axis=(0, 1), keepdims=True)
+
+
+def product(left, right):
+    value = 0.0
+    for a, b in zip(left, right):
+        value = value + a[...] * b[...]
+    return whole_sum(value)
+
+
+def in_lanes(values, rows):
+    lane = lax.broadcasted_iota(jnp.int32, (rows, LANES), 1)
+    out = jnp.zeros((rows, LANES), jnp.float32)
+    for k, value in values:
+        out = jnp.where(lane == k, value, out)
+    return out
+
+
+def setup_kernel(geo, stiffness, own, low, high, low_edge, high_edge, *refs):
+    st = dict(zip(STATIC, refs))
+    moved, duals, response, sums, raw, heat, vc, *work = refs[len(STATIC) :]
+    v, p, res, cor, cor2, cc0, cc1 = work
+    tl = Tiles(geo)
+    b, m, n_rows = geo.slab, geo.margin, geo.rows
+    granule = geo.block[1]
+
+    for source, base in ((low, m - b), (own, m), (high, m + b)):
+
+        def place(t, _, source=source, base=base):
+            groups = []
+            for u in range(b // SUB):
+                row = pl.multiple_of(t * b, b) + u * SUB
+                groups.append([source[q, pl.ds(row, SUB), :] for q in range(geo.group)])
+            for u, tiles in enumerate(groups):
+                for x, tile in enumerate(swap_granules(tiles, granule)):
+                    raw[t, x, base + u * SUB : base + (u + 1) * SUB, :] = tile
+            return 0
+
+        lax.fori_loop(0, FIELDS, place, 0)
+    for source, base in ((low_edge, m - b - EDGE), (high_edge, m + 2 * b)):
+        tiles = [source[q] for q in range(geo.group)]
+        for x, tile in enumerate(swap_granules(tiles, granule)):
+            for f in range(4):
+                raw[f, x, base : base + EDGE, :] = tile[f * EDGE : (f + 1) * EDGE]
+
+    one_up, one_down = tl.y_masks(1, 1.0)
+
+    def beside(load, x, z):
+        f = load(z, x)
+        up, down = tl.ys(f, 1)
+        near = [tl.x(lambda j: load(z, j), x, SUB, s) for s in (1, -1)]
+        return f, near + [one_up * up, one_down * down, load(z + 1, x), load(z - 1, x)]
+
+    def field(f):
+        return lambda z, x: get(raw, z, f, x)
+
+    def advance(old, new):
+        def body(z, put):
+            inside = geo.inside(z)
+            for x in range(SUB):
+                f, near = beside(old, x, z)
+                drift = 0.0
+                for k in range(3):
+                    flow = get(raw, z, 1 + k, x)
+                    drift = drift + jnp.maximum(flow, 0.0) * (f - near[2 * k + 1])
+                    drift = drift + jnp.minimum(flow, 0.0) * (near[2 * k] - f)
+                spread = sum(near) - 6.0 * f
+                value = f - INCREMENT_DT * drift + INCREMENT_DT * DIFFUSIVITY * spread
+                put(heat, jnp.where(inside, value, 0.0), z, new, x)
+
+        return body
+
+    def warm(new):
+        return lambda z, x: get(heat, z, new, x)
+
+    sweep(m - b - 4, m + 2 * b + 4, advance(field(0), 0))
+    sweep(m - b, m + 2 * b, advance(warm(0), 1))
+
+    def viscosity(z, put):
+        inside = geo.inside(z)
+        for pair in range(SUB // 2):
+            coarse = 0.0
+            for x in (2 * pair, 2 * pair + 1):
+                kind = get(raw, z, 5, x)
+                base = jnp.zeros(kind.shape, jnp.float32)
+                for layer in range(LAYERS):
+                    base = base + jnp.where(kind == float(layer), stiffness[layer], 0.0)
+                value = base * jnp.exp(-ACTIVATION_ENERGY * get(heat, z, 1, x))
+                value = jnp.where(inside, value, 0.0)
+                put(st["visc"], value, z, x)
+                coarse = coarse + value
+            put(vc, 0.125 * tl.pair_sum(coarse), z, pair)
+
+    sweep(m - b, m + 2 * b, viscosity)
+
+    def statics(z, put):
+        inside = geo.inside(z)
+        for x in range(SUB):
+            c, near = beside(lambda z, x: get(st["visc"], z, x), x, z)
+            face = [0.5 * (c + o) for o in near]
+            diag = sum(face)
+            face[2], face[3] = one_up * face[2], one_down * face[3]
+            for name, f in zip(("cxp", "cxm", "cyp", "cym", "cz"), face):
+                put(st[name], f, z, x)
+            put(st["diag"], diag, z, x)
+            put(st["w"], jnp.where(inside, JACOBI_WEIGHT / diag, 0.0), z, x)
+            f, near = beside(warm(1), x, z)
+            dual = -INCREMENT_DT * get(raw, z, 4, x)
+            for k in range(3):
+                flow = get(raw, z, 1 + k, x)
+                step = jnp.where(flow > 0, f - near[2 * k + 1], near[2 * k] - f)
+                put(st["s%d" % k], dual * step, z, x)
+
+    sweep(m - b, m + 2 * b, statics)
+
+    two_up, two_down = tl.y_masks(2, 1.0)
+
+    def coarse_statics(z, put):
+        inside = geo.inside(z)
+        for pair in range(SUB // 2):
+            c = get(vc, z, pair)
+            load = lambda j: get(vc, z, j)
+            up, down = tl.ys(c, 2)
+            near = [tl.x(load, pair, SUB // 2, s) for s in (1, -1)]
+            near += [two_up * up, two_down * down, get(vc, z + 2, pair), get(vc, z - 2, pair)]
+            face = [0.25 * (0.5 * (c + o)) for o in near]
+            wc = jnp.where(inside, JACOBI_WEIGHT / sum(face), 0.0)
+            face[2], face[3] = two_up * face[2], two_down * face[3]
+            for name, f in zip(STATIC_COARSE, face):
+                put(st[name], wc * f, z, pair)
+            put(st["wc"], wc, z, pair)
+
+    sweep(m - b, m + 2 * b, coarse_statics)
+
+    def transport(z, put):
+        for x in range(SUB):
+            dual, near = beside(field(4), x, z)
+            value = dual + INCREMENT_DT * DIFFUSIVITY * (sum(near) - 6.0 * dual)
+            for k in range(3):
+                flow, sides = beside(field(1 + k), x, z)
+                a = jnp.maximum(flow, 0.0) * dual
+                c = jnp.minimum(flow, 0.0) * dual
+                ahead = jnp.maximum(sides[2 * k], 0.0) * near[2 * k]
+                behind = jnp.minimum(sides[2 * k + 1], 0.0) * near[2 * k + 1]
+                value = value - INCREMENT_DT * (a - ahead + behind - c)
+            put(moved, value, z - m, x)
+
+    sweep(m, m + b, transport)
+
+    def unit(z, put):
+        value = jnp.where(geo.inside(z), 1.0, 0.0)
+        for x in range(SUB):
+            put(p, value, z, 0, x)
+            put(p, value, z, 1, x)
+            put(p, SCHUR_WEIGHT * get(st["visc"], z, x), z, 2, x)
+
+    sweep(0, n_rows, unit)
+
+    mine = slice(m, m + b)
+    iterate(geo, st, work, (ADJOINT,), m - PHASE, m + b + PHASE, (ADJOINT,))
+    for k in range(3):
+        duals[k] = cor[k, :, mine, :]
+    duals[3] = p[0, :, mine, :]
+    iterate(geo, st, work, (ADJOINT, RESPONSE), m, m + b, (RESPONSE,))
+    for k in range(3):
+        duals[4 + k] = cor[k, :, mine, :]
+        response[k] = v[3 + k, :, mine, :]
+    duals[7] = p[0, :, mine, :]
+    response[3] = p[1, :, mine, :]
+    sums_of = [
+        (1, whole_sum(duals[3])),
+        (4, whole_sum(duals[7])),
+        (7, product([duals.at[4 + k] for k in range(4)], [response.at[k] for k in range(4)])),
+    ]
+    sums[...] = in_lanes(sums_of, 1)
+
+
+def first_kernel(geo, *refs):
+    st = dict(zip(STATIC, refs))
+    duals, part, state, sums, *work = refs[len(STATIC) :]
+    v, p = work[:2]
+    b, m = geo.slab, geo.margin
+    mine = slice(m, m + b)
+
+    def fields():
+        return [v.at[k, :, mine, :] for k in range(3)] + [p.at[0, :, mine, :]]
+
+    near, far = [duals.at[k] for k in range(4)], [duals.at[4 + k] for k in range(4)]
+    iterate(geo, st, work, (FORWARD,), m - PHASE, m + b + PHASE, (FORWARD,))
+    sums_of = [(0, whole_sum(p[0, :, mine, :])), (2, product(near, fields()))]
+    iterate(geo, st, work, (FORWARD,), m, m + b)
+    sums_of += [(3, whole_sum(p[0, :, mine, :]))]
+    sums_of += [(5, product(near, fields())), (6, product(far, fields()))]
+    sums[...] = in_lanes(sums_of, sums.shape[0]) + part[...]
+    for k, ref in enumerate(fields()):
+        state[k] = ref[...]
+
+
+def means(geo, sums):
+    row = jnp.sum(sums, axis=0, keepdims=True) / geo.cells
+    lane = lax.broadcasted_iota(jnp.int32, row.shape, 1)
+
+    def at(k):
+        return jnp.sum(jnp.where(lane == k, row, 0.0), axis=1, keepdims=True)
+
+    p1, q1, l1_x1, p2, q2, l1_x2, l2_x2, l2_r1 = [at(k) for k in range(8)]
+    m1 = p1
+    m2 = p2 - m1 * q1
+    m3 = l1_x2 - m1 * q2 - m2 * q1 + p1
+    m4 = l2_x2 - m1 * l2_r1 - m2 * q2 + l1_x1 - m3 * q1 + p1
+    return m1, m2, m3, m4
+
+
+def second_kernel(geo, *refs):
+    st = dict(zip(STATIC, refs))
+    own, low, high, own_r, low_r, high_r, sums, moved, out, *work = refs[len(STATIC) :]
+    v, p = work[:2]
+    b, m = geo.slab, geo.margin
+    m1, m2, m3, m4 = means(geo, sums[...])
+    for source, turn, base in ((low, low_r, m - b), (own, own_r, m), (high, high_r, m + b)):
+        rows = slice(base, base + b)
+        for k in range(3):
+            v[k, :, rows, :] = source[k] - m1 * turn[k]
+        shift = jnp.where(geo.inside(base, b), m2, 0.0)
+        p[0, :, rows, :] = source[3] - m1 * turn[3] - shift[None]
+    iterate(geo, st, work, (FORWARD,), m - PHASE, m + b + PHASE, mean=m3)
+    iterate(geo, st, work, (FORWARD,), m, m + b, mean=m4)
+    for u in range(0, b, SUB):
+        at = slice(m + u, m + u + SUB)
+        columns = range(SUB)
+        fields = [[v[k, x, at, :] for x in columns] for k in range(3)]
+        fields.append([p[0, x, at, :] for x in columns])
+        fields.append([moved[x, u : u + SUB, :] + fields[2][x] for x in columns])
+        for f, tiles in enumerate(fields):
+            for q, tile in enumerate(swap_granules(tiles, geo.block[1])):
+                out[q, f * b + u : f * b + u + SUB, :] = tile
+
+
+def unpack_kernel(geo, chunks, heat, flow, pressure):
+    b = geo.slab
+    for f in range(BACK):
+        rows = [chunks[geo.holder[j], f * b : (f + 1) * b, :] for j in range(geo.group)]
+        block = jnp.concatenate(rows, 0).T.reshape(geo.block)
+        if f < 3:
+            flow[f] = block
+        elif f == 3:
+            pressure[...] = block
+        else:
+            heat[...] = block
+
+
+def call(kernel, out, scratch, *args, smem=(), hbm=()):
+    f32 = jnp.float32
+    specs = [
+        pl.BlockSpec(
+            memory_space=pltpu.SMEM if i in smem else pltpu.HBM if i in hbm else pltpu.VMEM
+        )
+        for i in range(len(args))
+    ]
+    return pl.pallas_call(
+        kernel,
+        out_shape=[jax.ShapeDtypeStruct(s, f32) for s in out],
+        in_specs=specs,
+        out_specs=[pl.BlockSpec(memory_space=pltpu.VMEM) for _ in out],
+        scratch_shapes=[pltpu.VMEM(s, f32) if isinstance(s, tuple) else s for s in scratch],
+        compiler_params=pltpu.CompilerParams(vmem_limit_bytes=VMEM_LIMIT),
+    )(*args)
+
+
+def slab_shards(geo, heat, flow, dual, kind, stiffness):
+    b, group = geo.slab, geo.group
+    rows = FIELDS * b
+    inputs = (heat, flow, dual, kind)
+    (chunks,) = call(
+        functools.partial(pack_kernel, geo),
+        [(group, rows + 2 * SUB, LANES)],
+        [pltpu.VMEM(a.shape, a.dtype) for a in inputs] + [pltpu.SemaphoreType.DMA((4,))],
+        *inputs,
+        hbm=range(4),
+    )
+    own = lax.all_to_all(chunks, ("gx", "gy"), 0, 0, tiled=True)
+    axes = ("gx", "gy", "gz")
+    low = lax.ppermute(own, axes, geo.shifts(1))
+    high = lax.ppermute(own, axes, geo.shifts(-1))
+    high_edge = lax.ppermute(own[:, rows : rows + SUB], axes, geo.shifts(-2))
+    low_edge = lax.ppermute(own[:, rows + SUB :], axes, geo.shifts(2))
+
+    fine, coarse = (SUB, geo.rows, LANES), (SUB // 2, geo.rows, LANES)
+    slab = (SUB, b, LANES)
+
+    def work(n, more=0):
+        fields = [(3 * n, *fine), (n + more, *fine)] + [(3 * n, *fine)] * 3
+        return fields + [(3 * n, *coarse)] * 2
+
+    *static, moved, duals, response, part = call(
+        functools.partial(setup_kernel, geo),
+        [fine] * len(STATIC_FINE)
+        + [coarse] * len(STATIC_COARSE)
+        + [slab, (8, *slab), (4, *slab), (1, LANES)],
+        [(FIELDS, *fine), (2, *fine), coarse] + work(2, 1),
+        stiffness,
+        own,
+        low,
+        high,
+        low_edge,
+        high_edge,
+        smem=(0,),
+    )
+    low_response = lax.ppermute(response, axes, geo.shifts(1))
+    high_response = lax.ppermute(response, axes, geo.shifts(-1))
+    state, sums = call(
+        functools.partial(first_kernel, geo),
+        [(4, *slab), (group * geo.nz, LANES)],
+        work(1),
+        *static,
+        duals,
+        part,
+    )
+    sums = lax.all_to_all(sums, axes, 0, 0, tiled=True)
+    low_state = lax.ppermute(state, axes, geo.shifts(1))
+    high_state = lax.ppermute(state, axes, geo.shifts(-1))
+    (chunks,) = call(
+        functools.partial(second_kernel, geo),
+        [(group, BACK * b, LANES)],
+        work(1),
+        *static,
+        state,
+        low_state,
+        high_state,
+        response,
+        low_response,
+        high_response,
+        sums,
+        moved,
+    )
+    chunks = lax.all_to_all(chunks, ("gx", "gy"), 0, 0, tiled=True)
+    return tuple(
+        call(
+            functools.partial(unpack_kernel, geo),
+            [geo.block, (3, *geo.block), geo.block],
+            [],
+            chunks,
+        )
+    )
+
+
 def solution(mesh):
     in_specs = (
         P("gx", "gy", "gz"),
@@ -256,4 +902,14 @@
         P(),
     )
     out_specs = (P("gx", "gy", "gz"), P(None, "gx", "gy", "gz"), P("gx", "gy", "gz"))
-    return jax.shard_map(shards, mesh=mesh, in_specs=in_specs, out_specs=out_specs, check_vma=False)
+
+    def program(saved_heat_state, *others):
+        shape = saved_heat_state.shape
+        plan = shards
+        if slab_plan_fits(mesh, shape):
+            plan = functools.partial(slab_shards, Slabs(mesh, shape))
+        return jax.shard_map(
+            plan, mesh=mesh, in_specs=in_specs, out_specs=out_specs, check_vma=False
+        )(saved_heat_state, *others)
+
+    return program

time: 936 us -> 113 us (0.12); the launches traced: 923 us -> 112 us
  starting transfers between devices: 324 us -> 24.4 us
  waiting for transfers between devices: 237 us -> 3.92 us
  blocking collectives: 188 us -> 45.8 us
  local copies, waits for them, and re-layouts: 98.3 us -> 3.45 us
  other arithmetic: 68.1 us -> 0 us
  Pallas kernels: 0 us -> 34 us
    ppermute x144 -> x8, starting transfers between devices: 324 us -> 24.4 us  [the longest x1 5.45 us: slab_shards(): low_edge = lax.ppermute(own[:, rows + SUB:], axes, geo.shifts(2))]
    ppermute x144 -> x8, waiting for transfers between devices: 237 us -> 3.92 us  [the longest x1 2.51 us: slab_shards(): low_edge = lax.ppermute(own[:, rows + SUB:], axes, geo.shifts(2))]
    psum x4 -> x0, blocking collectives: 188 us -> none  [shards(): lax.psum(jnp.sum(mean_stress), ('gx', 'gy', 'gz')) / total_cells]
    reshape x13 -> x0, local copies, waits for them, and re-layouts: 69.2 us -> none  [the longest x5 61.2 us: restrict(): field.reshape(leading + (cells_x // 2, 2, cells_y // 2, 2, cells_z // 2, 2))]
    all_to_all x0 -> x3, blocking collectives: none -> 45.8 us  [the longest x1 20.3 us: slab_shards(): own = lax.all_to_all(chunks, ('gx', 'gy'), 0, 0, tiled=True)]
    pallas_call x0 -> x5, Pallas kernels: none -> 34 us  [call(): pl.pallas_call(kernel, out_shape=[jax.ShapeDtypeStruct(s, f32) for s in o...]
    reduce_sum x9 -> x0, other arithmetic: 27.7 us -> none  [the longest x5 24.7 us: restrict(): return blocks.mean(axis=(-5, -3, -1))]
    concatenate x53 -> x0, other arithmetic: 16.9 us -> none  [the longest x52 11.8 us: extended(): block = jnp.concatenate([low, block, high], axis=dim)]
  transfers between devices with their start and end apart: 144 -> 8, of which waited for: 110 -> 2; matrix products, arithmetic and copies ran while one was open for 1% -> 0% of each run, Pallas kernels for 0% -> 0%
where the time goes in v5:
time: 113 us; the launch traced here: 112 us
  blocking collectives  45.8 us (41%)
  Pallas kernels  34 us (30%)
  starting transfers between devices  24.4 us (22%)
  waiting for transfers between devices  3.92 us (3%)
  local copies, waits for them, and re-layouts  3.45 us (3%)
    pallas_call x5, Pallas kernels, call(): pl.pallas_call(kernel, out_shape=[jax.ShapeDtypeStruct(s, f32) for s in o...  34 us
    all_to_all x1, blocking collectives, slab_shards(): own = lax.all_to_all(chunks, ('gx', 'gy'), 0, 0, tiled=True)  20.3 us
    all_to_all x1, blocking collectives, slab_shards(): chunks = lax.all_to_all(chunks, ('gx', 'gy'), 0, 0, tiled=True)  13.6 us
    all_to_all x1, blocking collectives, slab_shards(): sums = lax.all_to_all(sums, axes, 0, 0, tiled=True)  11.9 us
    ppermute x1, starting transfers between devices, slab_shards(): low_edge = lax.ppermute(own[:, rows + SUB:], axes, geo.shifts(2))  5.45 us
    ppermute x1, starting transfers between devices, slab_shards(): low_state = lax.ppermute(state, axes, geo.shifts(1))  4.65 us
    ppermute x1, starting transfers between devices, slab_shards(): low = lax.ppermute(own, axes, geo.shifts(1))  4.57 us
    ppermute x1, starting transfers between devices, slab_shards(): low_response = lax.ppermute(response, axes, geo.shifts(1))  4.56 us
  transfers between devices with their start and end apart: 8, of which 2 were waited for; matrix products, arithmetic and copies ran while one was open for 0% of the time, Pallas kernels for 0%

profile of v5, /device:TPU:0, one launch (start us, length us, event | category | flops | bytes accessed | tf_op | source)
XLA Modules:
  0.0 112.3 jit_solution(1914412401649629818)
XLA Ops:
  0.6 0.0 copy-start
  0.6 0.9 copy-done
  1.6 0.0 copy-start.1
  1.6 0.8 copy-done.1
  2.4 0.0 copy-start.2
  2.4 0.8 copy-done.2
  3.2 0.0 copy-start.3
  3.2 0.8 copy-done.3
  4.1 0.7 shard_map.76
  4.8 20.3 %all_to_all.21.own = f32[8,112,128]{2,1,0:T(8,128)S(1)} all-to-all(f32[8,112,128]{2,1,0:T(8,128)S(1)} %shard_map.76), channel_id=1, replica_groups=mesh['gx'=4,'gy'=2,'gz'=4] {'gx','gy'}, dimensions={0} | all-to-all | bytes 917504 | tf_op jit(solution)/shard_map/all_to_all | solution.py:830
  25.1 1.3 %collective-permute-start.1 = (f32[8,112,128]{2,1,0:T(8,128)S(1)}, f32[8,112,128]{2,1,0:T(8,128)S(1)}, u32[]{:S(2)}, u32[]{:S(2)}) collective-permute-start(f32[8,112,128]{2,1,0:T(8,128)S(1)} %all_to_all.21.own), channel_id=1, source_target_pairs={{8,0},{16,8},{24,16},{28,24},{20,28},{12,20},{4,12},{1,4},{9,1},{1... | collective-permute-start | bytes 1376264 | tf_op jit(solution)/shard_map/ppermute | solution.py:833
  26.4 4.6 %collective-permute-start = (f32[8,112,128]{2,1,0:T(8,128)S(1)}, f32[8,112,128]{2,1,0:T(8,128)S(1)}, u32[]{:S(2)}, u32[]{:S(2)}) collective-permute-start(f32[8,112,128]{2,1,0:T(8,128)S(1)} %all_to_all.21.own), channel_id=1, source_target_pairs={{0,8},{8,16},{16,24},{24,28},{28,20},{20,12},{12,4},{4,1},{1,9},{9... | collective-permute-start | bytes 1376264 | tf_op jit(solution)/shard_map/ppermute | solution.py:832
  31.0 0.0 copy-start.4
  31.0 1.3 %collective-permute-start.3 = (f32[8,8,128]{2,1,0:T(8,128)S(1)}, f32[8,8,128]{2,1,0:T(8,128)S(1)}, u32[]{:S(2)}, u32[]{:S(2)}) collective-permute-start(f32[8,8,128]{2,1,0:T(8,128)S(1)} %get-tuple-element.51), channel_id=1, source_target_pairs={{16,0},{24,8},{28,16},{20,24},{12,28},{4,20},{1,12},{9,4},{17,1},{... | collective-permute-start | bytes 98312 | tf_op jit(solution)/shard_map/ppermute | solution.py:834
  32.3 5.4 %collective-permute-start.2 = (f32[8,8,128]{2,1,0:T(8,128)S(1)}, f32[8,8,128]{2,1,0:T(8,128)S(1)}, u32[]{:S(2)}, u32[]{:S(2)}) collective-permute-start(f32[8,8,128]{2,1,0:T(8,128)S(1)} %get-tuple-element.52), channel_id=1, source_target_pairs={{0,16},{8,24},{16,28},{24,20},{28,12},{20,4},{12,1},{4,9},{1,17},{... | collective-permute-start | bytes 98312 | tf_op jit(solution)/shard_map/ppermute | solution.py:835
  37.7 1.4 %collective-permute-done.3.high_edge = f32[8,8,128]{2,1,0:T(8,128)S(1)} collective-permute-done((f32[8,8,128]{2,1,0:T(8,128)S(1)}, f32[8,8,128]{2,1,0:T(8,128)S(1)}, u32[]{:S(2)}, u32[]{:S(2)}) %collective-permute-start.3) | collective-permute-done | bytes 32800 | tf_op jit(solution)/shard_map/ppermute | solution.py:834
  39.1 2.5 %collective-permute-done.2.low_edge = f32[8,8,128]{2,1,0:T(8,128)S(1)} collective-permute-done((f32[8,8,128]{2,1,0:T(8,128)S(1)}, f32[8,8,128]{2,1,0:T(8,128)S(1)}, u32[]{:S(2)}, u32[]{:S(2)}) %collective-permute-start.2) | collective-permute-done | bytes 32800 | tf_op jit(solution)/shard_map/ppermute | solution.py:835
  41.6 0.0 collective-permute-done.1.high
  41.6 0.0 collective-permute-done.low
  41.6 0.0 copy-done.4
  41.6 17.2 %shard_map.77 = (f32[8,64,128]{2,1,0:T(8,128)S(1)}, f32[8,64,128]{2,1,0:T(8,128)S(1)}, f32[8,64,128]{2,1,0:T(8,128)S(1)}, f32[8,64,128]{2,1,0:T(8,128)S(1)}, f32...) custom-call(f32[8]{0:T(128)S(1)} %copy-done.4, ...), custom_call_target="tpu_custom_call" | custom-call | tf_op jit(solution)/shard_map/pallas_call | solution.py:809
  58.8 7.0 %shard_map.78 = (f32[4,8,16,128]{3,2,1,0:T(8,128)S(1)}, f32[32,128]{1,0:T(8,128)S(1)}) custom-call(f32[8,64,128]{2,1,0:T(8,128)S(1)} %get-tuple-element.27.refs_0_, f32[8,64,128]{2,1,0:T(8,128)S(1)} %get-tuple-element.28.refs_1_, f32[8,64,128]{2,1,0:T(8,128)S(1)} %get-tuple-element.29.refs_2_, f32[8,64,128]{2,1,0:T(8,128)S(1)} %get-tuple-element.30.refs_3_, ...), custom_call_target="tpu_custom_call" | custom-call | tf_op jit(solution)/shard_map/pallas_call | solution.py:809
  65.8 1.3 %collective-permute-start.5 = (f32[4,8,16,128]{3,2,1,0:T(8,128)S(1)}, f32[4,8,16,128]{3,2,1,0:T(8,128)S(1)}, u32[]{:S(2)}, u32[]{:S(2)}) collective-permute-start(f32[4,8,16,128]{3,2,1,0:T(8,128)S(1)} %get-tuple-element.47.refs_18_), channel_id=1, source_target_pairs={{8,0},{16,8},{24,16},{28,24},{20,28},{12,20},{4,12},{1,4},{9,1},{1... | collective-permute-start | bytes 786440 | tf_op jit(solution)/shard_map/ppermute | solution.py:870
  67.1 4.6 %collective-permute-start.4 = (f32[4,8,16,128]{3,2,1,0:T(8,128)S(1)}, f32[4,8,16,128]{3,2,1,0:T(8,128)S(1)}, u32[]{:S(2)}, u32[]{:S(2)}) collective-permute-start(f32[4,8,16,128]{3,2,1,0:T(8,128)S(1)} %get-tuple-element.47.refs_18_), channel_id=1, source_target_pairs={{0,8},{8,16},{16,24},{24,28},{28,20},{20,12},{12,4},{4,1},{1,9},{9... | collective-permute-start | bytes 786440 | tf_op jit(solution)/shard_map/ppermute | solution.py:869
  71.8 1.3 %collective-permute-start.7 = (f32[4,8,16,128]{3,2,1,0:T(8,128)S(1)}, f32[4,8,16,128]{3,2,1,0:T(8,128)S(1)}, u32[]{:S(2)}, u32[]{:S(2)}) collective-permute-start(f32[4,8,16,128]{3,2,1,0:T(8,128)S(1)} %get-tuple-element.48.refs_21_), channel_id=1, source_target_pairs={{8,0},{16,8},{24,16},{28,24},{20,28},{12,20},{4,12},{1,4},{9,1},{1... | collective-permute-start | bytes 786440 | tf_op jit(solution)/shard_map/ppermute | solution.py:859
  73.1 4.6 %collective-permute-start.6 = (f32[4,8,16,128]{3,2,1,0:T(8,128)S(1)}, f32[4,8,16,128]{3,2,1,0:T(8,128)S(1)}, u32[]{:S(2)}, u32[]{:S(2)}) collective-permute-start(f32[4,8,16,128]{3,2,1,0:T(8,128)S(1)} %get-tuple-element.48.refs_21_), channel_id=1, source_target_pairs={{0,8},{8,16},{16,24},{24,28},{28,20},{20,12},{12,4},{4,1},{1,9},{9... | collective-permute-start | bytes 786440 | tf_op jit(solution)/shard_map/ppermute | solution.py:858
  77.6 11.9 %all_to_all.22 = f32[32,1,128]{2,1,0:T(1,128)S(1)} all-to-all(f32[32,1,128]{2,1,0:T(1,128)S(1)} %bitcast.5), channel_id=1, replica_groups=mesh['gx'=4,'gy'=2,'gz'=4] {'gx','gy','gz'}, dimensions={0} | all-to-all | bytes 32768 | tf_op jit(solution)/shard_map/all_to_all | solution.py:868
  89.5 0.0 collective-permute-done.5.refs_20_
  89.5 0.0 collective-permute-done.4.refs_19_
  89.5 0.0 collective-permute-done.7.refs_23_
  89.5 0.0 collective-permute-done.6.refs_22_
  89.5 8.4 %shard_map.79 = f32[8,80,128]{2,1,0:T(8,128)S(1)} custom-call(f32[8,64,128]{2,1,0:T(8,128)S(1)} %get-tuple-element.27.refs_0_, f32[8,64,128]{2,1,0:T(8,128)S(1)} %get-tuple-element.28.refs_1_, f32[8,64,128]{2,1,0:T(8,128)S(1)} %get-tuple-element.29.refs_2_, f32[8,64,128]{2,1,0:T(8,128)S(1)} %get-tuple-element.30.refs_3_, ...), custom_call_target="tpu_custom_call" | custom-call | tf_op jit(solution)/shard_map/pallas_call | solution.py:809
  97.9 13.6 %all_to_all.23.chunks = f32[8,80,128]{2,1,0:T(8,128)S(1)} all-to-all(f32[8,80,128]{2,1,0:T(8,128)S(1)} %shard_map.79), channel_id=1, replica_groups=mesh['gx'=4,'gy'=2,'gz'=4] {'gx','gy'}, dimensions={0} | all-to-all | bytes 655360 | tf_op jit(solution)/shard_map/all_to_all | solution.py:885
  111.5 0.9 shard_map.80
  (1 shorter events, 0.0 us)
Async XLA Ops:
  0.6 0.9 copy-start
  1.6 0.8 copy-start.1
  2.4 0.8 copy-start.2
  3.2 0.8 copy-start.3
  25.1 16.6 %collective-permute-start.1 = (f32[8,112,128]{2,1,0:T(8,128)S(1)}, f32[8,112,128]{2,1,0:T(8,128)S(1)}, u32[]{:S(2)}, u32[]{:S(2)}) collective-permute-start(f32[8,112,128]{2,1,0:T(8,128)S(1)} %all_to_all.21.own), channel_id=1, source_target_pairs={{8,0},{16,8},{24,16},{28,24},{20,28},{12,20},{4,12},{1,4},{9,1},{1... | collective-permute-start | bytes 1376264 | tf_op jit(solution)/shard_map/ppermute | solution.py:833
  26.4 15.3 %collective-permute-start = (f32[8,112,128]{2,1,0:T(8,128)S(1)}, f32[8,112,128]{2,1,0:T(8,128)S(1)}, u32[]{:S(2)}, u32[]{:S(2)}) collective-permute-start(f32[8,112,128]{2,1,0:T(8,128)S(1)} %all_to_all.21.own), channel_id=1, source_target_pairs={{0,8},{8,16},{16,24},{24,28},{28,20},{20,12},{12,4},{4,1},{1,9},{9... | collective-permute-start | bytes 1376264 | tf_op jit(solution)/shard_map/ppermute | solution.py:832
  31.0 10.7 %copy-start.4 = (f32[8]{0:T(128)S(1)}, f32[8]{0:T(128)}, u32[]{:S(2)}) copy-start(f32[8]{0:T(128)} %stiffness.1) | copy-start | bytes 100
  31.0 8.1 %collective-permute-start.3 = (f32[8,8,128]{2,1,0:T(8,128)S(1)}, f32[8,8,128]{2,1,0:T(8,128)S(1)}, u32[]{:S(2)}, u32[]{:S(2)}) collective-permute-start(f32[8,8,128]{2,1,0:T(8,128)S(1)} %get-tuple-element.51), channel_id=1, source_target_pairs={{16,0},{24,8},{28,16},{20,24},{12,28},{4,20},{1,12},{9,4},{17,1},{... | collective-permute-start | bytes 98312 | tf_op jit(solution)/shard_map/ppermute | solution.py:834
  32.3 9.4 %collective-permute-start.2 = (f32[8,8,128]{2,1,0:T(8,128)S(1)}, f32[8,8,128]{2,1,0:T(8,128)S(1)}, u32[]{:S(2)}, u32[]{:S(2)}) collective-permute-start(f32[8,8,128]{2,1,0:T(8,128)S(1)} %get-tuple-element.52), channel_id=1, source_target_pairs={{0,16},{8,24},{16,28},{24,20},{28,12},{20,4},{12,1},{4,9},{1,17},{... | collective-permute-start | bytes 98312 | tf_op jit(solution)/shard_map/ppermute | solution.py:835
  65.8 23.7 %collective-permute-start.5 = (f32[4,8,16,128]{3,2,1,0:T(8,128)S(1)}, f32[4,8,16,128]{3,2,1,0:T(8,128)S(1)}, u32[]{:S(2)}, u32[]{:S(2)}) collective-permute-start(f32[4,8,16,128]{3,2,1,0:T(8,128)S(1)} %get-tuple-element.47.refs_18_), channel_id=1, source_target_pairs={{8,0},{16,8},{24,16},{28,24},{20,28},{12,20},{4,12},{1,4},{9,1},{1... | collective-permute-start | bytes 786440 | tf_op jit(solution)/shard_map/ppermute | solution.py:870
  67.1 22.4 %collective-permute-start.4 = (f32[4,8,16,128]{3,2,1,0:T(8,128)S(1)}, f32[4,8,16,128]{3,2,1,0:T(8,128)S(1)}, u32[]{:S(2)}, u32[]{:S(2)}) collective-permute-start(f32[4,8,16,128]{3,2,1,0:T(8,128)S(1)} %get-tuple-element.47.refs_18_), channel_id=1, source_target_pairs={{0,8},{8,16},{16,24},{24,28},{28,20},{20,12},{12,4},{4,1},{1,9},{9... | collective-permute-start | bytes 786440 | tf_op jit(solution)/shard_map/ppermute | solution.py:869
  71.8 17.8 %collective-permute-start.7 = (f32[4,8,16,128]{3,2,1,0:T(8,128)S(1)}, f32[4,8,16,128]{3,2,1,0:T(8,128)S(1)}, u32[]{:S(2)}, u32[]{:S(2)}) collective-permute-start(f32[4,8,16,128]{3,2,1,0:T(8,128)S(1)} %get-tuple-element.48.refs_21_), channel_id=1, source_target_pairs={{8,0},{16,8},{24,16},{28,24},{20,28},{12,20},{4,12},{1,4},{9,1},{1... | collective-permute-start | bytes 786440 | tf_op jit(solution)/shard_map/ppermute | solution.py:859
  73.1 16.5 %collective-permute-start.6 = (f32[4,8,16,128]{3,2,1,0:T(8,128)S(1)}, f32[4,8,16,128]{3,2,1,0:T(8,128)S(1)}, u32[]{:S(2)}, u32[]{:S(2)}) collective-permute-start(f32[4,8,16,128]{3,2,1,0:T(8,128)S(1)} %get-tuple-element.48.refs_21_), channel_id=1, source_target_pairs={{0,8},{8,16},{16,24},{24,28},{28,20},{20,12},{12,4},{4,1},{1,9},{9... | collective-permute-start | bytes 786440 | tf_op jit(solution)/shard_map/ppermute | solution.py:858

commit v6 on v5

--- a/solution.py
+++ b/solution.py
@@ -257,9 +257,10 @@
 BACK = 5
 EDGE = 2
 PHASE = 8
-HELD = 16
-VMEM_LIMIT = 48 * 1024 * 1024
-FORWARD, ADJOINT, RESPONSE = range(3)
+HELD = 24
+VMEM_LIMIT = 44 * 1024 * 1024
+PACK_LIMIT = 60 * 1024 * 1024
+FORWARD, ADJOINT = range(2)
 
 
 def slab_plan_fits(mesh, shape):
@@ -336,6 +337,20 @@
         self.row = lax.broadcasted_iota(jnp.int32, (SUB, LANES), 0)
         self.lane = lax.broadcasted_iota(jnp.int32, (SUB, LANES), 1)
         self.y = self.lane % self.breadth
+        self.kept = {}
+
+    def sliding(self, ref, z, c, x):
+        where = (id(ref), id(z), c)
+        for key in [k for k in self.kept if k[:3] == where and abs(k[3] - x) > 1]:
+            del self.kept[key]
+
+        def load(j):
+            key = (*where, j)
+            if key not in self.kept:
+                self.kept[key] = (ref, z, get(ref, z, c, j))
+            return self.kept[key][2]
+
+        return load
 
     def x(self, load, x, count, step):
         j = x + step
@@ -358,6 +373,12 @@
     def pair_sum(self, f):
         f = f + jnp.where(self.lane % 2 == 0, pltpu.roll(f, LANES - 1, 1), pltpu.roll(f, 1, 1))
         return f + jnp.where(self.row % 2 == 0, pltpu.roll(f, SUB - 1, 0), pltpu.roll(f, 1, 0))
+
+
+def tree(terms):
+    while len(terms) > 1:
+        terms = [sum(terms[k : k + 2]) for k in range(0, len(terms), 2)]
+    return terms[0]
 
 
 def get(ref, z, *index):
@@ -421,21 +442,21 @@
     half_up, half_down = tl.y_masks(1, 0.5)
     keep = 1.0 - JACOBI_WEIGHT
     slots = [(q, 3 * s + k) for s, q in enumerate(seqs) for k in range(3)]
-    transposed = 2
+    transposed = len(seqs)
 
     def faces(x, z):
         c = [get(st[name], z, x) for name in ("cxp", "cxm", "cyp", "cym", "cz")]
         return c + [get(st["cz"], z - 1, x)]
 
     def beside(ref, c, x, z):
-        f = get(ref, z, c, x)
-        load = lambda j: get(ref, z, c, j)
+        load = tl.sliding(ref, z, c, x)
+        f = load(x)
         near = [tl.x(load, x, SUB, 1), tl.x(load, x, SUB, -1), *tl.ys(f, 1)]
         return f, near + [get(ref, z + 1, c, x), get(ref, z - 1, c, x)]
 
     def around(coef, ref, c, x, z):
         f, near = beside(ref, c, x, z)
-        return f, sum(a * b for a, b in zip(coef, near))
+        return f, tree([a * b for a, b in zip(coef, near)])
 
     def residual(z, put):
         for x in range(SUB):
@@ -458,8 +479,6 @@
                         if not start:
                             f, total = around(coef, v, c, x, z)
                             value = value - slope[k] - (diag * f - total)
-                    elif q == RESPONSE:
-                        value = -slope[k]
                     else:
                         value = slope[k] if q in first else get(cor, z, c, x) + slope[k]
                     put(res, value, z, c, x)
@@ -485,10 +504,8 @@
         load = lambda j: get(ref, z, c, j)
         near = [tl.x(load, pair, SUB // 2, 1), tl.x(load, pair, SUB // 2, -1), *tl.ys(f, 2)]
         near += [get(ref, z + 2, c, pair), get(ref, z - 2, c, pair)]
-        value = get(cc0, z, c, pair) + keep * f
-        for name, b in zip(STATIC_COARSE, near):
-            value = value + get(st[name], z, pair) * b
-        return value
+        terms = [get(st[name], z, pair) * b for name, b in zip(STATIC_COARSE, near)]
+        return tree([get(cc0, z, c, pair), keep * f] + terms)
 
     def sweep_one(z, put):
         for pair in range(SUB // 2):
@@ -567,25 +584,26 @@
 
 def setup_kernel(geo, stiffness, own, low, high, low_edge, high_edge, *refs):
     st = dict(zip(STATIC, refs))
-    moved, duals, response, sums, raw, heat, vc, *work = refs[len(STATIC) :]
+    moved, duals, sums, raw, heat, vc, *work = refs[len(STATIC) :]
     v, p, res, cor, cor2, cc0, cc1 = work
     tl = Tiles(geo)
     b, m, n_rows = geo.slab, geo.margin, geo.rows
     granule = geo.block[1]
 
-    for source, base in ((low, m - b), (own, m), (high, m + b)):
-
-        def place(t, _, source=source, base=base):
-            groups = []
-            for u in range(b // SUB):
-                row = pl.multiple_of(t * b, b) + u * SUB
-                groups.append([source[q, pl.ds(row, SUB), :] for q in range(geo.group)])
-            for u, tiles in enumerate(groups):
-                for x, tile in enumerate(swap_granules(tiles, granule)):
-                    raw[t, x, base + u * SUB : base + (u + 1) * SUB, :] = tile
-            return 0
-
-        lax.fori_loop(0, FIELDS, place, 0)
+    def place(t, _):
+        groups = []
+        for source, base in ((low, m - b), (own, m), (high, m + b)):
+            for u in range(0, b, SUB):
+                row = pl.multiple_of(t * b, b) + u
+                tiles = [source[q, pl.ds(row, SUB), :] for q in range(geo.group)]
+                groups.append((base + u, tiles))
+        groups = [(row, swap_granules(tiles, granule)) for row, tiles in groups]
+        for row, tiles in groups:
+            for x, tile in enumerate(tiles):
+                raw[t, x, row : row + SUB, :] = tile
+        return 0
+
+    lax.fori_loop(0, FIELDS, place, 0)
     for source, base in ((low_edge, m - b - EDGE), (high_edge, m + 2 * b)):
         tiles = [source[q] for q in range(geo.group)]
         for x, tile in enumerate(swap_granules(tiles, granule)):
@@ -647,7 +665,7 @@
         for x in range(SUB):
             c, near = beside(lambda z, x: get(st["visc"], z, x), x, z)
             face = [0.5 * (c + o) for o in near]
-            diag = sum(face)
+            diag = tree(face)
             face[2], face[3] = one_up * face[2], one_down * face[3]
             for name, f in zip(("cxp", "cxm", "cyp", "cym", "cz"), face):
                 put(st[name], f, z, x)
@@ -700,79 +718,97 @@
         value = jnp.where(geo.inside(z), 1.0, 0.0)
         for x in range(SUB):
             put(p, value, z, 0, x)
-            put(p, value, z, 1, x)
-            put(p, SCHUR_WEIGHT * get(st["visc"], z, x), z, 2, x)
+            put(p, SCHUR_WEIGHT * get(st["visc"], z, x), z, 1, x)
 
     sweep(0, n_rows, unit)
 
     mine = slice(m, m + b)
+    source = [st["s%d" % k].at[:, mine, :] for k in range(3)]
+    step = [v.at[k, :, mine, :] for k in range(3)]
     iterate(geo, st, work, (ADJOINT,), m - PHASE, m + b + PHASE, (ADJOINT,))
-    for k in range(3):
-        duals[k] = cor[k, :, mine, :]
-    duals[3] = p[0, :, mine, :]
-    iterate(geo, st, work, (ADJOINT, RESPONSE), m, m + b, (RESPONSE,))
-    for k in range(3):
-        duals[4 + k] = cor[k, :, mine, :]
-        response[k] = v[3 + k, :, mine, :]
-    duals[7] = p[0, :, mine, :]
-    response[3] = p[1, :, mine, :]
-    sums_of = [
-        (1, whole_sum(duals[3])),
-        (4, whole_sum(duals[7])),
-        (7, product([duals.at[4 + k] for k in range(4)], [response.at[k] for k in range(4)])),
-    ]
-    sums[...] = in_lanes(sums_of, 1)
+    sums_of = [(0, product(step, source)), (1, whole_sum(p[0, :, mine, :]))]
+    for k in range(4):
+        duals[k] = cor[k, :, mine, :] if k < 3 else p[0, :, mine, :]
+    iterate(geo, st, work, (ADJOINT,), m, m + b)
+    sums_of += [(2, product(step, source))]
+    for k in range(4):
+        duals[4 + k] = cor[k, :, mine, :] if k < 3 else p[0, :, mine, :]
+    sums[...] = in_lanes(sums_of, sums.shape[0])
 
 
 def first_kernel(geo, *refs):
     st = dict(zip(STATIC, refs))
-    duals, part, state, sums, *work = refs[len(STATIC) :]
+    out, *work = refs[len(STATIC) :]
+    v, p = work[:2]
+    rows = slice(geo.margin - PHASE, geo.margin + geo.slab + PHASE)
+    iterate(geo, st, work, (FORWARD,), rows.start, rows.stop, (FORWARD,))
+    for k in range(4):
+        out[k] = v[k, :, rows, :] if k < 3 else p[0, :, rows, :]
+
+
+def refill(geo, v, p, state, rows, shift):
+    for k in range(3):
+        v[k, :, rows, :] = state[k]
+    if shift is None:
+        p[0, :, rows, :] = state[3]
+    else:
+        inside = geo.inside(rows.start, rows.stop - rows.start)
+        p[0, :, rows, :] = state[3] - jnp.where(inside, shift, 0.0)[None]
+
+
+def second_kernel(geo, *refs):
+    st = dict(zip(STATIC, refs))
+    earlier, early, duals, state, sums, *work = refs[len(STATIC) :]
     v, p = work[:2]
     b, m = geo.slab, geo.margin
+    m1, m2 = means(geo, early[...], None)[:2]
+    refill(geo, v, p, earlier, slice(m - PHASE, m + b + PHASE), m1)
+    iterate(geo, st, work, (FORWARD,), m, m + b, mean=m2)
     mine = slice(m, m + b)
-
-    def fields():
-        return [v.at[k, :, mine, :] for k in range(3)] + [p.at[0, :, mine, :]]
-
+    for k in range(4):
+        state[k] = v[k, :, mine, :] if k < 3 else p[0, :, mine, :]
+    fields = [state.at[k] for k in range(4)]
     near, far = [duals.at[k] for k in range(4)], [duals.at[4 + k] for k in range(4)]
-    iterate(geo, st, work, (FORWARD,), m - PHASE, m + b + PHASE, (FORWARD,))
-    sums_of = [(0, whole_sum(p[0, :, mine, :])), (2, product(near, fields()))]
-    iterate(geo, st, work, (FORWARD,), m, m + b)
-    sums_of += [(3, whole_sum(p[0, :, mine, :]))]
-    sums_of += [(5, product(near, fields())), (6, product(far, fields()))]
-    sums[...] = in_lanes(sums_of, sums.shape[0]) + part[...]
-    for k, ref in enumerate(fields()):
-        state[k] = ref[...]
-
-
-def means(geo, sums):
+    sums_of = [(3, product(near, fields)), (4, product(far, fields))]
+    sums[...] = in_lanes(sums_of, sums.shape[0])
+
+
+def means(geo, early, late):
+    sums = early if late is None else early + late
     row = jnp.sum(sums, axis=0, keepdims=True) / geo.cells
     lane = lax.broadcasted_iota(jnp.int32, row.shape, 1)
 
     def at(k):
         return jnp.sum(jnp.where(lane == k, row, 0.0), axis=1, keepdims=True)
 
-    p1, q1, l1_x1, p2, q2, l1_x2, l2_x2, l2_r1 = [at(k) for k in range(8)]
-    m1 = p1
-    m2 = p2 - m1 * q1
-    m3 = l1_x2 - m1 * q2 - m2 * q1 + p1
-    m4 = l2_x2 - m1 * l2_r1 - m2 * q2 + l1_x1 - m3 * q1 + p1
+    c1, l1, c2, l1_x2, l2_x2 = [at(k) for k in range(5)]
+    m1 = c1
+    m2 = c1 + c2 - m1 * l1
+    m3 = c1 + l1_x2
+    m4 = c1 + c2 + l2_x2 - m3 * l1
     return m1, m2, m3, m4
 
 
-def second_kernel(geo, *refs):
+def third_kernel(geo, *refs):
     st = dict(zip(STATIC, refs))
-    own, low, high, own_r, low_r, high_r, sums, moved, out, *work = refs[len(STATIC) :]
+    own, low, high, out, *work = refs[len(STATIC) :]
     v, p = work[:2]
     b, m = geo.slab, geo.margin
-    m1, m2, m3, m4 = means(geo, sums[...])
-    for source, turn, base in ((low, low_r, m - b), (own, own_r, m), (high, high_r, m + b)):
-        rows = slice(base, base + b)
-        for k in range(3):
-            v[k, :, rows, :] = source[k] - m1 * turn[k]
-        shift = jnp.where(geo.inside(base, b), m2, 0.0)
-        p[0, :, rows, :] = source[3] - m1 * turn[3] - shift[None]
-    iterate(geo, st, work, (FORWARD,), m - PHASE, m + b + PHASE, mean=m3)
+    for source, base in ((low, m - b), (own, m), (high, m + b)):
+        refill(geo, v, p, source, slice(base, base + b), None)
+    rows = slice(m - PHASE, m + b + PHASE)
+    iterate(geo, st, work, (FORWARD,), rows.start, rows.stop)
+    for k in range(4):
+        out[k] = v[k, :, rows, :] if k < 3 else p[0, :, rows, :]
+
+
+def fourth_kernel(geo, *refs):
+    st = dict(zip(STATIC, refs))
+    state, early, late, moved, out, *work = refs[len(STATIC) :]
+    v, p = work[:2]
+    b, m = geo.slab, geo.margin
+    m3, m4 = means(geo, early[...], late[...])[2:]
+    refill(geo, v, p, state, slice(m - PHASE, m + b + PHASE), m3)
     iterate(geo, st, work, (FORWARD,), m, m + b, mean=m4)
     for u in range(0, b, SUB):
         at = slice(m + u, m + u + SUB)
@@ -798,8 +834,11 @@
             heat[...] = block
 
 
-def call(kernel, out, scratch, *args, smem=(), hbm=()):
+def call(kernel, out, scratch, *args, smem=(), hbm=(), limit=VMEM_LIMIT, megabytes=2):
     f32 = jnp.float32
+    cost = pl.CostEstimate(
+        flops=megabytes * 1000000, bytes_accessed=megabytes * 1000000, transcendentals=0
+    )
     specs = [
         pl.BlockSpec(
             memory_space=pltpu.SMEM if i in smem else pltpu.HBM if i in hbm else pltpu.VMEM
@@ -812,7 +851,8 @@
         in_specs=specs,
         out_specs=[pl.BlockSpec(memory_space=pltpu.VMEM) for _ in out],
         scratch_shapes=[pltpu.VMEM(s, f32) if isinstance(s, tuple) else s for s in scratch],
-        compiler_params=pltpu.CompilerParams(vmem_limit_bytes=VMEM_LIMIT),
+        compiler_params=pltpu.CompilerParams(vmem_limit_bytes=limit),
+        cost_estimate=cost,
     )(*args)
 
 
@@ -826,6 +866,7 @@
         [pltpu.VMEM(a.shape, a.dtype) for a in inputs] + [pltpu.SemaphoreType.DMA((4,))],
         *inputs,
         hbm=range(4),
+        limit=PACK_LIMIT,
     )
     own = lax.all_to_all(chunks, ("gx", "gy"), 0, 0, tiled=True)
     axes = ("gx", "gy", "gz")
@@ -841,12 +882,14 @@
         fields = [(3 * n, *fine), (n + more, *fine)] + [(3 * n, *fine)] * 3
         return fields + [(3 * n, *coarse)] * 2
 
-    *static, moved, duals, response, part = call(
+    devices = group * geo.nz
+    wide = (4, SUB, b + 2 * PHASE, LANES)
+    *static, moved, duals, early = call(
         functools.partial(setup_kernel, geo),
         [fine] * len(STATIC_FINE)
         + [coarse] * len(STATIC_COARSE)
-        + [slab, (8, *slab), (4, *slab), (1, LANES)],
-        [(FIELDS, *fine), (2, *fine), coarse] + work(2, 1),
+        + [slab, (8, *slab), (devices, LANES)],
+        [(FIELDS, *fine), (2, *fine), coarse] + work(1, 1),
         stiffness,
         own,
         low,
@@ -854,33 +897,45 @@
         low_edge,
         high_edge,
         smem=(0,),
-    )
-    low_response = lax.ppermute(response, axes, geo.shifts(1))
-    high_response = lax.ppermute(response, axes, geo.shifts(-1))
-    state, sums = call(
-        functools.partial(first_kernel, geo),
-        [(4, *slab), (group * geo.nz, LANES)],
+        megabytes=60,
+    )
+    early = lax.all_to_all(early, axes, 0, 0, tiled=True)
+    (state,) = call(
+        functools.partial(first_kernel, geo), [wide], work(1), *static, megabytes=20
+    )
+    state, late = call(
+        functools.partial(second_kernel, geo),
+        [(4, *slab), (devices, LANES)],
         work(1),
         *static,
+        state,
+        early,
         duals,
-        part,
-    )
-    sums = lax.all_to_all(sums, axes, 0, 0, tiled=True)
+        megabytes=20,
+    )
     low_state = lax.ppermute(state, axes, geo.shifts(1))
     high_state = lax.ppermute(state, axes, geo.shifts(-1))
-    (chunks,) = call(
-        functools.partial(second_kernel, geo),
-        [(group, BACK * b, LANES)],
+    late = lax.all_to_all(late, axes, 0, 0, tiled=True)
+    (state,) = call(
+        functools.partial(third_kernel, geo),
+        [wide],
         work(1),
         *static,
         state,
         low_state,
         high_state,
-        response,
-        low_response,
-        high_response,
-        sums,
+        megabytes=30,
+    )
+    (chunks,) = call(
+        functools.partial(fourth_kernel, geo),
+        [(group, BACK * b, LANES)],
+        work(1),
+        *static,
+        state,
+        early,
+        late,
         moved,
+        megabytes=20,
     )
     chunks = lax.all_to_all(chunks, ("gx", "gy"), 0, 0, tiled=True)
     return tuple(

time: 113 us -> 138 us (1.22)
  local copies, waits for them, and re-layouts: 3.45 us -> 32.2 us
  blocking collectives: 45.8 us -> 37.3 us
  starting transfers between devices: 24.4 us -> 29.4 us
    unnamed x10 -> x80, local copies, waits for them, and re-layouts: 3.44 us -> 32.2 us
    all_to_all x1 -> x0, blocking collectives: 11.9 us -> none  [slab_shards(): sums = lax.all_to_all(sums, axes, 0, 0, tiled=True)]
    all_to_all x0 -> x2, starting transfers between devices: none -> 11 us  [the longest x1 5.96 us: slab_shards(): late = lax.all_to_all(late, axes, 0, 0, tiled=True)]
    ppermute x2 -> x0, starting transfers between devices: 5.85 us -> none  [the longest x1 4.56 us: slab_shards(): low_response = lax.ppermute(response, axes, geo.shifts(1))]
    all_to_all x1, blocking collectives: 13.6 us -> 16.8 us  [slab_shards(): chunks = lax.all_to_all(chunks, ('gx', 'gy'), 0, 0, tiled=True)]
    pallas_call x5 -> x7, Pallas kernels: 34 us -> 33.2 us  [call(): pl.pallas_call(kernel, out_shape=[jax.ShapeDtypeStruct(s, f32) for s in o...]
  transfers between devices with their start and end apart: 8 -> 8, of which waited for: 2 -> 2; matrix products, arithmetic and copies ran while one was open for 0% -> 0% of each run, Pallas kernels for 0% -> 7%
where the time goes in v6:
time: 138 us; the launch traced here: 137 us
  blocking collectives  37.3 us (27%)
  Pallas kernels  33.2 us (24%)
  local copies, waits for them, and re-layouts  32.2 us (23%)
  starting transfers between devices  29.4 us (21%)
  waiting for transfers between devices  3.92 us (3%)
    pallas_call x7, Pallas kernels, call(): pl.pallas_call(kernel, out_shape=[jax.ShapeDtypeStruct(s, f32) for s in o...  33.2 us
    unnamed x80, local copies, waits for them, and re-layouts  32.2 us
    all_to_all x1, blocking collectives, slab_shards(): own = lax.all_to_all(chunks, ('gx', 'gy'), 0, 0, tiled=True)  20.5 us
    all_to_all x1, blocking collectives, slab_shards(): chunks = lax.all_to_all(chunks, ('gx', 'gy'), 0, 0, tiled=True)  16.8 us
    all_to_all x1, starting transfers between devices, slab_shards(): late = lax.all_to_all(late, axes, 0, 0, tiled=True)  5.96 us
    ppermute x1, starting transfers between devices, slab_shards(): low_edge = lax.ppermute(own[:, rows + SUB:], axes, geo.shifts(2))  5.45 us
    all_to_all x1, starting transfers between devices, slab_shards(): early = lax.all_to_all(early, axes, 0, 0, tiled=True)  5.02 us
    ppermute x1, starting transfers between devices, slab_shards(): low = lax.ppermute(own, axes, geo.shifts(1))  4.57 us
  transfers between devices with their start and end apart: 8, of which 2 were waited for; matrix products, arithmetic and copies ran while one was open for 0% of the time, Pallas kernels for 7%

profile of v6, /device:TPU:0, one launch (start us, length us, event | category | flops | bytes accessed | tf_op | source)
XLA Modules:
  0.0 136.9 jit_solution(4784243292311005993)
XLA Ops:
  0.6 2.0 %shard_map.76 = f32[8,112,128]{2,1,0:T(8,128)} custom-call(f32[8,16,128]{2,1,0:T(8,128)} %heat_in.1, f32[3,8,16,128]{3,2,1,0:T(8,128)} %flow_in.1, f32[8,16,128]{2,1,0:T(8,128)} %dual_in.1, s32[8,16,128]{2,1,0:T(8,128)} %kind_in.1), custom_call_target="tpu_custom_call" | custom-call | flops 2000000 | bytes 2000000 | tf_op jit(solution)/shard_map/pallas_call | solution.py:848
  2.6 20.5 %all_to_all.32.own = f32[8,112,128]{2,1,0:T(8,128)S(1)} all-to-all(f32[8,112,128]{2,1,0:T(8,128)} %shard_map.76), channel_id=1, replica_groups=mesh['gx'=4,'gy'=2,'gz'=4] {'gx','gy'}, dimensions={0} | all-to-all | bytes 917504 | tf_op jit(solution)/shard_map/all_to_all | solution.py:871
  23.1 1.3 collective-permute-start.1
  24.4 4.6 %collective-permute-start = (f32[8,112,128]{2,1,0:T(8,128)S(1)}, f32[8,112,128]{2,1,0:T(8,128)S(1)}, u32[]{:S(2)}, u32[]{:S(2)}) collective-permute-start(f32[8,112,128]{2,1,0:T(8,128)S(1)} %all_to_all.32.own), channel_id=1, source_target_pairs={{0,8},{8,16},{16,24},{24,28},{28,20},{20,12},{12,4},{4,1},{1,9},{9... | collective-permute-start | bytes 1376264 | tf_op jit(solution)/shard_map/ppermute | solution.py:873
  29.0 0.0 copy-start.39
  29.0 1.3 collective-permute-start.3
  30.3 5.4 %collective-permute-start.2 = (f32[8,8,128]{2,1,0:T(8,128)S(1)}, f32[8,8,128]{2,1,0:T(8,128)S(1)}, u32[]{:S(2)}, u32[]{:S(2)}) collective-permute-start(f32[8,8,128]{2,1,0:T(8,128)S(1)} %get-tuple-element.50), channel_id=1, source_target_pairs={{0,16},{8,24},{16,28},{24,20},{28,12},{20,4},{12,1},{4,9},{1,17},{... | collective-permute-start | bytes 98312 | tf_op jit(solution)/shard_map/ppermute | solution.py:876
  35.8 1.4 %collective-permute-done.3.high_edge = f32[8,8,128]{2,1,0:T(8,128)S(1)} collective-permute-done((f32[8,8,128]{2,1,0:T(8,128)S(1)}, f32[8,8,128]{2,1,0:T(8,128)S(1)}, u32[]{:S(2)}, u32[]{:S(2)}) %collective-permute-start.3) | collective-permute-done | bytes 32800 | tf_op jit(solution)/shard_map/ppermute | solution.py:875
  37.2 2.5 %collective-permute-done.2.low_edge = f32[8,8,128]{2,1,0:T(8,128)S(1)} collective-permute-done((f32[8,8,128]{2,1,0:T(8,128)S(1)}, f32[8,8,128]{2,1,0:T(8,128)S(1)}, u32[]{:S(2)}, u32[]{:S(2)}) %collective-permute-start.2) | collective-permute-done | bytes 32800 | tf_op jit(solution)/shard_map/ppermute | solution.py:876
  39.7 13.7 %shard_map.77 = (f32[8,64,128]{2,1,0:T(8,128)S(1)}, f32[8,64,128]{2,1,0:T(8,128)S(1)}, f32[8,64,128]{2,1,0:T(8,128)S(1)}, f32[8,64,128]{2,1,0:T(8,128)S(1)}, f32...) custom-call(f32[8]{0:T(128)S(1)} %copy-done.39, ...), custom_call_target="tpu_custom_call" | custom-call | flops 60000000 | bytes 60000000 | tf_op jit(solution)/shard_map/pallas_call | solution.py:848
  53.4 0.7 copy-done
  54.0 0.7 copy-done.5
  54.7 0.6 copy-done.10
  55.3 0.7 copy-done.15
  56.0 0.7 copy-done.20
  56.6 0.7 copy-done.25
  57.3 0.8 copy-done.30
  58.1 5.0 %all-to-all-start.1 = ((f32[32,1,128]{2,1,0:T(1,128)}), f32[32,1,128]{2,1,0:T(1,128)S(1)}, u32[]{:S(2)}, u32[]{:S(2)}) async-start(f32[32,1,128]{2,1,0:T(1,128)} %bitcast.1), calls=%async_computation.1 | async-start | bytes 32768 | tf_op jit(solution)/shard_map/all_to_all | solution.py:902
  63.1 0.0 copy-start.1
  63.1 0.9 copy-done.1
  64.0 0.9 copy-done.6
  65.0 0.9 copy-done.11
  65.9 0.9 copy-done.16
  66.8 0.9 copy-done.21
  67.7 0.9 copy-done.26
  68.6 3.6 %shard_map.78.refs_18_ = f32[4,8,32,128]{3,2,1,0:T(8,128)S(1)} custom-call(f32[8,64,128]{2,1,0:T(8,128)S(1)} %get-tuple-element.26.refs_0_, f32[8,64,128]{2,1,0:T(8,128)S(1)} %get-tuple-element.27.refs_1_, f32[8,64,128]{2,1,0:T(8,128)S(1)} %get-tuple-element.28.refs_2_, f32[8,64,128]{2,1,0:T(8,128)S(1)} %get-tuple-element.29.refs_3_, ...), custom_call_target="tpu_custom_call" | custom-call | flops 20000000 | bytes 20000000 | tf_op jit(solution)/shard_map/pallas_call | solution.py:848
  72.1 0.0 all-to-all-done.1
  72.1 0.0 copy-start.2
  72.2 0.9 copy-done.2
  73.1 0.9 copy-done.7
  74.0 0.9 copy-done.12
  74.9 0.9 copy-done.17
  75.8 0.9 copy-done.22
  76.7 0.9 copy-done.27
  77.6 1.0 copy-done.31
  78.6 3.6 %shard_map.79 = (f32[4,8,16,128]{3,2,1,0:T(8,128)}, f32[32,128]{1,0:T(8,128)S(1)}) custom-call(f32[8,64,128]{2,1,0:T(8,128)S(1)} %get-tuple-element.26.refs_0_, f32[8,64,128]{2,1,0:T(8,128)S(1)} %get-tuple-element.27.refs_1_, f32[8,64,128]{2,1,0:T(8,128)S(1)} %get-tuple-element.28.refs_2_, f32[8,64,128]{2,1,0:T(8,128)S(1)} %get-tuple-element.29.refs_3_, ...), custom_call_target="tpu_custom_call" | custom-call | flops 20000000 | bytes 20000000 | tf_op jit(solution)/shard_map/pallas_call | solution.py:848
  82.2 0.6 copy-done.38
  82.8 1.3 collective-permute-start.5
  84.1 4.6 %collective-permute-start.4 = (f32[4,8,16,128]{3,2,1,0:T(8,128)}, f32[4,8,16,128]{3,2,1,0:T(8,128)S(1)}, u32[]{:S(2)}, u32[]{:S(2)}) collective-permute-start(f32[4,8,16,128]{3,2,1,0:T(8,128)} %get-tuple-element.46.refs_18_), channel_id=1, source_target_pairs={{0,8},{8,16},{16,24},{24,28},{28,20},{20,12},{12,4},{4,1},{1,9},{9... | collective-permute-start | bytes 786440 | tf_op jit(solution)/shard_map/ppermute | solution.py:916
  88.7 6.0 %all-to-all-start.2 = ((f32[32,1,128]{2,1,0:T(1,128)}), f32[32,1,128]{2,1,0:T(1,128)}, u32[]{:S(2)}, u32[]{:S(2)}) async-start(f32[32,1,128]{2,1,0:T(1,128)} %bitcast.10), calls=%async_computation.2 | async-start | bytes 32768 | tf_op jit(solution)/shard_map/all_to_all | solution.py:918
  94.6 0.0 collective-permute-done.5.refs_20_
  94.7 0.7 copy-done.32
  95.4 0.0 collective-permute-done.4.refs_19_
  95.4 0.7 copy-done.34
  96.1 0.9 copy-done.3
  97.0 0.9 copy-done.8
  97.9 0.9 copy-done.13
  98.8 0.9 copy-done.18
  99.7 0.9 copy-done.23
  100.6 0.9 copy-done.28
  101.5 0.9 copy-done.33
  102.5 0.9 copy-done.35
  103.4 5.4 %shard_map.80.refs_18_ = f32[4,8,32,128]{3,2,1,0:T(8,128)S(1)} custom-call(f32[8,64,128]{2,1,0:T(8,128)S(1)} %get-tuple-element.26.refs_0_, f32[8,64,128]{2,1,0:T(8,128)S(1)} %get-tuple-element.27.refs_1_, f32[8,64,128]{2,1,0:T(8,128)S(1)} %get-tuple-element.28.refs_2_, f32[8,64,128]{2,1,0:T(8,128)S(1)} %get-tuple-element.29.refs_3_, ...), custom_call_target="tpu_custom_call" | custom-call | flops 30000000 | bytes 30000000 | tf_op jit(solution)/shard_map/pallas_call | solution.py:848
  108.8 0.0 copy-start.4
  108.8 0.9 copy-done.4
  109.7 0.9 copy-done.9
  110.6 0.9 copy-done.14
  111.5 0.9 copy-done.19
  112.4 0.9 copy-done.24
  113.4 0.9 copy-done.29
  114.3 0.8 copy-done.37
  115.1 4.2 %shard_map.81 = f32[8,80,128]{2,1,0:T(8,128)S(1)} custom-call(f32[8,64,128]{2,1,0:T(8,128)S(1)} %get-tuple-element.26.refs_0_, f32[8,64,128]{2,1,0:T(8,128)S(1)} %get-tuple-element.27.refs_1_, f32[8,64,128]{2,1,0:T(8,128)S(1)} %get-tuple-element.28.refs_2_, f32[8,64,128]{2,1,0:T(8,128)S(1)} %get-tuple-element.29.refs_3_, ...), custom_call_target="tpu_custom_call" | custom-call | flops 20000000 | bytes 20000000 | tf_op jit(solution)/shard_map/pallas_call | solution.py:848
  119.3 16.8 %all_to_all.33.chunks = f32[8,80,128]{2,1,0:T(8,128)S(1)} all-to-all(f32[8,80,128]{2,1,0:T(8,128)S(1)} %shard_map.81), channel_id=1, replica_groups=mesh['gx'=4,'gy'=2,'gz'=4] {'gx','gy'}, dimensions={0} | all-to-all | bytes 655360 | tf_op jit(solution)/shard_map/all_to_all | solution.py:940
  136.1 0.9 shard_map.82
  (42 shorter events, 0.1 us)
Async XLA Ops:
  23.1 16.6 %collective-permute-start.1 = (f32[8,112,128]{2,1,0:T(8,128)S(1)}, f32[8,112,128]{2,1,0:T(8,128)S(1)}, u32[]{:S(2)}, u32[]{:S(2)}) collective-permute-start(f32[8,112,128]{2,1,0:T(8,128)S(1)} %all_to_all.32.own), channel_id=1, source_target_pairs={{8,0},{16,8},{24,16},{28,24},{20,28},{12,20},{4,12},{1,4},{9,1},{1... | collective-permute-start | bytes 1376264 | tf_op jit(solution)/shard_map/ppermute | solution.py:874
  24.4 15.3 %collective-permute-start = (f32[8,112,128]{2,1,0:T(8,128)S(1)}, f32[8,112,128]{2,1,0:T(8,128)S(1)}, u32[]{:S(2)}, u32[]{:S(2)}) collective-permute-start(f32[8,112,128]{2,1,0:T(8,128)S(1)} %all_to_all.32.own), channel_id=1, source_target_pairs={{0,8},{8,16},{16,24},{24,28},{28,20},{20,12},{12,4},{4,1},{1,9},{9... | collective-permute-start | bytes 1376264 | tf_op jit(solution)/shard_map/ppermute | solution.py:873
  29.0 10.7 %copy-start.39 = (f32[8]{0:T(128)S(1)}, f32[8]{0:T(128)}, u32[]{:S(2)}) copy-start(f32[8]{0:T(128)} %stiffness.1) | copy-start | bytes 100
  29.0 8.1 %collective-permute-start.3 = (f32[8,8,128]{2,1,0:T(8,128)S(1)}, f32[8,8,128]{2,1,0:T(8,128)S(1)}, u32[]{:S(2)}, u32[]{:S(2)}) collective-permute-start(f32[8,8,128]{2,1,0:T(8,128)S(1)} %get-tuple-element.49), channel_id=1, source_target_pairs={{16,0},{24,8},{28,16},{20,24},{12,28},{4,20},{1,12},{9,4},{17,1},{... | collective-permute-start | bytes 98312 | tf_op jit(solution)/shard_map/ppermute | solution.py:875
  30.3 9.4 %collective-permute-start.2 = (f32[8,8,128]{2,1,0:T(8,128)S(1)}, f32[8,8,128]{2,1,0:T(8,128)S(1)}, u32[]{:S(2)}, u32[]{:S(2)}) collective-permute-start(f32[8,8,128]{2,1,0:T(8,128)S(1)} %get-tuple-element.50), channel_id=1, source_target_pairs={{0,16},{8,24},{16,28},{24,20},{28,12},{20,4},{12,1},{4,9},{1,17},{... | collective-permute-start | bytes 98312 | tf_op jit(solution)/shard_map/ppermute | solution.py:876
  53.4 0.7 copy-start
  54.0 0.7 copy-start.5
  54.7 0.6 copy-start.10
  55.3 0.7 copy-start.15
  56.0 0.7 copy-start.20
  56.6 0.7 copy-start.25
  57.3 0.8 copy-start.30
  58.1 5.0 %copy-start.36 = (f32[8,16,128]{2,1,0:T(8,128)}, f32[8,16,128]{2,1,0:T(8,128)S(1)}, u32[]{:S(2)}) copy-start(f32[8,16,128]{2,1,0:T(8,128)S(1)} %get-tuple-element.48.refs_21_) | copy-start | bytes 196612
  58.1 14.0 %all-to-all-start.1 = ((f32[32,1,128]{2,1,0:T(1,128)}), f32[32,1,128]{2,1,0:T(1,128)S(1)}, u32[]{:S(2)}, u32[]{:S(2)}) async-start(f32[32,1,128]{2,1,0:T(1,128)} %bitcast.1), calls=%async_computation.1 | async-start | bytes 32768 | tf_op jit(solution)/shard_map/all_to_all | solution.py:902
  63.1 0.9 copy-start.1
  64.0 0.9 copy-start.6
  64.9 0.9 copy-start.11
  65.9 0.9 copy-start.16
  66.8 0.9 copy-start.21
  67.7 0.9 copy-start.26
  72.1 0.9 copy-start.2
  73.1 0.9 copy-start.7
  74.0 0.9 copy-start.12
  74.9 0.9 copy-start.17
  75.8 0.9 copy-start.22
  76.7 0.9 copy-start.27
  77.6 1.0 copy-start.31
  82.2 0.6 copy-start.38
  82.8 11.8 %collective-permute-start.5 = (f32[4,8,16,128]{3,2,1,0:T(8,128)}, f32[4,8,16,128]{3,2,1,0:T(8,128)S(1)}, u32[]{:S(2)}, u32[]{:S(2)}) collective-permute-start(f32[4,8,16,128]{3,2,1,0:T(8,128)} %get-tuple-element.46.refs_18_), channel_id=1, source_target_pairs={{8,0},{16,8},{24,16},{28,24},{20,28},{12,20},{4,12},{1,4},{9,1},{1... | collective-permute-start | bytes 786440 | tf_op jit(solution)/shard_map/ppermute | solution.py:917
  84.1 11.3 %collective-permute-start.4 = (f32[4,8,16,128]{3,2,1,0:T(8,128)}, f32[4,8,16,128]{3,2,1,0:T(8,128)S(1)}, u32[]{:S(2)}, u32[]{:S(2)}) collective-permute-start(f32[4,8,16,128]{3,2,1,0:T(8,128)} %get-tuple-element.46.refs_18_), channel_id=1, source_target_pairs={{0,8},{8,16},{16,24},{24,28},{28,20},{20,12},{12,4},{4,1},{1,9},{9... | collective-permute-start | bytes 786440 | tf_op jit(solution)/shard_map/ppermute | solution.py:916
  88.7 20.1 %all-to-all-start.2 = ((f32[32,1,128]{2,1,0:T(1,128)}), f32[32,1,128]{2,1,0:T(1,128)}, u32[]{:S(2)}, u32[]{:S(2)}) async-start(f32[32,1,128]{2,1,0:T(1,128)} %bitcast.10), calls=%async_computation.2 | async-start | bytes 32768 | tf_op jit(solution)/shard_map/all_to_all | solution.py:918
  94.6 0.7 copy-start.32
  95.4 0.7 copy-start.34
  96.1 0.9 copy-start.3
  97.0 0.9 copy-start.8
  97.9 0.9 copy-start.13
  98.8 0.9 copy-start.18
  99.7 0.9 copy-start.23
  100.6 0.9 copy-start.28
  101.5 0.9 copy-start.33
  102.4 0.9 copy-start.35
  108.8 0.9 copy-start.4
  109.7 0.9 copy-start.9
  110.6 0.9 copy-start.14
  111.5 0.9 copy-start.19
  112.4 0.9 copy-start.24
  113.3 0.9 copy-start.29
  114.3 0.8 copy-start.37

commit v7 on v6

--- a/solution.py
+++ b/solution.py
@@ -257,9 +257,8 @@
 BACK = 5
 EDGE = 2
 PHASE = 8
-HELD = 24
-VMEM_LIMIT = 44 * 1024 * 1024
-PACK_LIMIT = 60 * 1024 * 1024
+HELD = 64
+VMEM_LIMIT = 32 * 1024 * 1024
 FORWARD, ADJOINT = range(2)
 
 
@@ -834,7 +833,7 @@
             heat[...] = block
 
 
-def call(kernel, out, scratch, *args, smem=(), hbm=(), limit=VMEM_LIMIT, megabytes=2):
+def call(kernel, out, scratch, *args, smem=(), hbm=(), megabytes=2):
     f32 = jnp.float32
     cost = pl.CostEstimate(
         flops=megabytes * 1000000, bytes_accessed=megabytes * 1000000, transcendentals=0
@@ -851,7 +850,7 @@
         in_specs=specs,
         out_specs=[pl.BlockSpec(memory_space=pltpu.VMEM) for _ in out],
         scratch_shapes=[pltpu.VMEM(s, f32) if isinstance(s, tuple) else s for s in scratch],
-        compiler_params=pltpu.CompilerParams(vmem_limit_bytes=limit),
+        compiler_params=pltpu.CompilerParams(vmem_limit_bytes=VMEM_LIMIT),
         cost_estimate=cost,
     )(*args)
 
@@ -866,7 +865,6 @@
         [pltpu.VMEM(a.shape, a.dtype) for a in inputs] + [pltpu.SemaphoreType.DMA((4,))],
         *inputs,
         hbm=range(4),
-        limit=PACK_LIMIT,
     )
     own = lax.all_to_all(chunks, ("gx", "gy"), 0, 0, tiled=True)
     axes = ("gx", "gy", "gz")

time: 138 us -> 140 us (1.014)
  local copies, waits for them, and re-layouts: 32.2 us -> 35.7 us
    unnamed x80 -> x88, local copies, waits for them, and re-layouts: 32.2 us -> 35.7 us
  transfers between devices with their start and end apart: 8 -> 8, of which waited for: 2 -> 2; matrix products, arithmetic and copies ran while one was open for 0% -> 0% of each run, Pallas kernels for 7% -> 6%
where the time goes in v7:
time: 140 us; the launch traced here: 139 us
  blocking collectives  37.1 us (26%)
  local copies, waits for them, and re-layouts  35.7 us (26%)
  Pallas kernels  31.9 us (23%)
  starting transfers between devices  29.4 us (21%)
  waiting for transfers between devices  3.92 us (3%)
    unnamed x88, local copies, waits for them, and re-layouts  35.7 us
    pallas_call x7, Pallas kernels, call(): pl.pallas_call(kernel, out_shape=[jax.ShapeDtypeStruct(s, f32) for s in o...  31.9 us
    all_to_all x1, blocking collectives, slab_shards(): own = lax.all_to_all(chunks, ('gx', 'gy'), 0, 0, tiled=True)  20.3 us
    all_to_all x1, blocking collectives, slab_shards(): chunks = lax.all_to_all(chunks, ('gx', 'gy'), 0, 0, tiled=True)  16.8 us
    all_to_all x1, starting transfers between devices, slab_shards(): late = lax.all_to_all(late, axes, 0, 0, tiled=True)  5.96 us
    ppermute x1, starting transfers between devices, slab_shards(): low_edge = lax.ppermute(own[:, rows + SUB:], axes, geo.shifts(2))  5.45 us
    all_to_all x1, starting transfers between devices, slab_shards(): early = lax.all_to_all(early, axes, 0, 0, tiled=True)  5.02 us
    ppermute x1, starting transfers between devices, slab_shards(): low = lax.ppermute(own, axes, geo.shifts(1))  4.57 us
  transfers between devices with their start and end apart: 8, of which 2 were waited for; matrix products, arithmetic and copies ran while one was open for 0% of the time, Pallas kernels for 6%

profile of v7, /device:TPU:0, one launch (start us, length us, event | category | flops | bytes accessed | tf_op | source)
XLA Modules:
  0.0 138.9 jit_solution(10698744867964476232)
XLA Ops:
  0.6 0.9 copy-done.36
  1.6 0.8 copy-done.39
  2.4 0.8 copy-done.40
  3.2 0.8 copy-done.41
  4.1 0.7 shard_map.76
  4.8 20.3 %all_to_all.32.own = f32[8,112,128]{2,1,0:T(8,128)S(1)} all-to-all(f32[8,112,128]{2,1,0:T(8,128)S(1)} %shard_map.76), channel_id=1, replica_groups=mesh['gx'=4,'gy'=2,'gz'=4] {'gx','gy'}, dimensions={0} | all-to-all | bytes 917504 | tf_op jit(solution)/shard_map/all_to_all | solution.py:869
  25.1 1.3 collective-permute-start.1
  26.4 4.6 %collective-permute-start = (f32[8,112,128]{2,1,0:T(8,128)S(1)}, f32[8,112,128]{2,1,0:T(8,128)S(1)}, u32[]{:S(2)}, u32[]{:S(2)}) collective-permute-start(f32[8,112,128]{2,1,0:T(8,128)S(1)} %all_to_all.32.own), channel_id=1, source_target_pairs={{0,8},{8,16},{16,24},{24,28},{28,20},{20,12},{12,4},{4,1},{1,9},{9... | collective-permute-start | bytes 1376264 | tf_op jit(solution)/shard_map/ppermute | solution.py:871
  31.0 0.0 copy-start.43
  31.0 1.3 collective-permute-start.3
  32.3 5.4 %collective-permute-start.2 = (f32[8,8,128]{2,1,0:T(8,128)S(1)}, f32[8,8,128]{2,1,0:T(8,128)S(1)}, u32[]{:S(2)}, u32[]{:S(2)}) collective-permute-start(f32[8,8,128]{2,1,0:T(8,128)S(1)} %get-tuple-element.50), channel_id=1, source_target_pairs={{0,16},{8,24},{16,28},{24,20},{28,12},{20,4},{12,1},{4,9},{1,17},{... | collective-permute-start | bytes 98312 | tf_op jit(solution)/shard_map/ppermute | solution.py:874
  37.7 1.4 %collective-permute-done.3.high_edge = f32[8,8,128]{2,1,0:T(8,128)S(1)} collective-permute-done((f32[8,8,128]{2,1,0:T(8,128)S(1)}, f32[8,8,128]{2,1,0:T(8,128)S(1)}, u32[]{:S(2)}, u32[]{:S(2)}) %collective-permute-start.3) | collective-permute-done | bytes 32800 | tf_op jit(solution)/shard_map/ppermute | solution.py:873
  39.1 2.5 %collective-permute-done.2.low_edge = f32[8,8,128]{2,1,0:T(8,128)S(1)} collective-permute-done((f32[8,8,128]{2,1,0:T(8,128)S(1)}, f32[8,8,128]{2,1,0:T(8,128)S(1)}, u32[]{:S(2)}, u32[]{:S(2)}) %collective-permute-start.2) | collective-permute-done | bytes 32800 | tf_op jit(solution)/shard_map/ppermute | solution.py:874
  41.6 13.7 %shard_map.77 = (f32[8,64,128]{2,1,0:T(8,128)S(1)}, f32[8,64,128]{2,1,0:T(8,128)S(1)}, f32[8,64,128]{2,1,0:T(8,128)S(1)}, f32[8,64,128]{2,1,0:T(8,128)S(1)}, f32...) custom-call(f32[8]{0:T(128)S(1)} %copy-done.43, ...), custom_call_target="tpu_custom_call" | custom-call | flops 60000000 | bytes 60000000 | tf_op jit(solution)/shard_map/pallas_call | solution.py:847
  55.3 0.7 copy-done
  56.0 0.7 copy-done.5
  56.6 0.6 copy-done.10
  57.3 0.7 copy-done.15
  57.9 0.7 copy-done.20
  58.6 0.6 copy-done.25
  59.2 0.8 copy-done.30
  60.0 5.0 %all-to-all-start.1 = ((f32[32,1,128]{2,1,0:T(1,128)}), f32[32,1,128]{2,1,0:T(1,128)S(1)}, u32[]{:S(2)}, u32[]{:S(2)}) async-start(f32[32,1,128]{2,1,0:T(1,128)} %bitcast.1), calls=%async_computation.1 | async-start | bytes 32768 | tf_op jit(solution)/shard_map/all_to_all | solution.py:900
  65.1 0.0 copy-start.1
  65.1 0.9 copy-done.1
  66.0 0.9 copy-done.6
  66.9 0.9 copy-done.11
  67.8 0.9 copy-done.16
  68.7 0.9 copy-done.21
  69.6 0.9 copy-done.26
  70.5 3.6 %shard_map.78.refs_18_ = f32[4,8,32,128]{3,2,1,0:T(8,128)S(1)} custom-call(f32[8,64,128]{2,1,0:T(8,128)S(1)} %get-tuple-element.26.refs_0_, f32[8,64,128]{2,1,0:T(8,128)S(1)} %get-tuple-element.27.refs_1_, f32[8,64,128]{2,1,0:T(8,128)S(1)} %get-tuple-element.28.refs_2_, f32[8,64,128]{2,1,0:T(8,128)S(1)} %get-tuple-element.29.refs_3_, ...), custom_call_target="tpu_custom_call" | custom-call | flops 20000000 | bytes 20000000 | tf_op jit(solution)/shard_map/pallas_call | solution.py:847
  74.1 0.9 copy-done.2
  75.0 0.9 copy-done.7
  75.9 0.9 copy-done.12
  76.8 0.9 copy-done.17
  77.7 0.9 copy-done.22
  78.6 0.9 copy-done.27
  79.5 1.0 copy-done.31
  80.6 3.6 %shard_map.79 = (f32[4,8,16,128]{3,2,1,0:T(8,128)}, f32[32,128]{1,0:T(8,128)S(1)}) custom-call(f32[8,64,128]{2,1,0:T(8,128)S(1)} %get-tuple-element.26.refs_0_, f32[8,64,128]{2,1,0:T(8,128)S(1)} %get-tuple-element.27.refs_1_, f32[8,64,128]{2,1,0:T(8,128)S(1)} %get-tuple-element.28.refs_2_, f32[8,64,128]{2,1,0:T(8,128)S(1)} %get-tuple-element.29.refs_3_, ...), custom_call_target="tpu_custom_call" | custom-call | flops 20000000 | bytes 20000000 | tf_op jit(solution)/shard_map/pallas_call | solution.py:847
  84.2 0.6 copy-done.42
  84.8 1.3 collective-permute-start.5
  86.1 4.6 %collective-permute-start.4 = (f32[4,8,16,128]{3,2,1,0:T(8,128)}, f32[4,8,16,128]{3,2,1,0:T(8,128)S(1)}, u32[]{:S(2)}, u32[]{:S(2)}) collective-permute-start(f32[4,8,16,128]{3,2,1,0:T(8,128)} %get-tuple-element.46.refs_18_), channel_id=1, source_target_pairs={{0,8},{8,16},{16,24},{24,28},{28,20},{20,12},{12,4},{4,1},{1,9},{9... | collective-permute-start | bytes 786440 | tf_op jit(solution)/shard_map/ppermute | solution.py:914
  90.6 6.0 %all-to-all-start.2 = ((f32[32,1,128]{2,1,0:T(1,128)}), f32[32,1,128]{2,1,0:T(1,128)}, u32[]{:S(2)}, u32[]{:S(2)}) async-start(f32[32,1,128]{2,1,0:T(1,128)} %bitcast.10), calls=%async_computation.2 | async-start | bytes 32768 | tf_op jit(solution)/shard_map/all_to_all | solution.py:916
  96.6 0.7 copy-done.32
  97.3 0.7 copy-done.34
  98.0 0.9 copy-done.3
  98.9 0.9 copy-done.8
  99.8 0.9 copy-done.13
  100.7 0.9 copy-done.18
  101.6 0.9 copy-done.23
  102.5 0.9 copy-done.28
  103.4 0.9 copy-done.33
  104.4 0.9 copy-done.35
  105.3 5.4 %shard_map.80.refs_18_ = f32[4,8,32,128]{3,2,1,0:T(8,128)S(1)} custom-call(f32[8,64,128]{2,1,0:T(8,128)S(1)} %get-tuple-element.26.refs_0_, f32[8,64,128]{2,1,0:T(8,128)S(1)} %get-tuple-element.27.refs_1_, f32[8,64,128]{2,1,0:T(8,128)S(1)} %get-tuple-element.28.refs_2_, f32[8,64,128]{2,1,0:T(8,128)S(1)} %get-tuple-element.29.refs_3_, ...), custom_call_target="tpu_custom_call" | custom-call | flops 30000000 | bytes 30000000 | tf_op jit(solution)/shard_map/pallas_call | solution.py:847
  110.8 0.0 copy-start.4
  110.8 0.9 copy-done.4
  111.7 0.9 copy-done.9
  112.6 0.9 copy-done.14
  113.5 0.9 copy-done.19
  114.4 0.9 copy-done.24
  115.3 0.9 copy-done.29
  116.2 0.8 copy-done.38
  117.0 4.2 %shard_map.81 = f32[8,80,128]{2,1,0:T(8,128)S(1)} custom-call(f32[8,64,128]{2,1,0:T(8,128)S(1)} %get-tuple-element.26.refs_0_, f32[8,64,128]{2,1,0:T(8,128)S(1)} %get-tuple-element.27.refs_1_, f32[8,64,128]{2,1,0:T(8,128)S(1)} %get-tuple-element.28.refs_2_, f32[8,64,128]{2,1,0:T(8,128)S(1)} %get-tuple-element.29.refs_3_, ...), custom_call_target="tpu_custom_call" | custom-call | flops 20000000 | bytes 20000000 | tf_op jit(solution)/shard_map/pallas_call | solution.py:847
  121.2 16.8 %all_to_all.33.chunks = f32[8,80,128]{2,1,0:T(8,128)S(1)} all-to-all(f32[8,80,128]{2,1,0:T(8,128)S(1)} %shard_map.81), channel_id=1, replica_groups=mesh['gx'=4,'gy'=2,'gz'=4] {'gx','gy'}, dimensions={0} | all-to-all | bytes 655360 | tf_op jit(solution)/shard_map/all_to_all | solution.py:938
  138.0 0.9 shard_map.82
  (50 shorter events, 0.1 us)
Async XLA Ops:
  0.6 0.9 copy-start.36
  1.6 0.8 copy-start.39
  2.4 0.8 copy-start.40
  3.2 0.8 copy-start.41
  25.1 16.6 %collective-permute-start.1 = (f32[8,112,128]{2,1,0:T(8,128)S(1)}, f32[8,112,128]{2,1,0:T(8,128)S(1)}, u32[]{:S(2)}, u32[]{:S(2)}) collective-permute-start(f32[8,112,128]{2,1,0:T(8,128)S(1)} %all_to_all.32.own), channel_id=1, source_target_pairs={{8,0},{16,8},{24,16},{28,24},{20,28},{12,20},{4,12},{1,4},{9,1},{1... | collective-permute-start | bytes 1376264 | tf_op jit(solution)/shard_map/ppermute | solution.py:872
  26.4 15.3 %collective-permute-start = (f32[8,112,128]{2,1,0:T(8,128)S(1)}, f32[8,112,128]{2,1,0:T(8,128)S(1)}, u32[]{:S(2)}, u32[]{:S(2)}) collective-permute-start(f32[8,112,128]{2,1,0:T(8,128)S(1)} %all_to_all.32.own), channel_id=1, source_target_pairs={{0,8},{8,16},{16,24},{24,28},{28,20},{20,12},{12,4},{4,1},{1,9},{9... | collective-permute-start | bytes 1376264 | tf_op jit(solution)/shard_map/ppermute | solution.py:871
  31.0 10.7 %copy-start.43 = (f32[8]{0:T(128)S(1)}, f32[8]{0:T(128)}, u32[]{:S(2)}) copy-start(f32[8]{0:T(128)} %stiffness.1) | copy-start | bytes 100
  31.0 8.1 %collective-permute-start.3 = (f32[8,8,128]{2,1,0:T(8,128)S(1)}, f32[8,8,128]{2,1,0:T(8,128)S(1)}, u32[]{:S(2)}, u32[]{:S(2)}) collective-permute-start(f32[8,8,128]{2,1,0:T(8,128)S(1)} %get-tuple-element.49), channel_id=1, source_target_pairs={{16,0},{24,8},{28,16},{20,24},{12,28},{4,20},{1,12},{9,4},{17,1},{... | collective-permute-start | bytes 98312 | tf_op jit(solution)/shard_map/ppermute | solution.py:873
  32.3 9.4 %collective-permute-start.2 = (f32[8,8,128]{2,1,0:T(8,128)S(1)}, f32[8,8,128]{2,1,0:T(8,128)S(1)}, u32[]{:S(2)}, u32[]{:S(2)}) collective-permute-start(f32[8,8,128]{2,1,0:T(8,128)S(1)} %get-tuple-element.50), channel_id=1, source_target_pairs={{0,16},{8,24},{16,28},{24,20},{28,12},{20,4},{12,1},{4,9},{1,17},{... | collective-permute-start | bytes 98312 | tf_op jit(solution)/shard_map/ppermute | solution.py:874
  55.3 0.7 copy-start
  56.0 0.7 copy-start.5
  56.6 0.6 copy-start.10
  57.3 0.7 copy-start.15
  57.9 0.7 copy-start.20
  58.6 0.7 copy-start.25
  59.2 0.8 copy-start.30
  60.0 5.0 %copy-start.37 = (f32[8,16,128]{2,1,0:T(8,128)}, f32[8,16,128]{2,1,0:T(8,128)S(1)}, u32[]{:S(2)}) copy-start(f32[8,16,128]{2,1,0:T(8,128)S(1)} %get-tuple-element.48.refs_21_) | copy-start | bytes 196612
  60.0 14.0 %all-to-all-start.1 = ((f32[32,1,128]{2,1,0:T(1,128)}), f32[32,1,128]{2,1,0:T(1,128)S(1)}, u32[]{:S(2)}, u32[]{:S(2)}) async-start(f32[32,1,128]{2,1,0:T(1,128)} %bitcast.1), calls=%async_computation.1 | async-start | bytes 32768 | tf_op jit(solution)/shard_map/all_to_all | solution.py:900
  65.1 0.9 copy-start.1
  66.0 0.9 copy-start.6
  66.9 0.9 copy-start.11
  67.8 0.9 copy-start.16
  68.7 0.9 copy-start.21
  69.6 0.9 copy-start.26
  74.1 0.9 copy-start.2
  75.0 0.9 copy-start.7
  75.9 0.9 copy-start.12
  76.8 0.9 copy-start.17
  77.7 0.9 copy-start.22
  78.6 0.9 copy-start.27
  79.5 1.0 copy-start.31
  84.2 0.6 copy-start.42
  84.8 11.8 %collective-permute-start.5 = (f32[4,8,16,128]{3,2,1,0:T(8,128)}, f32[4,8,16,128]{3,2,1,0:T(8,128)S(1)}, u32[]{:S(2)}, u32[]{:S(2)}) collective-permute-start(f32[4,8,16,128]{3,2,1,0:T(8,128)} %get-tuple-element.46.refs_18_), channel_id=1, source_target_pairs={{8,0},{16,8},{24,16},{28,24},{20,28},{12,20},{4,12},{1,4},{9,1},{1... | collective-permute-start | bytes 786440 | tf_op jit(solution)/shard_map/ppermute | solution.py:915
  86.1 11.2 %collective-permute-start.4 = (f32[4,8,16,128]{3,2,1,0:T(8,128)}, f32[4,8,16,128]{3,2,1,0:T(8,128)S(1)}, u32[]{:S(2)}, u32[]{:S(2)}) collective-permute-start(f32[4,8,16,128]{3,2,1,0:T(8,128)} %get-tuple-element.46.refs_18_), channel_id=1, source_target_pairs={{0,8},{8,16},{16,24},{24,28},{28,20},{20,12},{12,4},{4,1},{1,9},{9... | collective-permute-start | bytes 786440 | tf_op jit(solution)/shard_map/ppermute | solution.py:914
  90.6 20.1 %all-to-all-start.2 = ((f32[32,1,128]{2,1,0:T(1,128)}), f32[32,1,128]{2,1,0:T(1,128)}, u32[]{:S(2)}, u32[]{:S(2)}) async-start(f32[32,1,128]{2,1,0:T(1,128)} %bitcast.10), calls=%async_computation.2 | async-start | bytes 32768 | tf_op jit(solution)/shard_map/all_to_all | solution.py:916
  96.6 0.7 copy-start.32
  97.3 0.7 copy-start.34
  98.0 0.9 copy-start.3
  98.9 0.9 copy-start.8
  99.8 0.9 copy-start.13
  100.7 0.9 copy-start.18
  101.6 0.9 copy-start.23
  102.5 0.9 copy-start.28
  103.4 0.9 copy-start.33
  104.4 0.9 copy-start.35
  110.8 0.9 copy-start.4
  111.7 0.9 copy-start.9
  112.6 0.9 copy-start.14
  113.5 0.9 copy-start.19
  114.4 0.9 copy-start.24
  115.3 0.9 copy-start.29
  116.2 0.8 copy-start.38

commit v8 on v7

--- a/solution.py
+++ b/solution.py
@@ -257,7 +257,8 @@
 BACK = 5
 EDGE = 2
 PHASE = 8
-HELD = 64
+HELD = 24
+TX, TY = 4, 2
 VMEM_LIMIT = 32 * 1024 * 1024
 FORWARD, ADJOINT = range(2)
 
@@ -291,6 +292,12 @@
             for iy in range(self.ny):
                 step = ix if iy % 2 == 0 else self.nx - 1 - ix
                 self.place.append(iy * self.nx + step)
+        self.order = [
+            (x + TX * part, y)
+            for x in range(TX)
+            for y in range(TY)
+            for part in range(self.block[0] // TX)
+        ]
         self.holder = [self.place.index(j) for j in range(self.group)]
 
     def device(self, slab):
@@ -315,63 +322,90 @@
         return (layer >= 0) & (layer < self.height)
 
 
-def swap_granules(tiles, granule):
-    lane = lax.broadcasted_iota(jnp.int32, (SUB, LANES), 1) // granule
-    for bit in (1, 2, 4):
-        low = (lane & bit) == 0
-        new = list(tiles)
-        for a in range(SUB):
-            if a & bit:
-                continue
+def exchange(tiles, bit, width):
+    lane = lax.broadcasted_iota(jnp.int32, (SUB, LANES), 1)
+    low = (lane & width) == 0
+    new = list(tiles)
+    for a in range(SUB):
+        if not a & bit:
             b = a | bit
-            new[a] = jnp.where(low, tiles[a], pltpu.roll(tiles[b], granule * bit, 1))
-            new[b] = jnp.where(low, pltpu.roll(tiles[a], LANES - granule * bit, 1), tiles[b])
-        tiles = new
+            new[a] = jnp.where(low, tiles[a], pltpu.roll(tiles[b], width, 1))
+            new[b] = jnp.where(low, pltpu.roll(tiles[a], LANES - width, 1), tiles[b])
+    return new
+
+
+def gather_tiles(tiles, granule):
+    for bit, width in ((1, granule // 2), (1, granule), (2, 2 * granule), (4, 4 * granule)):
+        tiles = exchange(tiles, bit, width)
+    return tiles
+
+
+def scatter_tiles(tiles, granule):
+    for bit, width in ((4, 4 * granule), (2, 2 * granule), (1, granule), (1, granule // 2)):
+        tiles = exchange(tiles, bit, width)
     return tiles
 
 
 class Tiles:
     def __init__(self, geo):
-        self.breadth = geo.breadth
+        self.span = geo.breadth // TY
         self.row = lax.broadcasted_iota(jnp.int32, (SUB, LANES), 0)
         self.lane = lax.broadcasted_iota(jnp.int32, (SUB, LANES), 1)
-        self.y = self.lane % self.breadth
+        self.y = self.lane % self.span
         self.kept = {}
 
-    def sliding(self, ref, z, c, x):
-        where = (id(ref), id(z), c)
-        for key in [k for k in self.kept if k[:3] == where and abs(k[3] - x) > 1]:
+    def sliding(self, ref, z, lead, t):
+        where = (id(ref), id(z), lead)
+        for key in [k for k in self.kept if k[:3] == where and abs(k[3] - t) > 3]:
             del self.kept[key]
 
         def load(j):
             key = (*where, j)
             if key not in self.kept:
-                self.kept[key] = (ref, z, get(ref, z, c, j))
+                self.kept[key] = (ref, z, get(ref, z, *lead, j))
             return self.kept[key][2]
 
         return load
 
-    def x(self, load, x, count, step):
-        j = x + step
+    def x(self, load, t, step, count=TX, stride=TY):
+        j = t // stride + step
         if 0 <= j < count:
-            return load(j)
+            return load(t + step * stride)
         if step > 0:
-            turned = pltpu.roll(load(0), LANES - self.breadth, 1)
-            return jnp.where(self.lane < LANES - self.breadth, turned, 0.0)
-        turned = pltpu.roll(load(count - 1), self.breadth, 1)
-        return jnp.where(self.lane >= self.breadth, turned, 0.0)
-
-    def ys(self, f, d):
-        return pltpu.roll(f, LANES - d, 1), pltpu.roll(f, d, 1)
-
-    def y_masks(self, d, value):
-        up, down = self.y < self.breadth - d, self.y >= d
-        value = jnp.float32(value)
-        return jnp.where(up, value, 0.0), jnp.where(down, value, 0.0)
+            turned = pltpu.roll(load(t % stride), LANES - self.span, 1)
+            return jnp.where(self.lane < LANES - self.span, turned, 0.0)
+        turned = pltpu.roll(load((count - 1) * stride + t % stride), self.span, 1)
+        return jnp.where(self.lane >= self.span, turned, 0.0)
+
+    def lanes(self, f, step):
+        if step > 0:
+            return jnp.where(self.y < self.span - 1, pltpu.roll(f, LANES - 1, 1), 0.0)
+        return jnp.where(self.y > 0, pltpu.roll(f, 1, 1), 0.0)
+
+    def y_side(self, load, t, step):
+        if (t % TY == 0) == (step > 0):
+            return load(t + step)
+        return self.lanes(load(t - step), step)
+
+    def beside(self, ref, z, lead, t):
+        load = self.sliding(ref, z, lead, t)
+        near = [self.x(load, t, 1), self.x(load, t, -1)]
+        near += [self.y_side(load, t, 1), self.y_side(load, t, -1)]
+        return load(t), near + [get(ref, z + 1, *lead, t), get(ref, z - 1, *lead, t)]
+
+    def coarse_beside(self, ref, z, lead, t):
+        load = lambda j: get(ref, z, *lead, j)
+        f = load(t)
+        near = [self.x(load, t, step, TX // 2, 1) for step in (1, -1)]
+        near += [self.lanes(f, 1), self.lanes(f, -1)]
+        return f, near + [get(ref, z + 2, *lead, t), get(ref, z - 2, *lead, t)]
 
     def pair_sum(self, f):
-        f = f + jnp.where(self.lane % 2 == 0, pltpu.roll(f, LANES - 1, 1), pltpu.roll(f, 1, 1))
         return f + jnp.where(self.row % 2 == 0, pltpu.roll(f, SUB - 1, 0), pltpu.roll(f, 1, 0))
+
+
+def block_of(t):
+    return range(2 * TY * t, 2 * TY * (t + 1))
 
 
 def tree(terms):
@@ -417,8 +451,11 @@
         copy.start()
     for copy in copies:
         copy.wait()
-    flat = [heat[...], flow[0], flow[1], flow[2], dual[...], kind[...].astype(jnp.float32)]
-    turned = [f.reshape(LANES, LANES).T for f in flat]
+    fields = [heat, flow.at[0], flow.at[1], flow.at[2], dual, kind]
+    turned = []
+    for ref in fields:
+        rows = [ref[x, pl.ds(y, SUB, stride=TY), :] for x, y in geo.order]
+        turned.append(jnp.concatenate(rows, 0).astype(jnp.float32).T)
     for j in range(geo.group):
         q = geo.holder[j]
         for f in range(FIELDS):
@@ -430,7 +467,7 @@
         out[q, tail + SUB : tail + 2 * SUB, :] = last
 
 
-STATIC_FINE = ("s0", "s1", "s2", "visc", "w", "diag", "cxp", "cxm", "cyp", "cym", "cz")
+STATIC_FINE = ("s0", "s1", "s2", "hv", "w")
 STATIC_COARSE = ("kxp", "kxm", "kyp", "kym", "kzp", "kzm", "wc")
 STATIC = STATIC_FINE + STATIC_COARSE
 
@@ -438,126 +475,117 @@
 def iterate(geo, st, work, seqs, lo, hi, first=(), mean=None):
     v, p, res, cor, cor2, cc0, cc1 = work
     tl = Tiles(geo)
-    half_up, half_down = tl.y_masks(1, 0.5)
     keep = 1.0 - JACOBI_WEIGHT
-    slots = [(q, 3 * s + k) for s, q in enumerate(seqs) for k in range(3)]
+    comps = range(3 * len(seqs))
     transposed = len(seqs)
 
-    def faces(x, z):
-        c = [get(st[name], z, x) for name in ("cxp", "cxm", "cyp", "cym", "cz")]
-        return c + [get(st["cz"], z - 1, x)]
-
-    def beside(ref, c, x, z):
-        load = tl.sliding(ref, z, c, x)
-        f = load(x)
-        near = [tl.x(load, x, SUB, 1), tl.x(load, x, SUB, -1), *tl.ys(f, 1)]
-        return f, near + [get(ref, z + 1, c, x), get(ref, z - 1, c, x)]
-
-    def around(coef, ref, c, x, z):
-        f, near = beside(ref, c, x, z)
-        return f, tree([a * b for a, b in zip(coef, near)])
+    def faces(t, z):
+        h, near = tl.beside(st["hv"], z, (), t)
+        return [h + other for other in near]
+
+    def around(face, ref, c, t, z):
+        f, near = tl.beside(ref, z, (c,), t)
+        return f, tree([a * b for a, b in zip(face, near)])
 
     def residual(z, put):
-        for x in range(SUB):
-            w = get(st["w"], z, x)
+        for t in range(SUB):
+            w = get(st["w"], z, t)
             if FORWARD in seqs and FORWARD not in first:
-                coef, diag = faces(x, z), get(st["diag"], z, x)
+                face = faces(t, z)
+                diag = tree(face)
             for s, q in enumerate(seqs):
                 start = q == FORWARD and q in first
                 if not start:
-                    _, near = beside(p, transposed if q == ADJOINT else s, x, z)
-                    slope = [
-                        0.5 * (near[0] - near[1]),
-                        half_up * near[2] - half_down * near[3],
-                        0.5 * (near[4] - near[5]),
-                    ]
+                    _, near = tl.beside(p, z, (transposed if q == ADJOINT else s,), t)
+                    slope = [0.5 * (near[2 * k] - near[2 * k + 1]) for k in range(3)]
                 for k in range(3):
                     c = 3 * s + k
                     if q == FORWARD:
-                        value = get(st["s%d" % k], z, x)
+                        value = get(st["s%d" % k], z, t)
                         if not start:
-                            f, total = around(coef, v, c, x, z)
+                            f, total = around(face, v, c, t, z)
                             value = value - slope[k] - (diag * f - total)
                     else:
-                        value = slope[k] if q in first else get(cor, z, c, x) + slope[k]
-                    put(res, value, z, c, x)
-                    put(cor, w * value, z, c, x)
+                        value = slope[k] if q in first else get(cor, z, c, t) + slope[k]
+                    put(res, value, z, c, t)
+                    put(cor, w * value, z, c, t)
 
     sweep(lo - 8, hi + 8, residual)
 
     def restricted(z, put):
-        for pair in range(SUB // 2):
-            coefs = [faces(2 * pair + side, z) for side in range(2)]
+        for pair in range(TX // 2):
+            left = [0.0 for _ in comps]
+            for t in block_of(pair):
+                face = faces(t, z)
+                for c in comps:
+                    _, total = around(face, cor, c, t, z)
+                    left[c] = left[c] + (keep * get(res, z, c, t) + total)
             wc = 0.125 * get(st["wc"], z, pair)
-            for _, c in slots:
-                left = 0.0
-                for side in range(2):
-                    _, total = around(coefs[side], cor, c, 2 * pair + side, z)
-                    left = left + (keep * get(res, z, c, 2 * pair + side) + total)
-                put(cc0, wc * tl.pair_sum(left), z, c, pair)
+            for c in comps:
+                put(cc0, wc * tl.pair_sum(left[c]), z, c, pair)
 
     sweep(lo - 8, hi + 8, restricted)
 
     def coarse_step(ref, c, pair, z):
-        f = get(ref, z, c, pair)
-        load = lambda j: get(ref, z, c, j)
-        near = [tl.x(load, pair, SUB // 2, 1), tl.x(load, pair, SUB // 2, -1), *tl.ys(f, 2)]
-        near += [get(ref, z + 2, c, pair), get(ref, z - 2, c, pair)]
+        f, near = tl.coarse_beside(ref, z, (c,), pair)
         terms = [get(st[name], z, pair) * b for name, b in zip(STATIC_COARSE, near)]
         return tree([get(cc0, z, c, pair), keep * f] + terms)
 
     def sweep_one(z, put):
-        for pair in range(SUB // 2):
-            for _, c in slots:
+        for pair in range(TX // 2):
+            for c in comps:
                 put(cc1, coarse_step(cc0, c, pair, z), z, c, pair)
 
     sweep(lo - 4, hi + 4, sweep_one)
 
     def sweep_two(z, put):
-        for pair in range(SUB // 2):
-            for _, c in slots:
+        for pair in range(TX // 2):
+            for c in comps:
                 value = coarse_step(cc1, c, pair, z)
-                for x in (2 * pair, 2 * pair + 1):
-                    put(cor2, get(cor, z, c, x) + value, z, c, x)
+                for t in block_of(pair):
+                    put(cor2, get(cor, z, c, t) + value, z, c, t)
 
     sweep(lo - 4, hi + 4, sweep_two)
 
     def velocity(z, put):
-        for x in range(SUB):
-            coef, w = faces(x, z), get(st["w"], z, x)
-            for q, c in slots:
-                f, total = around(coef, cor2, c, x, z)
-                value = get(cor, z, c, x) + keep * f + w * total
-                if q == FORWARD and q not in first:
-                    value = get(v, z, c, x) + value
-                put(v, value, z, c, x)
+        for t in range(SUB):
+            face, w = faces(t, z), get(st["w"], z, t)
+            for c in comps:
+                f, total = around(face, cor2, c, t, z)
+                value = get(cor, z, c, t) + keep * f + w * total
+                if seqs[c // 3] == FORWARD and FORWARD not in first:
+                    value = get(v, z, c, t) + value
+                put(v, value, z, c, t)
 
     sweep(lo - 4, hi + 4, velocity)
 
     def pressure(z, put):
-        for x in range(SUB):
-            visc = SCHUR_WEIGHT * get(st["visc"], z, x)
+        for t in range(SUB):
+            half = get(st["hv"], z, t)
             for s, q in enumerate(seqs):
-                load = lambda j: get(v, z, 3 * s, j)
-                div = 0.5 * (tl.x(load, x, SUB, 1) - tl.x(load, x, SUB, -1))
-                up, down = tl.ys(get(v, z, 3 * s + 1, x), 1)
-                div = div + (half_up * up - half_down * down)
-                div = div + 0.5 * (get(v, z + 1, 3 * s + 2, x) - get(v, z - 1, 3 * s + 2, x))
+                c = 3 * s
                 if q == ADJOINT:
-                    value = get(p, z, s, x) + div
-                    put(p, value, z, s, x)
-                    put(p, visc * value, z, transposed, x)
-                    coef, diag = faces(x, z), get(st["diag"], z, x)
-                    for c in range(3 * s, 3 * s + 3):
-                        f, total = around(coef, v, c, x, z)
-                        put(cor, get(res, z, c, x) - (diag * f - total), z, c, x)
+                    face = faces(t, z)
+                    diag, div = tree(face), 0.0
+                    for k in range(3):
+                        f, near = tl.beside(v, z, (c + k,), t)
+                        div = div + 0.5 * (near[2 * k] - near[2 * k + 1])
+                        total = tree([a * b for a, b in zip(face, near)])
+                        put(cor, get(res, z, c + k, t) - (diag * f - total), z, c + k, t)
+                    value = get(p, z, s, t) + div
+                    put(p, value, z, s, t)
+                    put(p, half * value, z, transposed, t)
                     continue
-                value = -(visc * div)
+                one, two = tl.sliding(v, z, (c,), t), tl.sliding(v, z, (c + 1,), t)
+                div = tl.x(one, t, 1) - tl.x(one, t, -1)
+                div = div + (tl.y_side(two, t, 1) - tl.y_side(two, t, -1))
+                div = div + (get(v, z + 1, c + 2, t) - get(v, z - 1, c + 2, t))
+                value = -(half * (0.5 * div))
                 if not (q == FORWARD and q in first):
-                    value = get(p, z, s, x) + value
+                    value = get(p, z, s, t) + value
                 if mean is not None:
                     value = value - jnp.where(geo.inside(z), mean, 0.0)
-                put(p, value, z, s, x)
+                put(p, value, z, s, t)
 
     sweep(lo, hi, pressure)
 
@@ -596,7 +624,7 @@
                 row = pl.multiple_of(t * b, b) + u
                 tiles = [source[q, pl.ds(row, SUB), :] for q in range(geo.group)]
                 groups.append((base + u, tiles))
-        groups = [(row, swap_granules(tiles, granule)) for row, tiles in groups]
+        groups = [(row, gather_tiles(tiles, granule)) for row, tiles in groups]
         for row, tiles in groups:
             for x, tile in enumerate(tiles):
                 raw[t, x, row : row + SUB, :] = tile
@@ -605,55 +633,41 @@
     lax.fori_loop(0, FIELDS, place, 0)
     for source, base in ((low_edge, m - b - EDGE), (high_edge, m + 2 * b)):
         tiles = [source[q] for q in range(geo.group)]
-        for x, tile in enumerate(swap_granules(tiles, granule)):
+        for x, tile in enumerate(gather_tiles(tiles, granule)):
             for f in range(4):
                 raw[f, x, base : base + EDGE, :] = tile[f * EDGE : (f + 1) * EDGE]
 
-    one_up, one_down = tl.y_masks(1, 1.0)
-
-    def beside(load, x, z):
-        f = load(z, x)
-        up, down = tl.ys(f, 1)
-        near = [tl.x(lambda j: load(z, j), x, SUB, s) for s in (1, -1)]
-        return f, near + [one_up * up, one_down * down, load(z + 1, x), load(z - 1, x)]
-
-    def field(f):
-        return lambda z, x: get(raw, z, f, x)
-
-    def advance(old, new):
+    def advance(ref, old, new):
         def body(z, put):
             inside = geo.inside(z)
-            for x in range(SUB):
-                f, near = beside(old, x, z)
+            for t in range(SUB):
+                f, near = tl.beside(ref, z, (old,), t)
                 drift = 0.0
                 for k in range(3):
-                    flow = get(raw, z, 1 + k, x)
+                    flow = get(raw, z, 1 + k, t)
                     drift = drift + jnp.maximum(flow, 0.0) * (f - near[2 * k + 1])
                     drift = drift + jnp.minimum(flow, 0.0) * (near[2 * k] - f)
-                spread = sum(near) - 6.0 * f
+                spread = tree(near) - 6.0 * f
                 value = f - INCREMENT_DT * drift + INCREMENT_DT * DIFFUSIVITY * spread
-                put(heat, jnp.where(inside, value, 0.0), z, new, x)
+                put(heat, jnp.where(inside, value, 0.0), z, new, t)
 
         return body
 
-    def warm(new):
-        return lambda z, x: get(heat, z, new, x)
-
-    sweep(m - b - 4, m + 2 * b + 4, advance(field(0), 0))
-    sweep(m - b, m + 2 * b, advance(warm(0), 1))
+    sweep(m - b - 4, m + 2 * b + 4, advance(raw, 0, 0))
+    sweep(m - b, m + 2 * b, advance(heat, 0, 1))
 
     def viscosity(z, put):
         inside = geo.inside(z)
-        for pair in range(SUB // 2):
+        for pair in range(TX // 2):
             coarse = 0.0
-            for x in (2 * pair, 2 * pair + 1):
-                kind = get(raw, z, 5, x)
+            for t in block_of(pair):
+                kind = get(raw, z, 5, t)
                 base = jnp.zeros(kind.shape, jnp.float32)
                 for layer in range(LAYERS):
-                    base = base + jnp.where(kind == float(layer), stiffness[layer], 0.0)
-                value = base * jnp.exp(-ACTIVATION_ENERGY * get(heat, z, 1, x))
+                    base = jnp.where(kind == float(layer), stiffness[layer], base)
+                value = base * jnp.exp(-ACTIVATION_ENERGY * get(heat, z, 1, t))
                 value = jnp.where(inside, value, 0.0)
-                put(st["visc"], value, z, x)
+                put(st["hv"], 0.5 * value, z, t)
                 coarse = coarse + value
             put(vc, 0.125 * tl.pair_sum(coarse), z, pair)
 
@@ -661,37 +675,25 @@
 
     def statics(z, put):
         inside = geo.inside(z)
-        for x in range(SUB):
-            c, near = beside(lambda z, x: get(st["visc"], z, x), x, z)
-            face = [0.5 * (c + o) for o in near]
-            diag = tree(face)
-            face[2], face[3] = one_up * face[2], one_down * face[3]
-            for name, f in zip(("cxp", "cxm", "cyp", "cym", "cz"), face):
-                put(st[name], f, z, x)
-            put(st["diag"], diag, z, x)
-            put(st["w"], jnp.where(inside, JACOBI_WEIGHT / diag, 0.0), z, x)
-            f, near = beside(warm(1), x, z)
-            dual = -INCREMENT_DT * get(raw, z, 4, x)
+        for t in range(SUB):
+            h, near = tl.beside(st["hv"], z, (), t)
+            diag = tree([h + other for other in near])
+            put(st["w"], jnp.where(inside, JACOBI_WEIGHT / diag, 0.0), z, t)
+            f, near = tl.beside(heat, z, (1,), t)
+            dual = -INCREMENT_DT * get(raw, z, 4, t)
             for k in range(3):
-                flow = get(raw, z, 1 + k, x)
+                flow = get(raw, z, 1 + k, t)
                 step = jnp.where(flow > 0, f - near[2 * k + 1], near[2 * k] - f)
-                put(st["s%d" % k], dual * step, z, x)
+                put(st["s%d" % k], dual * step, z, t)
 
     sweep(m - b, m + 2 * b, statics)
-
-    two_up, two_down = tl.y_masks(2, 1.0)
 
     def coarse_statics(z, put):
         inside = geo.inside(z)
-        for pair in range(SUB // 2):
-            c = get(vc, z, pair)
-            load = lambda j: get(vc, z, j)
-            up, down = tl.ys(c, 2)
-            near = [tl.x(load, pair, SUB // 2, s) for s in (1, -1)]
-            near += [two_up * up, two_down * down, get(vc, z + 2, pair), get(vc, z - 2, pair)]
+        for pair in range(TX // 2):
+            c, near = tl.coarse_beside(vc, z, (), pair)
             face = [0.25 * (0.5 * (c + o)) for o in near]
-            wc = jnp.where(inside, JACOBI_WEIGHT / sum(face), 0.0)
-            face[2], face[3] = two_up * face[2], two_down * face[3]
+            wc = jnp.where(inside, JACOBI_WEIGHT / tree(face), 0.0)
             for name, f in zip(STATIC_COARSE, face):
                 put(st[name], wc * f, z, pair)
             put(st["wc"], wc, z, pair)
@@ -699,25 +701,25 @@
     sweep(m - b, m + 2 * b, coarse_statics)
 
     def transport(z, put):
-        for x in range(SUB):
-            dual, near = beside(field(4), x, z)
-            value = dual + INCREMENT_DT * DIFFUSIVITY * (sum(near) - 6.0 * dual)
+        for t in range(SUB):
+            dual, near = tl.beside(raw, z, (4,), t)
+            value = dual + INCREMENT_DT * DIFFUSIVITY * (tree(near) - 6.0 * dual)
             for k in range(3):
-                flow, sides = beside(field(1 + k), x, z)
+                flow, sides = tl.beside(raw, z, (1 + k,), t)
                 a = jnp.maximum(flow, 0.0) * dual
                 c = jnp.minimum(flow, 0.0) * dual
                 ahead = jnp.maximum(sides[2 * k], 0.0) * near[2 * k]
                 behind = jnp.minimum(sides[2 * k + 1], 0.0) * near[2 * k + 1]
                 value = value - INCREMENT_DT * (a - ahead + behind - c)
-            put(moved, value, z - m, x)
+            put(moved, value, z - m, t)
 
     sweep(m, m + b, transport)
 
     def unit(z, put):
         value = jnp.where(geo.inside(z), 1.0, 0.0)
-        for x in range(SUB):
-            put(p, value, z, 0, x)
-            put(p, SCHUR_WEIGHT * get(st["visc"], z, x), z, 1, x)
+        for t in range(SUB):
+            put(p, value, z, 0, t)
+            put(p, get(st["hv"], z, t), z, 1, t)
 
     sweep(0, n_rows, unit)
 
@@ -816,21 +818,17 @@
         fields.append([p[0, x, at, :] for x in columns])
         fields.append([moved[x, u : u + SUB, :] + fields[2][x] for x in columns])
         for f, tiles in enumerate(fields):
-            for q, tile in enumerate(swap_granules(tiles, geo.block[1])):
+            for q, tile in enumerate(scatter_tiles(tiles, geo.block[1])):
                 out[q, f * b + u : f * b + u + SUB, :] = tile
 
 
 def unpack_kernel(geo, chunks, heat, flow, pressure):
     b = geo.slab
-    for f in range(BACK):
+    for f, ref in enumerate((flow.at[0], flow.at[1], flow.at[2], pressure, heat)):
         rows = [chunks[geo.holder[j], f * b : (f + 1) * b, :] for j in range(geo.group)]
-        block = jnp.concatenate(rows, 0).T.reshape(geo.block)
-        if f < 3:
-            flow[f] = block
-        elif f == 3:
-            pressure[...] = block
-        else:
-            heat[...] = block
+        block = jnp.concatenate(rows, 0).T
+        for k, (x, y) in enumerate(geo.order):
+            ref[x, pl.ds(y, SUB, stride=TY), :] = block[k * SUB : (k + 1) * SUB]
 
 
 def call(kernel, out, scratch, *args, smem=(), hbm=(), megabytes=2):
@@ -873,7 +871,7 @@
     high_edge = lax.ppermute(own[:, rows : rows + SUB], axes, geo.shifts(-2))
     low_edge = lax.ppermute(own[:, rows + SUB :], axes, geo.shifts(2))
 
-    fine, coarse = (SUB, geo.rows, LANES), (SUB // 2, geo.rows, LANES)
+    fine, coarse = (SUB, geo.rows, LANES), (TX // 2, geo.rows, LANES)
     slab = (SUB, b, LANES)
 
     def work(n, more=0):

time: 140 us -> 103 us (0.74)
  local copies, waits for them, and re-layouts: 35.7 us -> 3.45 us
  waiting for transfers between devices: 3.92 us -> 11.3 us
  Pallas kernels: 31.9 us -> 27 us
  starting transfers between devices: 29.4 us -> 26 us
  blocking collectives: 37.1 us -> 34 us
    unnamed x88 -> x10, local copies, waits for them, and re-layouts: 35.7 us -> 3.44 us
    pallas_call x7, Pallas kernels: 31.9 us -> 27 us  [call(): pl.pallas_call(kernel, out_shape=[jax.ShapeDtypeStruct(s, f32) for s in o...]
    all_to_all x1, waiting for transfers between devices: 0.01 us -> 4.09 us  [slab_shards(): early = lax.all_to_all(early, axes, 0, 0, tiled=True)]
    all_to_all x1, starting transfers between devices: 5.96 us -> 2.56 us  [slab_shards(): late = lax.all_to_all(late, axes, 0, 0, tiled=True)]
    all_to_all x1, blocking collectives: 16.8 us -> 13.7 us  [slab_shards(): chunks = lax.all_to_all(chunks, ('gx', 'gy'), 0, 0, tiled=True)]
    ppermute x1, waiting for transfers between devices: 0.01 us -> 1.54 us  [slab_shards(): high_state = lax.ppermute(state, axes, geo.shifts(-1))]
  transfers between devices with their start and end apart: 8 -> 8, of which waited for: 2 -> 6; matrix products, arithmetic and copies ran while one was open for 0% -> 0% of each run, Pallas kernels for 6% -> 7%
where the time goes in v8:
time: 103 us
  blocking collectives  34 us (33%)
  Pallas kernels  27 us (26%)
  starting transfers between devices  26 us (25%)
  waiting for transfers between devices  11.3 us (11%)
  local copies, waits for them, and re-layouts  3.45 us (3%)
    pallas_call x7, Pallas kernels, call(): pl.pallas_call(kernel, out_shape=[jax.ShapeDtypeStruct(s, f32) for s in o...  27 us
    all_to_all x1, blocking collectives, slab_shards(): own = lax.all_to_all(chunks, ('gx', 'gy'), 0, 0, tiled=True)  20.3 us
    all_to_all x1, blocking collectives, slab_shards(): chunks = lax.all_to_all(chunks, ('gx', 'gy'), 0, 0, tiled=True)  13.7 us
    ppermute x1, starting transfers between devices, slab_shards(): low_edge = lax.ppermute(own[:, rows + SUB:], axes, geo.shifts(2))  5.45 us
    all_to_all x1, starting transfers between devices, slab_shards(): early = lax.all_to_all(early, axes, 0, 0, tiled=True)  5.02 us
    ppermute x1, starting transfers between devices, slab_shards(): low = lax.ppermute(own, axes, geo.shifts(1))  4.57 us
    ppermute x1, starting transfers between devices, slab_shards(): low_state = lax.ppermute(state, axes, geo.shifts(1))  4.56 us
    all_to_all x1, waiting for transfers between devices, slab_shards(): early = lax.all_to_all(early, axes, 0, 0, tiled=True)  4.09 us
  transfers between devices with their start and end apart: 8, of which 6 were waited for; matrix products, arithmetic and copies ran while one was open for 0% of the time, Pallas kernels for 7%

profile of v8, /device:TPU:0, one launch (start us, length us, event | category | flops | bytes accessed | tf_op | source)
XLA Modules:
  0.0 102.5 jit_solution(6296406791452948744)
XLA Ops:
  0.6 0.0 copy-start
  0.6 0.9 copy-done
  1.6 0.0 copy-start.1
  1.6 0.8 copy-done.1
  2.4 0.0 copy-start.2
  2.4 0.8 copy-done.2
  3.2 0.0 copy-start.3
  3.2 0.8 copy-done.3
  4.1 0.7 shard_map.76
  4.8 20.3 %all_to_all.32.own = f32[8,112,128]{2,1,0:T(8,128)S(1)} all-to-all(f32[8,112,128]{2,1,0:T(8,128)S(1)} %shard_map.76), channel_id=1, replica_groups=mesh['gx'=4,'gy'=2,'gz'=4] {'gx','gy'}, dimensions={0} | all-to-all | bytes 917504 | tf_op jit(solution)/shard_map/all_to_all | solution.py:867
  25.1 1.3 %collective-permute-start.1 = (f32[8,112,128]{2,1,0:T(8,128)S(1)}, f32[8,112,128]{2,1,0:T(8,128)S(1)}, u32[]{:S(2)}, u32[]{:S(2)}) collective-permute-start(f32[8,112,128]{2,1,0:T(8,128)S(1)} %all_to_all.32.own), channel_id=1, source_target_pairs={{8,0},{16,8},{24,16},{28,24},{20,28},{12,20},{4,12},{1,4},{9,1},{1... | collective-permute-start | bytes 1376264 | tf_op jit(solution)/shard_map/ppermute | solution.py:870
  26.4 4.6 %collective-permute-start = (f32[8,112,128]{2,1,0:T(8,128)S(1)}, f32[8,112,128]{2,1,0:T(8,128)S(1)}, u32[]{:S(2)}, u32[]{:S(2)}) collective-permute-start(f32[8,112,128]{2,1,0:T(8,128)S(1)} %all_to_all.32.own), channel_id=1, source_target_pairs={{0,8},{8,16},{16,24},{24,28},{28,20},{20,12},{12,4},{4,1},{1,9},{9... | collective-permute-start | bytes 1376264 | tf_op jit(solution)/shard_map/ppermute | solution.py:869
  31.0 0.0 copy-start.4
  31.0 1.3 %collective-permute-start.3 = (f32[8,8,128]{2,1,0:T(8,128)S(1)}, f32[8,8,128]{2,1,0:T(8,128)S(1)}, u32[]{:S(2)}, u32[]{:S(2)}) collective-permute-start(f32[8,8,128]{2,1,0:T(8,128)S(1)} %get-tuple-element.37), channel_id=1, source_target_pairs={{16,0},{24,8},{28,16},{20,24},{12,28},{4,20},{1,12},{9,4},{17,1},{... | collective-permute-start | bytes 98312 | tf_op jit(solution)/shard_map/ppermute | solution.py:871
  32.3 5.4 %collective-permute-start.2 = (f32[8,8,128]{2,1,0:T(8,128)S(1)}, f32[8,8,128]{2,1,0:T(8,128)S(1)}, u32[]{:S(2)}, u32[]{:S(2)}) collective-permute-start(f32[8,8,128]{2,1,0:T(8,128)S(1)} %get-tuple-element.38), channel_id=1, source_target_pairs={{0,16},{8,24},{16,28},{24,20},{28,12},{20,4},{12,1},{4,9},{1,17},{... | collective-permute-start | bytes 98312 | tf_op jit(solution)/shard_map/ppermute | solution.py:872
  37.7 1.4 %collective-permute-done.3.high_edge = f32[8,8,128]{2,1,0:T(8,128)S(1)} collective-permute-done((f32[8,8,128]{2,1,0:T(8,128)S(1)}, f32[8,8,128]{2,1,0:T(8,128)S(1)}, u32[]{:S(2)}, u32[]{:S(2)}) %collective-permute-start.3) | collective-permute-done | bytes 32800 | tf_op jit(solution)/shard_map/ppermute | solution.py:871
  39.1 2.5 %collective-permute-done.2.low_edge = f32[8,8,128]{2,1,0:T(8,128)S(1)} collective-permute-done((f32[8,8,128]{2,1,0:T(8,128)S(1)}, f32[8,8,128]{2,1,0:T(8,128)S(1)}, u32[]{:S(2)}, u32[]{:S(2)}) %collective-permute-start.2) | collective-permute-done | bytes 32800 | tf_op jit(solution)/shard_map/ppermute | solution.py:872
  41.6 0.0 collective-permute-done.1.high
  41.6 0.0 collective-permute-done.low
  41.6 0.0 copy-done.4
  41.6 12.3 %shard_map.77 = (f32[8,64,128]{2,1,0:T(8,128)S(1)}, f32[8,64,128]{2,1,0:T(8,128)S(1)}, f32[8,64,128]{2,1,0:T(8,128)S(1)}, f32[8,64,128]{2,1,0:T(8,128)S(1)}, f32...) custom-call(f32[8]{0:T(128)S(1)} %copy-done.4, ...), custom_call_target="tpu_custom_call" | custom-call | flops 60000000 | bytes 60000000 | tf_op jit(solution)/shard_map/pallas_call | solution.py:845
  54.0 5.0 %all-to-all-start.1 = ((f32[32,1,128]{2,1,0:T(1,128)}), f32[32,1,128]{2,1,0:T(1,128)S(1)}, u32[]{:S(2)}, u32[]{:S(2)}) async-start(f32[32,1,128]{2,1,0:T(1,128)} %bitcast.1), calls=%async_computation.1 | async-start | bytes 32768 | tf_op jit(solution)/shard_map/all_to_all | solution.py:898
  59.0 3.0 %shard_map.78.refs_12_ = f32[4,8,32,128]{3,2,1,0:T(8,128)S(1)} custom-call(f32[8,64,128]{2,1,0:T(8,128)S(1)} %get-tuple-element.20.refs_0_, f32[8,64,128]{2,1,0:T(8,128)S(1)} %get-tuple-element.21.refs_1_, f32[8,64,128]{2,1,0:T(8,128)S(1)} %get-tuple-element.22.refs_2_, f32[8,64,128]{2,1,0:T(8,128)S(1)} %get-tuple-element.23.refs_3_, ...), custom_call_target="tpu_custom_call" | custom-call | flops 20000000 | bytes 20000000 | tf_op jit(solution)/shard_map/pallas_call | solution.py:845
  62.0 4.1 %all-to-all-done.1 = f32[32,1,128]{2,1,0:T(1,128)S(1)} async-done(((f32[32,1,128]{2,1,0:T(1,128)}), f32[32,1,128]{2,1,0:T(1,128)S(1)}, u32[]{:S(2)}, u32[]{:S(2)}) %all-to-all-start.1) | async-done | bytes 16416 | tf_op jit(solution)/shard_map/all_to_all | solution.py:898
  66.1 3.2 %shard_map.79 = (f32[4,8,16,128]{3,2,1,0:T(8,128)S(1)}, f32[32,128]{1,0:T(8,128)}) custom-call(f32[8,64,128]{2,1,0:T(8,128)S(1)} %get-tuple-element.20.refs_0_, f32[8,64,128]{2,1,0:T(8,128)S(1)} %get-tuple-element.21.refs_1_, f32[8,64,128]{2,1,0:T(8,128)S(1)} %get-tuple-element.22.refs_2_, f32[8,64,128]{2,1,0:T(8,128)S(1)} %get-tuple-element.23.refs_3_, ...), custom_call_target="tpu_custom_call" | custom-call | flops 20000000 | bytes 20000000 | tf_op jit(solution)/shard_map/pallas_call | solution.py:845
  69.3 1.3 %collective-permute-start.5 = (f32[4,8,16,128]{3,2,1,0:T(8,128)S(1)}, f32[4,8,16,128]{3,2,1,0:T(8,128)S(1)}, u32[]{:S(2)}, u32[]{:S(2)}) collective-permute-start(f32[4,8,16,128]{3,2,1,0:T(8,128)S(1)} %get-tuple-element.34.refs_12_), channel_id=1, source_target_pairs={{8,0},{16,8},{24,16},{28,24},{20,28},{12,20},{4,12},{1,4},{9,1},{1... | collective-permute-start | bytes 786440 | tf_op jit(solution)/shard_map/ppermute | solution.py:913
  70.6 4.6 %collective-permute-start.4 = (f32[4,8,16,128]{3,2,1,0:T(8,128)S(1)}, f32[4,8,16,128]{3,2,1,0:T(8,128)S(1)}, u32[]{:S(2)}, u32[]{:S(2)}) collective-permute-start(f32[4,8,16,128]{3,2,1,0:T(8,128)S(1)} %get-tuple-element.34.refs_12_), channel_id=1, source_target_pairs={{0,8},{8,16},{16,24},{24,28},{28,20},{20,12},{12,4},{4,1},{1,9},{9... | collective-permute-start | bytes 786440 | tf_op jit(solution)/shard_map/ppermute | solution.py:912
  75.2 2.6 %all-to-all-start.2 = ((f32[32,1,128]{2,1,0:T(1,128)}), f32[32,1,128]{2,1,0:T(1,128)S(1)}, u32[]{:S(2)}, u32[]{:S(2)}) async-start(f32[32,1,128]{2,1,0:T(1,128)} %bitcast.4), calls=%async_computation.2 | async-start | bytes 32768 | tf_op jit(solution)/shard_map/all_to_all | solution.py:914
  77.7 1.5 %collective-permute-done.5.refs_14_ = f32[4,8,16,128]{3,2,1,0:T(8,128)S(1)} collective-permute-done((f32[4,8,16,128]{3,2,1,0:T(8,128)S(1)}, f32[4,8,16,128]{3,2,1,0:T(8,128)S(1)}, u32[]{:S(2)}, u32[]{:S(2)}) %collective-permute-start.5) | collective-permute-done | bytes 262176 | tf_op jit(solution)/shard_map/ppermute | solution.py:913
  79.3 1.3 %collective-permute-done.4.refs_13_ = f32[4,8,16,128]{3,2,1,0:T(8,128)S(1)} collective-permute-done((f32[4,8,16,128]{3,2,1,0:T(8,128)S(1)}, f32[4,8,16,128]{3,2,1,0:T(8,128)S(1)}, u32[]{:S(2)}, u32[]{:S(2)}) %collective-permute-start.4) | collective-permute-done | bytes 262176 | tf_op jit(solution)/shard_map/ppermute | solution.py:912
  80.6 3.8 %shard_map.80.refs_12_ = f32[4,8,32,128]{3,2,1,0:T(8,128)S(1)} custom-call(f32[8,64,128]{2,1,0:T(8,128)S(1)} %get-tuple-element.20.refs_0_, f32[8,64,128]{2,1,0:T(8,128)S(1)} %get-tuple-element.21.refs_1_, f32[8,64,128]{2,1,0:T(8,128)S(1)} %get-tuple-element.22.refs_2_, f32[8,64,128]{2,1,0:T(8,128)S(1)} %get-tuple-element.23.refs_3_, ...), custom_call_target="tpu_custom_call" | custom-call | flops 30000000 | bytes 30000000 | tf_op jit(solution)/shard_map/pallas_call | solution.py:845
  84.4 0.4 all-to-all-done.2
  84.8 3.2 %shard_map.81 = f32[8,80,128]{2,1,0:T(8,128)S(1)} custom-call(f32[8,64,128]{2,1,0:T(8,128)S(1)} %get-tuple-element.20.refs_0_, f32[8,64,128]{2,1,0:T(8,128)S(1)} %get-tuple-element.21.refs_1_, f32[8,64,128]{2,1,0:T(8,128)S(1)} %get-tuple-element.22.refs_2_, f32[8,64,128]{2,1,0:T(8,128)S(1)} %get-tuple-element.23.refs_3_, ...), custom_call_target="tpu_custom_call" | custom-call | flops 20000000 | bytes 20000000 | tf_op jit(solution)/shard_map/pallas_call | solution.py:845
  88.0 13.7 %all_to_all.33.chunks = f32[8,80,128]{2,1,0:T(8,128)S(1)} all-to-all(f32[8,80,128]{2,1,0:T(8,128)S(1)} %shard_map.81), channel_id=1, replica_groups=mesh['gx'=4,'gy'=2,'gz'=4] {'gx','gy'}, dimensions={0} | all-to-all | bytes 655360 | tf_op jit(solution)/shard_map/all_to_all | solution.py:936
  101.7 0.9 shard_map.82
  (1 shorter events, 0.0 us)
Async XLA Ops:
  0.6 0.9 copy-start
  1.6 0.8 copy-start.1
  2.4 0.8 copy-start.2
  3.2 0.8 copy-start.3
  25.1 16.6 %collective-permute-start.1 = (f32[8,112,128]{2,1,0:T(8,128)S(1)}, f32[8,112,128]{2,1,0:T(8,128)S(1)}, u32[]{:S(2)}, u32[]{:S(2)}) collective-permute-start(f32[8,112,128]{2,1,0:T(8,128)S(1)} %all_to_all.32.own), channel_id=1, source_target_pairs={{8,0},{16,8},{24,16},{28,24},{20,28},{12,20},{4,12},{1,4},{9,1},{1... | collective-permute-start | bytes 1376264 | tf_op jit(solution)/shard_map/ppermute | solution.py:870
  26.4 15.3 %collective-permute-start = (f32[8,112,128]{2,1,0:T(8,128)S(1)}, f32[8,112,128]{2,1,0:T(8,128)S(1)}, u32[]{:S(2)}, u32[]{:S(2)}) collective-permute-start(f32[8,112,128]{2,1,0:T(8,128)S(1)} %all_to_all.32.own), channel_id=1, source_target_pairs={{0,8},{8,16},{16,24},{24,28},{28,20},{20,12},{12,4},{4,1},{1,9},{9... | collective-permute-start | bytes 1376264 | tf_op jit(solution)/shard_map/ppermute | solution.py:869
  31.0 10.7 %copy-start.4 = (f32[8]{0:T(128)S(1)}, f32[8]{0:T(128)}, u32[]{:S(2)}) copy-start(f32[8]{0:T(128)} %stiffness.1) | copy-start | bytes 100
  31.0 8.1 %collective-permute-start.3 = (f32[8,8,128]{2,1,0:T(8,128)S(1)}, f32[8,8,128]{2,1,0:T(8,128)S(1)}, u32[]{:S(2)}, u32[]{:S(2)}) collective-permute-start(f32[8,8,128]{2,1,0:T(8,128)S(1)} %get-tuple-element.37), channel_id=1, source_target_pairs={{16,0},{24,8},{28,16},{20,24},{12,28},{4,20},{1,12},{9,4},{17,1},{... | collective-permute-start | bytes 98312 | tf_op jit(solution)/shard_map/ppermute | solution.py:871
  32.3 9.4 %collective-permute-start.2 = (f32[8,8,128]{2,1,0:T(8,128)S(1)}, f32[8,8,128]{2,1,0:T(8,128)S(1)}, u32[]{:S(2)}, u32[]{:S(2)}) collective-permute-start(f32[8,8,128]{2,1,0:T(8,128)S(1)} %get-tuple-element.38), channel_id=1, source_target_pairs={{0,16},{8,24},{16,28},{24,20},{28,12},{20,4},{12,1},{4,9},{1,17},{... | collective-permute-start | bytes 98312 | tf_op jit(solution)/shard_map/ppermute | solution.py:872
  54.0 12.1 %all-to-all-start.1 = ((f32[32,1,128]{2,1,0:T(1,128)}), f32[32,1,128]{2,1,0:T(1,128)S(1)}, u32[]{:S(2)}, u32[]{:S(2)}) async-start(f32[32,1,128]{2,1,0:T(1,128)} %bitcast.1), calls=%async_computation.1 | async-start | bytes 32768 | tf_op jit(solution)/shard_map/all_to_all | solution.py:898
  69.3 10.0 %collective-permute-start.5 = (f32[4,8,16,128]{3,2,1,0:T(8,128)S(1)}, f32[4,8,16,128]{3,2,1,0:T(8,128)S(1)}, u32[]{:S(2)}, u32[]{:S(2)}) collective-permute-start(f32[4,8,16,128]{3,2,1,0:T(8,128)S(1)} %get-tuple-element.34.refs_12_), channel_id=1, source_target_pairs={{8,0},{16,8},{24,16},{28,24},{20,28},{12,20},{4,12},{1,4},{9,1},{1... | collective-permute-start | bytes 786440 | tf_op jit(solution)/shard_map/ppermute | solution.py:913
  70.6 10.0 %collective-permute-start.4 = (f32[4,8,16,128]{3,2,1,0:T(8,128)S(1)}, f32[4,8,16,128]{3,2,1,0:T(8,128)S(1)}, u32[]{:S(2)}, u32[]{:S(2)}) collective-permute-start(f32[4,8,16,128]{3,2,1,0:T(8,128)S(1)} %get-tuple-element.34.refs_12_), channel_id=1, source_target_pairs={{0,8},{8,16},{16,24},{24,28},{28,20},{20,12},{12,4},{4,1},{1,9},{9... | collective-permute-start | bytes 786440 | tf_op jit(solution)/shard_map/ppermute | solution.py:912
  75.2 9.6 %all-to-all-start.2 = ((f32[32,1,128]{2,1,0:T(1,128)}), f32[32,1,128]{2,1,0:T(1,128)S(1)}, u32[]{:S(2)}, u32[]{:S(2)}) async-start(f32[32,1,128]{2,1,0:T(1,128)} %bitcast.4), calls=%async_computation.2 | async-start | bytes 32768 | tf_op jit(solution)/shard_map/all_to_all | solution.py:914

commit v9 on v8

--- a/solution.py
+++ b/solution.py
@@ -260,6 +260,7 @@
 HELD = 24
 TX, TY = 4, 2
 VMEM_LIMIT = 32 * 1024 * 1024
+PACK_LIMIT = 60 * 1024 * 1024
 FORWARD, ADJOINT = range(2)
 
 
@@ -352,10 +353,12 @@
         self.row = lax.broadcasted_iota(jnp.int32, (SUB, LANES), 0)
         self.lane = lax.broadcasted_iota(jnp.int32, (SUB, LANES), 1)
         self.y = self.lane % self.span
-        self.kept = {}
+        self.kept, self.latest = {}, None
 
     def sliding(self, ref, z, lead, t):
-        where = (id(ref), id(z), lead)
+        if self.latest is not z:
+            self.latest, self.kept = z, {}
+        where = (id(ref), z if isinstance(z, int) else id(z), lead)
         for key in [k for k in self.kept if k[:3] == where and abs(k[3] - t) > 3]:
             del self.kept[key]
 
@@ -419,9 +422,11 @@
 
 
 def sweep(lo, hi, body):
-    assert (hi - lo) % SUB == 0
-
-    def step(t, _):
+    count = (hi - lo) // SUB
+    assert count * SUB == hi - lo
+    unroll = next(u for u in (3, 2, count) if count % u == 0)
+
+    def step(t):
         late = []
 
         def store(ref, value, z, *index):
@@ -432,16 +437,20 @@
             if len(late) > HELD:
                 store(*late.pop(0))
 
-        body(pl.multiple_of(t * SUB, SUB) + lo, put)
+        for u in range(unroll):
+            body(t + (lo + u * SUB), put)
         for item in late:
             store(*item)
-        return 0
-
-    lax.fori_loop(0, (hi - lo) // SUB, step, 0)
+
+    if unroll == count:
+        step(0)
+    else:
+        span = unroll * SUB
+        lax.fori_loop(0, count // unroll, lambda t, _: (step(pl.multiple_of(t * span, SUB)), 0)[1], 0)
 
 
 def pack_kernel(geo, heat_in, flow_in, dual_in, kind_in, out, heat, flow, dual, kind, sems):
-    b, e = geo.slab, EDGE
+    b = geo.slab
     pairs = ((heat_in, heat), (flow_in, flow), (dual_in, dual), (kind_in, kind))
     copies = [
         pltpu.make_async_copy(source, target, sems.at[k])
@@ -460,11 +469,14 @@
         q = geo.holder[j]
         for f in range(FIELDS):
             out[q, f * b : (f + 1) * b, :] = turned[f][j * b : (j + 1) * b]
-        tail = FIELDS * b
-        first = jnp.concatenate([turned[f][j * b : j * b + e] for f in range(4)], 0)
-        last = jnp.concatenate([turned[f][(j + 1) * b - e : (j + 1) * b] for f in range(4)], 0)
-        out[q, tail : tail + SUB, :] = first
-        out[q, tail + SUB : tail + 2 * SUB, :] = last
+
+
+def edge_kernel(geo, own, first, last):
+    b, e = geo.slab, EDGE
+    for q in range(geo.group):
+        for out, at in ((first, 0), (last, b - e)):
+            rows = [own[q, f * b + at : f * b + at + e, :] for f in range(4)]
+            out[q] = jnp.concatenate(rows, 0)
 
 
 STATIC_FINE = ("s0", "s1", "s2", "hv", "w")
@@ -831,7 +843,7 @@
             ref[x, pl.ds(y, SUB, stride=TY), :] = block[k * SUB : (k + 1) * SUB]
 
 
-def call(kernel, out, scratch, *args, smem=(), hbm=(), megabytes=2):
+def call(kernel, out, scratch, *args, smem=(), hbm=(), limit=VMEM_LIMIT, megabytes=2):
     f32 = jnp.float32
     cost = pl.CostEstimate(
         flops=megabytes * 1000000, bytes_accessed=megabytes * 1000000, transcendentals=0
@@ -848,28 +860,29 @@
         in_specs=specs,
         out_specs=[pl.BlockSpec(memory_space=pltpu.VMEM) for _ in out],
         scratch_shapes=[pltpu.VMEM(s, f32) if isinstance(s, tuple) else s for s in scratch],
-        compiler_params=pltpu.CompilerParams(vmem_limit_bytes=VMEM_LIMIT),
+        compiler_params=pltpu.CompilerParams(vmem_limit_bytes=limit),
         cost_estimate=cost,
     )(*args)
 
 
 def slab_shards(geo, heat, flow, dual, kind, stiffness):
     b, group = geo.slab, geo.group
-    rows = FIELDS * b
     inputs = (heat, flow, dual, kind)
     (chunks,) = call(
         functools.partial(pack_kernel, geo),
-        [(group, rows + 2 * SUB, LANES)],
+        [(group, FIELDS * b, LANES)],
         [pltpu.VMEM(a.shape, a.dtype) for a in inputs] + [pltpu.SemaphoreType.DMA((4,))],
         *inputs,
         hbm=range(4),
+        limit=PACK_LIMIT,
     )
     own = lax.all_to_all(chunks, ("gx", "gy"), 0, 0, tiled=True)
     axes = ("gx", "gy", "gz")
     low = lax.ppermute(own, axes, geo.shifts(1))
     high = lax.ppermute(own, axes, geo.shifts(-1))
-    high_edge = lax.ppermute(own[:, rows : rows + SUB], axes, geo.shifts(-2))
-    low_edge = lax.ppermute(own[:, rows + SUB :], axes, geo.shifts(2))
+    edges = call(functools.partial(edge_kernel, geo), [(group, SUB, LANES)] * 2, [], own)
+    high_edge = lax.ppermute(edges[0], axes, geo.shifts(-2))
+    low_edge = lax.ppermute(edges[1], axes, geo.shifts(2))
 
     fine, coarse = (SUB, geo.rows, LANES), (TX // 2, geo.rows, LANES)
     slab = (SUB, b, LANES)

time: 103 us -> 92.4 us (0.90)
  Pallas kernels: 27 us -> 20.1 us
  waiting for transfers between devices: 11.3 us -> 15.5 us
  local copies, waits for them, and re-layouts: 3.45 us -> 0.01 us
  starting transfers between devices: 26 us -> 22.6 us
    pallas_call x7 -> x8, Pallas kernels: 27 us -> 20.1 us  [call(): pl.pallas_call(kernel, out_shape=[jax.ShapeDtypeStruct(s, f32) for s in o...]
    unnamed x10 -> x2, local copies, waits for them, and re-layouts: 3.44 us -> 0.01 us
    ppermute x2, starting transfers between devices: 6.74 us -> 4.05 us  [the longest x1 2.75 us: slab_shards(): low_edge = lax.ppermute(edges[1], axes, geo.shifts(2))]
    ppermute x2, waiting for transfers between devices: 3.9 us -> 5.41 us  [the longest x1 4.92 us: slab_shards(): low_edge = lax.ppermute(edges[1], axes, geo.shifts(2))]
    all_to_all x1, waiting for transfers between devices: 0.41 us -> 1.89 us  [slab_shards(): late = lax.all_to_all(late, axes, 0, 0, tiled=True)]
    all_to_all x1, waiting for transfers between devices: 4.09 us -> 5.4 us  [slab_shards(): early = lax.all_to_all(early, axes, 0, 0, tiled=True)]
  transfers between devices with their start and end apart: 8 -> 8, of which waited for: 6 -> 6; matrix products, arithmetic and copies ran while one was open for 0% -> 0% of each run, Pallas kernels for 7% -> 4%
where the time goes in v9:
time: 92.4 us; the launch traced here: 92 us
  blocking collectives  33 us (36%)
  starting transfers between devices  22.6 us (24%)
  Pallas kernels  20.1 us (22%)
  waiting for transfers between devices  15.5 us (17%)
    pallas_call x8, Pallas kernels, call(): pl.pallas_call(kernel, out_shape=[jax.ShapeDtypeStruct(s, f32) for s in o...  20.1 us
    all_to_all x1, blocking collectives, slab_shards(): own = lax.all_to_all(chunks, ('gx', 'gy'), 0, 0, tiled=True)  19.4 us
    all_to_all x1, blocking collectives, slab_shards(): chunks = lax.all_to_all(chunks, ('gx', 'gy'), 0, 0, tiled=True)  13.6 us
    all_to_all x1, waiting for transfers between devices, slab_shards(): early = lax.all_to_all(early, axes, 0, 0, tiled=True)  5.4 us
    ppermute x1, waiting for transfers between devices, slab_shards(): low_edge = lax.ppermute(edges[1], axes, geo.shifts(2))  4.92 us
    ppermute x1, starting transfers between devices, slab_shards(): low = lax.ppermute(own, axes, geo.shifts(1))  4.57 us
    ppermute x1, starting transfers between devices, slab_shards(): low_state = lax.ppermute(state, axes, geo.shifts(1))  4.56 us
    all_to_all x1, starting transfers between devices, slab_shards(): early = lax.all_to_all(early, axes, 0, 0, tiled=True)  4.29 us
  transfers between devices with their start and end apart: 8, of which 6 were waited for; matrix products, arithmetic and copies ran while one was open for 0% of the time, Pallas kernels for 4%

profile of v9, /device:TPU:0, one launch (start us, length us, event | category | flops | bytes accessed | tf_op | source)
XLA Modules:
  0.0 92.0 jit_solution(9848958291046003348)
XLA Ops:
  0.6 1.9 %shard_map.76 = f32[8,96,128]{2,1,0:T(8,128)} custom-call(f32[8,16,128]{2,1,0:T(8,128)} %heat_in.1, f32[3,8,16,128]{3,2,1,0:T(8,128)} %flow_in.1, f32[8,16,128]{2,1,0:T(8,128)} %dual_in.1, s32[8,16,128]{2,1,0:T(8,128)} %kind_in.1), custom_call_target="tpu_custom_call" | custom-call | flops 2000000 | bytes 2000000 | tf_op jit(solution)/shard_map/pallas_call | solution.py:857
  2.6 19.4 %all_to_all.32.own = f32[8,96,128]{2,1,0:T(8,128)S(1)} all-to-all(f32[8,96,128]{2,1,0:T(8,128)} %shard_map.76), channel_id=1, replica_groups=mesh['gx'=4,'gy'=2,'gz'=4] {'gx','gy'}, dimensions={0} | all-to-all | bytes 786432 | tf_op jit(solution)/shard_map/all_to_all | solution.py:879
  22.0 1.3 %collective-permute-start.1 = (f32[8,96,128]{2,1,0:T(8,128)S(1)}, f32[8,96,128]{2,1,0:T(8,128)S(1)}, u32[]{:S(2)}, u32[]{:S(2)}) collective-permute-start(f32[8,96,128]{2,1,0:T(8,128)S(1)} %all_to_all.32.own), channel_id=1, source_target_pairs={{8,0},{16,8},{24,16},{28,24},{20,28},{12,20},{4,12},{1,4},{9,1},{1... | collective-permute-start | bytes 1179656 | tf_op jit(solution)/shard_map/ppermute | solution.py:882
  23.2 4.6 %collective-permute-start = (f32[8,96,128]{2,1,0:T(8,128)S(1)}, f32[8,96,128]{2,1,0:T(8,128)S(1)}, u32[]{:S(2)}, u32[]{:S(2)}) collective-permute-start(f32[8,96,128]{2,1,0:T(8,128)S(1)} %all_to_all.32.own), channel_id=1, source_target_pairs={{0,8},{8,16},{16,24},{24,28},{28,20},{20,12},{12,4},{4,1},{1,9},{9... | collective-permute-start | bytes 1179656 | tf_op jit(solution)/shard_map/ppermute | solution.py:881
  27.9 0.0 copy-start
  27.9 2.8 %collective-permute-start.2 = (f32[8,8,128]{2,1,0:T(8,128)S(1)}, f32[8,8,128]{2,1,0:T(8,128)S(1)}, u32[]{:S(2)}, u32[]{:S(2)}) collective-permute-start(f32[8,8,128]{2,1,0:T(8,128)S(1)} %get-tuple-element.22), channel_id=1, source_target_pairs={{0,16},{8,24},{16,28},{24,20},{28,12},{20,4},{12,1},{4,9},{1,17},{... | collective-permute-start | bytes 98312 | tf_op jit(solution)/shard_map/ppermute | solution.py:885
  30.6 1.3 %collective-permute-start.3 = (f32[8,8,128]{2,1,0:T(8,128)S(1)}, f32[8,8,128]{2,1,0:T(8,128)S(1)}, u32[]{:S(2)}, u32[]{:S(2)}) collective-permute-start(f32[8,8,128]{2,1,0:T(8,128)S(1)} %get-tuple-element.23), channel_id=1, source_target_pairs={{16,0},{24,8},{28,16},{20,24},{12,28},{4,20},{1,12},{9,4},{17,1},{... | collective-permute-start | bytes 98312 | tf_op jit(solution)/shard_map/ppermute | solution.py:884
  31.9 4.9 %collective-permute-done.2.low_edge = f32[8,8,128]{2,1,0:T(8,128)S(1)} collective-permute-done((f32[8,8,128]{2,1,0:T(8,128)S(1)}, f32[8,8,128]{2,1,0:T(8,128)S(1)}, u32[]{:S(2)}, u32[]{:S(2)}) %collective-permute-start.2) | collective-permute-done | bytes 32800 | tf_op jit(solution)/shard_map/ppermute | solution.py:885
  36.9 0.5 collective-permute-done.3.high_edge
  37.3 0.0 collective-permute-done.1.high
  37.3 0.0 collective-permute-done.low
  37.3 0.0 copy-done
  37.4 8.2 %shard_map.78 = (f32[8,64,128]{2,1,0:T(8,128)S(1)}, f32[8,64,128]{2,1,0:T(8,128)S(1)}, f32[8,64,128]{2,1,0:T(8,128)S(1)}, f32[8,64,128]{2,1,0:T(8,128)S(1)}, f32...) custom-call(f32[8]{0:T(128)S(1)} %copy-done, ...), custom_call_target="tpu_custom_call" | custom-call | flops 60000000 | bytes 60000000 | tf_op jit(solution)/shard_map/pallas_call | solution.py:857
  45.6 4.3 %all-to-all-start.1 = ((f32[32,1,128]{2,1,0:T(1,128)}), f32[32,1,128]{2,1,0:T(1,128)S(1)}, u32[]{:S(2)}, u32[]{:S(2)}) async-start(f32[32,1,128]{2,1,0:T(1,128)} %bitcast.1), calls=%async_computation.1 | async-start | bytes 32768 | tf_op jit(solution)/shard_map/all_to_all | solution.py:911
  49.9 1.7 %shard_map.79.refs_12_ = f32[4,8,32,128]{3,2,1,0:T(8,128)S(1)} custom-call(f32[8,64,128]{2,1,0:T(8,128)S(1)} %get-tuple-element.24.refs_0_, f32[8,64,128]{2,1,0:T(8,128)S(1)} %get-tuple-element.25.refs_1_, f32[8,64,128]{2,1,0:T(8,128)S(1)} %get-tuple-element.26.refs_2_, f32[8,64,128]{2,1,0:T(8,128)S(1)} %get-tuple-element.27.refs_3_, ...), custom_call_target="tpu_custom_call" | custom-call | flops 20000000 | bytes 20000000 | tf_op jit(solution)/shard_map/pallas_call | solution.py:857
  51.6 5.4 %all-to-all-done.1 = f32[32,1,128]{2,1,0:T(1,128)S(1)} async-done(((f32[32,1,128]{2,1,0:T(1,128)}), f32[32,1,128]{2,1,0:T(1,128)S(1)}, u32[]{:S(2)}, u32[]{:S(2)}) %all-to-all-start.1) | async-done | bytes 16416 | tf_op jit(solution)/shard_map/all_to_all | solution.py:911
  57.0 2.4 %shard_map.80 = (f32[4,8,16,128]{3,2,1,0:T(8,128)S(1)}, f32[32,128]{1,0:T(8,128)}) custom-call(f32[8,64,128]{2,1,0:T(8,128)S(1)} %get-tuple-element.24.refs_0_, f32[8,64,128]{2,1,0:T(8,128)S(1)} %get-tuple-element.25.refs_1_, f32[8,64,128]{2,1,0:T(8,128)S(1)} %get-tuple-element.26.refs_2_, f32[8,64,128]{2,1,0:T(8,128)S(1)} %get-tuple-element.27.refs_3_, ...), custom_call_target="tpu_custom_call" | custom-call | flops 20000000 | bytes 20000000 | tf_op jit(solution)/shard_map/pallas_call | solution.py:857
  59.3 1.3 %collective-permute-start.5 = (f32[4,8,16,128]{3,2,1,0:T(8,128)S(1)}, f32[4,8,16,128]{3,2,1,0:T(8,128)S(1)}, u32[]{:S(2)}, u32[]{:S(2)}) collective-permute-start(f32[4,8,16,128]{3,2,1,0:T(8,128)S(1)} %get-tuple-element.38.refs_12_), channel_id=1, source_target_pairs={{8,0},{16,8},{24,16},{28,24},{20,28},{12,20},{4,12},{1,4},{9,1},{1... | collective-permute-start | bytes 786440 | tf_op jit(solution)/shard_map/ppermute | solution.py:926
  60.6 4.6 %collective-permute-start.4 = (f32[4,8,16,128]{3,2,1,0:T(8,128)S(1)}, f32[4,8,16,128]{3,2,1,0:T(8,128)S(1)}, u32[]{:S(2)}, u32[]{:S(2)}) collective-permute-start(f32[4,8,16,128]{3,2,1,0:T(8,128)S(1)} %get-tuple-element.38.refs_12_), channel_id=1, source_target_pairs={{0,8},{8,16},{16,24},{24,28},{28,20},{20,12},{12,4},{4,1},{1,9},{9... | collective-permute-start | bytes 786440 | tf_op jit(solution)/shard_map/ppermute | solution.py:925
  65.2 2.6 %all-to-all-start.2 = ((f32[32,1,128]{2,1,0:T(1,128)}), f32[32,1,128]{2,1,0:T(1,128)S(1)}, u32[]{:S(2)}, u32[]{:S(2)}) async-start(f32[32,1,128]{2,1,0:T(1,128)} %bitcast.4), calls=%async_computation.2 | async-start | bytes 32768 | tf_op jit(solution)/shard_map/all_to_all | solution.py:927
  67.7 1.5 %collective-permute-done.5.refs_14_ = f32[4,8,16,128]{3,2,1,0:T(8,128)S(1)} collective-permute-done((f32[4,8,16,128]{3,2,1,0:T(8,128)S(1)}, f32[4,8,16,128]{3,2,1,0:T(8,128)S(1)}, u32[]{:S(2)}, u32[]{:S(2)}) %collective-permute-start.5) | collective-permute-done | bytes 262176 | tf_op jit(solution)/shard_map/ppermute | solution.py:926
  69.3 1.3 %collective-permute-done.4.refs_13_ = f32[4,8,16,128]{3,2,1,0:T(8,128)S(1)} collective-permute-done((f32[4,8,16,128]{3,2,1,0:T(8,128)S(1)}, f32[4,8,16,128]{3,2,1,0:T(8,128)S(1)}, u32[]{:S(2)}, u32[]{:S(2)}) %collective-permute-start.4) | collective-permute-done | bytes 262176 | tf_op jit(solution)/shard_map/ppermute | solution.py:925
  70.6 2.3 %shard_map.81.refs_12_ = f32[4,8,32,128]{3,2,1,0:T(8,128)S(1)} custom-call(f32[8,64,128]{2,1,0:T(8,128)S(1)} %get-tuple-element.24.refs_0_, f32[8,64,128]{2,1,0:T(8,128)S(1)} %get-tuple-element.25.refs_1_, f32[8,64,128]{2,1,0:T(8,128)S(1)} %get-tuple-element.26.refs_2_, f32[8,64,128]{2,1,0:T(8,128)S(1)} %get-tuple-element.27.refs_3_, ...), custom_call_target="tpu_custom_call" | custom-call | flops 30000000 | bytes 30000000 | tf_op jit(solution)/shard_map/pallas_call | solution.py:857
  72.9 1.9 %all-to-all-done.2 = f32[32,1,128]{2,1,0:T(1,128)S(1)} async-done(((f32[32,1,128]{2,1,0:T(1,128)}), f32[32,1,128]{2,1,0:T(1,128)S(1)}, u32[]{:S(2)}, u32[]{:S(2)}) %all-to-all-start.2) | async-done | bytes 16416 | tf_op jit(solution)/shard_map/all_to_all | solution.py:927
  74.8 2.7 %shard_map.82 = f32[8,80,128]{2,1,0:T(8,128)S(1)} custom-call(f32[8,64,128]{2,1,0:T(8,128)S(1)} %get-tuple-element.24.refs_0_, f32[8,64,128]{2,1,0:T(8,128)S(1)} %get-tuple-element.25.refs_1_, f32[8,64,128]{2,1,0:T(8,128)S(1)} %get-tuple-element.26.refs_2_, f32[8,64,128]{2,1,0:T(8,128)S(1)} %get-tuple-element.27.refs_3_, ...), custom_call_target="tpu_custom_call" | custom-call | flops 20000000 | bytes 20000000 | tf_op jit(solution)/shard_map/pallas_call | solution.py:857
  77.5 13.6 %all_to_all.33.chunks = f32[8,80,128]{2,1,0:T(8,128)S(1)} all-to-all(f32[8,80,128]{2,1,0:T(8,128)S(1)} %shard_map.82), channel_id=1, replica_groups=mesh['gx'=4,'gy'=2,'gz'=4] {'gx','gy'}, dimensions={0} | all-to-all | bytes 655360 | tf_op jit(solution)/shard_map/all_to_all | solution.py:949
  91.1 0.9 shard_map.83
  (1 shorter events, 0.0 us)
Async XLA Ops:
  22.0 15.4 %collective-permute-start.1 = (f32[8,96,128]{2,1,0:T(8,128)S(1)}, f32[8,96,128]{2,1,0:T(8,128)S(1)}, u32[]{:S(2)}, u32[]{:S(2)}) collective-permute-start(f32[8,96,128]{2,1,0:T(8,128)S(1)} %all_to_all.32.own), channel_id=1, source_target_pairs={{8,0},{16,8},{24,16},{28,24},{20,28},{12,20},{4,12},{1,4},{9,1},{1... | collective-permute-start | bytes 1179656 | tf_op jit(solution)/shard_map/ppermute | solution.py:882
  23.2 14.1 %collective-permute-start = (f32[8,96,128]{2,1,0:T(8,128)S(1)}, f32[8,96,128]{2,1,0:T(8,128)S(1)}, u32[]{:S(2)}, u32[]{:S(2)}) collective-permute-start(f32[8,96,128]{2,1,0:T(8,128)S(1)} %all_to_all.32.own), channel_id=1, source_target_pairs={{0,8},{8,16},{16,24},{24,28},{28,20},{20,12},{12,4},{4,1},{1,9},{9... | collective-permute-start | bytes 1179656 | tf_op jit(solution)/shard_map/ppermute | solution.py:881
  27.9 9.5 %copy-start = (f32[8]{0:T(128)S(1)}, f32[8]{0:T(128)}, u32[]{:S(2)}) copy-start(f32[8]{0:T(128)} %stiffness.1) | copy-start | bytes 100
  27.9 9.0 %collective-permute-start.2 = (f32[8,8,128]{2,1,0:T(8,128)S(1)}, f32[8,8,128]{2,1,0:T(8,128)S(1)}, u32[]{:S(2)}, u32[]{:S(2)}) collective-permute-start(f32[8,8,128]{2,1,0:T(8,128)S(1)} %get-tuple-element.22), channel_id=1, source_target_pairs={{0,16},{8,24},{16,28},{24,20},{28,12},{20,4},{12,1},{4,9},{1,17},{... | collective-permute-start | bytes 98312 | tf_op jit(solution)/shard_map/ppermute | solution.py:885
  30.6 6.7 %collective-permute-start.3 = (f32[8,8,128]{2,1,0:T(8,128)S(1)}, f32[8,8,128]{2,1,0:T(8,128)S(1)}, u32[]{:S(2)}, u32[]{:S(2)}) collective-permute-start(f32[8,8,128]{2,1,0:T(8,128)S(1)} %get-tuple-element.23), channel_id=1, source_target_pairs={{16,0},{24,8},{28,16},{20,24},{12,28},{4,20},{1,12},{9,4},{17,1},{... | collective-permute-start | bytes 98312 | tf_op jit(solution)/shard_map/ppermute | solution.py:884
  45.6 11.4 %all-to-all-start.1 = ((f32[32,1,128]{2,1,0:T(1,128)}), f32[32,1,128]{2,1,0:T(1,128)S(1)}, u32[]{:S(2)}, u32[]{:S(2)}) async-start(f32[32,1,128]{2,1,0:T(1,128)} %bitcast.1), calls=%async_computation.1 | async-start | bytes 32768 | tf_op jit(solution)/shard_map/all_to_all | solution.py:911
  59.3 10.0 %collective-permute-start.5 = (f32[4,8,16,128]{3,2,1,0:T(8,128)S(1)}, f32[4,8,16,128]{3,2,1,0:T(8,128)S(1)}, u32[]{:S(2)}, u32[]{:S(2)}) collective-permute-start(f32[4,8,16,128]{3,2,1,0:T(8,128)S(1)} %get-tuple-element.38.refs_12_), channel_id=1, source_target_pairs={{8,0},{16,8},{24,16},{28,24},{20,28},{12,20},{4,12},{1,4},{9,1},{1... | collective-permute-start | bytes 786440 | tf_op jit(solution)/shard_map/ppermute | solution.py:926
  60.6 10.0 %collective-permute-start.4 = (f32[4,8,16,128]{3,2,1,0:T(8,128)S(1)}, f32[4,8,16,128]{3,2,1,0:T(8,128)S(1)}, u32[]{:S(2)}, u32[]{:S(2)}) collective-permute-start(f32[4,8,16,128]{3,2,1,0:T(8,128)S(1)} %get-tuple-element.38.refs_12_), channel_id=1, source_target_pairs={{0,8},{8,16},{16,24},{24,28},{28,20},{20,12},{12,4},{4,1},{1,9},{9... | collective-permute-start | bytes 786440 | tf_op jit(solution)/shard_map/ppermute | solution.py:925
  65.2 9.6 %all-to-all-start.2 = ((f32[32,1,128]{2,1,0:T(1,128)}), f32[32,1,128]{2,1,0:T(1,128)S(1)}, u32[]{:S(2)}, u32[]{:S(2)}) async-start(f32[32,1,128]{2,1,0:T(1,128)} %bitcast.4), calls=%async_computation.2 | async-start | bytes 32768 | tf_op jit(solution)/shard_map/all_to_all | solution.py:927

commit v10 on v9

--- a/solution.py
+++ b/solution.py
@@ -261,7 +261,7 @@
 TX, TY = 4, 2
 VMEM_LIMIT = 32 * 1024 * 1024
 PACK_LIMIT = 60 * 1024 * 1024
-FORWARD, ADJOINT = range(2)
+FORWARD, ADJOINT, RESPONSE = range(3)
 
 
 def slab_plan_fits(mesh, shape):
@@ -484,6 +484,20 @@
 STATIC = STATIC_FINE + STATIC_COARSE
 
 
+class Static:
+    def __init__(self, refs):
+        self.refs = dict(zip(STATIC, refs))
+
+    def base(self, name):
+        return 0 if name == "hv" else SUB
+
+    def get(self, name, z, *index):
+        return get(self.refs[name], z - self.base(name), *index)
+
+    def put(self, put, name, value, z, *index):
+        put(self.refs[name], value, z - self.base(name), *index)
+
+
 def iterate(geo, st, work, seqs, lo, hi, first=(), mean=None):
     v, p, res, cor, cor2, cc0, cc1 = work
     tl = Tiles(geo)
@@ -492,7 +506,7 @@
     transposed = len(seqs)
 
     def faces(t, z):
-        h, near = tl.beside(st["hv"], z, (), t)
+        h, near = tl.beside(st.refs["hv"], z, (), t)
         return [h + other for other in near]
 
     def around(face, ref, c, t, z):
@@ -501,7 +515,7 @@
 
     def residual(z, put):
         for t in range(SUB):
-            w = get(st["w"], z, t)
+            w = st.get("w", z, t)
             if FORWARD in seqs and FORWARD not in first:
                 face = faces(t, z)
                 diag = tree(face)
@@ -513,10 +527,12 @@
                 for k in range(3):
                     c = 3 * s + k
                     if q == FORWARD:
-                        value = get(st["s%d" % k], z, t)
+                        value = st.get("s%d" % k, z, t)
                         if not start:
                             f, total = around(face, v, c, t, z)
                             value = value - slope[k] - (diag * f - total)
+                    elif q == RESPONSE:
+                        value = -slope[k]
                     else:
                         value = slope[k] if q in first else get(cor, z, c, t) + slope[k]
                     put(res, value, z, c, t)
@@ -532,7 +548,7 @@
                 for c in comps:
                     _, total = around(face, cor, c, t, z)
                     left[c] = left[c] + (keep * get(res, z, c, t) + total)
-            wc = 0.125 * get(st["wc"], z, pair)
+            wc = 0.125 * st.get("wc", z, pair)
             for c in comps:
                 put(cc0, wc * tl.pair_sum(left[c]), z, c, pair)
 
@@ -540,7 +556,7 @@
 
     def coarse_step(ref, c, pair, z):
         f, near = tl.coarse_beside(ref, z, (c,), pair)
-        terms = [get(st[name], z, pair) * b for name, b in zip(STATIC_COARSE, near)]
+        terms = [st.get(name, z, pair) * b for name, b in zip(STATIC_COARSE, near)]
         return tree([get(cc0, z, c, pair), keep * f] + terms)
 
     def sweep_one(z, put):
@@ -561,7 +577,7 @@
 
     def velocity(z, put):
         for t in range(SUB):
-            face, w = faces(t, z), get(st["w"], z, t)
+            face, w = faces(t, z), st.get("w", z, t)
             for c in comps:
                 f, total = around(face, cor2, c, t, z)
                 value = get(cor, z, c, t) + keep * f + w * total
@@ -573,7 +589,7 @@
 
     def pressure(z, put):
         for t in range(SUB):
-            half = get(st["hv"], z, t)
+            half = st.get("hv", z, t)
             for s, q in enumerate(seqs):
                 c = 3 * s
                 if q == ADJOINT:
@@ -622,8 +638,8 @@
 
 
 def setup_kernel(geo, stiffness, own, low, high, low_edge, high_edge, *refs):
-    st = dict(zip(STATIC, refs))
-    moved, duals, sums, raw, heat, vc, *work = refs[len(STATIC) :]
+    st = Static(refs)
+    moved, dual_out, sums, raw, heat, vc, *work = refs[len(STATIC) :]
     v, p, res, cor, cor2, cc0, cc1 = work
     tl = Tiles(geo)
     b, m, n_rows = geo.slab, geo.margin, geo.rows
@@ -679,7 +695,7 @@
                     base = jnp.where(kind == float(layer), stiffness[layer], base)
                 value = base * jnp.exp(-ACTIVATION_ENERGY * get(heat, z, 1, t))
                 value = jnp.where(inside, value, 0.0)
-                put(st["hv"], 0.5 * value, z, t)
+                st.put(put, "hv", 0.5 * value, z, t)
                 coarse = coarse + value
             put(vc, 0.125 * tl.pair_sum(coarse), z, pair)
 
@@ -688,15 +704,15 @@
     def statics(z, put):
         inside = geo.inside(z)
         for t in range(SUB):
-            h, near = tl.beside(st["hv"], z, (), t)
+            h, near = tl.beside(st.refs["hv"], z, (), t)
             diag = tree([h + other for other in near])
-            put(st["w"], jnp.where(inside, JACOBI_WEIGHT / diag, 0.0), z, t)
+            st.put(put, "w", jnp.where(inside, JACOBI_WEIGHT / diag, 0.0), z, t)
             f, near = tl.beside(heat, z, (1,), t)
             dual = -INCREMENT_DT * get(raw, z, 4, t)
             for k in range(3):
                 flow = get(raw, z, 1 + k, t)
                 step = jnp.where(flow > 0, f - near[2 * k + 1], near[2 * k] - f)
-                put(st["s%d" % k], dual * step, z, t)
+                st.put(put, "s%d" % k, dual * step, z, t)
 
     sweep(m - b, m + 2 * b, statics)
 
@@ -707,8 +723,8 @@
             face = [0.25 * (0.5 * (c + o)) for o in near]
             wc = jnp.where(inside, JACOBI_WEIGHT / tree(face), 0.0)
             for name, f in zip(STATIC_COARSE, face):
-                put(st[name], wc * f, z, pair)
-            put(st["wc"], wc, z, pair)
+                st.put(put, name, wc * f, z, pair)
+            st.put(put, "wc", wc, z, pair)
 
     sweep(m - b, m + 2 * b, coarse_statics)
 
@@ -731,84 +747,83 @@
         value = jnp.where(geo.inside(z), 1.0, 0.0)
         for t in range(SUB):
             put(p, value, z, 0, t)
-            put(p, get(st["hv"], z, t), z, 1, t)
+            put(p, st.get("hv", z, t), z, 1, t)
 
     sweep(0, n_rows, unit)
 
-    mine = slice(m, m + b)
-    source = [st["s%d" % k].at[:, mine, :] for k in range(3)]
-    step = [v.at[k, :, mine, :] for k in range(3)]
-    iterate(geo, st, work, (ADJOINT,), m - PHASE, m + b + PHASE, (ADJOINT,))
-    sums_of = [(0, product(step, source)), (1, whole_sum(p[0, :, mine, :]))]
+    mine, rows = slice(m, m + b), slice(m - PHASE, m + b + PHASE)
+    iterate(geo, st, work, (ADJOINT,), rows.start, rows.stop, (ADJOINT,))
     for k in range(4):
-        duals[k] = cor[k, :, mine, :] if k < 3 else p[0, :, mine, :]
-    iterate(geo, st, work, (ADJOINT,), m, m + b)
-    sums_of += [(2, product(step, source))]
+        dual_out[k] = cor[k, :, rows, :] if k < 3 else p[0, :, rows, :]
+    sums_of = [(0, source_product(geo, st, v, 0)), (1, whole_sum(p[0, :, mine, :]))]
+    sums[...] = in_lanes(sums_of, sums.shape[0])
+
+
+def source_product(geo, st, v, first):
+    mine = slice(geo.margin, geo.margin + geo.slab)
+    held = slice(geo.margin - SUB, geo.margin - SUB + geo.slab)
+    left = [st.refs["s%d" % k].at[:, held, :] for k in range(3)]
+    return product(left, [v.at[first + k, :, mine, :] for k in range(3)])
+
+
+def first_kernel(geo, *refs):
+    st = Static(refs)
+    dual, state, response, later, sums, *work = refs[len(STATIC) :]
+    v, p, res, cor = work[:4]
+    b, m = geo.slab, geo.margin
+    mine, rows = slice(m, m + b), slice(m - PHASE, m + b + PHASE)
+
+    def unit(z, put):
+        value = jnp.where(geo.inside(z), 1.0, 0.0)
+        for t in range(SUB):
+            put(p, value, z, 1, t)
+
+    sweep(0, geo.rows, unit)
+    both = (FORWARD, RESPONSE)
+    iterate(geo, st, work, both, rows.start, rows.stop, both)
     for k in range(4):
-        duals[4 + k] = cor[k, :, mine, :] if k < 3 else p[0, :, mine, :]
-    sums[...] = in_lanes(sums_of, sums.shape[0])
-
-
-def first_kernel(geo, *refs):
-    st = dict(zip(STATIC, refs))
-    out, *work = refs[len(STATIC) :]
-    v, p = work[:2]
-    rows = slice(geo.margin - PHASE, geo.margin + geo.slab + PHASE)
-    iterate(geo, st, work, (FORWARD,), rows.start, rows.stop, (FORWARD,))
-    for k in range(4):
-        out[k] = v[k, :, rows, :] if k < 3 else p[0, :, rows, :]
-
-
-def refill(geo, v, p, state, rows, shift):
+        response[k] = v[3 + k, :, rows, :] if k < 3 else p[1, :, rows, :]
     for k in range(3):
-        v[k, :, rows, :] = state[k]
-    if shift is None:
-        p[0, :, rows, :] = state[3]
-    else:
-        inside = geo.inside(rows.start, rows.stop - rows.start)
-        p[0, :, rows, :] = state[3] - jnp.where(inside, shift, 0.0)[None]
-
-
-def second_kernel(geo, *refs):
-    st = dict(zip(STATIC, refs))
-    earlier, early, duals, state, sums, *work = refs[len(STATIC) :]
-    v, p = work[:2]
-    b, m = geo.slab, geo.margin
-    m1, m2 = means(geo, early[...], None)[:2]
-    refill(geo, v, p, earlier, slice(m - PHASE, m + b + PHASE), m1)
-    iterate(geo, st, work, (FORWARD,), m, m + b, mean=m2)
-    mine = slice(m, m + b)
+        cor[3 + k, :, rows, :] = dual[k]
+    p[1, :, rows, :] = dual[3]
+    p[2, :, rows, :] = st.refs["hv"][:, rows, :] * dual[3]
+    iterate(geo, st, work, (FORWARD, ADJOINT), m, m + b)
     for k in range(4):
         state[k] = v[k, :, mine, :] if k < 3 else p[0, :, mine, :]
+        later[k] = cor[3 + k, :, mine, :] if k < 3 else p[1, :, mine, :]
+    sums_of = [(2, source_product(geo, st, v, 3)), (3, whole_sum(p[1, :, mine, :]))]
+    sums[...] = in_lanes(sums_of, 1)
+
+
+def second_kernel(geo, raw, response, dual, later, early, part, state, sums):
+    own = slice(PHASE, PHASE + geo.slab)
+    m1 = jnp.sum(early[:, 0:1], axis=0, keepdims=True) / geo.cells
+    for k in range(4):
+        state[k] = raw[k] - m1 * response[k, :, own, :]
     fields = [state.at[k] for k in range(4)]
-    near, far = [duals.at[k] for k in range(4)], [duals.at[4 + k] for k in range(4)]
-    sums_of = [(3, product(near, fields)), (4, product(far, fields))]
-    sums[...] = in_lanes(sums_of, sums.shape[0])
+    near, far = [dual.at[k, :, own, :] for k in range(4)], [later.at[k] for k in range(4)]
+    sums_of = [(4, product(near, fields)), (5, product(far, fields))]
+    sums[...] = in_lanes(sums_of, sums.shape[0]) + part[...]
 
 
 def means(geo, early, late):
-    sums = early if late is None else early + late
-    row = jnp.sum(sums, axis=0, keepdims=True) / geo.cells
-    lane = lax.broadcasted_iota(jnp.int32, row.shape, 1)
-
-    def at(k):
-        return jnp.sum(jnp.where(lane == k, row, 0.0), axis=1, keepdims=True)
-
-    c1, l1, c2, l1_x2, l2_x2 = [at(k) for k in range(5)]
-    m1 = c1
-    m2 = c1 + c2 - m1 * l1
-    m3 = c1 + l1_x2
-    m4 = c1 + c2 + l2_x2 - m3 * l1
-    return m1, m2, m3, m4
+    row = jnp.sum(early + late, axis=0, keepdims=True) / geo.cells
+    c1, l1, c2, l2, l1_x2, l2_x2 = [row[:, k : k + 1] for k in range(6)]
+    m2 = c1 + c2 - c1 * l1
+    m3 = c1 + l1_x2 - m2 * l1
+    m4 = c1 + c2 + l2_x2 - m2 * l2 - m3 * l1
+    return m2, m3, m4
 
 
 def third_kernel(geo, *refs):
-    st = dict(zip(STATIC, refs))
+    st = Static(refs)
     own, low, high, out, *work = refs[len(STATIC) :]
     v, p = work[:2]
     b, m = geo.slab, geo.margin
     for source, base in ((low, m - b), (own, m), (high, m + b)):
-        refill(geo, v, p, source, slice(base, base + b), None)
+        for k in range(3):
+            v[k, :, base : base + b, :] = source[k]
+        p[0, :, base : base + b, :] = source[3]
     rows = slice(m - PHASE, m + b + PHASE)
     iterate(geo, st, work, (FORWARD,), rows.start, rows.stop)
     for k in range(4):
@@ -816,12 +831,16 @@
 
 
 def fourth_kernel(geo, *refs):
-    st = dict(zip(STATIC, refs))
-    state, early, late, moved, out, *work = refs[len(STATIC) :]
+    st = Static(refs)
+    state, response, early, late, moved, out, *work = refs[len(STATIC) :]
     v, p = work[:2]
     b, m = geo.slab, geo.margin
-    m3, m4 = means(geo, early[...], late[...])[2:]
-    refill(geo, v, p, state, slice(m - PHASE, m + b + PHASE), m3)
+    m2, m3, m4 = means(geo, early[...], late[...])
+    rows = slice(m - PHASE, m + b + PHASE)
+    for k in range(3):
+        v[k, :, rows, :] = state[k] - m2 * response[k]
+    shift = jnp.where(geo.inside(rows.start, rows.stop - rows.start), m3, 0.0)
+    p[0, :, rows, :] = state[3] - m2 * response[3] - shift[None]
     iterate(geo, st, work, (FORWARD,), m, m + b, mean=m4)
     for u in range(0, b, SUB):
         at = slice(m + u, m + u + SUB)
@@ -885,6 +904,9 @@
     low_edge = lax.ppermute(edges[1], axes, geo.shifts(2))
 
     fine, coarse = (SUB, geo.rows, LANES), (TX // 2, geo.rows, LANES)
+    held = geo.rows - 2 * SUB
+    static_shapes = [(SUB, geo.rows if name == "hv" else held, LANES) for name in STATIC_FINE]
+    static_shapes += [(TX // 2, held, LANES)] * len(STATIC_COARSE)
     slab = (SUB, b, LANES)
 
     def work(n, more=0):
@@ -893,11 +915,9 @@
 
     devices = group * geo.nz
     wide = (4, SUB, b + 2 * PHASE, LANES)
-    *static, moved, duals, early = call(
+    *static, moved, dual_one, early = call(
         functools.partial(setup_kernel, geo),
-        [fine] * len(STATIC_FINE)
-        + [coarse] * len(STATIC_COARSE)
-        + [slab, (8, *slab), (devices, LANES)],
+        static_shapes + [slab, wide, (devices, LANES)],
         [(FIELDS, *fine), (2, *fine), coarse] + work(1, 1),
         stiffness,
         own,
@@ -909,18 +929,24 @@
         megabytes=60,
     )
     early = lax.all_to_all(early, axes, 0, 0, tiled=True)
-    (state,) = call(
-        functools.partial(first_kernel, geo), [wide], work(1), *static, megabytes=20
+    raw, response, dual_two, part = call(
+        functools.partial(first_kernel, geo),
+        [(4, *slab), wide, (4, *slab), (1, LANES)],
+        work(2, 1),
+        *static,
+        dual_one,
+        megabytes=40,
     )
     state, late = call(
         functools.partial(second_kernel, geo),
         [(4, *slab), (devices, LANES)],
-        work(1),
-        *static,
-        state,
+        [],
+        raw,
+        response,
+        dual_one,
+        dual_two,
         early,
-        duals,
-        megabytes=20,
+        part,
     )
     low_state = lax.ppermute(state, axes, geo.shifts(1))
     high_state = lax.ppermute(state, axes, geo.shifts(-1))
@@ -941,6 +967,7 @@
         work(1),
         *static,
         state,
+        response,
         early,
         late,
         moved,

time: 92.4 us -> 91.7 us (level)
  waiting for transfers between devices: 15.5 us -> 11.4 us
  starting transfers between devices: 22.6 us -> 24.6 us
  Pallas kernels: 20.1 us -> 21.5 us
    all_to_all x1, waiting for transfers between devices: 5.4 us -> 1.27 us  [slab_shards(): early = lax.all_to_all(early, axes, 0, 0, tiled=True)]
    all_to_all x1, waiting for transfers between devices: 1.89 us -> 4.06 us  [slab_shards(): late = lax.all_to_all(late, axes, 0, 0, tiled=True)]
    all_to_all x1, starting transfers between devices: 2.56 us -> 4.57 us  [slab_shards(): late = lax.all_to_all(late, axes, 0, 0, tiled=True)]
    ppermute x1, waiting for transfers between devices: 1.54 us -> 0.01 us  [slab_shards(): high_state = lax.ppermute(state, axes, geo.shifts(-1))]
    pallas_call x8, Pallas kernels: 20.1 us -> 21.5 us  [call(): pl.pallas_call(kernel, out_shape=[jax.ShapeDtypeStruct(s, f32) for s in o...]
  transfers between devices with their start and end apart: 8 -> 8, of which waited for: 6 -> 5; matrix products, arithmetic and copies ran while one was open for 0% -> 0% of each run, Pallas kernels for 4% -> 9%
where the time goes in v10:
time: 91.7 us; the launch traced here: 91.2 us
  blocking collectives  33 us (36%)
  starting transfers between devices  24.6 us (27%)
  Pallas kernels  21.5 us (23%)
  waiting for transfers between devices  11.4 us (12%)
    pallas_call x8, Pallas kernels, call(): pl.pallas_call(kernel, out_shape=[jax.ShapeDtypeStruct(s, f32) for s in o...  21.5 us
    all_to_all x1, blocking collectives, slab_shards(): own = lax.all_to_all(chunks, ('gx', 'gy'), 0, 0, tiled=True)  19.4 us
    all_to_all x1, blocking collectives, slab_shards(): chunks = lax.all_to_all(chunks, ('gx', 'gy'), 0, 0, tiled=True)  13.6 us
    ppermute x1, waiting for transfers between devices, slab_shards(): low_edge = lax.ppermute(edges[1], axes, geo.shifts(2))  4.92 us
    all_to_all x1, starting transfers between devices, slab_shards(): late = lax.all_to_all(late, axes, 0, 0, tiled=True)  4.57 us
    ppermute x1, starting transfers between devices, slab_shards(): low = lax.ppermute(own, axes, geo.shifts(1))  4.57 us
    ppermute x1, starting transfers between devices, slab_shards(): low_state = lax.ppermute(state, axes, geo.shifts(1))  4.56 us
    all_to_all x1, starting transfers between devices, slab_shards(): early = lax.all_to_all(early, axes, 0, 0, tiled=True)  4.29 us
  transfers between devices with their start and end apart: 8, of which 5 were waited for; matrix products, arithmetic and copies ran while one was open for 0% of the time, Pallas kernels for 9%

profile of v10, /device:TPU:0, one launch (start us, length us, event | category | flops | bytes accessed | tf_op | source)
XLA Modules:
  0.0 91.2 jit_solution(16998530442701726004)
XLA Ops:
  0.6 1.9 %shard_map.76 = f32[8,96,128]{2,1,0:T(8,128)} custom-call(f32[8,16,128]{2,1,0:T(8,128)} %heat_in.1, f32[3,8,16,128]{3,2,1,0:T(8,128)} %flow_in.1, f32[8,16,128]{2,1,0:T(8,128)} %dual_in.1, s32[8,16,128]{2,1,0:T(8,128)} %kind_in.1), custom_call_target="tpu_custom_call" | custom-call | flops 2000000 | bytes 2000000 | tf_op jit(solution)/shard_map/pallas_call | solution.py:876
  2.6 19.4 %all_to_all.32.own = f32[8,96,128]{2,1,0:T(8,128)S(1)} all-to-all(f32[8,96,128]{2,1,0:T(8,128)} %shard_map.76), channel_id=1, replica_groups=mesh['gx'=4,'gy'=2,'gz'=4] {'gx','gy'}, dimensions={0} | all-to-all | bytes 786432 | tf_op jit(solution)/shard_map/all_to_all | solution.py:898
  22.0 1.3 %collective-permute-start.1 = (f32[8,96,128]{2,1,0:T(8,128)S(1)}, f32[8,96,128]{2,1,0:T(8,128)S(1)}, u32[]{:S(2)}, u32[]{:S(2)}) collective-permute-start(f32[8,96,128]{2,1,0:T(8,128)S(1)} %all_to_all.32.own), channel_id=1, source_target_pairs={{8,0},{16,8},{24,16},{28,24},{20,28},{12,20},{4,12},{1,4},{9,1},{1... | collective-permute-start | bytes 1179656 | tf_op jit(solution)/shard_map/ppermute | solution.py:901
  23.2 4.6 %collective-permute-start = (f32[8,96,128]{2,1,0:T(8,128)S(1)}, f32[8,96,128]{2,1,0:T(8,128)S(1)}, u32[]{:S(2)}, u32[]{:S(2)}) collective-permute-start(f32[8,96,128]{2,1,0:T(8,128)S(1)} %all_to_all.32.own), channel_id=1, source_target_pairs={{0,8},{8,16},{16,24},{24,28},{28,20},{20,12},{12,4},{4,1},{1,9},{9... | collective-permute-start | bytes 1179656 | tf_op jit(solution)/shard_map/ppermute | solution.py:900
  27.9 0.0 copy-start
  27.9 2.8 %collective-permute-start.2 = (f32[8,8,128]{2,1,0:T(8,128)S(1)}, f32[8,8,128]{2,1,0:T(8,128)S(1)}, u32[]{:S(2)}, u32[]{:S(2)}) collective-permute-start(f32[8,8,128]{2,1,0:T(8,128)S(1)} %get-tuple-element.26), channel_id=1, source_target_pairs={{0,16},{8,24},{16,28},{24,20},{28,12},{20,4},{12,1},{4,9},{1,17},{... | collective-permute-start | bytes 98312 | tf_op jit(solution)/shard_map/ppermute | solution.py:904
  30.6 1.3 %collective-permute-start.3 = (f32[8,8,128]{2,1,0:T(8,128)S(1)}, f32[8,8,128]{2,1,0:T(8,128)S(1)}, u32[]{:S(2)}, u32[]{:S(2)}) collective-permute-start(f32[8,8,128]{2,1,0:T(8,128)S(1)} %get-tuple-element.27), channel_id=1, source_target_pairs={{16,0},{24,8},{28,16},{20,24},{12,28},{4,20},{1,12},{9,4},{17,1},{... | collective-permute-start | bytes 98312 | tf_op jit(solution)/shard_map/ppermute | solution.py:903
  31.9 4.9 %collective-permute-done.2.low_edge = f32[8,8,128]{2,1,0:T(8,128)S(1)} collective-permute-done((f32[8,8,128]{2,1,0:T(8,128)S(1)}, f32[8,8,128]{2,1,0:T(8,128)S(1)}, u32[]{:S(2)}, u32[]{:S(2)}) %collective-permute-start.2) | collective-permute-done | bytes 32800 | tf_op jit(solution)/shard_map/ppermute | solution.py:904
  36.9 0.5 collective-permute-done.3.high_edge
  37.3 0.0 collective-permute-done.1.high
  37.3 0.0 collective-permute-done.low
  37.3 0.0 copy-done
  37.4 6.9 %shard_map.78 = (f32[8,48,128]{2,1,0:T(8,128)S(1)}, f32[8,48,128]{2,1,0:T(8,128)S(1)}, f32[8,48,128]{2,1,0:T(8,128)S(1)}, f32[8,64,128]{2,1,0:T(8,128)S(1)}, f32...) custom-call(f32[8]{0:T(128)S(1)} %copy-done, ...), custom_call_target="tpu_custom_call" | custom-call | flops 60000000 | bytes 60000000 | tf_op jit(solution)/shard_map/pallas_call | solution.py:876
  44.3 4.3 %all-to-all-start.1 = ((f32[32,1,128]{2,1,0:T(1,128)}), f32[32,1,128]{2,1,0:T(1,128)S(1)}, u32[]{:S(2)}, u32[]{:S(2)}) async-start(f32[32,1,128]{2,1,0:T(1,128)} %bitcast.1), calls=%async_computation.1 | async-start | bytes 32768 | tf_op jit(solution)/shard_map/all_to_all | solution.py:931
  48.6 5.8 %shard_map.79 = (f32[4,8,16,128]{3,2,1,0:T(8,128)S(1)}, f32[4,8,32,128]{3,2,1,0:T(8,128)S(1)}, f32[4,8,16,128]{3,2,1,0:T(8,128)S(1)}, f32[1,128]{1,0:T(1,128)S(1)}) custom-call(f32[8,48,128]{2,1,0:T(8,128)S(1)} %get-tuple-element.28.refs_0_, f32[8,48,128]{2,1,0:T(8,128)S(1)} %get-tuple-element.29.refs_1_, f32[8,48,128]{2,1,0:T(8,128)S(1)} %get-tuple-element.30.refs_2_, ...), custom_call_target="tpu_custom_call" | custom-call | flops 40000000 | bytes 40000000 | tf_op jit(solution)/shard_map/pallas_call | solution.py:876
  54.4 1.3 %all-to-all-done.1 = f32[32,1,128]{2,1,0:T(1,128)S(1)} async-done(((f32[32,1,128]{2,1,0:T(1,128)}), f32[32,1,128]{2,1,0:T(1,128)S(1)}, u32[]{:S(2)}, u32[]{:S(2)}) %all-to-all-start.1) | async-done | bytes 16416 | tf_op jit(solution)/shard_map/all_to_all | solution.py:931
  55.6 0.9 shard_map.80
  56.5 1.3 %collective-permute-start.5 = (f32[4,8,16,128]{3,2,1,0:T(8,128)S(1)}, f32[4,8,16,128]{3,2,1,0:T(8,128)S(1)}, u32[]{:S(2)}, u32[]{:S(2)}) collective-permute-start(f32[4,8,16,128]{3,2,1,0:T(8,128)S(1)} %get-tuple-element.46.refs_12_), channel_id=1, source_target_pairs={{8,0},{16,8},{24,16},{28,24},{20,28},{12,20},{4,12},{1,4},{9,1},{1... | collective-permute-start | bytes 786440 | tf_op jit(solution)/shard_map/ppermute | solution.py:952
  57.8 4.6 %collective-permute-start.4 = (f32[4,8,16,128]{3,2,1,0:T(8,128)S(1)}, f32[4,8,16,128]{3,2,1,0:T(8,128)S(1)}, u32[]{:S(2)}, u32[]{:S(2)}) collective-permute-start(f32[4,8,16,128]{3,2,1,0:T(8,128)S(1)} %get-tuple-element.46.refs_12_), channel_id=1, source_target_pairs={{0,8},{8,16},{16,24},{24,28},{28,20},{20,12},{12,4},{4,1},{1,9},{9... | collective-permute-start | bytes 786440 | tf_op jit(solution)/shard_map/ppermute | solution.py:951
  62.4 4.6 %all-to-all-start.2 = ((f32[32,1,128]{2,1,0:T(1,128)}), f32[32,1,128]{2,1,0:T(1,128)S(1)}, u32[]{:S(2)}, u32[]{:S(2)}) async-start(f32[32,1,128]{2,1,0:T(1,128)} %bitcast.4), calls=%async_computation.2 | async-start | bytes 32768 | tf_op jit(solution)/shard_map/all_to_all | solution.py:953
  67.0 0.0 collective-permute-done.5.refs_14_
  67.0 0.7 collective-permute-done.4.refs_13_
  67.7 2.3 %shard_map.81.refs_12_ = f32[4,8,32,128]{3,2,1,0:T(8,128)S(1)} custom-call(f32[8,48,128]{2,1,0:T(8,128)S(1)} %get-tuple-element.28.refs_0_, f32[8,48,128]{2,1,0:T(8,128)S(1)} %get-tuple-element.29.refs_1_, f32[8,48,128]{2,1,0:T(8,128)S(1)} %get-tuple-element.30.refs_2_, f32[8,64,128]{2,1,0:T(8,128)S(1)} %get-tuple-element.31.refs_3_, ...), custom_call_target="tpu_custom_call" | custom-call | flops 30000000 | bytes 30000000 | tf_op jit(solution)/shard_map/pallas_call | solution.py:876
  70.0 4.1 %all-to-all-done.2 = f32[32,1,128]{2,1,0:T(1,128)S(1)} async-done(((f32[32,1,128]{2,1,0:T(1,128)}), f32[32,1,128]{2,1,0:T(1,128)S(1)}, u32[]{:S(2)}, u32[]{:S(2)}) %all-to-all-start.2) | async-done | bytes 16416 | tf_op jit(solution)/shard_map/all_to_all | solution.py:953
  74.0 2.7 %shard_map.82 = f32[8,80,128]{2,1,0:T(8,128)S(1)} custom-call(f32[8,48,128]{2,1,0:T(8,128)S(1)} %get-tuple-element.28.refs_0_, f32[8,48,128]{2,1,0:T(8,128)S(1)} %get-tuple-element.29.refs_1_, f32[8,48,128]{2,1,0:T(8,128)S(1)} %get-tuple-element.30.refs_2_, f32[8,64,128]{2,1,0:T(8,128)S(1)} %get-tuple-element.31.refs_3_, ...), custom_call_target="tpu_custom_call" | custom-call | flops 20000000 | bytes 20000000 | tf_op jit(solution)/shard_map/pallas_call | solution.py:876
  76.8 13.6 %all_to_all.33.chunks = f32[8,80,128]{2,1,0:T(8,128)S(1)} all-to-all(f32[8,80,128]{2,1,0:T(8,128)S(1)} %shard_map.82), channel_id=1, replica_groups=mesh['gx'=4,'gy'=2,'gz'=4] {'gx','gy'}, dimensions={0} | all-to-all | bytes 655360 | tf_op jit(solution)/shard_map/all_to_all | solution.py:976
  90.4 0.9 shard_map.83
  (1 shorter events, 0.0 us)
Async XLA Ops:
  22.0 15.4 %collective-permute-start.1 = (f32[8,96,128]{2,1,0:T(8,128)S(1)}, f32[8,96,128]{2,1,0:T(8,128)S(1)}, u32[]{:S(2)}, u32[]{:S(2)}) collective-permute-start(f32[8,96,128]{2,1,0:T(8,128)S(1)} %all_to_all.32.own), channel_id=1, source_target_pairs={{8,0},{16,8},{24,16},{28,24},{20,28},{12,20},{4,12},{1,4},{9,1},{1... | collective-permute-start | bytes 1179656 | tf_op jit(solution)/shard_map/ppermute | solution.py:901
  23.2 14.1 %collective-permute-start = (f32[8,96,128]{2,1,0:T(8,128)S(1)}, f32[8,96,128]{2,1,0:T(8,128)S(1)}, u32[]{:S(2)}, u32[]{:S(2)}) collective-permute-start(f32[8,96,128]{2,1,0:T(8,128)S(1)} %all_to_all.32.own), channel_id=1, source_target_pairs={{0,8},{8,16},{16,24},{24,28},{28,20},{20,12},{12,4},{4,1},{1,9},{9... | collective-permute-start | bytes 1179656 | tf_op jit(solution)/shard_map/ppermute | solution.py:900
  27.9 9.5 %copy-start = (f32[8]{0:T(128)S(1)}, f32[8]{0:T(128)}, u32[]{:S(2)}) copy-start(f32[8]{0:T(128)} %stiffness.1) | copy-start | bytes 100
  27.9 9.0 %collective-permute-start.2 = (f32[8,8,128]{2,1,0:T(8,128)S(1)}, f32[8,8,128]{2,1,0:T(8,128)S(1)}, u32[]{:S(2)}, u32[]{:S(2)}) collective-permute-start(f32[8,8,128]{2,1,0:T(8,128)S(1)} %get-tuple-element.26), channel_id=1, source_target_pairs={{0,16},{8,24},{16,28},{24,20},{28,12},{20,4},{12,1},{4,9},{1,17},{... | collective-permute-start | bytes 98312 | tf_op jit(solution)/shard_map/ppermute | solution.py:904
  30.6 6.7 %collective-permute-start.3 = (f32[8,8,128]{2,1,0:T(8,128)S(1)}, f32[8,8,128]{2,1,0:T(8,128)S(1)}, u32[]{:S(2)}, u32[]{:S(2)}) collective-permute-start(f32[8,8,128]{2,1,0:T(8,128)S(1)} %get-tuple-element.27), channel_id=1, source_target_pairs={{16,0},{24,8},{28,16},{20,24},{12,28},{4,20},{1,12},{9,4},{17,1},{... | collective-permute-start | bytes 98312 | tf_op jit(solution)/shard_map/ppermute | solution.py:903
  44.3 11.4 %all-to-all-start.1 = ((f32[32,1,128]{2,1,0:T(1,128)}), f32[32,1,128]{2,1,0:T(1,128)S(1)}, u32[]{:S(2)}, u32[]{:S(2)}) async-start(f32[32,1,128]{2,1,0:T(1,128)} %bitcast.1), calls=%async_computation.1 | async-start | bytes 32768 | tf_op jit(solution)/shard_map/all_to_all | solution.py:931
  56.5 10.4 %collective-permute-start.5 = (f32[4,8,16,128]{3,2,1,0:T(8,128)S(1)}, f32[4,8,16,128]{3,2,1,0:T(8,128)S(1)}, u32[]{:S(2)}, u32[]{:S(2)}) collective-permute-start(f32[4,8,16,128]{3,2,1,0:T(8,128)S(1)} %get-tuple-element.46.refs_12_), channel_id=1, source_target_pairs={{8,0},{16,8},{24,16},{28,24},{20,28},{12,20},{4,12},{1,4},{9,1},{1... | collective-permute-start | bytes 786440 | tf_op jit(solution)/shard_map/ppermute | solution.py:952
  57.8 9.9 %collective-permute-start.4 = (f32[4,8,16,128]{3,2,1,0:T(8,128)S(1)}, f32[4,8,16,128]{3,2,1,0:T(8,128)S(1)}, u32[]{:S(2)}, u32[]{:S(2)}) collective-permute-start(f32[4,8,16,128]{3,2,1,0:T(8,128)S(1)} %get-tuple-element.46.refs_12_), channel_id=1, source_target_pairs={{0,8},{8,16},{16,24},{24,28},{28,20},{20,12},{12,4},{4,1},{1,9},{9... | collective-permute-start | bytes 786440 | tf_op jit(solution)/shard_map/ppermute | solution.py:951
  62.4 11.7 %all-to-all-start.2 = ((f32[32,1,128]{2,1,0:T(1,128)}), f32[32,1,128]{2,1,0:T(1,128)S(1)}, u32[]{:S(2)}, u32[]{:S(2)}) async-start(f32[32,1,128]{2,1,0:T(1,128)} %bitcast.4), calls=%async_computation.2 | async-start | bytes 32768 | tf_op jit(solution)/shard_map/all_to_all | solution.py:953

commit v11 on v10

--- a/solution.py
+++ b/solution.py
@@ -353,20 +353,20 @@
         self.row = lax.broadcasted_iota(jnp.int32, (SUB, LANES), 0)
         self.lane = lax.broadcasted_iota(jnp.int32, (SUB, LANES), 1)
         self.y = self.lane % self.span
-        self.kept, self.latest = {}, None
+        self.kept, self.latest, self.sweep = {}, None, 0
 
     def sliding(self, ref, z, lead, t):
-        if self.latest is not z:
-            self.latest, self.kept = z, {}
-        where = (id(ref), z if isinstance(z, int) else id(z), lead)
-        for key in [k for k in self.kept if k[:3] == where and abs(k[3] - t) > 3]:
+        if self.latest != (self.sweep, z):
+            self.latest, self.kept = (self.sweep, z), {}
+        where = (id(ref), lead)
+        for key in [k for k in self.kept if k[:2] == where and abs(k[2] - t) > 3]:
             del self.kept[key]
 
         def load(j):
             key = (*where, j)
             if key not in self.kept:
-                self.kept[key] = (ref, z, get(ref, z, *lead, j))
-            return self.kept[key][2]
+                self.kept[key] = (ref, get(ref, z, *lead, j))
+            return self.kept[key][1]
 
         return load
 
@@ -421,32 +421,22 @@
     return ref[(*index, pl.ds(z, SUB), slice(None))]
 
 
-def sweep(lo, hi, body):
-    count = (hi - lo) // SUB
-    assert count * SUB == hi - lo
-    unroll = next(u for u in (3, 2, count) if count % u == 0)
-
-    def step(t):
-        late = []
-
-        def store(ref, value, z, *index):
-            ref[(*index, pl.ds(z, SUB), slice(None))] = value
-
-        def put(*item):
-            late.append(item)
-            if len(late) > HELD:
-                store(*late.pop(0))
-
-        for u in range(unroll):
-            body(t + (lo + u * SUB), put)
-        for item in late:
-            store(*item)
-
-    if unroll == count:
-        step(0)
-    else:
-        span = unroll * SUB
-        lax.fori_loop(0, count // unroll, lambda t, _: (step(pl.multiple_of(t * span, SUB)), 0)[1], 0)
+def sweep(tl, lo, hi, body):
+    tl.sweep += 1
+    late = []
+
+    def store(ref, value, z, *index):
+        ref[(*index, pl.ds(z, SUB), slice(None))] = value
+
+    def put(*item):
+        late.append(item)
+        if len(late) > HELD:
+            store(*late.pop(0))
+
+    for z in range(lo, hi, SUB):
+        body(z, put)
+    for item in late:
+        store(*item)
 
 
 def pack_kernel(geo, heat_in, flow_in, dual_in, kind_in, out, heat, flow, dual, kind, sems):
@@ -458,17 +448,14 @@
     ]
     for copy in copies:
         copy.start()
-    for copy in copies:
-        copy.wait()
     fields = [heat, flow.at[0], flow.at[1], flow.at[2], dual, kind]
-    turned = []
-    for ref in fields:
+    for f, (ref, copy) in enumerate(zip(fields, (0, 1, None, None, 2, 3))):
+        if copy is not None:
+            copies[copy].wait()
         rows = [ref[x, pl.ds(y, SUB, stride=TY), :] for x, y in geo.order]
-        turned.append(jnp.concatenate(rows, 0).astype(jnp.float32).T)
-    for j in range(geo.group):
-        q = geo.holder[j]
-        for f in range(FIELDS):
-            out[q, f * b : (f + 1) * b, :] = turned[f][j * b : (j + 1) * b]
+        turned = jnp.concatenate(rows, 0).astype(jnp.float32).T
+        for j in range(geo.group):
+            out[geo.holder[j], f * b : (f + 1) * b, :] = turned[j * b : (j + 1) * b]
 
 
 def edge_kernel(geo, own, first, last):
@@ -538,7 +525,7 @@
                     put(res, value, z, c, t)
                     put(cor, w * value, z, c, t)
 
-    sweep(lo - 8, hi + 8, residual)
+    sweep(tl, lo - 8, hi + 8, residual)
 
     def restricted(z, put):
         for pair in range(TX // 2):
@@ -552,7 +539,7 @@
             for c in comps:
                 put(cc0, wc * tl.pair_sum(left[c]), z, c, pair)
 
-    sweep(lo - 8, hi + 8, restricted)
+    sweep(tl, lo - 8, hi + 8, restricted)
 
     def coarse_step(ref, c, pair, z):
         f, near = tl.coarse_beside(ref, z, (c,), pair)
@@ -564,7 +551,7 @@
             for c in comps:
                 put(cc1, coarse_step(cc0, c, pair, z), z, c, pair)
 
-    sweep(lo - 4, hi + 4, sweep_one)
+    sweep(tl, lo - 4, hi + 4, sweep_one)
 
     def sweep_two(z, put):
         for pair in range(TX // 2):
@@ -573,7 +560,7 @@
                 for t in block_of(pair):
                     put(cor2, get(cor, z, c, t) + value, z, c, t)
 
-    sweep(lo - 4, hi + 4, sweep_two)
+    sweep(tl, lo - 4, hi + 4, sweep_two)
 
     def velocity(z, put):
         for t in range(SUB):
@@ -585,7 +572,7 @@
                     value = get(v, z, c, t) + value
                 put(v, value, z, c, t)
 
-    sweep(lo - 4, hi + 4, velocity)
+    sweep(tl, lo - 4, hi + 4, velocity)
 
     def pressure(z, put):
         for t in range(SUB):
@@ -615,7 +602,7 @@
                     value = value - jnp.where(geo.inside(z), mean, 0.0)
                 put(p, value, z, s, t)
 
-    sweep(lo, hi, pressure)
+    sweep(tl, lo, hi, pressure)
 
 
 def whole_sum(value):
@@ -681,8 +668,8 @@
 
         return body
 
-    sweep(m - b - 4, m + 2 * b + 4, advance(raw, 0, 0))
-    sweep(m - b, m + 2 * b, advance(heat, 0, 1))
+    sweep(tl, m - b - 4, m + 2 * b + 4, advance(raw, 0, 0))
+    sweep(tl, m - b, m + 2 * b, advance(heat, 0, 1))
 
     def viscosity(z, put):
         inside = geo.inside(z)
@@ -699,7 +686,7 @@
                 coarse = coarse + value
             put(vc, 0.125 * tl.pair_sum(coarse), z, pair)
 
-    sweep(m - b, m + 2 * b, viscosity)
+    sweep(tl, m - b, m + 2 * b, viscosity)
 
     def statics(z, put):
         inside = geo.inside(z)
@@ -714,7 +701,7 @@
                 step = jnp.where(flow > 0, f - near[2 * k + 1], near[2 * k] - f)
                 st.put(put, "s%d" % k, dual * step, z, t)
 
-    sweep(m - b, m + 2 * b, statics)
+    sweep(tl, m - b, m + 2 * b, statics)
 
     def coarse_statics(z, put):
         inside = geo.inside(z)
@@ -726,7 +713,7 @@
                 st.put(put, name, wc * f, z, pair)
             st.put(put, "wc", wc, z, pair)
 
-    sweep(m - b, m + 2 * b, coarse_statics)
+    sweep(tl, m - b, m + 2 * b, coarse_statics)
 
     def transport(z, put):
         for t in range(SUB):
@@ -741,7 +728,7 @@
                 value = value - INCREMENT_DT * (a - ahead + behind - c)
             put(moved, value, z - m, t)
 
-    sweep(m, m + b, transport)
+    sweep(tl, m, m + b, transport)
 
     def unit(z, put):
         value = jnp.where(geo.inside(z), 1.0, 0.0)
@@ -749,7 +736,7 @@
             put(p, value, z, 0, t)
             put(p, st.get("hv", z, t), z, 1, t)
 
-    sweep(0, n_rows, unit)
+    sweep(tl, 0, n_rows, unit)
 
     mine, rows = slice(m, m + b), slice(m - PHASE, m + b + PHASE)
     iterate(geo, st, work, (ADJOINT,), rows.start, rows.stop, (ADJOINT,))
@@ -768,17 +755,18 @@
 
 def first_kernel(geo, *refs):
     st = Static(refs)
-    dual, state, response, later, sums, *work = refs[len(STATIC) :]
+    dual, state, response, sums, later, *work = refs[len(STATIC) :]
     v, p, res, cor = work[:4]
     b, m = geo.slab, geo.margin
     mine, rows = slice(m, m + b), slice(m - PHASE, m + b + PHASE)
+    tl = Tiles(geo)
 
     def unit(z, put):
         value = jnp.where(geo.inside(z), 1.0, 0.0)
         for t in range(SUB):
             put(p, value, z, 1, t)
 
-    sweep(0, geo.rows, unit)
+    sweep(tl, 0, geo.rows, unit)
     both = (FORWARD, RESPONSE)
     iterate(geo, st, work, both, rows.start, rows.stop, both)
     for k in range(4):
@@ -791,27 +779,27 @@
     for k in range(4):
         state[k] = v[k, :, mine, :] if k < 3 else p[0, :, mine, :]
         later[k] = cor[3 + k, :, mine, :] if k < 3 else p[1, :, mine, :]
+    own = slice(PHASE, PHASE + b)
+    near, far = [dual.at[k, :, own, :] for k in range(4)], [later.at[k] for k in range(4)]
+    fields, turn = [state.at[k] for k in range(4)], [response.at[k, :, own, :] for k in range(4)]
     sums_of = [(2, source_product(geo, st, v, 3)), (3, whole_sum(p[1, :, mine, :]))]
-    sums[...] = in_lanes(sums_of, 1)
-
-
-def second_kernel(geo, raw, response, dual, later, early, part, state, sums):
+    sums_of += [(4, product(near, fields)), (5, product(far, fields)), (6, product(far, turn))]
+    sums[...] = in_lanes(sums_of, sums.shape[0])
+
+
+def second_kernel(geo, raw, response, early, state):
     own = slice(PHASE, PHASE + geo.slab)
-    m1 = jnp.sum(early[:, 0:1], axis=0, keepdims=True) / geo.cells
+    m1 = jnp.sum(early[...], axis=0, keepdims=True)[:, 0:1] / geo.cells
     for k in range(4):
         state[k] = raw[k] - m1 * response[k, :, own, :]
-    fields = [state.at[k] for k in range(4)]
-    near, far = [dual.at[k, :, own, :] for k in range(4)], [later.at[k] for k in range(4)]
-    sums_of = [(4, product(near, fields)), (5, product(far, fields))]
-    sums[...] = in_lanes(sums_of, sums.shape[0]) + part[...]
 
 
 def means(geo, early, late):
     row = jnp.sum(early + late, axis=0, keepdims=True) / geo.cells
-    c1, l1, c2, l2, l1_x2, l2_x2 = [row[:, k : k + 1] for k in range(6)]
+    c1, l1, c2, l2, l1_x2, l2_x2, l2_r1 = [row[:, k : k + 1] for k in range(7)]
     m2 = c1 + c2 - c1 * l1
-    m3 = c1 + l1_x2 - m2 * l1
-    m4 = c1 + c2 + l2_x2 - m2 * l2 - m3 * l1
+    m3 = c1 + (l1_x2 - c1 * l2) - m2 * l1
+    m4 = c1 + c2 + (l2_x2 - c1 * l2_r1) - m2 * l2 - m3 * l1
     return m2, m3, m4
 
 
@@ -929,28 +917,20 @@
         megabytes=60,
     )
     early = lax.all_to_all(early, axes, 0, 0, tiled=True)
-    raw, response, dual_two, part = call(
+    raw, response, late = call(
         functools.partial(first_kernel, geo),
-        [(4, *slab), wide, (4, *slab), (1, LANES)],
-        work(2, 1),
+        [(4, *slab), wide, (devices, LANES)],
+        [(4, *slab)] + work(2, 1),
         *static,
         dual_one,
         megabytes=40,
     )
-    state, late = call(
-        functools.partial(second_kernel, geo),
-        [(4, *slab), (devices, LANES)],
-        [],
-        raw,
-        response,
-        dual_one,
-        dual_two,
-        early,
-        part,
+    late = lax.all_to_all(late, axes, 0, 0, tiled=True)
+    (state,) = call(
+        functools.partial(second_kernel, geo), [(4, *slab)], [], raw, response, early
     )
     low_state = lax.ppermute(state, axes, geo.shifts(1))
     high_state = lax.ppermute(state, axes, geo.shifts(-1))
-    late = lax.all_to_all(late, axes, 0, 0, tiled=True)
     (state,) = call(
         functools.partial(third_kernel, geo),
         [wide],

time: 91.7 us -> 89.4 us (0.975)
  Pallas kernels: 21.5 us -> 18.7 us
  waiting for transfers between devices: 11.4 us -> 12.4 us
    pallas_call x8, Pallas kernels: 21.5 us -> 18.7 us  [call(): pl.pallas_call(kernel, out_shape=[jax.ShapeDtypeStruct(s, f32) for s in o...]
  transfers between devices with their start and end apart: 8 -> 8, of which waited for: 5 -> 5; matrix products, arithmetic and copies ran while one was open for 0% -> 0% of each run, Pallas kernels for 9% -> 8%
where the time goes in v11:
time: 89.4 us; the launch traced here: 89 us
  blocking collectives  33 us (37%)
  starting transfers between devices  24.2 us (27%)
  Pallas kernels  18.7 us (21%)
  waiting for transfers between devices  12.4 us (14%)
    all_to_all x1, blocking collectives, slab_shards(): own = lax.all_to_all(chunks, ('gx', 'gy'), 0, 0, tiled=True)  19.4 us
    pallas_call x8, Pallas kernels, call(): pl.pallas_call(kernel, out_shape=[jax.ShapeDtypeStruct(s, f32) for s in o...  18.7 us
    all_to_all x1, blocking collectives, slab_shards(): chunks = lax.all_to_all(chunks, ('gx', 'gy'), 0, 0, tiled=True)  13.6 us
    ppermute x1, waiting for transfers between devices, slab_shards(): low_edge = lax.ppermute(edges[1], axes, geo.shifts(2))  4.92 us
    ppermute x1, starting transfers between devices, slab_shards(): low = lax.ppermute(own, axes, geo.shifts(1))  4.57 us
    ppermute x1, starting transfers between devices, slab_shards(): low_state = lax.ppermute(state, axes, geo.shifts(1))  4.56 us
    all_to_all x1, starting transfers between devices, slab_shards(): early = lax.all_to_all(early, axes, 0, 0, tiled=True)  4.29 us
    all_to_all x1, starting transfers between devices, slab_shards(): late = lax.all_to_all(late, axes, 0, 0, tiled=True)  4.19 us
  transfers between devices with their start and end apart: 8, of which 5 were waited for; matrix products, arithmetic and copies ran while one was open for 0% of the time, Pallas kernels for 8%

profile of v11, /device:TPU:0, one launch (start us, length us, event | category | flops | bytes accessed | tf_op | source)
XLA Modules:
  0.0 89.0 jit_solution(13845580490100881823)
XLA Ops:
  0.6 2.1 %shard_map.76 = f32[8,96,128]{2,1,0:T(8,128)} custom-call(f32[8,16,128]{2,1,0:T(8,128)} %heat_in.1, f32[3,8,16,128]{3,2,1,0:T(8,128)} %flow_in.1, f32[8,16,128]{2,1,0:T(8,128)} %dual_in.1, s32[8,16,128]{2,1,0:T(8,128)} %kind_in.1), custom_call_target="tpu_custom_call" | custom-call | flops 2000000 | bytes 2000000 | tf_op jit(solution)/shard_map/pallas_call | solution.py:864
  2.7 19.4 %all_to_all.32.own = f32[8,96,128]{2,1,0:T(8,128)S(1)} all-to-all(f32[8,96,128]{2,1,0:T(8,128)} %shard_map.76), channel_id=1, replica_groups=mesh['gx'=4,'gy'=2,'gz'=4] {'gx','gy'}, dimensions={0} | all-to-all | bytes 786432 | tf_op jit(solution)/shard_map/all_to_all | solution.py:886
  22.1 1.3 %collective-permute-start.1 = (f32[8,96,128]{2,1,0:T(8,128)S(1)}, f32[8,96,128]{2,1,0:T(8,128)S(1)}, u32[]{:S(2)}, u32[]{:S(2)}) collective-permute-start(f32[8,96,128]{2,1,0:T(8,128)S(1)} %all_to_all.32.own), channel_id=1, source_target_pairs={{8,0},{16,8},{24,16},{28,24},{20,28},{12,20},{4,12},{1,4},{9,1},{1... | collective-permute-start | bytes 1179656 | tf_op jit(solution)/shard_map/ppermute | solution.py:889
  23.4 4.6 %collective-permute-start = (f32[8,96,128]{2,1,0:T(8,128)S(1)}, f32[8,96,128]{2,1,0:T(8,128)S(1)}, u32[]{:S(2)}, u32[]{:S(2)}) collective-permute-start(f32[8,96,128]{2,1,0:T(8,128)S(1)} %all_to_all.32.own), channel_id=1, source_target_pairs={{0,8},{8,16},{16,24},{24,28},{28,20},{20,12},{12,4},{4,1},{1,9},{9... | collective-permute-start | bytes 1179656 | tf_op jit(solution)/shard_map/ppermute | solution.py:888
  28.0 0.0 copy-start
  28.0 2.8 %collective-permute-start.2 = (f32[8,8,128]{2,1,0:T(8,128)S(1)}, f32[8,8,128]{2,1,0:T(8,128)S(1)}, u32[]{:S(2)}, u32[]{:S(2)}) collective-permute-start(f32[8,8,128]{2,1,0:T(8,128)S(1)} %get-tuple-element.23), channel_id=1, source_target_pairs={{0,16},{8,24},{16,28},{24,20},{28,12},{20,4},{12,1},{4,9},{1,17},{... | collective-permute-start | bytes 98312 | tf_op jit(solution)/shard_map/ppermute | solution.py:892
  30.8 1.3 %collective-permute-start.3 = (f32[8,8,128]{2,1,0:T(8,128)S(1)}, f32[8,8,128]{2,1,0:T(8,128)S(1)}, u32[]{:S(2)}, u32[]{:S(2)}) collective-permute-start(f32[8,8,128]{2,1,0:T(8,128)S(1)} %get-tuple-element.24), channel_id=1, source_target_pairs={{16,0},{24,8},{28,16},{20,24},{12,28},{4,20},{1,12},{9,4},{17,1},{... | collective-permute-start | bytes 98312 | tf_op jit(solution)/shard_map/ppermute | solution.py:891
  32.1 4.9 %collective-permute-done.2.low_edge = f32[8,8,128]{2,1,0:T(8,128)S(1)} collective-permute-done((f32[8,8,128]{2,1,0:T(8,128)S(1)}, f32[8,8,128]{2,1,0:T(8,128)S(1)}, u32[]{:S(2)}, u32[]{:S(2)}) %collective-permute-start.2) | collective-permute-done | bytes 32800 | tf_op jit(solution)/shard_map/ppermute | solution.py:892
  37.0 0.5 collective-permute-done.3.high_edge
  37.5 0.0 collective-permute-done.1.high
  37.5 0.0 collective-permute-done.low
  37.5 0.0 copy-done
  37.5 5.8 %shard_map.78 = (f32[8,48,128]{2,1,0:T(8,128)S(1)}, f32[8,48,128]{2,1,0:T(8,128)S(1)}, f32[8,48,128]{2,1,0:T(8,128)S(1)}, f32[8,64,128]{2,1,0:T(8,128)S(1)}, f32...) custom-call(f32[8]{0:T(128)S(1)} %copy-done, ...), custom_call_target="tpu_custom_call" | custom-call | flops 60000000 | bytes 60000000 | tf_op jit(solution)/shard_map/pallas_call | solution.py:864
  43.3 4.3 %all-to-all-start.1 = ((f32[32,1,128]{2,1,0:T(1,128)}), f32[32,1,128]{2,1,0:T(1,128)S(1)}, u32[]{:S(2)}, u32[]{:S(2)}) async-start(f32[32,1,128]{2,1,0:T(1,128)} %bitcast.1), calls=%async_computation.1 | async-start | bytes 32768 | tf_op jit(solution)/shard_map/all_to_all | solution.py:919
  47.6 5.3 %shard_map.79 = (f32[4,8,16,128]{3,2,1,0:T(8,128)S(1)}, f32[4,8,32,128]{3,2,1,0:T(8,128)S(1)}, f32[32,128]{1,0:T(8,128)}) custom-call(f32[8,48,128]{2,1,0:T(8,128)S(1)} %get-tuple-element.25.refs_0_, f32[8,48,128]{2,1,0:T(8,128)S(1)} %get-tuple-element.26.refs_1_, f32[8,48,128]{2,1,0:T(8,128)S(1)} %get-tuple-element.27.refs_2_, ...), custom_call_target="tpu_custom_call" | custom-call | flops 40000000 | bytes 40000000 | tf_op jit(solution)/shard_map/pallas_call | solution.py:864
  52.8 1.8 %all-to-all-done.1 = f32[32,1,128]{2,1,0:T(1,128)S(1)} async-done(((f32[32,1,128]{2,1,0:T(1,128)}), f32[32,1,128]{2,1,0:T(1,128)S(1)}, u32[]{:S(2)}, u32[]{:S(2)}) %all-to-all-start.1) | async-done | bytes 16416 | tf_op jit(solution)/shard_map/all_to_all | solution.py:919
  54.7 0.1 shard_map.80.refs_12_
  54.8 1.3 %collective-permute-start.5 = (f32[4,8,16,128]{3,2,1,0:T(8,128)S(1)}, f32[4,8,16,128]{3,2,1,0:T(8,128)S(1)}, u32[]{:S(2)}, u32[]{:S(2)}) collective-permute-start(f32[4,8,16,128]{3,2,1,0:T(8,128)S(1)} %shard_map.80.refs_12_), channel_id=1, source_target_pairs={{8,0},{16,8},{24,16},{28,24},{20,28},{12,20},{4,12},{1,4},{9,1},{1... | collective-permute-start | bytes 786440 | tf_op jit(solution)/shard_map/ppermute | solution.py:933
  56.1 4.6 %collective-permute-start.4 = (f32[4,8,16,128]{3,2,1,0:T(8,128)S(1)}, f32[4,8,16,128]{3,2,1,0:T(8,128)S(1)}, u32[]{:S(2)}, u32[]{:S(2)}) collective-permute-start(f32[4,8,16,128]{3,2,1,0:T(8,128)S(1)} %shard_map.80.refs_12_), channel_id=1, source_target_pairs={{0,8},{8,16},{16,24},{24,28},{28,20},{20,12},{12,4},{4,1},{1,9},{9... | collective-permute-start | bytes 786440 | tf_op jit(solution)/shard_map/ppermute | solution.py:932
  60.6 4.2 %all-to-all-start.2 = ((f32[32,1,128]{2,1,0:T(1,128)}), f32[32,1,128]{2,1,0:T(1,128)S(1)}, u32[]{:S(2)}, u32[]{:S(2)}) async-start(f32[32,1,128]{2,1,0:T(1,128)} %bitcast.4), calls=%async_computation.2 | async-start | bytes 32768 | tf_op jit(solution)/shard_map/all_to_all | solution.py:928
  64.8 0.0 collective-permute-done.5.refs_14_
  64.8 1.2 %collective-permute-done.4.refs_13_ = f32[4,8,16,128]{3,2,1,0:T(8,128)S(1)} collective-permute-done((f32[4,8,16,128]{3,2,1,0:T(8,128)S(1)}, f32[4,8,16,128]{3,2,1,0:T(8,128)S(1)}, u32[]{:S(2)}, u32[]{:S(2)}) %collective-permute-start.4) | collective-permute-done | bytes 262176 | tf_op jit(solution)/shard_map/ppermute | solution.py:932
  66.1 1.7 %shard_map.81.refs_12_ = f32[4,8,32,128]{3,2,1,0:T(8,128)S(1)} custom-call(f32[8,48,128]{2,1,0:T(8,128)S(1)} %get-tuple-element.25.refs_0_, f32[8,48,128]{2,1,0:T(8,128)S(1)} %get-tuple-element.26.refs_1_, f32[8,48,128]{2,1,0:T(8,128)S(1)} %get-tuple-element.27.refs_2_, f32[8,64,128]{2,1,0:T(8,128)S(1)} %get-tuple-element.28.refs_3_, ...), custom_call_target="tpu_custom_call" | custom-call | flops 30000000 | bytes 30000000 | tf_op jit(solution)/shard_map/pallas_call | solution.py:864
  67.8 3.9 %all-to-all-done.2 = f32[32,1,128]{2,1,0:T(1,128)S(1)} async-done(((f32[32,1,128]{2,1,0:T(1,128)}), f32[32,1,128]{2,1,0:T(1,128)S(1)}, u32[]{:S(2)}, u32[]{:S(2)}) %all-to-all-start.2) | async-done | bytes 16416 | tf_op jit(solution)/shard_map/all_to_all | solution.py:928
  71.7 2.8 %shard_map.82 = f32[8,80,128]{2,1,0:T(8,128)S(1)} custom-call(f32[8,48,128]{2,1,0:T(8,128)S(1)} %get-tuple-element.25.refs_0_, f32[8,48,128]{2,1,0:T(8,128)S(1)} %get-tuple-element.26.refs_1_, f32[8,48,128]{2,1,0:T(8,128)S(1)} %get-tuple-element.27.refs_2_, f32[8,64,128]{2,1,0:T(8,128)S(1)} %get-tuple-element.28.refs_3_, ...), custom_call_target="tpu_custom_call" | custom-call | flops 20000000 | bytes 20000000 | tf_op jit(solution)/shard_map/pallas_call | solution.py:864
  74.5 13.6 %all_to_all.33.chunks = f32[8,80,128]{2,1,0:T(8,128)S(1)} all-to-all(f32[8,80,128]{2,1,0:T(8,128)S(1)} %shard_map.82), channel_id=1, replica_groups=mesh['gx'=4,'gy'=2,'gz'=4] {'gx','gy'}, dimensions={0} | all-to-all | bytes 655360 | tf_op jit(solution)/shard_map/all_to_all | solution.py:956
  88.1 0.9 shard_map.83
  (1 shorter events, 0.0 us)
Async XLA Ops:
  22.1 15.4 %collective-permute-start.1 = (f32[8,96,128]{2,1,0:T(8,128)S(1)}, f32[8,96,128]{2,1,0:T(8,128)S(1)}, u32[]{:S(2)}, u32[]{:S(2)}) collective-permute-start(f32[8,96,128]{2,1,0:T(8,128)S(1)} %all_to_all.32.own), channel_id=1, source_target_pairs={{8,0},{16,8},{24,16},{28,24},{20,28},{12,20},{4,12},{1,4},{9,1},{1... | collective-permute-start | bytes 1179656 | tf_op jit(solution)/shard_map/ppermute | solution.py:889
  23.4 14.1 %collective-permute-start = (f32[8,96,128]{2,1,0:T(8,128)S(1)}, f32[8,96,128]{2,1,0:T(8,128)S(1)}, u32[]{:S(2)}, u32[]{:S(2)}) collective-permute-start(f32[8,96,128]{2,1,0:T(8,128)S(1)} %all_to_all.32.own), channel_id=1, source_target_pairs={{0,8},{8,16},{16,24},{24,28},{28,20},{20,12},{12,4},{4,1},{1,9},{9... | collective-permute-start | bytes 1179656 | tf_op jit(solution)/shard_map/ppermute | solution.py:888
  28.0 9.5 %copy-start = (f32[8]{0:T(128)S(1)}, f32[8]{0:T(128)}, u32[]{:S(2)}) copy-start(f32[8]{0:T(128)} %stiffness.1) | copy-start | bytes 100
  28.0 9.0 %collective-permute-start.2 = (f32[8,8,128]{2,1,0:T(8,128)S(1)}, f32[8,8,128]{2,1,0:T(8,128)S(1)}, u32[]{:S(2)}, u32[]{:S(2)}) collective-permute-start(f32[8,8,128]{2,1,0:T(8,128)S(1)} %get-tuple-element.23), channel_id=1, source_target_pairs={{0,16},{8,24},{16,28},{24,20},{28,12},{20,4},{12,1},{4,9},{1,17},{... | collective-permute-start | bytes 98312 | tf_op jit(solution)/shard_map/ppermute | solution.py:892
  30.8 6.7 %collective-permute-start.3 = (f32[8,8,128]{2,1,0:T(8,128)S(1)}, f32[8,8,128]{2,1,0:T(8,128)S(1)}, u32[]{:S(2)}, u32[]{:S(2)}) collective-permute-start(f32[8,8,128]{2,1,0:T(8,128)S(1)} %get-tuple-element.24), channel_id=1, source_target_pairs={{16,0},{24,8},{28,16},{20,24},{12,28},{4,20},{1,12},{9,4},{17,1},{... | collective-permute-start | bytes 98312 | tf_op jit(solution)/shard_map/ppermute | solution.py:891
  43.3 11.4 %all-to-all-start.1 = ((f32[32,1,128]{2,1,0:T(1,128)}), f32[32,1,128]{2,1,0:T(1,128)S(1)}, u32[]{:S(2)}, u32[]{:S(2)}) async-start(f32[32,1,128]{2,1,0:T(1,128)} %bitcast.1), calls=%async_computation.1 | async-start | bytes 32768 | tf_op jit(solution)/shard_map/all_to_all | solution.py:919
  54.8 10.1 %collective-permute-start.5 = (f32[4,8,16,128]{3,2,1,0:T(8,128)S(1)}, f32[4,8,16,128]{3,2,1,0:T(8,128)S(1)}, u32[]{:S(2)}, u32[]{:S(2)}) collective-permute-start(f32[4,8,16,128]{3,2,1,0:T(8,128)S(1)} %shard_map.80.refs_12_), channel_id=1, source_target_pairs={{8,0},{16,8},{24,16},{28,24},{20,28},{12,20},{4,12},{1,4},{9,1},{1... | collective-permute-start | bytes 786440 | tf_op jit(solution)/shard_map/ppermute | solution.py:933
  56.1 10.0 %collective-permute-start.4 = (f32[4,8,16,128]{3,2,1,0:T(8,128)S(1)}, f32[4,8,16,128]{3,2,1,0:T(8,128)S(1)}, u32[]{:S(2)}, u32[]{:S(2)}) collective-permute-start(f32[4,8,16,128]{3,2,1,0:T(8,128)S(1)} %shard_map.80.refs_12_), channel_id=1, source_target_pairs={{0,8},{8,16},{16,24},{24,28},{28,20},{20,12},{12,4},{4,1},{1,9},{9... | collective-permute-start | bytes 786440 | tf_op jit(solution)/shard_map/ppermute | solution.py:932
  60.6 11.1 %all-to-all-start.2 = ((f32[32,1,128]{2,1,0:T(1,128)}), f32[32,1,128]{2,1,0:T(1,128)S(1)}, u32[]{:S(2)}, u32[]{:S(2)}) async-start(f32[32,1,128]{2,1,0:T(1,128)} %bitcast.4), calls=%async_computation.2 | async-start | bytes 32768 | tf_op jit(solution)/shard_map/all_to_all | solution.py:928

commit v12 on v11

--- a/solution.py
+++ b/solution.py
@@ -355,7 +355,7 @@
         self.y = self.lane % self.span
         self.kept, self.latest, self.sweep = {}, None, 0
 
-    def sliding(self, ref, z, lead, t):
+    def sliding(self, ref, z, lead, t, shift=0):
         if self.latest != (self.sweep, z):
             self.latest, self.kept = (self.sweep, z), {}
         where = (id(ref), lead)
@@ -365,7 +365,7 @@
         def load(j):
             key = (*where, j)
             if key not in self.kept:
-                self.kept[key] = (ref, get(ref, z, *lead, j))
+                self.kept[key] = (ref, get(ref, z - shift, *lead, j))
             return self.kept[key][1]
 
         return load
@@ -390,10 +390,11 @@
             return load(t + step)
         return self.lanes(load(t - step), step)
 
-    def beside(self, ref, z, lead, t):
-        load = self.sliding(ref, z, lead, t)
+    def beside(self, ref, z, lead, t, shift=0):
+        load = self.sliding(ref, z, lead, t, shift)
         near = [self.x(load, t, 1), self.x(load, t, -1)]
         near += [self.y_side(load, t, 1), self.y_side(load, t, -1)]
+        z = z - shift
         return load(t), near + [get(ref, z + 1, *lead, t), get(ref, z - 1, *lead, t)]
 
     def coarse_beside(self, ref, z, lead, t):
@@ -466,26 +467,32 @@
             out[q] = jnp.concatenate(rows, 0)
 
 
-STATIC_FINE = ("s0", "s1", "s2", "hv", "w")
-STATIC_COARSE = ("kxp", "kxm", "kyp", "kym", "kzp", "kzm", "wc")
+STATIC_FINE = ("s0", "s1", "s2", "w", "hv")
+STATIC_COARSE = ("wc", "vh")
 STATIC = STATIC_FINE + STATIC_COARSE
+CUT = {name: SUB // 2 if name in ("hv", "vh") else SUB for name in STATIC}
 
 
 class Static:
     def __init__(self, refs):
         self.refs = dict(zip(STATIC, refs))
 
-    def base(self, name):
-        return 0 if name == "hv" else SUB
-
     def get(self, name, z, *index):
-        return get(self.refs[name], z - self.base(name), *index)
+        return get(self.refs[name], z - CUT[name], *index)
 
     def put(self, put, name, value, z, *index):
-        put(self.refs[name], value, z - self.base(name), *index)
-
-
-def iterate(geo, st, work, seqs, lo, hi, first=(), mean=None):
+        put(self.refs[name], value, z - CUT[name], *index)
+
+    def faces(self, tl, z, t):
+        h, near = tl.beside(self.refs["hv"], z, (), t, CUT["hv"])
+        return [h + other for other in near]
+
+    def coarse_faces(self, tl, z, pair):
+        h, near = tl.coarse_beside(self.refs["vh"], z - CUT["vh"], (), pair)
+        return [h + other for other in near]
+
+
+def iterate(geo, st, work, seqs, lo, hi, first=()):
     v, p, res, cor, cor2, cc0, cc1 = work
     tl = Tiles(geo)
     keep = 1.0 - JACOBI_WEIGHT
@@ -493,8 +500,7 @@
     transposed = len(seqs)
 
     def faces(t, z):
-        h, near = tl.beside(st.refs["hv"], z, (), t)
-        return [h + other for other in near]
+        return st.faces(tl, z, t)
 
     def around(face, ref, c, t, z):
         f, near = tl.beside(ref, z, (c,), t)
@@ -503,25 +509,26 @@
     def residual(z, put):
         for t in range(SUB):
             w = st.get("w", z, t)
-            if FORWARD in seqs and FORWARD not in first:
+            if any(q != ADJOINT and q not in first for q in seqs):
                 face = faces(t, z)
                 diag = tree(face)
             for s, q in enumerate(seqs):
-                start = q == FORWARD and q in first
-                if not start:
+                if not (q == FORWARD and q in first):
                     _, near = tl.beside(p, z, (transposed if q == ADJOINT else s,), t)
                     slope = [0.5 * (near[2 * k] - near[2 * k + 1]) for k in range(3)]
                 for k in range(3):
                     c = 3 * s + k
-                    if q == FORWARD:
-                        value = st.get("s%d" % k, z, t)
-                        if not start:
+                    if q == ADJOINT:
+                        value = slope[k] if q in first else get(cor, z, c, t) + slope[k]
+                    else:
+                        if q == FORWARD:
+                            value = st.get("s%d" % k, z, t)
+                            value = value if q in first else value - slope[k]
+                        else:
+                            value = -slope[k]
+                        if q not in first:
                             f, total = around(face, v, c, t, z)
-                            value = value - slope[k] - (diag * f - total)
-                    elif q == RESPONSE:
-                        value = -slope[k]
-                    else:
-                        value = slope[k] if q in first else get(cor, z, c, t) + slope[k]
+                            value = value - (diag * f - total)
                     put(res, value, z, c, t)
                     put(cor, w * value, z, c, t)
 
@@ -541,22 +548,24 @@
 
     sweep(tl, lo - 8, hi + 8, restricted)
 
-    def coarse_step(ref, c, pair, z):
+    def coarse_step(face, wc, ref, c, pair, z):
         f, near = tl.coarse_beside(ref, z, (c,), pair)
-        terms = [st.get(name, z, pair) * b for name, b in zip(STATIC_COARSE, near)]
-        return tree([get(cc0, z, c, pair), keep * f] + terms)
+        total = tree([a * b for a, b in zip(face, near)])
+        return get(cc0, z, c, pair) + keep * f + wc * total
 
     def sweep_one(z, put):
         for pair in range(TX // 2):
+            face, wc = st.coarse_faces(tl, z, pair), st.get("wc", z, pair)
             for c in comps:
-                put(cc1, coarse_step(cc0, c, pair, z), z, c, pair)
+                put(cc1, coarse_step(face, wc, cc0, c, pair, z), z, c, pair)
 
     sweep(tl, lo - 4, hi + 4, sweep_one)
 
     def sweep_two(z, put):
         for pair in range(TX // 2):
+            face, wc = st.coarse_faces(tl, z, pair), st.get("wc", z, pair)
             for c in comps:
-                value = coarse_step(cc1, c, pair, z)
+                value = coarse_step(face, wc, cc1, c, pair, z)
                 for t in block_of(pair):
                     put(cor2, get(cor, z, c, t) + value, z, c, t)
 
@@ -568,7 +577,7 @@
             for c in comps:
                 f, total = around(face, cor2, c, t, z)
                 value = get(cor, z, c, t) + keep * f + w * total
-                if seqs[c // 3] == FORWARD and FORWARD not in first:
+                if seqs[c // 3] != ADJOINT and seqs[c // 3] not in first:
                     value = get(v, z, c, t) + value
                 put(v, value, z, c, t)
 
@@ -598,8 +607,6 @@
                 value = -(half * (0.5 * div))
                 if not (q == FORWARD and q in first):
                     value = get(p, z, s, t) + value
-                if mean is not None:
-                    value = value - jnp.where(geo.inside(z), mean, 0.0)
                 put(p, value, z, s, t)
 
     sweep(tl, lo, hi, pressure)
@@ -626,26 +633,22 @@
 
 def setup_kernel(geo, stiffness, own, low, high, low_edge, high_edge, *refs):
     st = Static(refs)
-    moved, dual_out, sums, raw, heat, vc, *work = refs[len(STATIC) :]
+    moved, response, down, up, sums, raw, heat, vc, one, *work = refs[len(STATIC) :]
     v, p, res, cor, cor2, cc0, cc1 = work
     tl = Tiles(geo)
     b, m, n_rows = geo.slab, geo.margin, geo.rows
     granule = geo.block[1]
 
-    def place(t, _):
+    for f in range(FIELDS):
         groups = []
         for source, base in ((low, m - b), (own, m), (high, m + b)):
             for u in range(0, b, SUB):
-                row = pl.multiple_of(t * b, b) + u
-                tiles = [source[q, pl.ds(row, SUB), :] for q in range(geo.group)]
+                row = f * b + u
+                tiles = [source[q, row : row + SUB, :] for q in range(geo.group)]
                 groups.append((base + u, tiles))
-        groups = [(row, gather_tiles(tiles, granule)) for row, tiles in groups]
         for row, tiles in groups:
-            for x, tile in enumerate(tiles):
-                raw[t, x, row : row + SUB, :] = tile
-        return 0
-
-    lax.fori_loop(0, FIELDS, place, 0)
+            for x, tile in enumerate(gather_tiles(tiles, granule)):
+                raw[f, x, row : row + SUB, :] = tile
     for source, base in ((low_edge, m - b - EDGE), (high_edge, m + 2 * b)):
         tiles = [source[q] for q in range(geo.group)]
         for x, tile in enumerate(gather_tiles(tiles, granule)):
@@ -691,8 +694,7 @@
     def statics(z, put):
         inside = geo.inside(z)
         for t in range(SUB):
-            h, near = tl.beside(st.refs["hv"], z, (), t)
-            diag = tree([h + other for other in near])
+            diag = tree(st.faces(tl, z, t))
             st.put(put, "w", jnp.where(inside, JACOBI_WEIGHT / diag, 0.0), z, t)
             f, near = tl.beside(heat, z, (1,), t)
             dual = -INCREMENT_DT * get(raw, z, 4, t)
@@ -708,10 +710,8 @@
         for pair in range(TX // 2):
             c, near = tl.coarse_beside(vc, z, (), pair)
             face = [0.25 * (0.5 * (c + o)) for o in near]
-            wc = jnp.where(inside, JACOBI_WEIGHT / tree(face), 0.0)
-            for name, f in zip(STATIC_COARSE, face):
-                st.put(put, name, wc * f, z, pair)
-            st.put(put, "wc", wc, z, pair)
+            st.put(put, "wc", jnp.where(inside, JACOBI_WEIGHT / tree(face), 0.0), z, pair)
+            st.put(put, "vh", 0.125 * c, z, pair)
 
     sweep(tl, m - b, m + 2 * b, coarse_statics)
 
@@ -733,109 +733,89 @@
     def unit(z, put):
         value = jnp.where(geo.inside(z), 1.0, 0.0)
         for t in range(SUB):
-            put(p, value, z, 0, t)
-            put(p, st.get("hv", z, t), z, 1, t)
-
-    sweep(tl, 0, n_rows, unit)
-
-    mine, rows = slice(m, m + b), slice(m - PHASE, m + b + PHASE)
-    iterate(geo, st, work, (ADJOINT,), rows.start, rows.stop, (ADJOINT,))
-    for k in range(4):
-        dual_out[k] = cor[k, :, rows, :] if k < 3 else p[0, :, rows, :]
-    sums_of = [(0, source_product(geo, st, v, 0)), (1, whole_sum(p[0, :, mine, :]))]
+            put(p, value, z, 1, t)
+            put(p, value, z, 2, t)
+            put(p, st.get("hv", z, t), z, 3, t)
+
+    sweep(tl, m - b, m + 2 * b, unit)
+
+    mine = slice(m, m + b)
+
+    def fields(s, three=v):
+        return [three.at[3 * s + k, :, mine, :] for k in range(3)] + [p.at[s, :, mine, :]]
+
+    every = (FORWARD, ADJOINT, RESPONSE)
+    iterate(geo, st, work, every, m - PHASE, m + b + PHASE, every)
+    for k, (a, r) in enumerate(zip(fields(1, cor), fields(2))):
+        one[k] = a[...]
+        response[k] = r[...]
+    sums_of = [(0, source_product(geo, st, v, 3)), (1, whole_sum(one[3]))]
+    iterate(geo, st, work, every, m, m + b)
+    near, far, turn = [one.at[k] for k in range(4)], fields(1, cor), [response.at[k] for k in range(4)]
+    sums_of += [(2, source_product(geo, st, v, 3)), (3, whole_sum(p[1, :, mine, :]))]
+    sums_of += [(4, product(near, fields(0))), (5, product(far, fields(0))), (6, product(far, turn))]
     sums[...] = in_lanes(sums_of, sums.shape[0])
+    for k, (x, r) in enumerate(zip(fields(0), fields(2))):
+        state, turned = x[...], r[...]
+        for out, part in ((down, turned[:, :PHASE]), (up, turned[:, b - PHASE :])):
+            out[:, k * b : (k + 1) * b, :] = state
+            out[:, 4 * b + k * PHASE : 4 * b + (k + 1) * PHASE, :] = part
 
 
 def source_product(geo, st, v, first):
     mine = slice(geo.margin, geo.margin + geo.slab)
-    held = slice(geo.margin - SUB, geo.margin - SUB + geo.slab)
+    held = slice(geo.margin - CUT["s0"], geo.margin - CUT["s0"] + geo.slab)
     left = [st.refs["s%d" % k].at[:, held, :] for k in range(3)]
     return product(left, [v.at[first + k, :, mine, :] for k in range(3)])
 
 
-def first_kernel(geo, *refs):
+def second_kernel(geo, *refs):
     st = Static(refs)
-    dual, state, response, sums, later, *work = refs[len(STATIC) :]
-    v, p, res, cor = work[:4]
-    b, m = geo.slab, geo.margin
-    mine, rows = slice(m, m + b), slice(m - PHASE, m + b + PHASE)
-    tl = Tiles(geo)
-
-    def unit(z, put):
-        value = jnp.where(geo.inside(z), 1.0, 0.0)
-        for t in range(SUB):
-            put(p, value, z, 1, t)
-
-    sweep(tl, 0, geo.rows, unit)
-    both = (FORWARD, RESPONSE)
-    iterate(geo, st, work, both, rows.start, rows.stop, both)
-    for k in range(4):
-        response[k] = v[3 + k, :, rows, :] if k < 3 else p[1, :, rows, :]
-    for k in range(3):
-        cor[3 + k, :, rows, :] = dual[k]
-    p[1, :, rows, :] = dual[3]
-    p[2, :, rows, :] = st.refs["hv"][:, rows, :] * dual[3]
-    iterate(geo, st, work, (FORWARD, ADJOINT), m, m + b)
-    for k in range(4):
-        state[k] = v[k, :, mine, :] if k < 3 else p[0, :, mine, :]
-        later[k] = cor[3 + k, :, mine, :] if k < 3 else p[1, :, mine, :]
-    own = slice(PHASE, PHASE + b)
-    near, far = [dual.at[k, :, own, :] for k in range(4)], [later.at[k] for k in range(4)]
-    fields, turn = [state.at[k] for k in range(4)], [response.at[k, :, own, :] for k in range(4)]
-    sums_of = [(2, source_product(geo, st, v, 3)), (3, whole_sum(p[1, :, mine, :]))]
-    sums_of += [(4, product(near, fields)), (5, product(far, fields)), (6, product(far, turn))]
-    sums[...] = in_lanes(sums_of, sums.shape[0])
-
-
-def second_kernel(geo, raw, response, early, state):
-    own = slice(PHASE, PHASE + geo.slab)
-    m1 = jnp.sum(early[...], axis=0, keepdims=True)[:, 0:1] / geo.cells
-    for k in range(4):
-        state[k] = raw[k] - m1 * response[k, :, own, :]
-
-
-def means(geo, early, late):
-    row = jnp.sum(early + late, axis=0, keepdims=True) / geo.cells
-    c1, l1, c2, l2, l1_x2, l2_x2, l2_r1 = [row[:, k : k + 1] for k in range(7)]
-    m2 = c1 + c2 - c1 * l1
-    m3 = c1 + (l1_x2 - c1 * l2) - m2 * l1
-    m4 = c1 + c2 + (l2_x2 - c1 * l2_r1) - m2 * l2 - m3 * l1
-    return m2, m3, m4
-
-
-def third_kernel(geo, *refs):
-    st = Static(refs)
-    own, low, high, out, *work = refs[len(STATIC) :]
+    down, up, low, high, final, *work = refs[len(STATIC) :]
     v, p = work[:2]
     b, m = geo.slab, geo.margin
-    for source, base in ((low, m - b), (own, m), (high, m + b)):
-        for k in range(3):
-            v[k, :, base : base + b, :] = source[k]
-        p[0, :, base : base + b, :] = source[3]
-    rows = slice(m - PHASE, m + b + PHASE)
-    iterate(geo, st, work, (FORWARD,), rows.start, rows.stop)
     for k in range(4):
-        out[k] = v[k, :, rows, :] if k < 3 else p[0, :, rows, :]
-
-
-def fourth_kernel(geo, *refs):
-    st = Static(refs)
-    state, response, early, late, moved, out, *work = refs[len(STATIC) :]
-    v, p = work[:2]
-    b, m = geo.slab, geo.margin
-    m2, m3, m4 = means(geo, early[...], late[...])
-    rows = slice(m - PHASE, m + b + PHASE)
-    for k in range(3):
-        v[k, :, rows, :] = state[k] - m2 * response[k]
-    shift = jnp.where(geo.inside(rows.start, rows.stop - rows.start), m3, 0.0)
-    p[0, :, rows, :] = state[3] - m2 * response[3] - shift[None]
-    iterate(geo, st, work, (FORWARD,), m, m + b, mean=m4)
+        rows, part = slice(k * b, (k + 1) * b), slice(4 * b + k * PHASE, 4 * b + (k + 1) * PHASE)
+        state, turned = (v.at[k], v.at[3 + k]) if k < 3 else (p.at[0], p.at[1])
+        for source, base in ((low, m - b), (down, m), (high, m + b)):
+            state[:, base : base + b, :] = source[:, rows, :]
+        for source, base in ((low, m - PHASE), (down, m), (up, m + b - PHASE), (high, m + b)):
+            turned[:, base : base + PHASE, :] = source[:, part, :]
+    iterate(geo, st, work, (FORWARD,), m - PHASE, m + b + PHASE)
+    iterate(geo, st, work, (FORWARD, RESPONSE), m, m + b)
+    mine = slice(m, m + b)
+    for s in range(2):
+        for k in range(4):
+            final[4 * s + k] = v[3 * s + k, :, mine, :] if k < 3 else p[s, :, mine, :]
+
+
+def means(geo, sums):
+    row = jnp.sum(sums, axis=0, keepdims=True) / geo.cells
+    c1, l1, c2, l2, l1_x2, l2_x2, l2_r1 = [row[:, k : k + 1] for k in range(7)]
+    m1 = c1
+    m2 = c1 + c2 - m1 * l1
+    m3 = c1 + (l1_x2 - m1 * l2) - m2 * l1
+    m4 = c1 + c2 + (l2_x2 - m1 * l2_r1) - m2 * l2 - m3 * l1
+    return m1, m2, m3, m4
+
+
+def combine_kernel(geo, sums, final, down, up, response, moved, out):
+    b = geo.slab
+    means_of = [jnp.broadcast_to(value, (SUB, LANES)) for value in means(geo, sums[...])]
+    m1, m2, m3, m4 = means_of
     for u in range(0, b, SUB):
-        at = slice(m + u, m + u + SUB)
-        columns = range(SUB)
-        fields = [[v[k, x, at, :] for x in columns] for k in range(3)]
-        fields.append([p[0, x, at, :] for x in columns])
-        fields.append([moved[x, u : u + SUB, :] + fields[2][x] for x in columns])
+        rows = slice(u, u + SUB)
+        fields = []
+        for k in range(4):
+            turned = down if u < PHASE else up
+            at = 4 * b + k * PHASE + (u if u < PHASE else u - (b - PHASE))
+            tiles = []
+            for t in range(SUB):
+                value = final[k, t, rows, :] - m1 * final[4 + k, t, rows, :]
+                value = value - m2 * turned[t, at : at + SUB, :] - m3 * response[k, t, rows, :]
+                tiles.append(value - m4 if k == 3 else value)
+            fields.append(tiles)
+        fields.append([moved[t, rows, :] + fields[2][t] for t in range(SUB)])
         for f, tiles in enumerate(fields):
             for q, tile in enumerate(scatter_tiles(tiles, geo.block[1])):
                 out[q, f * b + u : f * b + u + SUB, :] = tile
@@ -892,9 +872,10 @@
     low_edge = lax.ppermute(edges[1], axes, geo.shifts(2))
 
     fine, coarse = (SUB, geo.rows, LANES), (TX // 2, geo.rows, LANES)
-    held = geo.rows - 2 * SUB
-    static_shapes = [(SUB, geo.rows if name == "hv" else held, LANES) for name in STATIC_FINE]
-    static_shapes += [(TX // 2, held, LANES)] * len(STATIC_COARSE)
+    static_shapes = [
+        (SUB if name in STATIC_FINE else TX // 2, geo.rows - 2 * CUT[name], LANES)
+        for name in STATIC
+    ]
     slab = (SUB, b, LANES)
 
     def work(n, more=0):
@@ -902,11 +883,11 @@
         return fields + [(3 * n, *coarse)] * 2
 
     devices = group * geo.nz
-    wide = (4, SUB, b + 2 * PHASE, LANES)
-    *static, moved, dual_one, early = call(
+    message = (SUB, 4 * b + 4 * PHASE, LANES)
+    *static, moved, response, down, up, sums = call(
         functools.partial(setup_kernel, geo),
-        static_shapes + [slab, wide, (devices, LANES)],
-        [(FIELDS, *fine), (2, *fine), coarse] + work(1, 1),
+        static_shapes + [slab, (4, *slab), message, message, (devices, LANES)],
+        [(FIELDS, *fine), (2, *fine), coarse, (4, *slab)] + work(3, 1),
         stiffness,
         own,
         low,
@@ -916,42 +897,30 @@
         smem=(0,),
         megabytes=60,
     )
-    early = lax.all_to_all(early, axes, 0, 0, tiled=True)
-    raw, response, late = call(
-        functools.partial(first_kernel, geo),
-        [(4, *slab), wide, (devices, LANES)],
-        [(4, *slab)] + work(2, 1),
+    from_low = lax.ppermute(up, axes, geo.shifts(1))
+    from_high = lax.ppermute(down, axes, geo.shifts(-1))
+    sums = lax.all_to_all(sums, axes, 0, 0, tiled=True)
+    (final,) = call(
+        functools.partial(second_kernel, geo),
+        [(8, *slab)],
+        work(2),
         *static,
-        dual_one,
-        megabytes=40,
-    )
-    late = lax.all_to_all(late, axes, 0, 0, tiled=True)
-    (state,) = call(
-        functools.partial(second_kernel, geo), [(4, *slab)], [], raw, response, early
-    )
-    low_state = lax.ppermute(state, axes, geo.shifts(1))
-    high_state = lax.ppermute(state, axes, geo.shifts(-1))
-    (state,) = call(
-        functools.partial(third_kernel, geo),
-        [wide],
-        work(1),
-        *static,
-        state,
-        low_state,
-        high_state,
+        down,
+        up,
+        from_low,
+        from_high,
         megabytes=30,
     )
     (chunks,) = call(
-        functools.partial(fourth_kernel, geo),
+        functools.partial(combine_kernel, geo),
         [(group, BACK * b, LANES)],
-        work(1),
-        *static,
-        state,
+        [],
+        sums,
+        final,
+        down,
+        up,
         response,
-        early,
-        late,
         moved,
-        megabytes=20,
     )
     chunks = lax.all_to_all(chunks, ("gx", "gy"), 0, 0, tiled=True)
     return tuple(

time: 89.4 us -> 93.4 us (1.045)
  Pallas kernels: 18.7 us -> 24.9 us
  starting transfers between devices: 24.2 us -> 20.2 us
  blocking collectives: 33 us -> 36.2 us
  waiting for transfers between devices: 12.4 us -> 9.43 us
  local copies, waits for them, and re-layouts: 0.01 us -> 1.42 us
    pallas_call x8 -> x6, Pallas kernels: 18.7 us -> 24.9 us  [call(): pl.pallas_call(kernel, out_shape=[jax.ShapeDtypeStruct(s, f32) for s in o...]
    all_to_all x2 -> x1, waiting for transfers between devices: 5.75 us -> 0.01 us  [slab_shards(): sums = lax.all_to_all(sums, axes, 0, 0, tiled=True)]
    all_to_all x2 -> x1, starting transfers between devices: 8.48 us -> 4.45 us  [slab_shards(): sums = lax.all_to_all(sums, axes, 0, 0, tiled=True)]
    all_to_all x1, blocking collectives: 13.6 us -> 16.8 us  [slab_shards(): chunks = lax.all_to_all(chunks, ('gx', 'gy'), 0, 0, tiled=True)]
    ppermute x2, waiting for transfers between devices: 1.21 us -> 4.01 us  [the longest x1 2.72 us: slab_shards(): from_high = lax.ppermute(down, axes, geo.shifts(-1))]
    unnamed x2 -> x6, local copies, waits for them, and re-layouts: 0.01 us -> 1.42 us
  transfers between devices with their start and end apart: 8 -> 7, of which waited for: 5 -> 4; matrix products, arithmetic and copies ran while one was open for 0% -> 0% of each run, Pallas kernels for 8% -> 4%
where the time goes in v12:
time: 93.4 us; the launch traced here: 92.9 us
  blocking collectives  36.2 us (39%)
  Pallas kernels  24.9 us (27%)
  starting transfers between devices  20.2 us (22%)
  waiting for transfers between devices  9.43 us (10%)
  local copies, waits for them, and re-layouts  1.42 us (2%)
    pallas_call x6, Pallas kernels, call(): pl.pallas_call(kernel, out_shape=[jax.ShapeDtypeStruct(s, f32) for s in o...  24.9 us
    all_to_all x1, blocking collectives, slab_shards(): own = lax.all_to_all(chunks, ('gx', 'gy'), 0, 0, tiled=True)  19.4 us
    all_to_all x1, blocking collectives, slab_shards(): chunks = lax.all_to_all(chunks, ('gx', 'gy'), 0, 0, tiled=True)  16.8 us
    ppermute x1, waiting for transfers between devices, slab_shards(): low_edge = lax.ppermute(edges[1], axes, geo.shifts(2))  4.92 us
    ppermute x1, starting transfers between devices, slab_shards(): low = lax.ppermute(own, axes, geo.shifts(1))  4.57 us
    ppermute x1, starting transfers between devices, slab_shards(): from_low = lax.ppermute(up, axes, geo.shifts(1))  4.57 us
    all_to_all x1, starting transfers between devices, slab_shards(): sums = lax.all_to_all(sums, axes, 0, 0, tiled=True)  4.45 us
    ppermute x1, starting transfers between devices, slab_shards(): low_edge = lax.ppermute(edges[1], axes, geo.shifts(2))  2.75 us
  transfers between devices with their start and end apart: 7, of which 4 were waited for; matrix products, arithmetic and copies ran while one was open for 0% of the time, Pallas kernels for 4%

profile of v12, /device:TPU:0, one launch (start us, length us, event | category | flops | bytes accessed | tf_op | source)
XLA Modules:
  0.0 92.9 jit_solution(3577613723928561804)
XLA Ops:
  0.6 2.1 %shard_map.76 = f32[8,96,128]{2,1,0:T(8,128)} custom-call(f32[8,16,128]{2,1,0:T(8,128)} %heat_in.1, f32[3,8,16,128]{3,2,1,0:T(8,128)} %flow_in.1, f32[8,16,128]{2,1,0:T(8,128)} %dual_in.1, s32[8,16,128]{2,1,0:T(8,128)} %kind_in.1), custom_call_target="tpu_custom_call" | custom-call | flops 2000000 | bytes 2000000 | tf_op jit(solution)/shard_map/pallas_call | solution.py:844
  2.7 19.4 %all_to_all.21.own = f32[8,96,128]{2,1,0:T(8,128)S(1)} all-to-all(f32[8,96,128]{2,1,0:T(8,128)} %shard_map.76), channel_id=1, replica_groups=mesh['gx'=4,'gy'=2,'gz'=4] {'gx','gy'}, dimensions={0} | all-to-all | bytes 786432 | tf_op jit(solution)/shard_map/all_to_all | solution.py:866
  22.1 1.3 %collective-permute-start.1 = (f32[8,96,128]{2,1,0:T(8,128)S(1)}, f32[8,96,128]{2,1,0:T(8,128)S(1)}, u32[]{:S(2)}, u32[]{:S(2)}) collective-permute-start(f32[8,96,128]{2,1,0:T(8,128)S(1)} %all_to_all.21.own), channel_id=1, source_target_pairs={{8,0},{16,8},{24,16},{28,24},{20,28},{12,20},{4,12},{1,4},{9,1},{1... | collective-permute-start | bytes 1179656 | tf_op jit(solution)/shard_map/ppermute | solution.py:869
  23.4 4.6 %collective-permute-start = (f32[8,96,128]{2,1,0:T(8,128)S(1)}, f32[8,96,128]{2,1,0:T(8,128)S(1)}, u32[]{:S(2)}, u32[]{:S(2)}) collective-permute-start(f32[8,96,128]{2,1,0:T(8,128)S(1)} %all_to_all.21.own), channel_id=1, source_target_pairs={{0,8},{8,16},{16,24},{24,28},{28,20},{20,12},{12,4},{4,1},{1,9},{9... | collective-permute-start | bytes 1179656 | tf_op jit(solution)/shard_map/ppermute | solution.py:868
  28.0 0.0 copy-start.2
  28.0 2.8 %collective-permute-start.2 = (f32[8,8,128]{2,1,0:T(8,128)S(1)}, f32[8,8,128]{2,1,0:T(8,128)S(1)}, u32[]{:S(2)}, u32[]{:S(2)}) collective-permute-start(f32[8,8,128]{2,1,0:T(8,128)S(1)} %get-tuple-element.17), channel_id=1, source_target_pairs={{0,16},{8,24},{16,28},{24,20},{28,12},{20,4},{12,1},{4,9},{1,17},{... | collective-permute-start | bytes 98312 | tf_op jit(solution)/shard_map/ppermute | solution.py:872
  30.8 1.3 %collective-permute-start.3 = (f32[8,8,128]{2,1,0:T(8,128)S(1)}, f32[8,8,128]{2,1,0:T(8,128)S(1)}, u32[]{:S(2)}, u32[]{:S(2)}) collective-permute-start(f32[8,8,128]{2,1,0:T(8,128)S(1)} %get-tuple-element.18), channel_id=1, source_target_pairs={{16,0},{24,8},{28,16},{20,24},{12,28},{4,20},{1,12},{9,4},{17,1},{... | collective-permute-start | bytes 98312 | tf_op jit(solution)/shard_map/ppermute | solution.py:871
  32.1 4.9 %collective-permute-done.2.low_edge = f32[8,8,128]{2,1,0:T(8,128)S(1)} collective-permute-done((f32[8,8,128]{2,1,0:T(8,128)S(1)}, f32[8,8,128]{2,1,0:T(8,128)S(1)}, u32[]{:S(2)}, u32[]{:S(2)}) %collective-permute-start.2) | collective-permute-done | bytes 32800 | tf_op jit(solution)/shard_map/ppermute | solution.py:872
  37.0 0.5 collective-permute-done.3.high_edge
  37.5 0.0 collective-permute-done.1.high
  37.5 0.0 collective-permute-done.low
  37.5 0.0 copy-done.2
  37.5 17.2 %shard_map.78 = (f32[8,48,128]{2,1,0:T(8,128)S(1)}, f32[8,48,128]{2,1,0:T(8,128)S(1)}, f32[8,48,128]{2,1,0:T(8,128)S(1)}, f32[8,48,128]{2,1,0:T(8,128)S(1)}, f32...) custom-call(f32[8]{0:T(128)S(1)} %copy-done.2, ...), custom_call_target="tpu_custom_call" | custom-call | flops 60000000 | bytes 60000000 | tf_op jit(solution)/shard_map/pallas_call | solution.py:844
  54.7 0.0 copy-start
  54.7 0.6 copy-done
  55.3 1.3 %collective-permute-start.5 = (f32[8,96,128]{2,1,0:T(8,128)S(1)}, f32[8,96,128]{2,1,0:T(8,128)S(1)}, u32[]{:S(2)}, u32[]{:S(2)}) collective-permute-start(f32[8,96,128]{2,1,0:T(8,128)S(1)} %get-tuple-element.27.refs_7_.down), channel_id=1, source_target_pairs={{8,0},{16,8},{24,16},{28,24},{20,28},{12,20},{4,12},{1,4},{9,1},{1... | collective-permute-start | bytes 1179656 | tf_op jit(solution)/shard_map/ppermute | solution.py:901
  56.6 4.6 %collective-permute-start.4 = (f32[8,96,128]{2,1,0:T(8,128)S(1)}, f32[8,96,128]{2,1,0:T(8,128)S(1)}, u32[]{:S(2)}, u32[]{:S(2)}) collective-permute-start(f32[8,96,128]{2,1,0:T(8,128)S(1)} %get-tuple-element.28.refs_8_.up), channel_id=1, source_target_pairs={{0,8},{8,16},{16,24},{24,28},{28,20},{20,12},{12,4},{4,1},{1,9},{9... | collective-permute-start | bytes 1179656 | tf_op jit(solution)/shard_map/ppermute | solution.py:900
  61.2 4.5 %all-to-all-start.1 = ((f32[32,1,128]{2,1,0:T(1,128)}), f32[32,1,128]{2,1,0:T(1,128)S(1)}, u32[]{:S(2)}, u32[]{:S(2)}) async-start(f32[32,1,128]{2,1,0:T(1,128)} %bitcast.1), calls=%async_computation.1 | async-start | bytes 32768 | tf_op jit(solution)/shard_map/all_to_all | solution.py:902
  65.7 2.7 %collective-permute-done.5.refs_10_ = f32[8,96,128]{2,1,0:T(8,128)S(1)} collective-permute-done((f32[8,96,128]{2,1,0:T(8,128)S(1)}, f32[8,96,128]{2,1,0:T(8,128)S(1)}, u32[]{:S(2)}, u32[]{:S(2)}) %collective-permute-start.5) | collective-permute-done | bytes 393248 | tf_op jit(solution)/shard_map/ppermute | solution.py:901
  68.4 1.3 %collective-permute-done.4.refs_9_ = f32[8,96,128]{2,1,0:T(8,128)S(1)} collective-permute-done((f32[8,96,128]{2,1,0:T(8,128)S(1)}, f32[8,96,128]{2,1,0:T(8,128)S(1)}, u32[]{:S(2)}, u32[]{:S(2)}) %collective-permute-start.4) | collective-permute-done | bytes 393248 | tf_op jit(solution)/shard_map/ppermute | solution.py:900
  69.7 0.0 copy-start.1
  69.7 0.8 copy-done.1
  70.5 4.0 %shard_map.79.final = f32[8,8,16,128]{3,2,1,0:T(8,128)S(1)} custom-call(f32[8,48,128]{2,1,0:T(8,128)S(1)} %get-tuple-element.20.refs_0_, f32[8,48,128]{2,1,0:T(8,128)S(1)} %get-tuple-element.21.refs_1_, f32[8,48,128]{2,1,0:T(8,128)S(1)} %get-tuple-element.22.refs_2_, f32[8,48,128]{2,1,0:T(8,128)S(1)} %get-tuple-element.23.refs_3_, ...), custom_call_target="tpu_custom_call" | custom-call | flops 30000000 | bytes 30000000 | tf_op jit(solution)/shard_map/pallas_call | solution.py:844
  74.5 0.0 all-to-all-done.1
  74.5 0.7 shard_map.80
  75.2 16.8 %all_to_all.22.chunks = f32[8,80,128]{2,1,0:T(8,128)S(1)} all-to-all(f32[8,80,128]{2,1,0:T(8,128)S(1)} %shard_map.80), channel_id=1, replica_groups=mesh['gx'=4,'gy'=2,'gz'=4] {'gx','gy'}, dimensions={0} | all-to-all | bytes 655360 | tf_op jit(solution)/shard_map/all_to_all | solution.py:925
  92.0 0.9 shard_map.81
  (1 shorter events, 0.0 us)
Async XLA Ops:
  22.1 15.4 %collective-permute-start.1 = (f32[8,96,128]{2,1,0:T(8,128)S(1)}, f32[8,96,128]{2,1,0:T(8,128)S(1)}, u32[]{:S(2)}, u32[]{:S(2)}) collective-permute-start(f32[8,96,128]{2,1,0:T(8,128)S(1)} %all_to_all.21.own), channel_id=1, source_target_pairs={{8,0},{16,8},{24,16},{28,24},{20,28},{12,20},{4,12},{1,4},{9,1},{1... | collective-permute-start | bytes 1179656 | tf_op jit(solution)/shard_map/ppermute | solution.py:869
  23.4 14.1 %collective-permute-start = (f32[8,96,128]{2,1,0:T(8,128)S(1)}, f32[8,96,128]{2,1,0:T(8,128)S(1)}, u32[]{:S(2)}, u32[]{:S(2)}) collective-permute-start(f32[8,96,128]{2,1,0:T(8,128)S(1)} %all_to_all.21.own), channel_id=1, source_target_pairs={{0,8},{8,16},{16,24},{24,28},{28,20},{20,12},{12,4},{4,1},{1,9},{9... | collective-permute-start | bytes 1179656 | tf_op jit(solution)/shard_map/ppermute | solution.py:868
  28.0 9.5 %copy-start.2 = (f32[8]{0:T(128)S(1)}, f32[8]{0:T(128)}, u32[]{:S(2)}) copy-start(f32[8]{0:T(128)} %stiffness.1) | copy-start | bytes 100
  28.0 9.0 %collective-permute-start.2 = (f32[8,8,128]{2,1,0:T(8,128)S(1)}, f32[8,8,128]{2,1,0:T(8,128)S(1)}, u32[]{:S(2)}, u32[]{:S(2)}) collective-permute-start(f32[8,8,128]{2,1,0:T(8,128)S(1)} %get-tuple-element.17), channel_id=1, source_target_pairs={{0,16},{8,24},{16,28},{24,20},{28,12},{20,4},{12,1},{4,9},{1,17},{... | collective-permute-start | bytes 98312 | tf_op jit(solution)/shard_map/ppermute | solution.py:872
  30.8 6.7 %collective-permute-start.3 = (f32[8,8,128]{2,1,0:T(8,128)S(1)}, f32[8,8,128]{2,1,0:T(8,128)S(1)}, u32[]{:S(2)}, u32[]{:S(2)}) collective-permute-start(f32[8,8,128]{2,1,0:T(8,128)S(1)} %get-tuple-element.18), channel_id=1, source_target_pairs={{16,0},{24,8},{28,16},{20,24},{12,28},{4,20},{1,12},{9,4},{17,1},{... | collective-permute-start | bytes 98312 | tf_op jit(solution)/shard_map/ppermute | solution.py:871
  54.7 0.6 copy-start
  55.3 13.0 %collective-permute-start.5 = (f32[8,96,128]{2,1,0:T(8,128)S(1)}, f32[8,96,128]{2,1,0:T(8,128)S(1)}, u32[]{:S(2)}, u32[]{:S(2)}) collective-permute-start(f32[8,96,128]{2,1,0:T(8,128)S(1)} %get-tuple-element.27.refs_7_.down), channel_id=1, source_target_pairs={{8,0},{16,8},{24,16},{28,24},{20,28},{12,20},{4,12},{1,4},{9,1},{1... | collective-permute-start | bytes 1179656 | tf_op jit(solution)/shard_map/ppermute | solution.py:901
  56.6 13.1 %collective-permute-start.4 = (f32[8,96,128]{2,1,0:T(8,128)S(1)}, f32[8,96,128]{2,1,0:T(8,128)S(1)}, u32[]{:S(2)}, u32[]{:S(2)}) collective-permute-start(f32[8,96,128]{2,1,0:T(8,128)S(1)} %get-tuple-element.28.refs_8_.up), channel_id=1, source_target_pairs={{0,8},{8,16},{16,24},{24,28},{28,20},{20,12},{12,4},{4,1},{1,9},{9... | collective-permute-start | bytes 1179656 | tf_op jit(solution)/shard_map/ppermute | solution.py:900
  61.2 13.3 %all-to-all-start.1 = ((f32[32,1,128]{2,1,0:T(1,128)}), f32[32,1,128]{2,1,0:T(1,128)S(1)}, u32[]{:S(2)}, u32[]{:S(2)}) async-start(f32[32,1,128]{2,1,0:T(1,128)} %bitcast.1), calls=%async_computation.1 | async-start | bytes 32768 | tf_op jit(solution)/shard_map/all_to_all | solution.py:902
  69.7 0.8 copy-start.1

commit v13 on v12

--- a/solution.py
+++ b/solution.py
@@ -262,6 +262,7 @@
 VMEM_LIMIT = 32 * 1024 * 1024
 PACK_LIMIT = 60 * 1024 * 1024
 FORWARD, ADJOINT, RESPONSE = range(3)
+TURNED = 3
 
 
 def slab_plan_fits(mesh, shape):
@@ -468,7 +469,7 @@
 
 
 STATIC_FINE = ("s0", "s1", "s2", "w", "hv")
-STATIC_COARSE = ("wc", "vh")
+STATIC_COARSE = ("vh",)
 STATIC = STATIC_FINE + STATIC_COARSE
 CUT = {name: SUB // 2 if name in ("hv", "vh") else SUB for name in STATIC}
 
@@ -490,14 +491,17 @@
     def coarse_faces(self, tl, z, pair):
         h, near = tl.coarse_beside(self.refs["vh"], z - CUT["vh"], (), pair)
         return [h + other for other in near]
+
+    def coarse_weight(self, geo, face, z):
+        return jnp.where(geo.inside(z), JACOBI_WEIGHT / tree(face), 0.0)
 
 
 def iterate(geo, st, work, seqs, lo, hi, first=()):
     v, p, res, cor, cor2, cc0, cc1 = work
     tl = Tiles(geo)
     keep = 1.0 - JACOBI_WEIGHT
-    comps = range(3 * len(seqs))
-    transposed = len(seqs)
+    kinds = {3 * s + k: q for q, s in seqs.items() for k in range(3)}
+    comps = list(kinds)
 
     def faces(t, z):
         return st.faces(tl, z, t)
@@ -512,9 +516,9 @@
             if any(q != ADJOINT and q not in first for q in seqs):
                 face = faces(t, z)
                 diag = tree(face)
-            for s, q in enumerate(seqs):
+            for q, s in seqs.items():
                 if not (q == FORWARD and q in first):
-                    _, near = tl.beside(p, z, (transposed if q == ADJOINT else s,), t)
+                    _, near = tl.beside(p, z, (TURNED if q == ADJOINT else s,), t)
                     slope = [0.5 * (near[2 * k] - near[2 * k + 1]) for k in range(3)]
                 for k in range(3):
                     c = 3 * s + k
@@ -536,13 +540,13 @@
 
     def restricted(z, put):
         for pair in range(TX // 2):
-            left = [0.0 for _ in comps]
+            left = dict.fromkeys(comps, 0.0)
             for t in block_of(pair):
                 face = faces(t, z)
                 for c in comps:
                     _, total = around(face, cor, c, t, z)
                     left[c] = left[c] + (keep * get(res, z, c, t) + total)
-            wc = 0.125 * st.get("wc", z, pair)
+            wc = 0.125 * st.coarse_weight(geo, st.coarse_faces(tl, z, pair), z)
             for c in comps:
                 put(cc0, wc * tl.pair_sum(left[c]), z, c, pair)
 
@@ -555,7 +559,8 @@
 
     def sweep_one(z, put):
         for pair in range(TX // 2):
-            face, wc = st.coarse_faces(tl, z, pair), st.get("wc", z, pair)
+            face = st.coarse_faces(tl, z, pair)
+            wc = st.coarse_weight(geo, face, z)
             for c in comps:
                 put(cc1, coarse_step(face, wc, cc0, c, pair, z), z, c, pair)
 
@@ -563,7 +568,8 @@
 
     def sweep_two(z, put):
         for pair in range(TX // 2):
-            face, wc = st.coarse_faces(tl, z, pair), st.get("wc", z, pair)
+            face = st.coarse_faces(tl, z, pair)
+            wc = st.coarse_weight(geo, face, z)
             for c in comps:
                 value = coarse_step(face, wc, cc1, c, pair, z)
                 for t in block_of(pair):
@@ -577,7 +583,7 @@
             for c in comps:
                 f, total = around(face, cor2, c, t, z)
                 value = get(cor, z, c, t) + keep * f + w * total
-                if seqs[c // 3] != ADJOINT and seqs[c // 3] not in first:
+                if kinds[c] != ADJOINT and kinds[c] not in first:
                     value = get(v, z, c, t) + value
                 put(v, value, z, c, t)
 
@@ -586,7 +592,7 @@
     def pressure(z, put):
         for t in range(SUB):
             half = st.get("hv", z, t)
-            for s, q in enumerate(seqs):
+            for q, s in seqs.items():
                 c = 3 * s
                 if q == ADJOINT:
                     face = faces(t, z)
@@ -598,7 +604,7 @@
                         put(cor, get(res, z, c + k, t) - (diag * f - total), z, c + k, t)
                     value = get(p, z, s, t) + div
                     put(p, value, z, s, t)
-                    put(p, half * value, z, transposed, t)
+                    put(p, half * value, z, TURNED, t)
                     continue
                 one, two = tl.sliding(v, z, (c,), t), tl.sliding(v, z, (c + 1,), t)
                 div = tl.x(one, t, 1) - tl.x(one, t, -1)
@@ -633,7 +639,7 @@
 
 def setup_kernel(geo, stiffness, own, low, high, low_edge, high_edge, *refs):
     st = Static(refs)
-    moved, response, down, up, sums, raw, heat, vc, one, *work = refs[len(STATIC) :]
+    moved, response, down, up, sums, raw, heat, one, *work = refs[len(STATIC) :]
     v, p, res, cor, cor2, cc0, cc1 = work
     tl = Tiles(geo)
     b, m, n_rows = geo.slab, geo.margin, geo.rows
@@ -687,7 +693,7 @@
                 value = jnp.where(inside, value, 0.0)
                 st.put(put, "hv", 0.5 * value, z, t)
                 coarse = coarse + value
-            put(vc, 0.125 * tl.pair_sum(coarse), z, pair)
+            st.put(put, "vh", 0.125 * 0.125 * tl.pair_sum(coarse), z, pair)
 
     sweep(tl, m - b, m + 2 * b, viscosity)
 
@@ -704,16 +710,6 @@
                 st.put(put, "s%d" % k, dual * step, z, t)
 
     sweep(tl, m - b, m + 2 * b, statics)
-
-    def coarse_statics(z, put):
-        inside = geo.inside(z)
-        for pair in range(TX // 2):
-            c, near = tl.coarse_beside(vc, z, (), pair)
-            face = [0.25 * (0.5 * (c + o)) for o in near]
-            st.put(put, "wc", jnp.where(inside, JACOBI_WEIGHT / tree(face), 0.0), z, pair)
-            st.put(put, "vh", 0.125 * c, z, pair)
-
-    sweep(tl, m - b, m + 2 * b, coarse_statics)
 
     def transport(z, put):
         for t in range(SUB):
@@ -744,13 +740,15 @@
     def fields(s, three=v):
         return [three.at[3 * s + k, :, mine, :] for k in range(3)] + [p.at[s, :, mine, :]]
 
-    every = (FORWARD, ADJOINT, RESPONSE)
-    iterate(geo, st, work, every, m - PHASE, m + b + PHASE, every)
+    pair, dual = {FORWARD: 0, RESPONSE: 2}, {ADJOINT: 1}
+    iterate(geo, st, work, dual, m - PHASE, m + b + PHASE, dual)
+    iterate(geo, st, work, pair, m - PHASE, m + b + PHASE, pair)
     for k, (a, r) in enumerate(zip(fields(1, cor), fields(2))):
         one[k] = a[...]
         response[k] = r[...]
     sums_of = [(0, source_product(geo, st, v, 3)), (1, whole_sum(one[3]))]
-    iterate(geo, st, work, every, m, m + b)
+    iterate(geo, st, work, dual, m, m + b)
+    iterate(geo, st, work, pair, m, m + b)
     near, far, turn = [one.at[k] for k in range(4)], fields(1, cor), [response.at[k] for k in range(4)]
     sums_of += [(2, source_product(geo, st, v, 3)), (3, whole_sum(p[1, :, mine, :]))]
     sums_of += [(4, product(near, fields(0))), (5, product(far, fields(0))), (6, product(far, turn))]
@@ -781,8 +779,8 @@
             state[:, base : base + b, :] = source[:, rows, :]
         for source, base in ((low, m - PHASE), (down, m), (up, m + b - PHASE), (high, m + b)):
             turned[:, base : base + PHASE, :] = source[:, part, :]
-    iterate(geo, st, work, (FORWARD,), m - PHASE, m + b + PHASE)
-    iterate(geo, st, work, (FORWARD, RESPONSE), m, m + b)
+    iterate(geo, st, work, {FORWARD: 0}, m - PHASE, m + b + PHASE)
+    iterate(geo, st, work, {FORWARD: 0, RESPONSE: 1}, m, m + b)
     mine = slice(m, m + b)
     for s in range(2):
         for k in range(4):
@@ -887,7 +885,7 @@
     *static, moved, response, down, up, sums = call(
         functools.partial(setup_kernel, geo),
         static_shapes + [slab, (4, *slab), message, message, (devices, LANES)],
-        [(FIELDS, *fine), (2, *fine), coarse, (4, *slab)] + work(3, 1),
+        [(FIELDS, *fine), (2, *fine), (4, *slab)] + work(3, 1),
         stiffness,
         own,
         low,

time: 93.4 us -> 91.9 us (0.984)
  local copies, waits for them, and re-layouts: 1.42 us -> 0.01 us
    unnamed x6 -> x2, local copies, waits for them, and re-layouts: 1.42 us -> 0.01 us
  transfers between devices with their start and end apart: 7 -> 7, of which waited for: 4 -> 4; matrix products, arithmetic and copies ran while one was open for 0% -> 0% of each run, Pallas kernels for 4% -> 5%
where the time goes in v13:
time: 91.9 us; the launch traced here: 91.5 us
  blocking collectives  36.2 us (39%)
  Pallas kernels  24.9 us (27%)
  starting transfers between devices  20.2 us (22%)
  waiting for transfers between devices  9.43 us (10%)
    pallas_call x6, Pallas kernels, call(): pl.pallas_call(kernel, out_shape=[jax.ShapeDtypeStruct(s, f32) for s in o...  24.9 us
    all_to_all x1, blocking collectives, slab_shards(): own = lax.all_to_all(chunks, ('gx', 'gy'), 0, 0, tiled=True)  19.4 us
    all_to_all x1, blocking collectives, slab_shards(): chunks = lax.all_to_all(chunks, ('gx', 'gy'), 0, 0, tiled=True)  16.8 us
    ppermute x1, waiting for transfers between devices, slab_shards(): low_edge = lax.ppermute(edges[1], axes, geo.shifts(2))  4.92 us
    ppermute x1, starting transfers between devices, slab_shards(): low = lax.ppermute(own, axes, geo.shifts(1))  4.57 us
    ppermute x1, starting transfers between devices, slab_shards(): from_low = lax.ppermute(up, axes, geo.shifts(1))  4.57 us
    all_to_all x1, starting transfers between devices, slab_shards(): sums = lax.all_to_all(sums, axes, 0, 0, tiled=True)  4.45 us
    ppermute x1, starting transfers between devices, slab_shards(): low_edge = lax.ppermute(edges[1], axes, geo.shifts(2))  2.75 us
  transfers between devices with their start and end apart: 7, of which 4 were waited for; matrix products, arithmetic and copies ran while one was open for 0% of the time, Pallas kernels for 5%

profile of v13, /device:TPU:0, one launch (start us, length us, event | category | flops | bytes accessed | tf_op | source)
XLA Modules:
  0.0 91.5 jit_solution(7703244153351562458)
XLA Ops:
  0.6 2.1 %shard_map.76 = f32[8,96,128]{2,1,0:T(8,128)} custom-call(f32[8,16,128]{2,1,0:T(8,128)} %heat_in.1, f32[3,8,16,128]{3,2,1,0:T(8,128)} %flow_in.1, f32[8,16,128]{2,1,0:T(8,128)} %dual_in.1, s32[8,16,128]{2,1,0:T(8,128)} %kind_in.1), custom_call_target="tpu_custom_call" | custom-call | flops 2000000 | bytes 2000000 | tf_op jit(solution)/shard_map/pallas_call | solution.py:842
  2.7 19.4 %all_to_all.21.own = f32[8,96,128]{2,1,0:T(8,128)S(1)} all-to-all(f32[8,96,128]{2,1,0:T(8,128)} %shard_map.76), channel_id=1, replica_groups=mesh['gx'=4,'gy'=2,'gz'=4] {'gx','gy'}, dimensions={0} | all-to-all | bytes 786432 | tf_op jit(solution)/shard_map/all_to_all | solution.py:864
  22.1 1.3 %collective-permute-start.1 = (f32[8,96,128]{2,1,0:T(8,128)S(1)}, f32[8,96,128]{2,1,0:T(8,128)S(1)}, u32[]{:S(2)}, u32[]{:S(2)}) collective-permute-start(f32[8,96,128]{2,1,0:T(8,128)S(1)} %all_to_all.21.own), channel_id=1, source_target_pairs={{8,0},{16,8},{24,16},{28,24},{20,28},{12,20},{4,12},{1,4},{9,1},{1... | collective-permute-start | bytes 1179656 | tf_op jit(solution)/shard_map/ppermute | solution.py:867
  23.4 4.6 %collective-permute-start = (f32[8,96,128]{2,1,0:T(8,128)S(1)}, f32[8,96,128]{2,1,0:T(8,128)S(1)}, u32[]{:S(2)}, u32[]{:S(2)}) collective-permute-start(f32[8,96,128]{2,1,0:T(8,128)S(1)} %all_to_all.21.own), channel_id=1, source_target_pairs={{0,8},{8,16},{16,24},{24,28},{28,20},{20,12},{12,4},{4,1},{1,9},{9... | collective-permute-start | bytes 1179656 | tf_op jit(solution)/shard_map/ppermute | solution.py:866
  28.0 0.0 copy-start
  28.0 2.8 %collective-permute-start.2 = (f32[8,8,128]{2,1,0:T(8,128)S(1)}, f32[8,8,128]{2,1,0:T(8,128)S(1)}, u32[]{:S(2)}, u32[]{:S(2)}) collective-permute-start(f32[8,8,128]{2,1,0:T(8,128)S(1)} %get-tuple-element.16), channel_id=1, source_target_pairs={{0,16},{8,24},{16,28},{24,20},{28,12},{20,4},{12,1},{4,9},{1,17},{... | collective-permute-start | bytes 98312 | tf_op jit(solution)/shard_map/ppermute | solution.py:870
  30.8 1.3 %collective-permute-start.3 = (f32[8,8,128]{2,1,0:T(8,128)S(1)}, f32[8,8,128]{2,1,0:T(8,128)S(1)}, u32[]{:S(2)}, u32[]{:S(2)}) collective-permute-start(f32[8,8,128]{2,1,0:T(8,128)S(1)} %get-tuple-element.17), channel_id=1, source_target_pairs={{16,0},{24,8},{28,16},{20,24},{12,28},{4,20},{1,12},{9,4},{17,1},{... | collective-permute-start | bytes 98312 | tf_op jit(solution)/shard_map/ppermute | solution.py:869
  32.1 4.9 %collective-permute-done.2.low_edge = f32[8,8,128]{2,1,0:T(8,128)S(1)} collective-permute-done((f32[8,8,128]{2,1,0:T(8,128)S(1)}, f32[8,8,128]{2,1,0:T(8,128)S(1)}, u32[]{:S(2)}, u32[]{:S(2)}) %collective-permute-start.2) | collective-permute-done | bytes 32800 | tf_op jit(solution)/shard_map/ppermute | solution.py:870
  37.0 0.5 collective-permute-done.3.high_edge
  37.5 0.0 collective-permute-done.1.high
  37.5 0.0 collective-permute-done.low
  37.5 0.0 copy-done
  37.5 17.1 %shard_map.78 = (f32[8,48,128]{2,1,0:T(8,128)S(1)}, f32[8,48,128]{2,1,0:T(8,128)S(1)}, f32[8,48,128]{2,1,0:T(8,128)S(1)}, f32[8,48,128]{2,1,0:T(8,128)S(1)}, f32...) custom-call(f32[8]{0:T(128)S(1)} %copy-done, ...), custom_call_target="tpu_custom_call" | custom-call | flops 60000000 | bytes 60000000 | tf_op jit(solution)/shard_map/pallas_call | solution.py:842
  54.6 1.3 %collective-permute-start.5 = (f32[8,96,128]{2,1,0:T(8,128)S(1)}, f32[8,96,128]{2,1,0:T(8,128)S(1)}, u32[]{:S(2)}, u32[]{:S(2)}) collective-permute-start(f32[8,96,128]{2,1,0:T(8,128)S(1)} %get-tuple-element.25.refs_6_.down), channel_id=1, source_target_pairs={{8,0},{16,8},{24,16},{28,24},{20,28},{12,20},{4,12},{1,4},{9,1},{1... | collective-permute-start | bytes 1179656 | tf_op jit(solution)/shard_map/ppermute | solution.py:899
  55.9 4.6 %collective-permute-start.4 = (f32[8,96,128]{2,1,0:T(8,128)S(1)}, f32[8,96,128]{2,1,0:T(8,128)S(1)}, u32[]{:S(2)}, u32[]{:S(2)}) collective-permute-start(f32[8,96,128]{2,1,0:T(8,128)S(1)} %get-tuple-element.26.refs_7_.up), channel_id=1, source_target_pairs={{0,8},{8,16},{16,24},{24,28},{28,20},{20,12},{12,4},{4,1},{1,9},{9... | collective-permute-start | bytes 1179656 | tf_op jit(solution)/shard_map/ppermute | solution.py:898
  60.4 4.5 %all-to-all-start.1 = ((f32[32,1,128]{2,1,0:T(1,128)}), f32[32,1,128]{2,1,0:T(1,128)S(1)}, u32[]{:S(2)}, u32[]{:S(2)}) async-start(f32[32,1,128]{2,1,0:T(1,128)} %bitcast.1), calls=%async_computation.1 | async-start | bytes 32768 | tf_op jit(solution)/shard_map/all_to_all | solution.py:900
  64.9 2.7 %collective-permute-done.5.refs_9_ = f32[8,96,128]{2,1,0:T(8,128)S(1)} collective-permute-done((f32[8,96,128]{2,1,0:T(8,128)S(1)}, f32[8,96,128]{2,1,0:T(8,128)S(1)}, u32[]{:S(2)}, u32[]{:S(2)}) %collective-permute-start.5) | collective-permute-done | bytes 393248 | tf_op jit(solution)/shard_map/ppermute | solution.py:899
  67.6 1.3 %collective-permute-done.4.refs_8_ = f32[8,96,128]{2,1,0:T(8,128)S(1)} collective-permute-done((f32[8,96,128]{2,1,0:T(8,128)S(1)}, f32[8,96,128]{2,1,0:T(8,128)S(1)}, u32[]{:S(2)}, u32[]{:S(2)}) %collective-permute-start.4) | collective-permute-done | bytes 393248 | tf_op jit(solution)/shard_map/ppermute | solution.py:898
  68.9 4.2 %shard_map.79.final = f32[8,8,16,128]{3,2,1,0:T(8,128)S(1)} custom-call(f32[8,48,128]{2,1,0:T(8,128)S(1)} %get-tuple-element.19.refs_0_, f32[8,48,128]{2,1,0:T(8,128)S(1)} %get-tuple-element.20.refs_1_, f32[8,48,128]{2,1,0:T(8,128)S(1)} %get-tuple-element.21.refs_2_, f32[8,48,128]{2,1,0:T(8,128)S(1)} %get-tuple-element.22.refs_3_, ...), custom_call_target="tpu_custom_call" | custom-call | flops 30000000 | bytes 30000000 | tf_op jit(solution)/shard_map/pallas_call | solution.py:842
  73.1 0.0 all-to-all-done.1
  73.1 0.7 shard_map.80
  73.8 16.8 %all_to_all.22.chunks = f32[8,80,128]{2,1,0:T(8,128)S(1)} all-to-all(f32[8,80,128]{2,1,0:T(8,128)S(1)} %shard_map.80), channel_id=1, replica_groups=mesh['gx'=4,'gy'=2,'gz'=4] {'gx','gy'}, dimensions={0} | all-to-all | bytes 655360 | tf_op jit(solution)/shard_map/all_to_all | solution.py:923
  90.6 0.9 shard_map.81
  (1 shorter events, 0.0 us)
Async XLA Ops:
  22.1 15.4 %collective-permute-start.1 = (f32[8,96,128]{2,1,0:T(8,128)S(1)}, f32[8,96,128]{2,1,0:T(8,128)S(1)}, u32[]{:S(2)}, u32[]{:S(2)}) collective-permute-start(f32[8,96,128]{2,1,0:T(8,128)S(1)} %all_to_all.21.own), channel_id=1, source_target_pairs={{8,0},{16,8},{24,16},{28,24},{20,28},{12,20},{4,12},{1,4},{9,1},{1... | collective-permute-start | bytes 1179656 | tf_op jit(solution)/shard_map/ppermute | solution.py:867
  23.4 14.1 %collective-permute-start = (f32[8,96,128]{2,1,0:T(8,128)S(1)}, f32[8,96,128]{2,1,0:T(8,128)S(1)}, u32[]{:S(2)}, u32[]{:S(2)}) collective-permute-start(f32[8,96,128]{2,1,0:T(8,128)S(1)} %all_to_all.21.own), channel_id=1, source_target_pairs={{0,8},{8,16},{16,24},{24,28},{28,20},{20,12},{12,4},{4,1},{1,9},{9... | collective-permute-start | bytes 1179656 | tf_op jit(solution)/shard_map/ppermute | solution.py:866
  28.0 9.5 %copy-start = (f32[8]{0:T(128)S(1)}, f32[8]{0:T(128)}, u32[]{:S(2)}) copy-start(f32[8]{0:T(128)} %stiffness.1) | copy-start | bytes 100
  28.0 9.0 %collective-permute-start.2 = (f32[8,8,128]{2,1,0:T(8,128)S(1)}, f32[8,8,128]{2,1,0:T(8,128)S(1)}, u32[]{:S(2)}, u32[]{:S(2)}) collective-permute-start(f32[8,8,128]{2,1,0:T(8,128)S(1)} %get-tuple-element.16), channel_id=1, source_target_pairs={{0,16},{8,24},{16,28},{24,20},{28,12},{20,4},{12,1},{4,9},{1,17},{... | collective-permute-start | bytes 98312 | tf_op jit(solution)/shard_map/ppermute | solution.py:870
  30.8 6.7 %collective-permute-start.3 = (f32[8,8,128]{2,1,0:T(8,128)S(1)}, f32[8,8,128]{2,1,0:T(8,128)S(1)}, u32[]{:S(2)}, u32[]{:S(2)}) collective-permute-start(f32[8,8,128]{2,1,0:T(8,128)S(1)} %get-tuple-element.17), channel_id=1, source_target_pairs={{16,0},{24,8},{28,16},{20,24},{12,28},{4,20},{1,12},{9,4},{17,1},{... | collective-permute-start | bytes 98312 | tf_op jit(solution)/shard_map/ppermute | solution.py:869
  54.6 13.0 %collective-permute-start.5 = (f32[8,96,128]{2,1,0:T(8,128)S(1)}, f32[8,96,128]{2,1,0:T(8,128)S(1)}, u32[]{:S(2)}, u32[]{:S(2)}) collective-permute-start(f32[8,96,128]{2,1,0:T(8,128)S(1)} %get-tuple-element.25.refs_6_.down), channel_id=1, source_target_pairs={{8,0},{16,8},{24,16},{28,24},{20,28},{12,20},{4,12},{1,4},{9,1},{1... | collective-permute-start | bytes 1179656 | tf_op jit(solution)/shard_map/ppermute | solution.py:899
  55.9 13.1 %collective-permute-start.4 = (f32[8,96,128]{2,1,0:T(8,128)S(1)}, f32[8,96,128]{2,1,0:T(8,128)S(1)}, u32[]{:S(2)}, u32[]{:S(2)}) collective-permute-start(f32[8,96,128]{2,1,0:T(8,128)S(1)} %get-tuple-element.26.refs_7_.up), channel_id=1, source_target_pairs={{0,8},{8,16},{16,24},{24,28},{28,20},{20,12},{12,4},{4,1},{1,9},{9... | collective-permute-start | bytes 1179656 | tf_op jit(solution)/shard_map/ppermute | solution.py:898
  60.4 12.7 %all-to-all-start.1 = ((f32[32,1,128]{2,1,0:T(1,128)}), f32[32,1,128]{2,1,0:T(1,128)S(1)}, u32[]{:S(2)}, u32[]{:S(2)}) async-start(f32[32,1,128]{2,1,0:T(1,128)} %bitcast.1), calls=%async_computation.1 | async-start | bytes 32768 | tf_op jit(solution)/shard_map/all_to_all | solution.py:900

commit v14 on v13

--- a/solution.py
+++ b/solution.py
@@ -262,7 +262,7 @@
 VMEM_LIMIT = 32 * 1024 * 1024
 PACK_LIMIT = 60 * 1024 * 1024
 FORWARD, ADJOINT, RESPONSE = range(3)
-TURNED = 3
+TURNED = 2
 
 
 def slab_plan_fits(mesh, shape):
@@ -639,7 +639,7 @@
 
 def setup_kernel(geo, stiffness, own, low, high, low_edge, high_edge, *refs):
     st = Static(refs)
-    moved, response, down, up, sums, raw, heat, one, *work = refs[len(STATIC) :]
+    moved, dual_out, sums, raw, heat, *work = refs[len(STATIC) :]
     v, p, res, cor, cor2, cc0, cc1 = work
     tl = Tiles(geo)
     b, m, n_rows = geo.slab, geo.margin, geo.rows
@@ -729,35 +729,18 @@
     def unit(z, put):
         value = jnp.where(geo.inside(z), 1.0, 0.0)
         for t in range(SUB):
-            put(p, value, z, 1, t)
-            put(p, value, z, 2, t)
-            put(p, st.get("hv", z, t), z, 3, t)
+            put(p, value, z, 0, t)
+            put(p, st.get("hv", z, t), z, TURNED, t)
 
     sweep(tl, m - b, m + 2 * b, unit)
 
-    mine = slice(m, m + b)
-
-    def fields(s, three=v):
-        return [three.at[3 * s + k, :, mine, :] for k in range(3)] + [p.at[s, :, mine, :]]
-
-    pair, dual = {FORWARD: 0, RESPONSE: 2}, {ADJOINT: 1}
-    iterate(geo, st, work, dual, m - PHASE, m + b + PHASE, dual)
-    iterate(geo, st, work, pair, m - PHASE, m + b + PHASE, pair)
-    for k, (a, r) in enumerate(zip(fields(1, cor), fields(2))):
-        one[k] = a[...]
-        response[k] = r[...]
-    sums_of = [(0, source_product(geo, st, v, 3)), (1, whole_sum(one[3]))]
-    iterate(geo, st, work, dual, m, m + b)
-    iterate(geo, st, work, pair, m, m + b)
-    near, far, turn = [one.at[k] for k in range(4)], fields(1, cor), [response.at[k] for k in range(4)]
-    sums_of += [(2, source_product(geo, st, v, 3)), (3, whole_sum(p[1, :, mine, :]))]
-    sums_of += [(4, product(near, fields(0))), (5, product(far, fields(0))), (6, product(far, turn))]
+    mine, rows = slice(m, m + b), slice(m - PHASE, m + b + PHASE)
+    dual = {ADJOINT: 0}
+    iterate(geo, st, work, dual, rows.start, rows.stop, dual)
+    for k in range(4):
+        dual_out[k] = cor[k, :, rows, :] if k < 3 else p[0, :, rows, :]
+    sums_of = [(0, source_product(geo, st, v, 0)), (1, whole_sum(p[0, :, mine, :]))]
     sums[...] = in_lanes(sums_of, sums.shape[0])
-    for k, (x, r) in enumerate(zip(fields(0), fields(2))):
-        state, turned = x[...], r[...]
-        for out, part in ((down, turned[:, :PHASE]), (up, turned[:, b - PHASE :])):
-            out[:, k * b : (k + 1) * b, :] = state
-            out[:, 4 * b + k * PHASE : 4 * b + (k + 1) * PHASE, :] = part
 
 
 def source_product(geo, st, v, first):
@@ -767,24 +750,63 @@
     return product(left, [v.at[first + k, :, mine, :] for k in range(3)])
 
 
-def second_kernel(geo, *refs):
+def first_kernel(geo, *refs):
     st = Static(refs)
-    down, up, low, high, final, *work = refs[len(STATIC) :]
+    dual, state, response, second, sums, *work = refs[len(STATIC) :]
+    v, p, res, cor = work[:4]
+    b, m = geo.slab, geo.margin
+    mine, rows = slice(m, m + b), slice(m - PHASE, m + b + PHASE)
+    tl = Tiles(geo)
+
+    def unit(z, put):
+        value = jnp.where(geo.inside(z), 1.0, 0.0)
+        for t in range(SUB):
+            put(p, value, z, 1, t)
+
+    def fields(s, three=v):
+        return [three.at[3 * s + k, :, mine, :] for k in range(3)] + [p.at[s, :, mine, :]]
+
+    sweep(tl, m - b, m + 2 * b, unit)
+    pair = {FORWARD: 0, RESPONSE: 1}
+    iterate(geo, st, work, pair, rows.start, rows.stop, pair)
+    for k, ref in enumerate(fields(1)):
+        response[k] = ref[...]
+    iterate(geo, st, work, pair, m, m + b)
+    for k, (x, r) in enumerate(zip(fields(0), fields(1))):
+        state[k], second[k] = x[...], r[...]
+    for k in range(3):
+        cor[k, :, rows, :] = dual[k]
+    p[0, :, rows, :] = dual[3]
+    held = slice(rows.start - CUT["hv"], rows.stop - CUT["hv"])
+    p[TURNED, :, rows, :] = st.refs["hv"][:, held, :] * dual[3]
+    iterate(geo, st, work, {ADJOINT: 0}, m, m + b)
+    own = slice(PHASE, PHASE + b)
+    near, far = [dual.at[k, :, own, :] for k in range(4)], fields(0, cor)
+    last, turn = [state.at[k] for k in range(4)], [response.at[k] for k in range(4)]
+    sums_of = [(2, source_product(geo, st, v, 0)), (3, whole_sum(p[0, :, mine, :]))]
+    sums_of += [(4, product(near, last)), (5, product(far, last)), (6, product(far, turn))]
+    sums[...] = in_lanes(sums_of, sums.shape[0])
+
+
+def second_kernel(geo, raw, response, early, state):
+    m1 = jnp.sum(early[...], axis=0, keepdims=True)[:, 0:1] / geo.cells
+    for k in range(4):
+        state[k] = raw[k] - m1 * response[k]
+
+
+def third_kernel(geo, *refs):
+    st = Static(refs)
+    own, low, high, final, *work = refs[len(STATIC) :]
     v, p = work[:2]
     b, m = geo.slab, geo.margin
     for k in range(4):
-        rows, part = slice(k * b, (k + 1) * b), slice(4 * b + k * PHASE, 4 * b + (k + 1) * PHASE)
-        state, turned = (v.at[k], v.at[3 + k]) if k < 3 else (p.at[0], p.at[1])
-        for source, base in ((low, m - b), (down, m), (high, m + b)):
-            state[:, base : base + b, :] = source[:, rows, :]
-        for source, base in ((low, m - PHASE), (down, m), (up, m + b - PHASE), (high, m + b)):
-            turned[:, base : base + PHASE, :] = source[:, part, :]
+        state = v.at[k] if k < 3 else p.at[0]
+        for source, base in ((low, m - b), (own, m), (high, m + b)):
+            state[:, base : base + b, :] = source[k]
     iterate(geo, st, work, {FORWARD: 0}, m - PHASE, m + b + PHASE)
-    iterate(geo, st, work, {FORWARD: 0, RESPONSE: 1}, m, m + b)
-    mine = slice(m, m + b)
-    for s in range(2):
-        for k in range(4):
-            final[4 * s + k] = v[3 * s + k, :, mine, :] if k < 3 else p[s, :, mine, :]
+    iterate(geo, st, work, {FORWARD: 0}, m, m + b)
+    for k in range(4):
+        final[k] = v[k, :, m : m + b, :] if k < 3 else p[0, :, m : m + b, :]
 
 
 def means(geo, sums):
@@ -794,23 +816,21 @@
     m2 = c1 + c2 - m1 * l1
     m3 = c1 + (l1_x2 - m1 * l2) - m2 * l1
     m4 = c1 + c2 + (l2_x2 - m1 * l2_r1) - m2 * l2 - m3 * l1
-    return m1, m2, m3, m4
-
-
-def combine_kernel(geo, sums, final, down, up, response, moved, out):
+    return m2, m3, m4
+
+
+def combine_kernel(geo, early, late, final, second, response, moved, out):
     b = geo.slab
-    means_of = [jnp.broadcast_to(value, (SUB, LANES)) for value in means(geo, sums[...])]
-    m1, m2, m3, m4 = means_of
+    values = means(geo, early[...] + late[...])
+    m2, m3, m4 = [jnp.broadcast_to(value, (SUB, LANES)) for value in values]
     for u in range(0, b, SUB):
         rows = slice(u, u + SUB)
         fields = []
         for k in range(4):
-            turned = down if u < PHASE else up
-            at = 4 * b + k * PHASE + (u if u < PHASE else u - (b - PHASE))
             tiles = []
             for t in range(SUB):
-                value = final[k, t, rows, :] - m1 * final[4 + k, t, rows, :]
-                value = value - m2 * turned[t, at : at + SUB, :] - m3 * response[k, t, rows, :]
+                value = final[k, t, rows, :] - m2 * second[k, t, rows, :]
+                value = value - m3 * response[k, t, rows, :]
                 tiles.append(value - m4 if k == 3 else value)
             fields.append(tiles)
         fields.append([moved[t, rows, :] + fields[2][t] for t in range(SUB)])
@@ -876,16 +896,16 @@
     ]
     slab = (SUB, b, LANES)
 
-    def work(n, more=0):
-        fields = [(3 * n, *fine), (n + more, *fine)] + [(3 * n, *fine)] * 3
+    def work(n):
+        fields = [(3 * n, *fine), (TURNED + 1, *fine)] + [(3 * n, *fine)] * 3
         return fields + [(3 * n, *coarse)] * 2
 
     devices = group * geo.nz
-    message = (SUB, 4 * b + 4 * PHASE, LANES)
-    *static, moved, response, down, up, sums = call(
+    wide, state = (4, SUB, b + 2 * PHASE, LANES), (4, *slab)
+    *static, moved, dual_one, early = call(
         functools.partial(setup_kernel, geo),
-        static_shapes + [slab, (4, *slab), message, message, (devices, LANES)],
-        [(FIELDS, *fine), (2, *fine), (4, *slab)] + work(3, 1),
+        static_shapes + [slab, wide, (devices, LANES)],
+        [(FIELDS, *fine), (2, *fine)] + work(1),
         stiffness,
         own,
         low,
@@ -895,28 +915,37 @@
         smem=(0,),
         megabytes=60,
     )
-    from_low = lax.ppermute(up, axes, geo.shifts(1))
-    from_high = lax.ppermute(down, axes, geo.shifts(-1))
-    sums = lax.all_to_all(sums, axes, 0, 0, tiled=True)
-    (final,) = call(
-        functools.partial(second_kernel, geo),
-        [(8, *slab)],
+    early = lax.all_to_all(early, axes, 0, 0, tiled=True)
+    raw, response, second, late = call(
+        functools.partial(first_kernel, geo),
+        [state, state, state, (devices, LANES)],
         work(2),
         *static,
-        down,
-        up,
-        from_low,
-        from_high,
+        dual_one,
+        megabytes=40,
+    )
+    late = lax.all_to_all(late, axes, 0, 0, tiled=True)
+    (mine,) = call(functools.partial(second_kernel, geo), [state], [], raw, response, early)
+    low_state = lax.ppermute(mine, axes, geo.shifts(1))
+    high_state = lax.ppermute(mine, axes, geo.shifts(-1))
+    (final,) = call(
+        functools.partial(third_kernel, geo),
+        [state],
+        work(1),
+        *static,
+        mine,
+        low_state,
+        high_state,
         megabytes=30,
     )
     (chunks,) = call(
         functools.partial(combine_kernel, geo),
         [(group, BACK * b, LANES)],
         [],
-        sums,
+        early,
+        late,
         final,
-        down,
-        up,
+        second,
         response,
         moved,
     )

time: 91.9 us -> 94 us (1.023)
  starting transfers between devices: 20.2 us -> 25.7 us
  blocking collectives: 36.2 us -> 33 us
    all_to_all x1 -> x2, starting transfers between devices: 4.45 us -> 9.96 us  [the longest x1 5.67 us: slab_shards(): late = lax.all_to_all(late, axes, 0, 0, tiled=True)]
    all_to_all x1 -> x2, waiting for transfers between devices: 0.01 us -> 4.04 us  [the longest x1 3.7 us: slab_shards(): late = lax.all_to_all(late, axes, 0, 0, tiled=True)]
    ppermute x2, waiting for transfers between devices: 4.01 us -> 0.01 us  [the longest x1 0.01 us: slab_shards(): high_state = lax.ppermute(mine, axes, geo.shifts(-1))]
    all_to_all x1, blocking collectives: 16.8 us -> 13.6 us  [slab_shards(): chunks = lax.all_to_all(chunks, ('gx', 'gy'), 0, 0, tiled=True)]
    pallas_call x6 -> x8, Pallas kernels: 24.9 us -> 24.6 us  [call(): pl.pallas_call(kernel, out_shape=[jax.ShapeDtypeStruct(s, f32) for s in o...]
  transfers between devices with their start and end apart: 7 -> 8, of which waited for: 4 -> 4; matrix products, arithmetic and copies ran while one was open for 0% -> 0% of each run, Pallas kernels for 5% -> 11%
where the time goes in v14:
time: 94 us; the launch traced here: 93.5 us
  blocking collectives  33 us (35%)
  starting transfers between devices  25.7 us (27%)
  Pallas kernels  24.6 us (26%)
  waiting for transfers between devices  9.46 us (10%)
    pallas_call x8, Pallas kernels, call(): pl.pallas_call(kernel, out_shape=[jax.ShapeDtypeStruct(s, f32) for s in o...  24.6 us
    all_to_all x1, blocking collectives, slab_shards(): own = lax.all_to_all(chunks, ('gx', 'gy'), 0, 0, tiled=True)  19.4 us
    all_to_all x1, blocking collectives, slab_shards(): chunks = lax.all_to_all(chunks, ('gx', 'gy'), 0, 0, tiled=True)  13.6 us
    all_to_all x1, starting transfers between devices, slab_shards(): late = lax.all_to_all(late, axes, 0, 0, tiled=True)  5.67 us
    ppermute x1, waiting for transfers between devices, slab_shards(): low_edge = lax.ppermute(edges[1], axes, geo.shifts(2))  4.92 us
    ppermute x1, starting transfers between devices, slab_shards(): low = lax.ppermute(own, axes, geo.shifts(1))  4.57 us
    ppermute x1, starting transfers between devices, slab_shards(): low_state = lax.ppermute(mine, axes, geo.shifts(1))  4.56 us
    all_to_all x1, starting transfers between devices, slab_shards(): early = lax.all_to_all(early, axes, 0, 0, tiled=True)  4.29 us
  transfers between devices with their start and end apart: 8, of which 4 were waited for; matrix products, arithmetic and copies ran while one was open for 0% of the time, Pallas kernels for 11%

profile of v14, /device:TPU:0, one launch (start us, length us, event | category | flops | bytes accessed | tf_op | source)
XLA Modules:
  0.0 93.5 jit_solution(299045165209104722)
XLA Ops:
  0.6 2.1 %shard_map.76 = f32[8,96,128]{2,1,0:T(8,128)} custom-call(f32[8,16,128]{2,1,0:T(8,128)} %heat_in.1, f32[3,8,16,128]{3,2,1,0:T(8,128)} %flow_in.1, f32[8,16,128]{2,1,0:T(8,128)} %dual_in.1, s32[8,16,128]{2,1,0:T(8,128)} %kind_in.1), custom_call_target="tpu_custom_call" | custom-call | flops 2000000 | bytes 2000000 | tf_op jit(solution)/shard_map/pallas_call | solution.py:862
  2.7 19.4 %all_to_all.32.own = f32[8,96,128]{2,1,0:T(8,128)S(1)} all-to-all(f32[8,96,128]{2,1,0:T(8,128)} %shard_map.76), channel_id=1, replica_groups=mesh['gx'=4,'gy'=2,'gz'=4] {'gx','gy'}, dimensions={0} | all-to-all | bytes 786432 | tf_op jit(solution)/shard_map/all_to_all | solution.py:884
  22.1 1.3 %collective-permute-start.1 = (f32[8,96,128]{2,1,0:T(8,128)S(1)}, f32[8,96,128]{2,1,0:T(8,128)S(1)}, u32[]{:S(2)}, u32[]{:S(2)}) collective-permute-start(f32[8,96,128]{2,1,0:T(8,128)S(1)} %all_to_all.32.own), channel_id=1, source_target_pairs={{8,0},{16,8},{24,16},{28,24},{20,28},{12,20},{4,12},{1,4},{9,1},{1... | collective-permute-start | bytes 1179656 | tf_op jit(solution)/shard_map/ppermute | solution.py:887
  23.4 4.6 %collective-permute-start = (f32[8,96,128]{2,1,0:T(8,128)S(1)}, f32[8,96,128]{2,1,0:T(8,128)S(1)}, u32[]{:S(2)}, u32[]{:S(2)}) collective-permute-start(f32[8,96,128]{2,1,0:T(8,128)S(1)} %all_to_all.32.own), channel_id=1, source_target_pairs={{0,8},{8,16},{16,24},{24,28},{28,20},{20,12},{12,4},{4,1},{1,9},{9... | collective-permute-start | bytes 1179656 | tf_op jit(solution)/shard_map/ppermute | solution.py:886
  28.0 0.0 copy-start
  28.0 2.8 %collective-permute-start.2 = (f32[8,8,128]{2,1,0:T(8,128)S(1)}, f32[8,8,128]{2,1,0:T(8,128)S(1)}, u32[]{:S(2)}, u32[]{:S(2)}) collective-permute-start(f32[8,8,128]{2,1,0:T(8,128)S(1)} %get-tuple-element.18), channel_id=1, source_target_pairs={{0,16},{8,24},{16,28},{24,20},{28,12},{20,4},{12,1},{4,9},{1,17},{... | collective-permute-start | bytes 98312 | tf_op jit(solution)/shard_map/ppermute | solution.py:890
  30.8 1.3 %collective-permute-start.3 = (f32[8,8,128]{2,1,0:T(8,128)S(1)}, f32[8,8,128]{2,1,0:T(8,128)S(1)}, u32[]{:S(2)}, u32[]{:S(2)}) collective-permute-start(f32[8,8,128]{2,1,0:T(8,128)S(1)} %get-tuple-element.19), channel_id=1, source_target_pairs={{16,0},{24,8},{28,16},{20,24},{12,28},{4,20},{1,12},{9,4},{17,1},{... | collective-permute-start | bytes 98312 | tf_op jit(solution)/shard_map/ppermute | solution.py:889
  32.1 4.9 %collective-permute-done.2.low_edge = f32[8,8,128]{2,1,0:T(8,128)S(1)} collective-permute-done((f32[8,8,128]{2,1,0:T(8,128)S(1)}, f32[8,8,128]{2,1,0:T(8,128)S(1)}, u32[]{:S(2)}, u32[]{:S(2)}) %collective-permute-start.2) | collective-permute-done | bytes 32800 | tf_op jit(solution)/shard_map/ppermute | solution.py:890
  37.0 0.5 collective-permute-done.3.high_edge
  37.5 0.0 collective-permute-done.1.high
  37.5 0.0 collective-permute-done.low
  37.5 0.0 copy-done
  37.5 11.0 %shard_map.78 = (f32[8,48,128]{2,1,0:T(8,128)S(1)}, f32[8,48,128]{2,1,0:T(8,128)S(1)}, f32[8,48,128]{2,1,0:T(8,128)S(1)}, f32[8,48,128]{2,1,0:T(8,128)S(1)}, f32...) custom-call(f32[8]{0:T(128)S(1)} %copy-done, ...), custom_call_target="tpu_custom_call" | custom-call | flops 60000000 | bytes 60000000 | tf_op jit(solution)/shard_map/pallas_call | solution.py:862
  48.5 4.3 %all-to-all-start.1 = ((f32[32,1,128]{2,1,0:T(1,128)}), f32[32,1,128]{2,1,0:T(1,128)S(1)}, u32[]{:S(2)}, u32[]{:S(2)}) async-start(f32[32,1,128]{2,1,0:T(1,128)} %bitcast.1), calls=%async_computation.1 | async-start | bytes 32768 | tf_op jit(solution)/shard_map/all_to_all | solution.py:918
  52.8 6.7 %shard_map.79 = (f32[4,8,16,128]{3,2,1,0:T(8,128)S(1)}, f32[4,8,16,128]{3,2,1,0:T(8,128)S(1)}, f32[4,8,16,128]{3,2,1,0:T(8,128)S(1)}, f32[32,128]{1,0:T(8,128)}) custom-call(f32[8,48,128]{2,1,0:T(8,128)S(1)} %get-tuple-element.21.refs_0_, f32[8,48,128]{2,1,0:T(8,128)S(1)} %get-tuple-element.22.refs_1_, f32[8,48,128]{2,1,0:T(8,128)S(1)} %get-tuple-element.23.refs_2_, ...), custom_call_target="tpu_custom_call" | custom-call | flops 40000000 | bytes 40000000 | tf_op jit(solution)/shard_map/pallas_call | solution.py:862
  59.5 0.3 all-to-all-done.1
  59.8 0.1 shard_map.80.refs_6_
  59.9 1.3 %collective-permute-start.5 = (f32[4,8,16,128]{3,2,1,0:T(8,128)S(1)}, f32[4,8,16,128]{3,2,1,0:T(8,128)S(1)}, u32[]{:S(2)}, u32[]{:S(2)}) collective-permute-start(f32[4,8,16,128]{3,2,1,0:T(8,128)S(1)} %shard_map.80.refs_6_), channel_id=1, source_target_pairs={{8,0},{16,8},{24,16},{28,24},{20,28},{12,20},{4,12},{1,4},{9,1},{1... | collective-permute-start | bytes 786440 | tf_op jit(solution)/shard_map/ppermute | solution.py:930
  61.2 4.6 %collective-permute-start.4 = (f32[4,8,16,128]{3,2,1,0:T(8,128)S(1)}, f32[4,8,16,128]{3,2,1,0:T(8,128)S(1)}, u32[]{:S(2)}, u32[]{:S(2)}) collective-permute-start(f32[4,8,16,128]{3,2,1,0:T(8,128)S(1)} %shard_map.80.refs_6_), channel_id=1, source_target_pairs={{0,8},{8,16},{16,24},{24,28},{28,20},{20,12},{12,4},{4,1},{1,9},{9... | collective-permute-start | bytes 786440 | tf_op jit(solution)/shard_map/ppermute | solution.py:929
  65.8 5.7 %all-to-all-start.2 = ((f32[32,1,128]{2,1,0:T(1,128)}), f32[32,1,128]{2,1,0:T(1,128)S(1)}, u32[]{:S(2)}, u32[]{:S(2)}) async-start(f32[32,1,128]{2,1,0:T(1,128)} %bitcast.4), calls=%async_computation.2 | async-start | bytes 32768 | tf_op jit(solution)/shard_map/all_to_all | solution.py:927
  71.5 0.0 collective-permute-done.5.refs_8_
  71.5 0.0 collective-permute-done.4.refs_7_
  71.5 3.2 %shard_map.81.final = f32[4,8,16,128]{3,2,1,0:T(8,128)S(1)} custom-call(f32[8,48,128]{2,1,0:T(8,128)S(1)} %get-tuple-element.21.refs_0_, f32[8,48,128]{2,1,0:T(8,128)S(1)} %get-tuple-element.22.refs_1_, f32[8,48,128]{2,1,0:T(8,128)S(1)} %get-tuple-element.23.refs_2_, f32[8,48,128]{2,1,0:T(8,128)S(1)} %get-tuple-element.24.refs_3_, ...), custom_call_target="tpu_custom_call" | custom-call | flops 30000000 | bytes 30000000 | tf_op jit(solution)/shard_map/pallas_call | solution.py:862
  74.7 3.7 %all-to-all-done.2 = f32[32,1,128]{2,1,0:T(1,128)S(1)} async-done(((f32[32,1,128]{2,1,0:T(1,128)}), f32[32,1,128]{2,1,0:T(1,128)S(1)}, u32[]{:S(2)}, u32[]{:S(2)}) %all-to-all-start.2) | async-done | bytes 16416 | tf_op jit(solution)/shard_map/all_to_all | solution.py:927
  78.4 0.7 shard_map.82
  79.1 13.6 %all_to_all.33.chunks = f32[8,80,128]{2,1,0:T(8,128)S(1)} all-to-all(f32[8,80,128]{2,1,0:T(8,128)S(1)} %shard_map.82), channel_id=1, replica_groups=mesh['gx'=4,'gy'=2,'gz'=4] {'gx','gy'}, dimensions={0} | all-to-all | bytes 655360 | tf_op jit(solution)/shard_map/all_to_all | solution.py:952
  92.7 0.9 shard_map.83
  (1 shorter events, 0.0 us)
Async XLA Ops:
  22.1 15.4 %collective-permute-start.1 = (f32[8,96,128]{2,1,0:T(8,128)S(1)}, f32[8,96,128]{2,1,0:T(8,128)S(1)}, u32[]{:S(2)}, u32[]{:S(2)}) collective-permute-start(f32[8,96,128]{2,1,0:T(8,128)S(1)} %all_to_all.32.own), channel_id=1, source_target_pairs={{8,0},{16,8},{24,16},{28,24},{20,28},{12,20},{4,12},{1,4},{9,1},{1... | collective-permute-start | bytes 1179656 | tf_op jit(solution)/shard_map/ppermute | solution.py:887
  23.4 14.1 %collective-permute-start = (f32[8,96,128]{2,1,0:T(8,128)S(1)}, f32[8,96,128]{2,1,0:T(8,128)S(1)}, u32[]{:S(2)}, u32[]{:S(2)}) collective-permute-start(f32[8,96,128]{2,1,0:T(8,128)S(1)} %all_to_all.32.own), channel_id=1, source_target_pairs={{0,8},{8,16},{16,24},{24,28},{28,20},{20,12},{12,4},{4,1},{1,9},{9... | collective-permute-start | bytes 1179656 | tf_op jit(solution)/shard_map/ppermute | solution.py:886
  28.0 9.5 %copy-start = (f32[8]{0:T(128)S(1)}, f32[8]{0:T(128)}, u32[]{:S(2)}) copy-start(f32[8]{0:T(128)} %stiffness.1) | copy-start | bytes 100
  28.0 9.0 %collective-permute-start.2 = (f32[8,8,128]{2,1,0:T(8,128)S(1)}, f32[8,8,128]{2,1,0:T(8,128)S(1)}, u32[]{:S(2)}, u32[]{:S(2)}) collective-permute-start(f32[8,8,128]{2,1,0:T(8,128)S(1)} %get-tuple-element.18), channel_id=1, source_target_pairs={{0,16},{8,24},{16,28},{24,20},{28,12},{20,4},{12,1},{4,9},{1,17},{... | collective-permute-start | bytes 98312 | tf_op jit(solution)/shard_map/ppermute | solution.py:890
  30.8 6.7 %collective-permute-start.3 = (f32[8,8,128]{2,1,0:T(8,128)S(1)}, f32[8,8,128]{2,1,0:T(8,128)S(1)}, u32[]{:S(2)}, u32[]{:S(2)}) collective-permute-start(f32[8,8,128]{2,1,0:T(8,128)S(1)} %get-tuple-element.19), channel_id=1, source_target_pairs={{16,0},{24,8},{28,16},{20,24},{12,28},{4,20},{1,12},{9,4},{17,1},{... | collective-permute-start | bytes 98312 | tf_op jit(solution)/shard_map/ppermute | solution.py:889
  48.5 11.4 %all-to-all-start.1 = ((f32[32,1,128]{2,1,0:T(1,128)}), f32[32,1,128]{2,1,0:T(1,128)S(1)}, u32[]{:S(2)}, u32[]{:S(2)}) async-start(f32[32,1,128]{2,1,0:T(1,128)} %bitcast.1), calls=%async_computation.1 | async-start | bytes 32768 | tf_op jit(solution)/shard_map/all_to_all | solution.py:918
  59.9 11.6 %collective-permute-start.5 = (f32[4,8,16,128]{3,2,1,0:T(8,128)S(1)}, f32[4,8,16,128]{3,2,1,0:T(8,128)S(1)}, u32[]{:S(2)}, u32[]{:S(2)}) collective-permute-start(f32[4,8,16,128]{3,2,1,0:T(8,128)S(1)} %shard_map.80.refs_6_), channel_id=1, source_target_pairs={{8,0},{16,8},{24,16},{28,24},{20,28},{12,20},{4,12},{1,4},{9,1},{1... | collective-permute-start | bytes 786440 | tf_op jit(solution)/shard_map/ppermute | solution.py:930
  61.2 10.3 %collective-permute-start.4 = (f32[4,8,16,128]{3,2,1,0:T(8,128)S(1)}, f32[4,8,16,128]{3,2,1,0:T(8,128)S(1)}, u32[]{:S(2)}, u32[]{:S(2)}) collective-permute-start(f32[4,8,16,128]{3,2,1,0:T(8,128)S(1)} %shard_map.80.refs_6_), channel_id=1, source_target_pairs={{0,8},{8,16},{16,24},{24,28},{28,20},{20,12},{12,4},{4,1},{1,9},{9... | collective-permute-start | bytes 786440 | tf_op jit(solution)/shard_map/ppermute | solution.py:929
  65.8 12.6 %all-to-all-start.2 = ((f32[32,1,128]{2,1,0:T(1,128)}), f32[32,1,128]{2,1,0:T(1,128)S(1)}, u32[]{:S(2)}, u32[]{:S(2)}) async-start(f32[32,1,128]{2,1,0:T(1,128)} %bitcast.4), calls=%async_computation.2 | async-start | bytes 32768 | tf_op jit(solution)/shard_map/all_to_all | solution.py:927

commit v15 on v13

--- a/solution.py
+++ b/solution.py
@@ -645,16 +645,20 @@
     b, m, n_rows = geo.slab, geo.margin, geo.rows
     granule = geo.block[1]
 
-    for f in range(FIELDS):
+    def place(f, _):
         groups = []
         for source, base in ((low, m - b), (own, m), (high, m + b)):
             for u in range(0, b, SUB):
-                row = f * b + u
-                tiles = [source[q, row : row + SUB, :] for q in range(geo.group)]
+                row = pl.multiple_of(f * b, b) + u
+                tiles = [source[q, pl.ds(row, SUB), :] for q in range(geo.group)]
                 groups.append((base + u, tiles))
+        groups = [(row, gather_tiles(tiles, granule)) for row, tiles in groups]
         for row, tiles in groups:
-            for x, tile in enumerate(gather_tiles(tiles, granule)):
+            for x, tile in enumerate(tiles):
                 raw[f, x, row : row + SUB, :] = tile
+        return 0
+
+    lax.fori_loop(0, FIELDS, place, 0)
     for source, base in ((low_edge, m - b - EDGE), (high_edge, m + 2 * b)):
         tiles = [source[q] for q in range(geo.group)]
         for x, tile in enumerate(gather_tiles(tiles, granule)):

time: 91.9 us -> 86.7 us (0.943)
  Pallas kernels: 24.9 us -> 19.7 us
    pallas_call x6, Pallas kernels: 24.9 us -> 19.7 us  [call(): pl.pallas_call(kernel, out_shape=[jax.ShapeDtypeStruct(s, f32) for s in o...]
where the time goes in v15:
time: 86.7 us; the launch traced here: 86.3 us
  blocking collectives  36.2 us (42%)
  starting transfers between devices  20.2 us (23%)
  Pallas kernels  19.7 us (23%)
  waiting for transfers between devices  9.43 us (11%)
    pallas_call x6, Pallas kernels, call(): pl.pallas_call(kernel, out_shape=[jax.ShapeDtypeStruct(s, f32) for s in o...  19.7 us
    all_to_all x1, blocking collectives, slab_shards(): own = lax.all_to_all(chunks, ('gx', 'gy'), 0, 0, tiled=True)  19.4 us
    all_to_all x1, blocking collectives, slab_shards(): chunks = lax.all_to_all(chunks, ('gx', 'gy'), 0, 0, tiled=True)  16.8 us
    ppermute x1, waiting for transfers between devices, slab_shards(): low_edge = lax.ppermute(edges[1], axes, geo.shifts(2))  4.92 us
    ppermute x1, starting transfers between devices, slab_shards(): low = lax.ppermute(own, axes, geo.shifts(1))  4.57 us
    ppermute x1, starting transfers between devices, slab_shards(): from_low = lax.ppermute(up, axes, geo.shifts(1))  4.57 us
    all_to_all x1, starting transfers between devices, slab_shards(): sums = lax.all_to_all(sums, axes, 0, 0, tiled=True)  4.45 us
    ppermute x1, starting transfers between devices, slab_shards(): low_edge = lax.ppermute(edges[1], axes, geo.shifts(2))  2.75 us
  transfers between devices with their start and end apart: 7, of which 4 were waited for; matrix products, arithmetic and copies ran while one was open for 0% of the time, Pallas kernels for 5%

profile of v15, /device:TPU:0, one launch (start us, length us, event | category | flops | bytes accessed | tf_op | source)
XLA Modules:
  0.0 86.3 jit_solution(6777592857422297273)
XLA Ops:
  0.6 2.1 %shard_map.76 = f32[8,96,128]{2,1,0:T(8,128)} custom-call(f32[8,16,128]{2,1,0:T(8,128)} %heat_in.1, f32[3,8,16,128]{3,2,1,0:T(8,128)} %flow_in.1, f32[8,16,128]{2,1,0:T(8,128)} %dual_in.1, s32[8,16,128]{2,1,0:T(8,128)} %kind_in.1), custom_call_target="tpu_custom_call" | custom-call | flops 2000000 | bytes 2000000 | tf_op jit(solution)/shard_map/pallas_call | solution.py:846
  2.7 19.4 %all_to_all.21.own = f32[8,96,128]{2,1,0:T(8,128)S(1)} all-to-all(f32[8,96,128]{2,1,0:T(8,128)} %shard_map.76), channel_id=1, replica_groups=mesh['gx'=4,'gy'=2,'gz'=4] {'gx','gy'}, dimensions={0} | all-to-all | bytes 786432 | tf_op jit(solution)/shard_map/all_to_all | solution.py:868
  22.1 1.3 %collective-permute-start.1 = (f32[8,96,128]{2,1,0:T(8,128)S(1)}, f32[8,96,128]{2,1,0:T(8,128)S(1)}, u32[]{:S(2)}, u32[]{:S(2)}) collective-permute-start(f32[8,96,128]{2,1,0:T(8,128)S(1)} %all_to_all.21.own), channel_id=1, source_target_pairs={{8,0},{16,8},{24,16},{28,24},{20,28},{12,20},{4,12},{1,4},{9,1},{1... | collective-permute-start | bytes 1179656 | tf_op jit(solution)/shard_map/ppermute | solution.py:871
  23.4 4.6 %collective-permute-start = (f32[8,96,128]{2,1,0:T(8,128)S(1)}, f32[8,96,128]{2,1,0:T(8,128)S(1)}, u32[]{:S(2)}, u32[]{:S(2)}) collective-permute-start(f32[8,96,128]{2,1,0:T(8,128)S(1)} %all_to_all.21.own), channel_id=1, source_target_pairs={{0,8},{8,16},{16,24},{24,28},{28,20},{20,12},{12,4},{4,1},{1,9},{9... | collective-permute-start | bytes 1179656 | tf_op jit(solution)/shard_map/ppermute | solution.py:870
  28.0 0.0 copy-start
  28.0 2.8 %collective-permute-start.2 = (f32[8,8,128]{2,1,0:T(8,128)S(1)}, f32[8,8,128]{2,1,0:T(8,128)S(1)}, u32[]{:S(2)}, u32[]{:S(2)}) collective-permute-start(f32[8,8,128]{2,1,0:T(8,128)S(1)} %get-tuple-element.16), channel_id=1, source_target_pairs={{0,16},{8,24},{16,28},{24,20},{28,12},{20,4},{12,1},{4,9},{1,17},{... | collective-permute-start | bytes 98312 | tf_op jit(solution)/shard_map/ppermute | solution.py:874
  30.8 1.3 %collective-permute-start.3 = (f32[8,8,128]{2,1,0:T(8,128)S(1)}, f32[8,8,128]{2,1,0:T(8,128)S(1)}, u32[]{:S(2)}, u32[]{:S(2)}) collective-permute-start(f32[8,8,128]{2,1,0:T(8,128)S(1)} %get-tuple-element.17), channel_id=1, source_target_pairs={{16,0},{24,8},{28,16},{20,24},{12,28},{4,20},{1,12},{9,4},{17,1},{... | collective-permute-start | bytes 98312 | tf_op jit(solution)/shard_map/ppermute | solution.py:873
  32.1 4.9 %collective-permute-done.2.low_edge = f32[8,8,128]{2,1,0:T(8,128)S(1)} collective-permute-done((f32[8,8,128]{2,1,0:T(8,128)S(1)}, f32[8,8,128]{2,1,0:T(8,128)S(1)}, u32[]{:S(2)}, u32[]{:S(2)}) %collective-permute-start.2) | collective-permute-done | bytes 32800 | tf_op jit(solution)/shard_map/ppermute | solution.py:874
  37.0 0.5 collective-permute-done.3.high_edge
  37.5 0.0 collective-permute-done.1.high
  37.5 0.0 collective-permute-done.low
  37.5 0.0 copy-done
  37.5 11.9 %shard_map.78 = (f32[8,48,128]{2,1,0:T(8,128)S(1)}, f32[8,48,128]{2,1,0:T(8,128)S(1)}, f32[8,48,128]{2,1,0:T(8,128)S(1)}, f32[8,48,128]{2,1,0:T(8,128)S(1)}, f32...) custom-call(f32[8]{0:T(128)S(1)} %copy-done, ...), custom_call_target="tpu_custom_call" | custom-call | flops 60000000 | bytes 60000000 | tf_op jit(solution)/shard_map/pallas_call | solution.py:846
  49.4 1.3 %collective-permute-start.5 = (f32[8,96,128]{2,1,0:T(8,128)S(1)}, f32[8,96,128]{2,1,0:T(8,128)S(1)}, u32[]{:S(2)}, u32[]{:S(2)}) collective-permute-start(f32[8,96,128]{2,1,0:T(8,128)S(1)} %get-tuple-element.25.refs_6_.down), channel_id=1, source_target_pairs={{8,0},{16,8},{24,16},{28,24},{20,28},{12,20},{4,12},{1,4},{9,1},{1... | collective-permute-start | bytes 1179656 | tf_op jit(solution)/shard_map/ppermute | solution.py:903
  50.7 4.6 %collective-permute-start.4 = (f32[8,96,128]{2,1,0:T(8,128)S(1)}, f32[8,96,128]{2,1,0:T(8,128)S(1)}, u32[]{:S(2)}, u32[]{:S(2)}) collective-permute-start(f32[8,96,128]{2,1,0:T(8,128)S(1)} %get-tuple-element.26.refs_7_.up), channel_id=1, source_target_pairs={{0,8},{8,16},{16,24},{24,28},{28,20},{20,12},{12,4},{4,1},{1,9},{9... | collective-permute-start | bytes 1179656 | tf_op jit(solution)/shard_map/ppermute | solution.py:902
  55.3 4.5 %all-to-all-start.1 = ((f32[32,1,128]{2,1,0:T(1,128)}), f32[32,1,128]{2,1,0:T(1,128)S(1)}, u32[]{:S(2)}, u32[]{:S(2)}) async-start(f32[32,1,128]{2,1,0:T(1,128)} %bitcast.1), calls=%async_computation.1 | async-start | bytes 32768 | tf_op jit(solution)/shard_map/all_to_all | solution.py:904
  59.7 2.7 %collective-permute-done.5.refs_9_ = f32[8,96,128]{2,1,0:T(8,128)S(1)} collective-permute-done((f32[8,96,128]{2,1,0:T(8,128)S(1)}, f32[8,96,128]{2,1,0:T(8,128)S(1)}, u32[]{:S(2)}, u32[]{:S(2)}) %collective-permute-start.5) | collective-permute-done | bytes 393248 | tf_op jit(solution)/shard_map/ppermute | solution.py:903
  62.5 1.3 %collective-permute-done.4.refs_8_ = f32[8,96,128]{2,1,0:T(8,128)S(1)} collective-permute-done((f32[8,96,128]{2,1,0:T(8,128)S(1)}, f32[8,96,128]{2,1,0:T(8,128)S(1)}, u32[]{:S(2)}, u32[]{:S(2)}) %collective-permute-start.4) | collective-permute-done | bytes 393248 | tf_op jit(solution)/shard_map/ppermute | solution.py:902
  63.8 4.2 %shard_map.79.final = f32[8,8,16,128]{3,2,1,0:T(8,128)S(1)} custom-call(f32[8,48,128]{2,1,0:T(8,128)S(1)} %get-tuple-element.19.refs_0_, f32[8,48,128]{2,1,0:T(8,128)S(1)} %get-tuple-element.20.refs_1_, f32[8,48,128]{2,1,0:T(8,128)S(1)} %get-tuple-element.21.refs_2_, f32[8,48,128]{2,1,0:T(8,128)S(1)} %get-tuple-element.22.refs_3_, ...), custom_call_target="tpu_custom_call" | custom-call | flops 30000000 | bytes 30000000 | tf_op jit(solution)/shard_map/pallas_call | solution.py:846
  67.9 0.0 all-to-all-done.1
  68.0 0.7 shard_map.80
  68.6 16.8 %all_to_all.22.chunks = f32[8,80,128]{2,1,0:T(8,128)S(1)} all-to-all(f32[8,80,128]{2,1,0:T(8,128)S(1)} %shard_map.80), channel_id=1, replica_groups=mesh['gx'=4,'gy'=2,'gz'=4] {'gx','gy'}, dimensions={0} | all-to-all | bytes 655360 | tf_op jit(solution)/shard_map/all_to_all | solution.py:927
  85.5 0.9 shard_map.81
  (1 shorter events, 0.0 us)
Async XLA Ops:
  22.1 15.4 %collective-permute-start.1 = (f32[8,96,128]{2,1,0:T(8,128)S(1)}, f32[8,96,128]{2,1,0:T(8,128)S(1)}, u32[]{:S(2)}, u32[]{:S(2)}) collective-permute-start(f32[8,96,128]{2,1,0:T(8,128)S(1)} %all_to_all.21.own), channel_id=1, source_target_pairs={{8,0},{16,8},{24,16},{28,24},{20,28},{12,20},{4,12},{1,4},{9,1},{1... | collective-permute-start | bytes 1179656 | tf_op jit(solution)/shard_map/ppermute | solution.py:871
  23.4 14.1 %collective-permute-start = (f32[8,96,128]{2,1,0:T(8,128)S(1)}, f32[8,96,128]{2,1,0:T(8,128)S(1)}, u32[]{:S(2)}, u32[]{:S(2)}) collective-permute-start(f32[8,96,128]{2,1,0:T(8,128)S(1)} %all_to_all.21.own), channel_id=1, source_target_pairs={{0,8},{8,16},{16,24},{24,28},{28,20},{20,12},{12,4},{4,1},{1,9},{9... | collective-permute-start | bytes 1179656 | tf_op jit(solution)/shard_map/ppermute | solution.py:870
  28.0 9.5 %copy-start = (f32[8]{0:T(128)S(1)}, f32[8]{0:T(128)}, u32[]{:S(2)}) copy-start(f32[8]{0:T(128)} %stiffness.1) | copy-start | bytes 100
  28.0 9.0 %collective-permute-start.2 = (f32[8,8,128]{2,1,0:T(8,128)S(1)}, f32[8,8,128]{2,1,0:T(8,128)S(1)}, u32[]{:S(2)}, u32[]{:S(2)}) collective-permute-start(f32[8,8,128]{2,1,0:T(8,128)S(1)} %get-tuple-element.16), channel_id=1, source_target_pairs={{0,16},{8,24},{16,28},{24,20},{28,12},{20,4},{12,1},{4,9},{1,17},{... | collective-permute-start | bytes 98312 | tf_op jit(solution)/shard_map/ppermute | solution.py:874
  30.8 6.7 %collective-permute-start.3 = (f32[8,8,128]{2,1,0:T(8,128)S(1)}, f32[8,8,128]{2,1,0:T(8,128)S(1)}, u32[]{:S(2)}, u32[]{:S(2)}) collective-permute-start(f32[8,8,128]{2,1,0:T(8,128)S(1)} %get-tuple-element.17), channel_id=1, source_target_pairs={{16,0},{24,8},{28,16},{20,24},{12,28},{4,20},{1,12},{9,4},{17,1},{... | collective-permute-start | bytes 98312 | tf_op jit(solution)/shard_map/ppermute | solution.py:873
  49.4 13.0 %collective-permute-start.5 = (f32[8,96,128]{2,1,0:T(8,128)S(1)}, f32[8,96,128]{2,1,0:T(8,128)S(1)}, u32[]{:S(2)}, u32[]{:S(2)}) collective-permute-start(f32[8,96,128]{2,1,0:T(8,128)S(1)} %get-tuple-element.25.refs_6_.down), channel_id=1, source_target_pairs={{8,0},{16,8},{24,16},{28,24},{20,28},{12,20},{4,12},{1,4},{9,1},{1... | collective-permute-start | bytes 1179656 | tf_op jit(solution)/shard_map/ppermute | solution.py:903
  50.7 13.1 %collective-permute-start.4 = (f32[8,96,128]{2,1,0:T(8,128)S(1)}, f32[8,96,128]{2,1,0:T(8,128)S(1)}, u32[]{:S(2)}, u32[]{:S(2)}) collective-permute-start(f32[8,96,128]{2,1,0:T(8,128)S(1)} %get-tuple-element.26.refs_7_.up), channel_id=1, source_target_pairs={{0,8},{8,16},{16,24},{24,28},{28,20},{20,12},{12,4},{4,1},{1,9},{9... | collective-permute-start | bytes 1179656 | tf_op jit(solution)/shard_map/ppermute | solution.py:902
  55.3 12.7 %all-to-all-start.1 = ((f32[32,1,128]{2,1,0:T(1,128)}), f32[32,1,128]{2,1,0:T(1,128)S(1)}, u32[]{:S(2)}, u32[]{:S(2)}) async-start(f32[32,1,128]{2,1,0:T(1,128)} %bitcast.1), calls=%async_computation.1 | async-start | bytes 32768 | tf_op jit(solution)/shard_map/all_to_all | solution.py:904

commit v16 on v15

--- a/solution.py
+++ b/solution.py
@@ -355,6 +355,7 @@
         self.lane = lax.broadcasted_iota(jnp.int32, (SUB, LANES), 1)
         self.y = self.lane % self.span
         self.kept, self.latest, self.sweep = {}, None, 0
+        self.masked, self.done, self.trimmed = True, None, None
 
     def sliding(self, ref, z, lead, t, shift=0):
         if self.latest != (self.sweep, z):
@@ -377,14 +378,27 @@
             return load(t + step * stride)
         if step > 0:
             turned = pltpu.roll(load(t % stride), LANES - self.span, 1)
-            return jnp.where(self.lane < LANES - self.span, turned, 0.0)
+            return self.keep(self.lane < LANES - self.span, turned)
         turned = pltpu.roll(load((count - 1) * stride + t % stride), self.span, 1)
-        return jnp.where(self.lane >= self.span, turned, 0.0)
+        return self.keep(self.lane >= self.span, turned)
 
     def lanes(self, f, step):
         if step > 0:
-            return jnp.where(self.y < self.span - 1, pltpu.roll(f, LANES - 1, 1), 0.0)
-        return jnp.where(self.y > 0, pltpu.roll(f, 1, 1), 0.0)
+            return self.keep(self.y < self.span - 1, pltpu.roll(f, LANES - 1, 1))
+        return self.keep(self.y > 0, pltpu.roll(f, 1, 1))
+
+    def keep(self, inside, f):
+        return jnp.where(inside, f, 0.0) if self.masked else f
+
+    def cut(self, face, t):
+        if self.done is not face:
+            a, b, c, d, e, f = face
+            a = jnp.where(self.lane < LANES - self.span, a, 0.0) if t // TY == TX - 1 else a
+            b = jnp.where(self.lane >= self.span, b, 0.0) if t // TY == 0 else b
+            c = jnp.where(self.y < self.span - 1, c, 0.0) if t % TY else c
+            d = d if t % TY else jnp.where(self.y > 0, d, 0.0)
+            self.done, self.trimmed = face, [a, b, c, d, e, f]
+        return self.trimmed
 
     def y_side(self, load, t, step):
         if (t % TY == 0) == (step > 0):
@@ -507,8 +521,10 @@
         return st.faces(tl, z, t)
 
     def around(face, ref, c, t, z):
+        tl.masked = False
         f, near = tl.beside(ref, z, (c,), t)
-        return f, tree([a * b for a, b in zip(face, near)])
+        tl.masked = True
+        return f, tree([a * b for a, b in zip(tl.cut(face, t), near)])
 
     def residual(z, put):
         for t in range(SUB):

time: 86.7 us -> 86.8 us (level)
  no operation moved by 1% of the time
where the time goes in v16:
time: 86.8 us; the launch traced here: 86.4 us
  blocking collectives  36.2 us (42%)
  starting transfers between devices  20.2 us (23%)
  Pallas kernels  19.8 us (23%)
  waiting for transfers between devices  9.43 us (11%)
    pallas_call x6, Pallas kernels, call(): pl.pallas_call(kernel, out_shape=[jax.ShapeDtypeStruct(s, f32) for s in o...  19.8 us
    all_to_all x1, blocking collectives, slab_shards(): own = lax.all_to_all(chunks, ('gx', 'gy'), 0, 0, tiled=True)  19.4 us
    all_to_all x1, blocking collectives, slab_shards(): chunks = lax.all_to_all(chunks, ('gx', 'gy'), 0, 0, tiled=True)  16.8 us
    ppermute x1, waiting for transfers between devices, slab_shards(): low_edge = lax.ppermute(edges[1], axes, geo.shifts(2))  4.92 us
    ppermute x1, starting transfers between devices, slab_shards(): low = lax.ppermute(own, axes, geo.shifts(1))  4.57 us
    ppermute x1, starting transfers between devices, slab_shards(): from_low = lax.ppermute(up, axes, geo.shifts(1))  4.57 us
    all_to_all x1, starting transfers between devices, slab_shards(): sums = lax.all_to_all(sums, axes, 0, 0, tiled=True)  4.45 us
    ppermute x1, starting transfers between devices, slab_shards(): low_edge = lax.ppermute(edges[1], axes, geo.shifts(2))  2.75 us
  transfers between devices with their start and end apart: 7, of which 4 were waited for; matrix products, arithmetic and copies ran while one was open for 0% of the time, Pallas kernels for 5%

profile of v16, /device:TPU:0, one launch (start us, length us, event | category | flops | bytes accessed | tf_op | source)
XLA Modules:
  0.0 86.4 jit_solution(5081995036888172580)
XLA Ops:
  0.6 2.1 %shard_map.76 = f32[8,96,128]{2,1,0:T(8,128)} custom-call(f32[8,16,128]{2,1,0:T(8,128)} %heat_in.1, f32[3,8,16,128]{3,2,1,0:T(8,128)} %flow_in.1, f32[8,16,128]{2,1,0:T(8,128)} %dual_in.1, s32[8,16,128]{2,1,0:T(8,128)} %kind_in.1), custom_call_target="tpu_custom_call" | custom-call | flops 2000000 | bytes 2000000 | tf_op jit(solution)/shard_map/pallas_call | solution.py:862
  2.7 19.4 %all_to_all.21.own = f32[8,96,128]{2,1,0:T(8,128)S(1)} all-to-all(f32[8,96,128]{2,1,0:T(8,128)} %shard_map.76), channel_id=1, replica_groups=mesh['gx'=4,'gy'=2,'gz'=4] {'gx','gy'}, dimensions={0} | all-to-all | bytes 786432 | tf_op jit(solution)/shard_map/all_to_all | solution.py:884
  22.1 1.3 %collective-permute-start.1 = (f32[8,96,128]{2,1,0:T(8,128)S(1)}, f32[8,96,128]{2,1,0:T(8,128)S(1)}, u32[]{:S(2)}, u32[]{:S(2)}) collective-permute-start(f32[8,96,128]{2,1,0:T(8,128)S(1)} %all_to_all.21.own), channel_id=1, source_target_pairs={{8,0},{16,8},{24,16},{28,24},{20,28},{12,20},{4,12},{1,4},{9,1},{1... | collective-permute-start | bytes 1179656 | tf_op jit(solution)/shard_map/ppermute | solution.py:887
  23.4 4.6 %collective-permute-start = (f32[8,96,128]{2,1,0:T(8,128)S(1)}, f32[8,96,128]{2,1,0:T(8,128)S(1)}, u32[]{:S(2)}, u32[]{:S(2)}) collective-permute-start(f32[8,96,128]{2,1,0:T(8,128)S(1)} %all_to_all.21.own), channel_id=1, source_target_pairs={{0,8},{8,16},{16,24},{24,28},{28,20},{20,12},{12,4},{4,1},{1,9},{9... | collective-permute-start | bytes 1179656 | tf_op jit(solution)/shard_map/ppermute | solution.py:886
  28.0 0.0 copy-start
  28.0 2.8 %collective-permute-start.2 = (f32[8,8,128]{2,1,0:T(8,128)S(1)}, f32[8,8,128]{2,1,0:T(8,128)S(1)}, u32[]{:S(2)}, u32[]{:S(2)}) collective-permute-start(f32[8,8,128]{2,1,0:T(8,128)S(1)} %get-tuple-element.16), channel_id=1, source_target_pairs={{0,16},{8,24},{16,28},{24,20},{28,12},{20,4},{12,1},{4,9},{1,17},{... | collective-permute-start | bytes 98312 | tf_op jit(solution)/shard_map/ppermute | solution.py:890
  30.8 1.3 %collective-permute-start.3 = (f32[8,8,128]{2,1,0:T(8,128)S(1)}, f32[8,8,128]{2,1,0:T(8,128)S(1)}, u32[]{:S(2)}, u32[]{:S(2)}) collective-permute-start(f32[8,8,128]{2,1,0:T(8,128)S(1)} %get-tuple-element.17), channel_id=1, source_target_pairs={{16,0},{24,8},{28,16},{20,24},{12,28},{4,20},{1,12},{9,4},{17,1},{... | collective-permute-start | bytes 98312 | tf_op jit(solution)/shard_map/ppermute | solution.py:889
  32.1 4.9 %collective-permute-done.2.low_edge = f32[8,8,128]{2,1,0:T(8,128)S(1)} collective-permute-done((f32[8,8,128]{2,1,0:T(8,128)S(1)}, f32[8,8,128]{2,1,0:T(8,128)S(1)}, u32[]{:S(2)}, u32[]{:S(2)}) %collective-permute-start.2) | collective-permute-done | bytes 32800 | tf_op jit(solution)/shard_map/ppermute | solution.py:890
  37.0 0.5 collective-permute-done.3.high_edge
  37.5 0.0 collective-permute-done.1.high
  37.5 0.0 collective-permute-done.low
  37.5 0.0 copy-done
  37.5 12.0 %shard_map.78 = (f32[8,48,128]{2,1,0:T(8,128)S(1)}, f32[8,48,128]{2,1,0:T(8,128)S(1)}, f32[8,48,128]{2,1,0:T(8,128)S(1)}, f32[8,48,128]{2,1,0:T(8,128)S(1)}, f32...) custom-call(f32[8]{0:T(128)S(1)} %copy-done, ...), custom_call_target="tpu_custom_call" | custom-call | flops 60000000 | bytes 60000000 | tf_op jit(solution)/shard_map/pallas_call | solution.py:862
  49.5 1.3 %collective-permute-start.5 = (f32[8,96,128]{2,1,0:T(8,128)S(1)}, f32[8,96,128]{2,1,0:T(8,128)S(1)}, u32[]{:S(2)}, u32[]{:S(2)}) collective-permute-start(f32[8,96,128]{2,1,0:T(8,128)S(1)} %get-tuple-element.25.refs_6_.down), channel_id=1, source_target_pairs={{8,0},{16,8},{24,16},{28,24},{20,28},{12,20},{4,12},{1,4},{9,1},{1... | collective-permute-start | bytes 1179656 | tf_op jit(solution)/shard_map/ppermute | solution.py:919
  50.8 4.6 %collective-permute-start.4 = (f32[8,96,128]{2,1,0:T(8,128)S(1)}, f32[8,96,128]{2,1,0:T(8,128)S(1)}, u32[]{:S(2)}, u32[]{:S(2)}) collective-permute-start(f32[8,96,128]{2,1,0:T(8,128)S(1)} %get-tuple-element.26.refs_7_.up), channel_id=1, source_target_pairs={{0,8},{8,16},{16,24},{24,28},{28,20},{20,12},{12,4},{4,1},{1,9},{9... | collective-permute-start | bytes 1179656 | tf_op jit(solution)/shard_map/ppermute | solution.py:918
  55.4 4.5 %all-to-all-start.1 = ((f32[32,1,128]{2,1,0:T(1,128)}), f32[32,1,128]{2,1,0:T(1,128)S(1)}, u32[]{:S(2)}, u32[]{:S(2)}) async-start(f32[32,1,128]{2,1,0:T(1,128)} %bitcast.1), calls=%async_computation.1 | async-start | bytes 32768 | tf_op jit(solution)/shard_map/all_to_all | solution.py:920
  59.8 2.7 %collective-permute-done.5.refs_9_ = f32[8,96,128]{2,1,0:T(8,128)S(1)} collective-permute-done((f32[8,96,128]{2,1,0:T(8,128)S(1)}, f32[8,96,128]{2,1,0:T(8,128)S(1)}, u32[]{:S(2)}, u32[]{:S(2)}) %collective-permute-start.5) | collective-permute-done | bytes 393248 | tf_op jit(solution)/shard_map/ppermute | solution.py:919
  62.5 1.3 %collective-permute-done.4.refs_8_ = f32[8,96,128]{2,1,0:T(8,128)S(1)} collective-permute-done((f32[8,96,128]{2,1,0:T(8,128)S(1)}, f32[8,96,128]{2,1,0:T(8,128)S(1)}, u32[]{:S(2)}, u32[]{:S(2)}) %collective-permute-start.4) | collective-permute-done | bytes 393248 | tf_op jit(solution)/shard_map/ppermute | solution.py:918
  63.8 4.1 %shard_map.79.final = f32[8,8,16,128]{3,2,1,0:T(8,128)S(1)} custom-call(f32[8,48,128]{2,1,0:T(8,128)S(1)} %get-tuple-element.19.refs_0_, f32[8,48,128]{2,1,0:T(8,128)S(1)} %get-tuple-element.20.refs_1_, f32[8,48,128]{2,1,0:T(8,128)S(1)} %get-tuple-element.21.refs_2_, f32[8,48,128]{2,1,0:T(8,128)S(1)} %get-tuple-element.22.refs_3_, ...), custom_call_target="tpu_custom_call" | custom-call | flops 30000000 | bytes 30000000 | tf_op jit(solution)/shard_map/pallas_call | solution.py:862
  68.0 0.0 all-to-all-done.1
  68.0 0.7 shard_map.80
  68.7 16.8 %all_to_all.22.chunks = f32[8,80,128]{2,1,0:T(8,128)S(1)} all-to-all(f32[8,80,128]{2,1,0:T(8,128)S(1)} %shard_map.80), channel_id=1, replica_groups=mesh['gx'=4,'gy'=2,'gz'=4] {'gx','gy'}, dimensions={0} | all-to-all | bytes 655360 | tf_op jit(solution)/shard_map/all_to_all | solution.py:943
  85.5 0.9 shard_map.81
  (1 shorter events, 0.0 us)
Async XLA Ops:
  22.1 15.4 %collective-permute-start.1 = (f32[8,96,128]{2,1,0:T(8,128)S(1)}, f32[8,96,128]{2,1,0:T(8,128)S(1)}, u32[]{:S(2)}, u32[]{:S(2)}) collective-permute-start(f32[8,96,128]{2,1,0:T(8,128)S(1)} %all_to_all.21.own), channel_id=1, source_target_pairs={{8,0},{16,8},{24,16},{28,24},{20,28},{12,20},{4,12},{1,4},{9,1},{1... | collective-permute-start | bytes 1179656 | tf_op jit(solution)/shard_map/ppermute | solution.py:887
  23.4 14.1 %collective-permute-start = (f32[8,96,128]{2,1,0:T(8,128)S(1)}, f32[8,96,128]{2,1,0:T(8,128)S(1)}, u32[]{:S(2)}, u32[]{:S(2)}) collective-permute-start(f32[8,96,128]{2,1,0:T(8,128)S(1)} %all_to_all.21.own), channel_id=1, source_target_pairs={{0,8},{8,16},{16,24},{24,28},{28,20},{20,12},{12,4},{4,1},{1,9},{9... | collective-permute-start | bytes 1179656 | tf_op jit(solution)/shard_map/ppermute | solution.py:886
  28.0 9.5 %copy-start = (f32[8]{0:T(128)S(1)}, f32[8]{0:T(128)}, u32[]{:S(2)}) copy-start(f32[8]{0:T(128)} %stiffness.1) | copy-start | bytes 100
  28.0 9.0 %collective-permute-start.2 = (f32[8,8,128]{2,1,0:T(8,128)S(1)}, f32[8,8,128]{2,1,0:T(8,128)S(1)}, u32[]{:S(2)}, u32[]{:S(2)}) collective-permute-start(f32[8,8,128]{2,1,0:T(8,128)S(1)} %get-tuple-element.16), channel_id=1, source_target_pairs={{0,16},{8,24},{16,28},{24,20},{28,12},{20,4},{12,1},{4,9},{1,17},{... | collective-permute-start | bytes 98312 | tf_op jit(solution)/shard_map/ppermute | solution.py:890
  30.8 6.7 %collective-permute-start.3 = (f32[8,8,128]{2,1,0:T(8,128)S(1)}, f32[8,8,128]{2,1,0:T(8,128)S(1)}, u32[]{:S(2)}, u32[]{:S(2)}) collective-permute-start(f32[8,8,128]{2,1,0:T(8,128)S(1)} %get-tuple-element.17), channel_id=1, source_target_pairs={{16,0},{24,8},{28,16},{20,24},{12,28},{4,20},{1,12},{9,4},{17,1},{... | collective-permute-start | bytes 98312 | tf_op jit(solution)/shard_map/ppermute | solution.py:889
  49.5 13.0 %collective-permute-start.5 = (f32[8,96,128]{2,1,0:T(8,128)S(1)}, f32[8,96,128]{2,1,0:T(8,128)S(1)}, u32[]{:S(2)}, u32[]{:S(2)}) collective-permute-start(f32[8,96,128]{2,1,0:T(8,128)S(1)} %get-tuple-element.25.refs_6_.down), channel_id=1, source_target_pairs={{8,0},{16,8},{24,16},{28,24},{20,28},{12,20},{4,12},{1,4},{9,1},{1... | collective-permute-start | bytes 1179656 | tf_op jit(solution)/shard_map/ppermute | solution.py:919
  50.8 13.1 %collective-permute-start.4 = (f32[8,96,128]{2,1,0:T(8,128)S(1)}, f32[8,96,128]{2,1,0:T(8,128)S(1)}, u32[]{:S(2)}, u32[]{:S(2)}) collective-permute-start(f32[8,96,128]{2,1,0:T(8,128)S(1)} %get-tuple-element.26.refs_7_.up), channel_id=1, source_target_pairs={{0,8},{8,16},{16,24},{24,28},{28,20},{20,12},{12,4},{4,1},{1,9},{9... | collective-permute-start | bytes 1179656 | tf_op jit(solution)/shard_map/ppermute | solution.py:918
  55.4 12.6 %all-to-all-start.1 = ((f32[32,1,128]{2,1,0:T(1,128)}), f32[32,1,128]{2,1,0:T(1,128)S(1)}, u32[]{:S(2)}, u32[]{:S(2)}) async-start(f32[32,1,128]{2,1,0:T(1,128)} %bitcast.1), calls=%async_computation.1 | async-start | bytes 32768 | tf_op jit(solution)/shard_map/all_to_all | solution.py:920
